TPU v7x, 32 devices: a whole 2x2x4 slice. The times are simulated.
32 devices in a mesh: row: 4 (over z), col: 8 (over y, x, core).
Axes of the slice: x: 2, y: 2, z: 4, core: 2. Of those that a mesh axis runs over, the one named last changes fastest.
Arguments:
- amplitudes: bfloat16 [4096, 2048], P('row', 'col'), may hold values from -6 to 6
- amp_mask: int32 [32, 16], P('row', 'col'), may hold values 0 or 1
- integrals: bfloat16 [2048, 16384], P('row', 'col'), may hold values from -0.25 to 0.25
- int_tiles: int32 [4, 8, 32], P(None, 'col'), may hold values from 0 to 64, as said below
- pair_dest: int32 [4096], P('row'), may hold values from 0 to 7, as said below
Outputs:
- moved: bfloat16 [8192, 16384], P(('row', 'col'))
Inputs may be any that keep to these rules, and one draw needn't show every extreme that they name: `int_tiles`: entry t of a list names the nonzero tile (t // 16, t mod 16) of that integral block; the entries naming tiles are distinct, the value 64 marks an empty entry, and some block has all 32 entries filled. `pair_dest`: within each row block of 1024 consecutive pairs no column index is named by more than 256 pairs, and one is named by exactly 256.
All inputs are finite; a program needn't handle non-finite values. No bound on the sum of `amp_mask` on one device may be relied on, other than what follows from the above.
Results may differ from a plain program's by a relative error of at most 0.001.
Values may be sent and summed in bfloat16 or wider, within the bound.
No kernel may reach another device: no remote copies, remote signals or barrier semaphores. Data moves between devices by JAX's collectives and lax.ppermute only.
A program may use at most 128 MiB of HBM per device.

v0:
```python
import jax
import jax.numpy as jnp
from jax import lax
from jax.sharding import PartitionSpec as P

TILE = 128


def on_device(amplitudes, amp_mask, integrals, int_tiles, pair_dest):
    pair_rows, amp_cols = amplitudes.shape
    int_rows, int_cols = integrals.shape
    row_tiles = int_rows // TILE
    col_tiles = int_cols // TILE
    block_tiles = row_tiles * col_tiles
    amp_scale = amp_mask.astype(jnp.bfloat16)
    amp_used = (
        amplitudes.reshape(amp_mask.shape[0], TILE, amp_mask.shape[1], TILE)
        * amp_scale[:, None, :, None]
    ).reshape(pair_rows, amp_cols)
    all_lists = int_tiles[:, 0, :]
    tile_ids = jnp.arange(block_tiles, dtype=jnp.int32)
    own_list = lax.dynamic_index_in_dim(all_lists, lax.axis_index("row"), 0, keepdims=False)
    tile_major = (
        integrals.reshape(row_tiles, TILE, col_tiles, TILE)
        .transpose(0, 2, 1, 3)
        .reshape(block_tiles, TILE * TILE)
    )
    filled = own_list < block_tiles
    picked = jnp.take(tile_major, jnp.minimum(own_list, block_tiles - 1), axis=0)
    packed = jnp.where(filled[:, None], picked, jnp.zeros_like(picked))
    gathered = lax.all_gather(packed[None], "row", axis=0, tiled=True)
    row_count = gathered.shape[0]
    list_len = gathered.shape[1]
    tiles_four = gathered.reshape(row_count, list_len, TILE, TILE)
    selector = (all_lists[:, :, None] == tile_ids[None, None, :]).astype(jnp.bfloat16)
    selector = selector.reshape(row_count, list_len, row_tiles, col_tiles)
    dense_tiles = jnp.einsum(
        "rzkn,rzij->rkinj", selector, tiles_four, preferred_element_type=jnp.bfloat16
    )
    int_panel = dense_tiles.reshape(row_count * int_rows, int_cols)
    ladder = jnp.dot(
        lax.all_gather(amp_used, "col", axis=1, tiled=True),
        int_panel,
        preferred_element_type=jnp.float32,
    ).astype(jnp.bfloat16)
    col_count = lax.axis_size("col")
    capacity = 2 * pair_rows // col_count
    col_ids = jnp.arange(col_count, dtype=jnp.int32)
    onehot = (pair_dest[:, None] == col_ids[None, :]).astype(jnp.int32)
    before = jnp.cumsum(onehot, axis=0) - onehot
    slot_of = jnp.sum(before * onehot, axis=1)
    outgoing = (
        jnp.zeros((col_count, capacity, int_cols), jnp.bfloat16).at[pair_dest, slot_of].set(ladder)
    )
    arrived = lax.all_to_all(outgoing, "col", split_axis=0, concat_axis=2, tiled=True)
    return arrived.reshape(capacity, col_count * int_cols)


def solution(mesh):
    in_specs = (P("row", "col"), P("row", "col"), P("row", "col"), P(None, "col", None), P("row"))
    out_specs = P(("row", "col"), None)
    return jax.shard_map(
        on_device, mesh=mesh, in_specs=in_specs, out_specs=out_specs, check_vma=False
    )
```

profile of v0, /device:TPU:0, one launch (start us, length us, event | category | flops | bytes accessed | tf_op | source)
XLA Modules:
  0.0 294.1 jit_solution(1683987705869560508)
XLA Ops:
  6.5 0.0 all-gather.5.cloned.1.call-start
  6.5 0.7 fusion.16
  7.2 0.7 compare_and_fusion
  7.9 0.7 compare_bitcast_fusion
  8.5 2.2 copy.30
  10.7 0.5 copy.19
  11.3 1.4 copy.43
  12.7 0.0 copy-start.4
  12.7 1.2 gather_fusion
  13.9 0.0 copy-start
  13.9 0.0 copy-start.3
  13.9 0.0 copy-start.2
  13.9 1.2 fusion.7
  15.1 0.0 all-gather.5.cloned.1.call-update
  15.1 0.2 all-gather.3.cloned.1.call-start
  15.3 0.0 copy-done.4
  15.4 0.1 copy.18
  15.5 0.3 mul.15
  15.8 1.9 bitcast_multiply_fusion
  17.7 0.0 all-gather.3.cloned.1.call-update
  17.8 0.0 copy-done
  17.8 2.3 reduce-window.6
  20.1 0.3 slice_reduce_fusion
  20.4 0.2 reduce-window.9
  20.5 0.1 add_bitcast_fusion
  20.6 0.0 copy-done.3
  20.7 0.1 multiply_reduce_fusion
  20.7 0.0 copy-done.2
  20.8 0.1 and_reduce_fusion
  20.9 77.9 %all-gather.5.cloned.1.call-done = bf16[4,32,16384]{2,1,0:T(8,128)(2,1)} async-done(((bf16[1,32,16384]{2,1,0:T(8,128)(2,1)}), bf16[4,32,16384]{2,1,0:T(8,128)(2,1)}) %all-gather.5.cloned.1.call-update) | async-done | bytes 4194320 | tf_op jit(solution)/shard_map/all_gather | solution.py:31
  98.7 3.4 %copy.32 = bf16[16,8,128,128]{3,2,1,0:T(8,128)(2,1)S(1)} copy(bf16[16,8,128,128]{3,1,2,0:T(8,128)(2,1)} %bitcast.82) | data formatting | bytes 8388608
  102.2 0.0 copy-start.1
  102.2 0.3 bitcast_bitcast_fusion
  102.5 0.4 copy-done.1
  102.8 6.8 %convolution_bitcast_fusion = bf16[4,4,128,16,128]{4,3,1,2,0:T(8,128)(2,1)} fusion(bf16[4,32,128,128,1]{3,2,1,0,4:T(8,128)(2,1)S(1)} %bitcast_bitcast_fusion, s32[4,16]{1,0:T(4,128)S(1)} %multiply_add_fusion, s32[4,32]{1,0:T(4,128)S(1)} %bitcast.88), kind=kOutput, calls=%fused_computation.5 | convolution fusion | flops 268443648 | bytes 12583680 | tf_op jit(solution)/shard_map/rzkn,rzij->rkinj/dot_general | solution.py:37
  109.6 8.6 %copy.21 = bf16[4,4,128,16,128]{4,3,2,1,0:T(8,128)(2,1)} copy(bf16[4,4,128,16,128]{4,3,1,2,0:T(8,128)(2,1)} %convolution_bitcast_fusion) | data formatting | bytes 16777216 | tf_op jit(solution)/shard_map/rzkn,rzij->rkinj/transpose | solution.py:37
  118.2 18.4 %all-gather.3.cloned.1.call-done = bf16[1024,2048]{1,0:T(8,128)(2,1)} async-done(((bf16[1024,256]{1,0:T(8,128)(2,1)}), bf16[1024,2048]{1,0:T(8,128)(2,1)}) %all-gather.3.cloned.1.call-update) | async-done | bytes 4194320 | tf_op jit(solution)/shard_map/all_gather | solution.py:42
  136.6 14.6 %fusion = f32[1024,2048]{1,0:T(8,128)} fusion(bf16[1024,2048]{1,0:T(8,128)(2,1)} %all-gather.3.cloned.1.call-done, bf16[256,8,16,128]{3,2,1,0:T(8,128)(2,1)} %bitcast.79), kind=kOutput, calls=%fused_computation.2 | convolution fusion | flops 8589934592 | bytes 20971520 | tf_op jit(solution)/shard_map/dot_general | solution.py:41
  151.2 13.1 %scatter_custom_fusion = bf16[2048,2048]{1,0:T(8,128)(2,1)} fusion(s32[1024]{0:T(1024)S(1)} %broadcast_select_fusion, bf16[]{:T(256)} %constant.17.clone.1, f32[1024,2048]{1,0:T(8,128)} %fusion), kind=kCustom, calls=%fused_computation.8 | custom fusion | flops 2097152 | bytes 16777218
  164.2 99.7 %all_to_all.15 = bf16[8,256,2048]{2,1,0:T(8,128)(2,1)} all-to-all(bf16[8,256,2048]{2,1,0:T(8,128)(2,1)} %bitcast.75), channel_id=1, replica_groups=mesh['row'=4,'col'=8] {'col'}, dimensions={0} | all-to-all | bytes 16777216 | tf_op jit(solution)/shard_map/all_to_all | solution.py:55
  264.0 11.4 %copy.22 = bf16[1,256,8,2048]{1,3,2,0:T(8,128)(2,1)} copy(bf16[1,256,8,2048]{3,1,2,0:T(8,128)(2,1)} %bitcast.76) | data formatting | bytes 16777216 | tf_op jit(solution)/shard_map/all_to_all | solution.py:55
  275.3 11.9 %copy.23 = bf16[256,16384]{1,0:T(8,128)(2,1)} copy(bf16[256,16384]{0,1:T(8,128)(2,1)} %bitcast.77) | data formatting | bytes 16777216 | tf_op jit(solution)/shard_map/reshape | solution.py:56
  (8 shorter events, 0.1 us)
Async XLA Ops:
  6.5 92.2 %all-gather.5.cloned.1.call-start = ((), (), s32[]{:S(2)}) async-start(), calls=%async_computation.2 | async-start | bytes 5242880 | tf_op jit(solution)/shard_map/all_gather | solution.py:31
  12.7 2.7 copy-start.4
  13.9 3.9 %copy-start = (s32[1024]{0:T(1024)S(1)}, s32[1024]{0:T(1024)}, u32[]{:S(2)}) copy-start(s32[1024]{0:T(1024)} %param.9) | copy-start | bytes 12292
  13.9 6.7 %copy-start.3 = (s32[2]{0:T(128)S(1)}, s32[2]{0:T(128)}, u32[]{:S(2)}) copy-start(s32[2]{0:T(128)} %constant.46) | copy-start | bytes 28
  13.9 6.8 %copy-start.2 = (s32[2]{0:T(128)S(1)}, s32[2]{0:T(128)}, u32[]{:S(2)}) copy-start(s32[2]{0:T(128)} %constant.49) | copy-start | bytes 28
  15.1 121.5 %all-gather.3.cloned.1.call-start = ((), (), s32[]{:S(2)}) async-start(), calls=%async_computation.1 | async-start | bytes 4718592 | tf_op jit(solution)/shard_map/all_gather | solution.py:42
  102.2 0.7 copy-start.1
Sparse Core Ops, SparseCore 0:
  15.2 83.4 all-gather.4
  100.6 35.9 all-gather.2
where the time goes:
time: 295 us; the launch traced here: 294 us
  blocking collectives  99.7 us (34%)
  waiting for transfers between devices  96.3 us (33%)
  local copies, waits for them, and re-layouts  42 us (14%)
  matrix products  21.3 us (7%)
  other arithmetic  20.9 us (7%)
  between operations  13.6 us (5%)
    all_to_all x1, blocking collectives, on_device(): lax.all_to_all(outgoing, 'col', split_axis=0, concat_axis=2, tiled=True)  99.7 us
    all_gather x1, waiting for transfers between devices, on_device(): gathered = lax.all_gather(packed[None], 'row', axis=0, tiled=True)  77.9 us
    all_gather x1, waiting for transfers between devices, on_device(): lax.all_gather(amp_used, 'col', axis=1, tiled=True)  18.4 us
    dot_general x1, matrix products, on_device(): jnp.dot(lax.all_gather(amp_used, 'col', axis=1, tiled=True), int_panel, p...  14.6 us
    unnamed x5, other arithmetic  13.3 us
    reshape x1, local copies, waits for them, and re-layouts, on_device(): return arrived.reshape(capacity, col_count * int_cols)  11.9 us
    all_to_all x1, local copies, waits for them, and re-layouts, on_device(): lax.all_to_all(outgoing, 'col', split_axis=0, concat_axis=2, tiled=True)  11.4 us
    transpose x1, local copies, waits for them, and re-layouts, on_device(): jnp.einsum('rzkn,rzij->rkinj', selector, tiles_four, preferred_element_ty...  8.58 us
  transfers between devices with their start and end apart: 2, of which 2 were waited for; matrix products, arithmetic and copies ran while one was open for 8% of the time, Pallas kernels for 0%

commit v1 on v0

v1 whole, which is shorter than its diff:
```python
import functools

import jax
import jax.numpy as jnp
from jax import lax
from jax.experimental import pallas as pl
from jax.experimental.pallas import tpu as pltpu
from jax.sharding import PartitionSpec as P

TILE = 128
MM_COLS = 512
DENSE_BUDGET = 48 << 20
VMEM_LIMIT = 48 << 20


def params():
    return pltpu.CompilerParams(vmem_limit_bytes=VMEM_LIMIT)


def pack_body(row_ref, ids_ref, src_ref, out_ref, sem):
    col_tiles = src_ref.shape[1] // TILE
    tiles = col_tiles * (src_ref.shape[0] // TILE)
    for e in range(out_ref.shape[0]):
        t = jnp.minimum(ids_ref[row_ref[0], e], tiles - 1)
        k = pl.multiple_of(lax.div(t, col_tiles) * TILE, TILE)
        n = pl.multiple_of(lax.rem(t, col_tiles) * TILE, TILE)
        pltpu.make_async_copy(src_ref.at[pl.ds(k, TILE), pl.ds(n, TILE)], out_ref.at[e], sem).start()
    pltpu.make_async_copy(out_ref, out_ref, sem).wait()


def pack(row, lists, integrals):
    count = lists.shape[1]
    return pl.pallas_call(
        pack_body,
        out_shape=jax.ShapeDtypeStruct((count, TILE, TILE), integrals.dtype),
        in_specs=[
            pl.BlockSpec(memory_space=pltpu.SMEM),
            pl.BlockSpec(memory_space=pltpu.SMEM),
            pl.BlockSpec(memory_space=pl.ANY),
        ],
        out_specs=pl.BlockSpec(memory_space=pltpu.VMEM),
        scratch_shapes=[pltpu.SemaphoreType.DMA],
        compiler_params=params(),
        name="pack_tiles",
    )(row, lists, integrals)


def densify_body(row_ref, ids_ref, packed_ref, *rest):
    out_ref = rest[-1]
    col_tiles = out_ref.shape[1] // TILE
    tiles = col_tiles * (out_ref.shape[0] // TILE)
    out_ref[...] = jnp.zeros_like(out_ref)
    for e in range(packed_ref.shape[0]):
        t = ids_ref[row_ref[0], e]

        @pl.when(t < tiles)
        def _():
            k = pl.multiple_of(lax.div(t, col_tiles) * TILE, TILE)
            n = pl.multiple_of(lax.rem(t, col_tiles) * TILE, TILE)
            out_ref[pl.ds(k, TILE), pl.ds(n, TILE)] = packed_ref[e]


def densify(row, lists, packed, dense, shape, block_rows):
    in_specs = [pl.BlockSpec(packed.shape, lambda i, r, l: (0, 0, 0))]
    operands = [row, lists, packed]
    aliases = {}
    if dense is not None:
        in_specs.append(pl.BlockSpec(memory_space=pl.ANY))
        operands.append(dense)
        aliases = {3: 0}
    return pl.pallas_call(
        densify_body,
        out_shape=jax.ShapeDtypeStruct(shape, packed.dtype),
        grid_spec=pltpu.PrefetchScalarGridSpec(
            num_scalar_prefetch=2,
            grid=(1,),
            in_specs=in_specs,
            out_specs=pl.BlockSpec((block_rows, shape[1]), lambda i, r, l: (r[0], 0)),
        ),
        input_output_aliases=aliases,
        compiler_params=params(),
        cost_estimate=pl.CostEstimate(flops=0, bytes_accessed=6 * block_rows * shape[1], transcendentals=0),
        name="densify",
    )(*operands)


def multiply_body(place_ref, lhs_ref, rhs_ref, *rest):
    out_ref = rest[-1]
    out_ref[...] = jnp.dot(lhs_ref[0], rhs_ref[...], preferred_element_type=jnp.float32).astype(out_ref.dtype)


def multiply(lhs, which, dense, whole=None, total_cols=None, place=None):
    _, m, k = lhs.shape
    n = dense.shape[1]
    width = min(MM_COLS, n)
    steps = n // width
    own = total_cols is None
    scalars = jnp.stack([which, jnp.int32(0) if own else place]).astype(jnp.int32)
    in_specs = [
        pl.BlockSpec((1, m, k), lambda i, s: (s[0], 0, 0)),
        pl.BlockSpec((k, width), lambda i, s: (0, i)),
    ]
    operands = [scalars, lhs, dense]
    aliases = {}
    if whole is not None:
        in_specs.append(pl.BlockSpec(memory_space=pl.ANY))
        operands.append(whole)
        aliases = {3: 0}
    return pl.pallas_call(
        multiply_body,
        out_shape=jax.ShapeDtypeStruct((m, n if own else total_cols), lhs.dtype),
        grid_spec=pltpu.PrefetchScalarGridSpec(
            num_scalar_prefetch=1,
            grid=(steps,),
            in_specs=in_specs,
            out_specs=pl.BlockSpec((m, width), lambda i, s: (0, s[1] * steps + i)),
        ),
        input_output_aliases=aliases,
        compiler_params=params(),
        cost_estimate=pl.CostEstimate(flops=2 * m * k * n, bytes_accessed=2 * (m * k + k * n + m * n), transcendentals=0),
        name="multiply",
    )(*operands)


def place_body(place_ref, piece_ref, whole_ref, out_ref):
    out_ref[...] = piece_ref[...]


def put(piece, whole, place):
    m, n = piece.shape
    width = min(2 * MM_COLS, n)
    steps = n // width
    return pl.pallas_call(
        place_body,
        out_shape=jax.ShapeDtypeStruct(whole.shape, whole.dtype),
        grid_spec=pltpu.PrefetchScalarGridSpec(
            num_scalar_prefetch=1,
            grid=(steps,),
            in_specs=[pl.BlockSpec((m, width), lambda i, s: (0, i)), pl.BlockSpec(memory_space=pl.ANY)],
            out_specs=pl.BlockSpec((m, width), lambda i, s: (0, s[0] * steps + i)),
        ),
        input_output_aliases={2: 0},
        compiler_params=params(),
        cost_estimate=pl.CostEstimate(flops=0, bytes_accessed=4 * m * n, transcendentals=0),
        name="put",
    )(place.astype(jnp.int32).reshape(1), piece, whole)


def col_index(ie, ia, ib, core):
    return ((ie * 2 + ia) * 2 + ib) * 2 + core


def on_device(amplitudes, amp_mask, integrals, int_tiles, pair_dest):
    rows = lax.axis_size("row")
    cols = lax.axis_size("col")
    extra = cols // 8
    pair_rows, amp_cols = amplitudes.shape
    int_rows, int_cols = integrals.shape
    capacity = 2 * pair_rows // cols
    panel_shape = (rows * int_rows, int_cols)
    z = lax.axis_index("row")
    me = lax.axis_index("col")
    core = lax.rem(me, 2)
    ib = lax.rem(lax.div(me, 2), 2)
    ia = lax.rem(lax.div(me, 4), 2)
    ie = lax.div(me, 8)
    every = [(e, a, b, c) for e in range(extra) for a in range(2) for b in range(2) for c in range(2)]

    own_lists = int_tiles[:, 0, :]
    packed = pack(z.astype(jnp.int32).reshape(1), own_lists, integrals)
    up, down = {0: packed}, {0: packed}
    for k in range(1, rows):
        up[k] = lax.ppermute(up[k - 1], "row", [(i + 1, i) for i in range(rows - k)])
        down[k] = lax.ppermute(down[k - 1], "row", [(i, i + 1) for i in range(k - 1, rows - 1)])

    order = []
    for i in range(rows):
        near = [(abs(r - i), 0 if (r > i) == (i < rows // 2) else 1, r - i) for r in range(rows) if r != i]
        order.append([(d, off > 0) for d, _, off in sorted(near)])
    slots, slot_row = [packed], [z]
    for j in range(rows - 1):
        kinds = sorted({order[i][j] for i in range(rows)})
        value, row = None, jnp.int32(0)
        for d, upward in kinds:
            here = functools.reduce(jnp.logical_or, [z == i for i in range(rows) if order[i][j] == (d, upward)])
            source = up[d] if upward else down[d]
            value = source if value is None else jnp.where(here, source, value)
            row = jnp.where(here, z + d if upward else z - d, row)
        slots.append(value)
        slot_row.append(row)
    slot_row = [r.astype(jnp.int32).reshape(1) for r in slot_row]

    along = [
        (col_index(e, a, b, c), col_index(e, a ^ (c == 1), b ^ (c == 0), c)) for e, a, b, c in every
    ]
    across = [(col_index(e, a, b, c), col_index(e, a, b, 1 - c)) for e, a, b, c in every]
    lists_next = lax.ppermute(own_lists, "col", along)
    pair_lists = lax.ppermute(jnp.concatenate([own_lists, lists_next], axis=0), "col", across)
    all_lists = [own_lists, lists_next, pair_lists[:rows], pair_lists[rows:]]
    blocks = [[], [], [], []]
    for slot in slots:
        mine_next = lax.ppermute(slot, "col", along)
        blocks[0].append(slot)
        blocks[1].append(mine_next)
        blocks[2].append(lax.ppermute(slot, "col", across))
        blocks[3].append(lax.ppermute(mine_next, "col", across))

    amp_scale = amp_mask.astype(jnp.bfloat16)
    amp_used = (
        amplitudes.reshape(amp_mask.shape[0], TILE, amp_mask.shape[1], TILE) * amp_scale[:, None, :, None]
    ).reshape(pair_rows, amp_cols)
    amp_all = lax.all_gather(amp_used, "col", axis=1, tiled=True)
    col_ids = jnp.arange(cols, dtype=jnp.int32)
    onehot = (pair_dest[:, None] == col_ids[None, :]).astype(jnp.int32)
    before = jnp.cumsum(onehot, axis=0) - onehot
    target = pair_dest * capacity + jnp.sum(before * onehot, axis=1)
    turns = [(de, da, db) for de in range(extra) for da, db in ((0, 0), (1, 0), (0, 1))]
    wanted = jnp.stack(
        [col_index(lax.rem(ie + de, extra), ia ^ da, ib ^ db, core) for de, da, db in turns]
    ).astype(jnp.int32)
    row_ids = (wanted[:, None] * capacity + jnp.arange(capacity, dtype=jnp.int32)[None, :]).reshape(-1)
    picker = (row_ids[:, None] == target[None, :]).astype(jnp.bfloat16)
    lhs = jnp.dot(picker, amp_all, preferred_element_type=jnp.bfloat16).reshape(len(turns), capacity, -1)

    live = 2 if 4 * panel_shape[0] * panel_shape[1] * 2 > DENSE_BUDGET else 4
    spare = []
    out = None
    total_cols = cols * int_cols
    arrived = []
    for q in (0, 2, 1, 3):
        dense = spare.pop(0) if len(spare) == live else None
        for slot, row in zip(blocks[q], slot_row):
            dense = densify(row, all_lists[q], slot, dense, panel_shape, int_rows)
        kind = core if q < 2 else 1 - core
        second = q % 2
        made = []
        for de in range(extra):
            for turn in (0, 1):
                if (de, turn) == (0, 0):
                    continue
                which = jnp.int32(3 * de) + turn * (1 + kind)
                piece = multiply(lhs, which, dense)
                made.append(piece)
                pairs = []
                for e, a, b, c in every:
                    to_kind = c if q < 2 else 1 - c
                    flip_a = turn if to_kind == 0 else 0
                    flip_b = turn if to_kind == 1 else 0
                    pairs.append(
                        (col_index(e, a, b, c), col_index((e + de) % extra, a ^ flip_a, b ^ flip_b, c))
                    )
                got = lax.ppermute(piece, "col", pairs)
                from_e = lax.rem(ie - de + extra, extra)
                swap = jnp.int32(turn)
                a_of = jnp.where(kind == 0, ia ^ swap, ia ^ second)
                b_of = jnp.where(kind == 0, ib ^ second, ib ^ swap)
                arrived.append((got, col_index(from_e, a_of, b_of, kind)))
        a_own = jnp.where(kind == 0, ia, ia ^ second)
        b_own = jnp.where(kind == 0, ib ^ second, ib)
        out = multiply(lhs, jnp.int32(0), dense, out, total_cols, col_index(ie, a_own, b_own, kind))
        if live < 4:
            dense, out, *_ = lax.optimization_barrier((dense, out, *made))
            spare.append(dense)
    for got, place in arrived:
        out = put(got, out, place)
    return out


def solution(mesh):
    in_specs = (P("row", "col"), P("row", "col"), P("row", "col"), P(None, "col", None), P("row"))
    out_specs = P(("row", "col"), None)
    return jax.shard_map(
        on_device, mesh=mesh, in_specs=in_specs, out_specs=out_specs, check_vma=False
    )
```

time: 295 us -> 278 us (0.942)
  Pallas kernels: 0 us -> 123 us
  blocking collectives: 99.7 us -> 0 us
  local copies, waits for them, and re-layouts: 42 us -> 3.34 us
  starting transfers between devices: 0.22 us -> 24.1 us
  matrix products: 21.3 us -> 5.95 us
  other arithmetic: 20.9 us -> 9.23 us
    pallas_call x0 -> x29, Pallas kernels: none -> 123 us  [the longest x16 57.8 us: densify(): pl.pallas_call(densify_body, out_shape=jax.ShapeDtypeStruct(shape, packed...]
    all_to_all x1 -> x0, blocking collectives: 99.7 us -> none  [on_device(): lax.all_to_all(outgoing, 'col', split_axis=0, concat_axis=2, tiled=True)]
    ppermute x0 -> x24, waiting for transfers between devices: none -> 97.1 us  [the longest x3 43.7 us: on_device(): lax.ppermute(up[k - 1], 'row', [(i + 1, i) for i in range(rows - k)])]
    all_gather x2 -> x1, waiting for transfers between devices: 96.3 us -> 0.01 us  [on_device(): amp_all = lax.all_gather(amp_used, 'col', axis=1, tiled=True)]
    ppermute x0 -> x24, starting transfers between devices: none -> 24.1 us  [the longest x3 8.32 us: on_device(): lax.ppermute(down[k - 1], 'row', [(i, i + 1) for i in range(k - 1, rows -...]
    dot_general x2 -> x1, matrix products: 21.3 us -> 5.95 us  [on_device(): jnp.dot(picker, amp_all, preferred_element_type=jnp.bfloat16)]
    unnamed x5 -> x1, other arithmetic: 13.3 us -> 0.07 us
    reshape x3 -> x0, local copies, waits for them, and re-layouts: 12.8 us -> none  [the longest x1 11.9 us: on_device(): return arrived.reshape(capacity, col_count * int_cols)]
  transfers between devices with their start and end apart: 2 -> 25, of which waited for: 2 -> 8; matrix products, arithmetic and copies ran while one was open for 8% -> 3% of each run, Pallas kernels for 0% -> 41%
where the time goes in v1:
time: 278 us; the launch traced here: 276 us
  Pallas kernels  123 us (44%)
  waiting for transfers between devices  97.1 us (35%)
  starting transfers between devices  24.1 us (9%)
  between operations  13.6 us (5%)
  other arithmetic  9.23 us (3%)
  matrix products  5.95 us (2%)
  local copies, waits for them, and re-layouts  3.34 us (1%)
    pallas_call x16, Pallas kernels, densify(): pl.pallas_call(densify_body, out_shape=jax.ShapeDtypeStruct(shape, packed...  57.8 us
    pallas_call x8, Pallas kernels, multiply(): pl.pallas_call(multiply_body, out_shape=jax.ShapeDtypeStruct((m, n if own...  54.8 us
    ppermute x3, waiting for transfers between devices, on_device(): lax.ppermute(up[k - 1], 'row', [(i + 1, i) for i in range(rows - k)])  43.7 us
    ppermute x4, waiting for transfers between devices, on_device(): mine_next = lax.ppermute(slot, 'col', along)  30.6 us
    ppermute x3, waiting for transfers between devices, on_device(): lax.ppermute(down[k - 1], 'row', [(i, i + 1) for i in range(k - 1, rows -...  20.5 us
    ppermute x3, starting transfers between devices, on_device(): lax.ppermute(down[k - 1], 'row', [(i, i + 1) for i in range(k - 1, rows -...  8.32 us
    pallas_call x4, Pallas kernels, put(): pl.pallas_call(place_body, out_shape=jax.ShapeDtypeStruct(whole.shape, wh...  8.17 us
    dot_general x1, matrix products, on_device(): jnp.dot(picker, amp_all, preferred_element_type=jnp.bfloat16)  5.95 us
  transfers between devices with their start and end apart: 25, of which 8 were waited for; matrix products, arithmetic and copies ran while one was open for 3% of the time, Pallas kernels for 41%

profile of v1, /device:TPU:0, one launch (start us, length us, event | category | flops | bytes accessed | tf_op | source)
XLA Modules:
  0.0 276.4 jit_solution(322756546045328852)
XLA Ops:
  7.7 1.9 bitcast_multiply_fusion
  9.6 1.6 copy-done
  11.2 2.3 pack_tiles.1.packed_ref
  13.5 5.9 %collective-permute-start.5 = (bf16[32,128,128]{2,1,0:T(8,128)(2,1)}, bf16[32,128,128]{2,1,0:T(8,128)(2,1)}, u32[]{:S(2)}, u32[]{:S(2)}) collective-permute-start(bf16[32,128,128]{2,1,0:T(8,128)(2,1)} %pack_tiles.1.packed_ref), channel_id=1, source_target_pairs={{0,8},{8,16},{16,24},{1,9},{9,17},{17,25},{2,10},{10,18},{18,26},{... | collective-permute-start | bytes 3145736 | tf_op jit(solution)/shard_map/ppermute | solution.py:174
  20.7 20.5 %collective-permute-done.5 = bf16[32,128,128]{2,1,0:T(8,128)(2,1)} collective-permute-done((bf16[32,128,128]{2,1,0:T(8,128)(2,1)}, bf16[32,128,128]{2,1,0:T(8,128)(2,1)}, u32[]{:S(2)}, u32[]{:S(2)}) %collective-permute-start.5) | collective-permute-done | bytes 1048608 | tf_op jit(solution)/shard_map/ppermute | solution.py:174
  41.2 1.7 collective-permute-start.6
  42.9 3.4 %collective-permute-done.2 = bf16[32,128,128]{2,1,0:T(8,128)(2,1)} collective-permute-done((bf16[32,128,128]{2,1,0:T(8,128)(2,1)}, bf16[32,128,128]{2,1,0:T(8,128)(2,1)}, u32[]{:S(2)}, u32[]{:S(2)}) %collective-permute-start.2) | collective-permute-done | bytes 1048608 | tf_op jit(solution)/shard_map/ppermute | solution.py:173
  49.8 22.6 %collective-permute-done.3 = bf16[32,128,128]{2,1,0:T(8,128)(2,1)} collective-permute-done((bf16[32,128,128]{2,1,0:T(8,128)(2,1)}, bf16[32,128,128]{2,1,0:T(8,128)(2,1)}, u32[]{:S(2)}, u32[]{:S(2)}) %collective-permute-start.3) | collective-permute-done | bytes 1048608 | tf_op jit(solution)/shard_map/ppermute | solution.py:173
  73.8 1.6 collective-permute-start
  75.3 2.3 collective-permute-done.ids_ref
  79.9 17.8 %collective-permute-done.4 = bf16[32,128,128]{2,1,0:T(8,128)(2,1)} collective-permute-done((bf16[32,128,128]{2,1,0:T(8,128)(2,1)}, bf16[32,128,128]{2,1,0:T(8,128)(2,1)}, u32[]{:S(2)}, u32[]{:S(2)}) %collective-permute-start.4) | collective-permute-done | bytes 1048608 | tf_op jit(solution)/shard_map/ppermute | solution.py:173
  97.6 2.8 %broadcast_select_fusion = (bf16[32,128,128]{2,1,0:T(8,128)(2,1)S(1)}, bf16[32,128,128]{2,1,0:T(8,128)(2,1)S(1)}, bf16[32,128,128]{2,1,0:T(8,128)(2,1)S(1)}) fusion(bf16[32,128,128]{2,1,0:T(8,128)(2,1)} %collective-permute-done.2, bf16[32,128,128]{2,1,0:T(8,128)(2,1)} %collective-permute-done.5, pred[]{:T(512)S(6)} %or.6, ...), kind=kLoop, calls=%fused_computation.6 | loop fusion | flops 3670016 | bytes 9437189 | tf_op jit(solution)/shard_map/jit(_where)/select_n | solution.py:187
  100.5 1.6 collective-permute-start.12
  104.1 2.3 reduce-window.6
  107.3 8.1 %collective-permute-done.12.packed_ref = bf16[32,128,128]{2,1,0:T(8,128)(2,1)} collective-permute-done((bf16[32,128,128]{2,1,0:T(8,128)(2,1)S(1)}, bf16[32,128,128]{2,1,0:T(8,128)(2,1)}, u32[]{:S(2)}, u32[]{:S(2)}) %collective-permute-start.12) | collective-permute-done | bytes 1048608 | tf_op jit(solution)/shard_map/ppermute | solution.py:202
  115.5 11.2 %collective-permute-done.10.packed_ref = bf16[32,128,128]{2,1,0:T(8,128)(2,1)} collective-permute-done((bf16[32,128,128]{2,1,0:T(8,128)(2,1)S(1)}, bf16[32,128,128]{2,1,0:T(8,128)(2,1)}, u32[]{:S(2)}, u32[]{:S(2)}) %collective-permute-start.10) | collective-permute-done | bytes 1048608 | tf_op jit(solution)/shard_map/ppermute | solution.py:202
  126.7 11.2 %collective-permute-done.8.packed_ref = bf16[32,128,128]{2,1,0:T(8,128)(2,1)} collective-permute-done((bf16[32,128,128]{2,1,0:T(8,128)(2,1)S(1)}, bf16[32,128,128]{2,1,0:T(8,128)(2,1)}, u32[]{:S(2)}, u32[]{:S(2)}) %collective-permute-start.8) | collective-permute-done | bytes 1048608 | tf_op jit(solution)/shard_map/ppermute | solution.py:202
  138.0 3.9 %densify.28.rest_0_ = bf16[2048,2048]{1,0:T(8,128)(2,1)} custom-call(s32[1]{0:T(128)} %bitcast.10.row_ref, s32[4,32]{1,0:T(4,128)} %bitcast.9.ids_ref, bf16[32,128,128]{2,1,0:T(8,128)(2,1)} %pack_tiles.1.packed_ref), custom_call_target="tpu_custom_call" | custom-call | bytes 6291456 | tf_op jit(solution)/shard_map/densify/pallas_call | solution.py:71
  142.4 3.9 %densify.20.rest_0_ = bf16[2048,2048]{1,0:T(8,128)(2,1)} custom-call(s32[1]{0:T(128)} %bitcast.10.row_ref, s32[4,32]{1,0:T(4,128)S(1)} %collective-permute-done.ids_ref, bf16[32,128,128]{2,1,0:T(8,128)(2,1)} %collective-permute-done.14.packed_ref), custom_call_target="tpu_custom_call" | custom-call | bytes 6291456 | tf_op jit(solution)/shard_map/densify/pallas_call | solution.py:71
  146.3 3.9 %densify.24.rest_0_ = bf16[2048,2048]{1,0:T(8,128)(2,1)} custom-call(s32[1]{0:T(128)} %bitcast.10.row_ref, s32[4,32]{1,0:T(4,128)S(1)} %get-tuple-element.8.ids_ref, bf16[32,128,128]{2,1,0:T(8,128)(2,1)} %collective-permute-done.21.packed_ref), custom_call_target="tpu_custom_call" | custom-call | bytes 6291456 | tf_op jit(solution)/shard_map/densify/pallas_call | solution.py:71
  150.1 3.8 %densify.16.rest_0_ = bf16[2048,2048]{1,0:T(8,128)(2,1)} custom-call(s32[1]{0:T(128)} %bitcast.10.row_ref, s32[4,32]{1,0:T(4,128)S(1)} %get-tuple-element.9.ids_ref, bf16[32,128,128]{2,1,0:T(8,128)(2,1)} %collective-permute-done.15.packed_ref), custom_call_target="tpu_custom_call" | custom-call | bytes 6291456 | tf_op jit(solution)/shard_map/densify/pallas_call | solution.py:71
  153.9 2.7 densify.29.rest_0_
  156.6 2.7 densify.30.rest_0_
  159.3 2.8 %densify.31.rhs_ref = bf16[2048,2048]{1,0:T(8,128)(2,1)} custom-call(s32[1]{0:T(128)} %bitcast.8.row_ref, s32[4,32]{1,0:T(4,128)} %bitcast.9.ids_ref, bf16[32,128,128]{2,1,0:T(8,128)(2,1)S(1)} %get-tuple-element.7.packed_ref, bf16[2048,2048]{1,0:T(8,128)(2,1)} %densify.30.rest_0_), custom_call_target="tpu_custom_call", output_to_operand_aliasing={{}: (3, {})} | custom-call | bytes 6291456 | tf_op jit(solution)/shard_map/densify/pallas_call | solution.py:71
  162.1 3.8 %densify.21.rest_0_ = bf16[2048,2048]{1,0:T(8,128)(2,1)} custom-call(s32[1]{0:T(128)} %bitcast.12.row_ref, s32[4,32]{1,0:T(4,128)S(1)} %collective-permute-done.ids_ref, bf16[32,128,128]{2,1,0:T(8,128)(2,1)} %collective-permute-done.12.packed_ref, bf16[2048,2048]{1,0:T(8,128)(2,1)} %densify.20.rest_0_), custom_call_target="tpu_custom_call", output_to_operand_aliasing={{}: (3, {})} | custom-call | bytes 6291456 | tf_op jit(solution)/shard_map/densify/pallas_call | solution.py:71
  165.9 3.7 %densify.22.rest_0_ = bf16[2048,2048]{1,0:T(8,128)(2,1)} custom-call(s32[1]{0:T(128)} %bitcast.11.row_ref, s32[4,32]{1,0:T(4,128)S(1)} %collective-permute-done.ids_ref, bf16[32,128,128]{2,1,0:T(8,128)(2,1)} %collective-permute-done.10.packed_ref, bf16[2048,2048]{1,0:T(8,128)(2,1)} %densify.21.rest_0_), custom_call_target="tpu_custom_call", output_to_operand_aliasing={{}: (3, {})} | custom-call | bytes 6291456 | tf_op jit(solution)/shard_map/densify/pallas_call | solution.py:71
  169.7 3.7 %densify.23.rhs_ref = bf16[2048,2048]{1,0:T(8,128)(2,1)} custom-call(s32[1]{0:T(128)} %bitcast.8.row_ref, s32[4,32]{1,0:T(4,128)S(1)} %collective-permute-done.ids_ref, bf16[32,128,128]{2,1,0:T(8,128)(2,1)} %collective-permute-done.8.packed_ref, bf16[2048,2048]{1,0:T(8,128)(2,1)} %densify.22.rest_0_), custom_call_target="tpu_custom_call", output_to_operand_aliasing={{}: (3, {})} | custom-call | bytes 6291456 | tf_op jit(solution)/shard_map/densify/pallas_call | solution.py:71
  173.4 3.8 %densify.25.rest_0_ = bf16[2048,2048]{1,0:T(8,128)(2,1)} custom-call(s32[1]{0:T(128)} %bitcast.12.row_ref, s32[4,32]{1,0:T(4,128)S(1)} %get-tuple-element.8.ids_ref, bf16[32,128,128]{2,1,0:T(8,128)(2,1)} %collective-permute-done.20.packed_ref, bf16[2048,2048]{1,0:T(8,128)(2,1)} %densify.24.rest_0_), custom_call_target="tpu_custom_call", output_to_operand_aliasing={{}: (3, {})} | custom-call | bytes 6291456 | tf_op jit(solution)/shard_map/densify/pallas_call | solution.py:71
  177.2 3.8 %densify.26.rest_0_ = bf16[2048,2048]{1,0:T(8,128)(2,1)} custom-call(s32[1]{0:T(128)} %bitcast.11.row_ref, s32[4,32]{1,0:T(4,128)S(1)} %get-tuple-element.8.ids_ref, bf16[32,128,128]{2,1,0:T(8,128)(2,1)} %collective-permute-done.19.packed_ref, bf16[2048,2048]{1,0:T(8,128)(2,1)} %densify.25.rest_0_), custom_call_target="tpu_custom_call", output_to_operand_aliasing={{}: (3, {})} | custom-call | bytes 6291456 | tf_op jit(solution)/shard_map/densify/pallas_call | solution.py:71
  180.9 3.9 %densify.27.rhs_ref = bf16[2048,2048]{1,0:T(8,128)(2,1)} custom-call(s32[1]{0:T(128)} %bitcast.8.row_ref, s32[4,32]{1,0:T(4,128)S(1)} %get-tuple-element.8.ids_ref, bf16[32,128,128]{2,1,0:T(8,128)(2,1)} %collective-permute-done.18.packed_ref, bf16[2048,2048]{1,0:T(8,128)(2,1)} %densify.26.rest_0_), custom_call_target="tpu_custom_call", output_to_operand_aliasing={{}: (3, {})} | custom-call | bytes 6291456 | tf_op jit(solution)/shard_map/densify/pallas_call | solution.py:71
  184.8 3.8 %densify.17.rest_0_ = bf16[2048,2048]{1,0:T(8,128)(2,1)} custom-call(s32[1]{0:T(128)} %bitcast.12.row_ref, s32[4,32]{1,0:T(4,128)S(1)} %get-tuple-element.9.ids_ref, bf16[32,128,128]{2,1,0:T(8,128)(2,1)} %collective-permute-done.13.packed_ref, bf16[2048,2048]{1,0:T(8,128)(2,1)} %densify.16.rest_0_), custom_call_target="tpu_custom_call", output_to_operand_aliasing={{}: (3, {})} | custom-call | bytes 6291456 | tf_op jit(solution)/shard_map/densify/pallas_call | solution.py:71
  188.6 3.9 %densify.18.rest_0_ = bf16[2048,2048]{1,0:T(8,128)(2,1)} custom-call(s32[1]{0:T(128)} %bitcast.11.row_ref, s32[4,32]{1,0:T(4,128)S(1)} %get-tuple-element.9.ids_ref, bf16[32,128,128]{2,1,0:T(8,128)(2,1)} %collective-permute-done.11.packed_ref, bf16[2048,2048]{1,0:T(8,128)(2,1)} %densify.17.rest_0_), custom_call_target="tpu_custom_call", output_to_operand_aliasing={{}: (3, {})} | custom-call | bytes 6291456 | tf_op jit(solution)/shard_map/densify/pallas_call | solution.py:71
  192.5 3.8 %densify.19.rhs_ref = bf16[2048,2048]{1,0:T(8,128)(2,1)} custom-call(s32[1]{0:T(128)} %bitcast.8.row_ref, s32[4,32]{1,0:T(4,128)S(1)} %get-tuple-element.9.ids_ref, bf16[32,128,128]{2,1,0:T(8,128)(2,1)} %collective-permute-done.9.packed_ref, bf16[2048,2048]{1,0:T(8,128)(2,1)} %densify.18.rest_0_), custom_call_target="tpu_custom_call", output_to_operand_aliasing={{}: (3, {})} | custom-call | bytes 6291456 | tf_op jit(solution)/shard_map/densify/pallas_call | solution.py:71
  196.3 5.9 %fusion = bf16[768,2048]{1,0:T(8,128)(2,1)S(1)} fusion(bf16[1024,2048]{1,0:T(8,128)(2,1)} %all-gather.2.cloned.1.call-done, s32[1024]{0:T(1024)S(1)} %multiply_add_fusion, s32[768]{0:T(1024)S(1)} %add.141), kind=kOutput, calls=%fused_computation | convolution fusion | flops 3222011904 | bytes 7347200 | tf_op jit(solution)/shard_map/dot_general | solution.py:223
  202.3 6.9 %multiply.8 = bf16[256,2048]{1,0:T(8,128)(2,1)} custom-call(s32[2]{0:T(128)S(1)} %pad_add_fusion.6.place_ref, bf16[3,256,2048]{2,1,0:T(8,128)(2,1)S(1)} %bitcast.44, bf16[2048,2048]{1,0:T(8,128)(2,1)} %densify.19.rhs_ref), custom_call_target="tpu_custom_call" | custom-call | flops 2147483648 | bytes 10485760 | tf_op jit(solution)/shard_map/multiply/pallas_call | solution.py:109
  209.1 1.7 collective-permute-start.16
  210.8 6.9 %multiply.10 = bf16[256,2048]{1,0:T(8,128)(2,1)} custom-call(s32[2]{0:T(128)S(1)} %pad_add_fusion.6.place_ref, bf16[3,256,2048]{2,1,0:T(8,128)(2,1)S(1)} %bitcast.45, bf16[2048,2048]{1,0:T(8,128)(2,1)} %densify.27.rhs_ref), custom_call_target="tpu_custom_call" | custom-call | flops 2147483648 | bytes 10485760 | tf_op jit(solution)/shard_map/multiply/pallas_call | solution.py:109
  218.1 6.9 %multiply.9 = bf16[256,2048]{1,0:T(8,128)(2,1)} custom-call(s32[2]{0:T(128)S(1)} %pad_add_fusion.5.place_ref, bf16[3,256,2048]{2,1,0:T(8,128)(2,1)S(1)} %bitcast.46, bf16[2048,2048]{1,0:T(8,128)(2,1)} %densify.23.rhs_ref), custom_call_target="tpu_custom_call" | custom-call | flops 2147483648 | bytes 10485760 | tf_op jit(solution)/shard_map/multiply/pallas_call | solution.py:109
  224.9 1.6 collective-permute-start.17
  226.6 6.8 %multiply.11 = bf16[256,2048]{1,0:T(8,128)(2,1)} custom-call(s32[2]{0:T(128)S(1)} %pad_add_fusion.5.place_ref, bf16[3,256,2048]{2,1,0:T(8,128)(2,1)S(1)} %bitcast.47, bf16[2048,2048]{1,0:T(8,128)(2,1)} %densify.31.rhs_ref), custom_call_target="tpu_custom_call" | custom-call | flops 2147483648 | bytes 10485760 | tf_op jit(solution)/shard_map/multiply/pallas_call | solution.py:109
  234.0 6.8 %multiply.12.rest_0_ = bf16[256,16384]{1,0:T(8,128)(2,1)} custom-call(s32[2]{0:T(128)S(1)} %pad_add_fusion.1.place_ref, bf16[3,256,2048]{2,1,0:T(8,128)(2,1)S(1)} %bitcast.48, bf16[2048,2048]{1,0:T(8,128)(2,1)} %densify.31.rhs_ref), custom_call_target="tpu_custom_call" | custom-call | flops 2147483648 | bytes 10485760 | tf_op jit(solution)/shard_map/multiply/pallas_call | solution.py:109
  240.9 6.8 %multiply.13.rest_0_ = bf16[256,16384]{1,0:T(8,128)(2,1)} custom-call(s32[2]{0:T(128)S(1)} %pad_add_fusion.2.place_ref, bf16[3,256,2048]{2,1,0:T(8,128)(2,1)S(1)} %bitcast.49, bf16[2048,2048]{1,0:T(8,128)(2,1)} %densify.27.rhs_ref, bf16[256,16384]{1,0:T(8,128)(2,1)} %multiply.12.rest_0_), custom_call_target="tpu_custom_call", output_to_operand_aliasing={{}: (3, {})} | custom-call | flops 2147483648 | bytes 10485760 | tf_op jit(solution)/shard_map/multiply/pallas_call | solution.py:109
  247.7 6.8 %multiply.14.rest_0_ = bf16[256,16384]{1,0:T(8,128)(2,1)} custom-call(s32[2]{0:T(128)S(1)} %pad_add_fusion.3.place_ref, bf16[3,256,2048]{2,1,0:T(8,128)(2,1)S(1)} %bitcast.50, bf16[2048,2048]{1,0:T(8,128)(2,1)} %densify.23.rhs_ref, bf16[256,16384]{1,0:T(8,128)(2,1)} %multiply.13.rest_0_), custom_call_target="tpu_custom_call", output_to_operand_aliasing={{}: (3, {})} | custom-call | flops 2147483648 | bytes 10485760 | tf_op jit(solution)/shard_map/multiply/pallas_call | solution.py:109
  254.6 6.8 %multiply.15.whole_ref = bf16[256,16384]{1,0:T(8,128)(2,1)} custom-call(s32[2]{0:T(128)S(1)} %pad_add_fusion.4.place_ref, bf16[3,256,2048]{2,1,0:T(8,128)(2,1)S(1)} %bitcast.51, bf16[2048,2048]{1,0:T(8,128)(2,1)} %densify.19.rhs_ref, bf16[256,16384]{1,0:T(8,128)(2,1)} %multiply.14.rest_0_), custom_call_target="tpu_custom_call", output_to_operand_aliasing={{}: (3, {})} | custom-call | flops 2147483648 | bytes 10485760 | tf_op jit(solution)/shard_map/multiply/pallas_call | solution.py:109
  261.4 2.0 put.4.whole_ref
  263.5 2.0 put.5.whole_ref
  265.5 2.0 put.6.whole_ref
  267.6 2.0 put.7
  (62 shorter events, 14.1 us)
Async XLA Ops:
  6.5 97.6 %copy-start.2 = (s32[1024]{0:T(1024)S(1)}, s32[1024]{0:T(1024)}, u32[]{:S(2)}) copy-start(s32[1024]{0:T(1024)} %param.9) | copy-start | bytes 12292
  6.5 189.8 %all-gather.2.cloned.1.call-start = ((), (), s32[]{:S(2)}) async-start(), calls=%async_computation | async-start | bytes 4718592 | tf_op jit(solution)/shard_map/all_gather | solution.py:212
  9.6 1.6 copy-start
  13.5 27.7 %collective-permute-start.5 = (bf16[32,128,128]{2,1,0:T(8,128)(2,1)}, bf16[32,128,128]{2,1,0:T(8,128)(2,1)}, u32[]{:S(2)}, u32[]{:S(2)}) collective-permute-start(bf16[32,128,128]{2,1,0:T(8,128)(2,1)} %pack_tiles.1.packed_ref), channel_id=1, source_target_pairs={{0,8},{8,16},{16,24},{1,9},{9,17},{17,25},{2,10},{10,18},{18,26},{... | collective-permute-start | bytes 3145736 | tf_op jit(solution)/shard_map/ppermute | solution.py:174
  19.4 26.8 %collective-permute-start.2 = (bf16[32,128,128]{2,1,0:T(8,128)(2,1)}, bf16[32,128,128]{2,1,0:T(8,128)(2,1)}, u32[]{:S(2)}, u32[]{:S(2)}) collective-permute-start(bf16[32,128,128]{2,1,0:T(8,128)(2,1)} %pack_tiles.1.packed_ref), channel_id=1, source_target_pairs={{8,0},{16,8},{24,16},{9,1},{17,9},{25,17},{10,2},{18,10},{26,18},{... | collective-permute-start | bytes 3145736 | tf_op jit(solution)/shard_map/ppermute | solution.py:173
  41.2 7.9 %collective-permute-start.6 = (bf16[32,128,128]{2,1,0:T(8,128)(2,1)}, bf16[32,128,128]{2,1,0:T(8,128)(2,1)}, u32[]{:S(2)}, u32[]{:S(2)}) collective-permute-start(bf16[32,128,128]{2,1,0:T(8,128)(2,1)} %collective-permute-done.5), channel_id=1, source_target_pairs={{8,16},{16,24},{9,17},{17,25},{10,18},{18,26},{11,19},{19,27},{12,... | collective-permute-start | bytes 3145736 | tf_op jit(solution)/shard_map/ppermute | solution.py:174
  46.3 26.1 %collective-permute-start.3 = (bf16[32,128,128]{2,1,0:T(8,128)(2,1)}, bf16[32,128,128]{2,1,0:T(8,128)(2,1)}, u32[]{:S(2)}, u32[]{:S(2)}) collective-permute-start(bf16[32,128,128]{2,1,0:T(8,128)(2,1)} %collective-permute-done.2), channel_id=1, source_target_pairs={{8,0},{16,8},{9,1},{17,9},{10,2},{18,10},{11,3},{19,11},{12,4},{20... | collective-permute-start | bytes 3145736 | tf_op jit(solution)/shard_map/ppermute | solution.py:173
  47.5 30.8 %collective-permute-start.14 = (bf16[32,128,128]{2,1,0:T(8,128)(2,1)}, bf16[32,128,128]{2,1,0:T(8,128)(2,1)}, u32[]{:S(2)}, u32[]{:S(2)}) collective-permute-start(bf16[32,128,128]{2,1,0:T(8,128)(2,1)} %pack_tiles.1.packed_ref), channel_id=1, source_target_pairs={{0,2},{1,5},{2,0},{3,7},{4,6},{5,1},{6,4},{7,3},{8,10},{9,13},{10,... | collective-permute-start | bytes 3145736 | tf_op jit(solution)/shard_map/ppermute | solution.py:202
  49.1 29.7 %collective-permute-start.7 = (bf16[32,128,128]{2,1,0:T(8,128)(2,1)}, bf16[32,128,128]{2,1,0:T(8,128)(2,1)S(1)}, u32[]{:S(2)}, u32[]{:S(2)}) collective-permute-start(bf16[32,128,128]{2,1,0:T(8,128)(2,1)} %collective-permute-done.6), channel_id=1, source_target_pairs={{16,24},{17,25},{18,26},{19,27},{20,28},{21,29},{22,30},{23,31}} | collective-permute-start | bytes 3145736 | tf_op jit(solution)/shard_map/ppermute | solution.py:174
  72.4 25.2 %collective-permute-start.4 = (bf16[32,128,128]{2,1,0:T(8,128)(2,1)}, bf16[32,128,128]{2,1,0:T(8,128)(2,1)}, u32[]{:S(2)}, u32[]{:S(2)}) collective-permute-start(bf16[32,128,128]{2,1,0:T(8,128)(2,1)} %collective-permute-done.3), channel_id=1, source_target_pairs={{8,0},{9,1},{10,2},{11,3},{12,4},{13,5},{14,6},{15,7}} | collective-permute-start | bytes 3145736 | tf_op jit(solution)/shard_map/ppermute | solution.py:173
  73.7 28.9 %collective-permute-start.21 = (bf16[32,128,128]{2,1,0:T(8,128)(2,1)}, bf16[32,128,128]{2,1,0:T(8,128)(2,1)}, u32[]{:S(2)}, u32[]{:S(2)}) collective-permute-start(bf16[32,128,128]{2,1,0:T(8,128)(2,1)} %pack_tiles.1.packed_ref), channel_id=1, source_target_pairs={{0,1},{1,0},{2,3},{3,2},{4,5},{5,4},{6,7},{7,6},{8,9},{9,8},{10,11... | collective-permute-start | bytes 3145736 | tf_op jit(solution)/shard_map/ppermute | solution.py:205
  73.8 3.9 %collective-permute-start = (s32[4,32]{1,0:T(4,128)}, s32[4,32]{1,0:T(4,128)S(1)}, u32[]{:S(2)}, u32[]{:S(2)}) collective-permute-start(s32[4,32]{1,0:T(4,128)} %bitcast.9.ids_ref), channel_id=1, source_target_pairs={{0,2},{1,5},{2,0},{3,7},{4,6},{5,1},{6,4},{7,3},{8,10},{9,13},{10,... | collective-permute-start | bytes 1544 | tf_op jit(solution)/shard_map/ppermute | solution.py:197
  78.3 23.8 %collective-permute-start.1 = (s32[8,32]{1,0:T(8,128)S(1)}, s32[8,32]{1,0:T(8,128)S(1)}, u32[]{:S(2)}, u32[]{:S(2)}) collective-permute-start(s32[8,32]{1,0:T(8,128)S(1)} %pad_add_fusion), channel_id=1, source_target_pairs={{0,1},{1,0},{2,3},{3,2},{4,5},{5,4},{6,7},{7,6},{8,9},{9,8},{10,11... | collective-permute-start | bytes 3080 | tf_op jit(solution)/shard_map/ppermute | solution.py:198
  78.3 28.5 %collective-permute-start.15 = (bf16[32,128,128]{2,1,0:T(8,128)(2,1)}, bf16[32,128,128]{2,1,0:T(8,128)(2,1)}, u32[]{:S(2)}, u32[]{:S(2)}) collective-permute-start(bf16[32,128,128]{2,1,0:T(8,128)(2,1)} %collective-permute-done.14.packed_ref), channel_id=1, source_target_pairs={{0,1},{1,0},{2,3},{3,2},{4,5},{5,4},{6,7},{7,6},{8,9},{9,8},{10,11... | collective-permute-start | bytes 3145736 | tf_op jit(solution)/shard_map/ppermute | solution.py:206
  78.8 1.0 copy-start.1
  100.4 6.4 %collective-permute-start.20 = (bf16[32,128,128]{2,1,0:T(8,128)(2,1)S(1)}, bf16[32,128,128]{2,1,0:T(8,128)(2,1)}, u32[]{:S(2)}, u32[]{:S(2)}) collective-permute-start(bf16[32,128,128]{2,1,0:T(8,128)(2,1)S(1)} %get-tuple-element.5.packed_ref), channel_id=1, source_target_pairs={{0,1},{1,0},{2,3},{3,2},{4,5},{5,4},{6,7},{7,6},{8,9},{9,8},{10,11... | collective-permute-start | bytes 3145736 | tf_op jit(solution)/shard_map/ppermute | solution.py:205
  100.5 15.0 %collective-permute-start.12 = (bf16[32,128,128]{2,1,0:T(8,128)(2,1)S(1)}, bf16[32,128,128]{2,1,0:T(8,128)(2,1)}, u32[]{:S(2)}, u32[]{:S(2)}) collective-permute-start(bf16[32,128,128]{2,1,0:T(8,128)(2,1)S(1)} %get-tuple-element.5.packed_ref), channel_id=1, source_target_pairs={{0,2},{1,5},{2,0},{3,7},{4,6},{5,1},{6,4},{7,3},{8,10},{9,13},{10,... | collective-permute-start | bytes 3145736 | tf_op jit(solution)/shard_map/ppermute | solution.py:202
  102.1 24.6 %collective-permute-start.10 = (bf16[32,128,128]{2,1,0:T(8,128)(2,1)S(1)}, bf16[32,128,128]{2,1,0:T(8,128)(2,1)}, u32[]{:S(2)}, u32[]{:S(2)}) collective-permute-start(bf16[32,128,128]{2,1,0:T(8,128)(2,1)S(1)} %get-tuple-element.6.packed_ref), channel_id=1, source_target_pairs={{0,2},{1,5},{2,0},{3,7},{4,6},{5,1},{6,4},{7,3},{8,10},{9,13},{10,... | collective-permute-start | bytes 3145736 | tf_op jit(solution)/shard_map/ppermute | solution.py:202
  102.6 35.3 %collective-permute-start.8 = (bf16[32,128,128]{2,1,0:T(8,128)(2,1)S(1)}, bf16[32,128,128]{2,1,0:T(8,128)(2,1)}, u32[]{:S(2)}, u32[]{:S(2)}) collective-permute-start(bf16[32,128,128]{2,1,0:T(8,128)(2,1)S(1)} %get-tuple-element.7.packed_ref), channel_id=1, source_target_pairs={{0,2},{1,5},{2,0},{3,7},{4,6},{5,1},{6,4},{7,3},{8,10},{9,13},{10,... | collective-permute-start | bytes 3145736 | tf_op jit(solution)/shard_map/ppermute | solution.py:202
  106.8 70.3 %collective-permute-start.19 = (bf16[32,128,128]{2,1,0:T(8,128)(2,1)S(1)}, bf16[32,128,128]{2,1,0:T(8,128)(2,1)}, u32[]{:S(2)}, u32[]{:S(2)}) collective-permute-start(bf16[32,128,128]{2,1,0:T(8,128)(2,1)S(1)} %get-tuple-element.6.packed_ref), channel_id=1, source_target_pairs={{0,1},{1,0},{2,3},{3,2},{4,5},{5,4},{6,7},{7,6},{8,9},{9,8},{10,11... | collective-permute-start | bytes 3145736 | tf_op jit(solution)/shard_map/ppermute | solution.py:205
  106.9 74.1 %collective-permute-start.18 = (bf16[32,128,128]{2,1,0:T(8,128)(2,1)S(1)}, bf16[32,128,128]{2,1,0:T(8,128)(2,1)}, u32[]{:S(2)}, u32[]{:S(2)}) collective-permute-start(bf16[32,128,128]{2,1,0:T(8,128)(2,1)S(1)} %get-tuple-element.7.packed_ref), channel_id=1, source_target_pairs={{0,1},{1,0},{2,3},{3,2},{4,5},{5,4},{6,7},{7,6},{8,9},{9,8},{10,11... | collective-permute-start | bytes 3145736 | tf_op jit(solution)/shard_map/ppermute | solution.py:205
  115.5 69.3 %collective-permute-start.13 = (bf16[32,128,128]{2,1,0:T(8,128)(2,1)}, bf16[32,128,128]{2,1,0:T(8,128)(2,1)}, u32[]{:S(2)}, u32[]{:S(2)}) collective-permute-start(bf16[32,128,128]{2,1,0:T(8,128)(2,1)} %collective-permute-done.12.packed_ref), channel_id=1, source_target_pairs={{0,1},{1,0},{2,3},{3,2},{4,5},{5,4},{6,7},{7,6},{8,9},{9,8},{10,11... | collective-permute-start | bytes 3145736 | tf_op jit(solution)/shard_map/ppermute | solution.py:206
  126.7 61.9 %collective-permute-start.11 = (bf16[32,128,128]{2,1,0:T(8,128)(2,1)}, bf16[32,128,128]{2,1,0:T(8,128)(2,1)}, u32[]{:S(2)}, u32[]{:S(2)}) collective-permute-start(bf16[32,128,128]{2,1,0:T(8,128)(2,1)} %collective-permute-done.10.packed_ref), channel_id=1, source_target_pairs={{0,1},{1,0},{2,3},{3,2},{4,5},{5,4},{6,7},{7,6},{8,9},{9,8},{10,11... | collective-permute-start | bytes 3145736 | tf_op jit(solution)/shard_map/ppermute | solution.py:206
  138.0 54.5 %collective-permute-start.9 = (bf16[32,128,128]{2,1,0:T(8,128)(2,1)}, bf16[32,128,128]{2,1,0:T(8,128)(2,1)}, u32[]{:S(2)}, u32[]{:S(2)}) collective-permute-start(bf16[32,128,128]{2,1,0:T(8,128)(2,1)} %collective-permute-done.8.packed_ref), channel_id=1, source_target_pairs={{0,1},{1,0},{2,3},{3,2},{4,5},{5,4},{6,7},{7,6},{8,9},{9,8},{10,11... | collective-permute-start | bytes 3145736 | tf_op jit(solution)/shard_map/ppermute | solution.py:206
  209.1 58.4 %collective-permute-start.16 = (bf16[256,2048]{1,0:T(8,128)(2,1)}, bf16[256,2048]{1,0:T(8,128)(2,1)}, u32[]{:S(2)}, u32[]{:S(2)}) collective-permute-start(bf16[256,2048]{1,0:T(8,128)(2,1)} %multiply.8), channel_id=1, source_target_pairs={{0,2},{1,5},{2,0},{3,7},{4,6},{5,1},{6,4},{7,3},{8,10},{9,13},{10,... | collective-permute-start | bytes 3145736 | tf_op jit(solution)/shard_map/ppermute | solution.py:252
  217.7 45.7 %collective-permute-start.22 = (bf16[256,2048]{1,0:T(8,128)(2,1)}, bf16[256,2048]{1,0:T(8,128)(2,1)}, u32[]{:S(2)}, u32[]{:S(2)}) collective-permute-start(bf16[256,2048]{1,0:T(8,128)(2,1)} %multiply.10), channel_id=1, source_target_pairs={{0,2},{1,5},{2,0},{3,7},{4,6},{5,1},{6,4},{7,3},{8,10},{9,13},{10,... | collective-permute-start | bytes 3145736 | tf_op jit(solution)/shard_map/ppermute | solution.py:252
  224.9 40.6 %collective-permute-start.17 = (bf16[256,2048]{1,0:T(8,128)(2,1)}, bf16[256,2048]{1,0:T(8,128)(2,1)}, u32[]{:S(2)}, u32[]{:S(2)}) collective-permute-start(bf16[256,2048]{1,0:T(8,128)(2,1)} %multiply.9), channel_id=1, source_target_pairs={{0,4},{1,3},{2,6},{3,1},{4,0},{5,7},{6,2},{7,5},{8,12},{9,11},{10,... | collective-permute-start | bytes 3145736 | tf_op jit(solution)/shard_map/ppermute | solution.py:252
  233.4 28.0 %collective-permute-start.23 = (bf16[256,2048]{1,0:T(8,128)(2,1)}, bf16[256,2048]{1,0:T(8,128)(2,1)}, u32[]{:S(2)}, u32[]{:S(2)}) collective-permute-start(bf16[256,2048]{1,0:T(8,128)(2,1)} %multiply.11), channel_id=1, source_target_pairs={{0,4},{1,3},{2,6},{3,1},{4,0},{5,7},{6,2},{7,5},{8,12},{9,11},{10,... | collective-permute-start | bytes 3145736 | tf_op jit(solution)/shard_map/ppermute | solution.py:252
Sparse Core Ops, SparseCore 0:
  9.7 40.1 all-gather.1

commit v2 on v1

v2 whole, which is shorter than its diff:
```python
import functools

import jax
import jax.numpy as jnp
from jax import lax
from jax.experimental import pallas as pl
from jax.experimental.pallas import tpu as pltpu
from jax.sharding import PartitionSpec as P

TILE = 128
MM_COLS = 512
VMEM_LIMIT = 63 << 20


def params():
    return pltpu.CompilerParams(vmem_limit_bytes=VMEM_LIMIT)


def pack_body(row_ref, ids_ref, src_ref, out_ref, sem):
    col_tiles = src_ref.shape[1] // TILE
    tiles = col_tiles * (src_ref.shape[0] // TILE)
    for e in range(out_ref.shape[0]):
        t = jnp.minimum(ids_ref[row_ref[0], e], tiles - 1)
        k = pl.multiple_of(lax.div(t, col_tiles) * TILE, TILE)
        n = pl.multiple_of(lax.rem(t, col_tiles) * TILE, TILE)
        pltpu.make_async_copy(src_ref.at[pl.ds(k, TILE), pl.ds(n, TILE)], out_ref.at[e], sem).start()
    pltpu.make_async_copy(out_ref, out_ref, sem).wait()


def pack(row, lists, integrals):
    count = lists.shape[1]
    return pl.pallas_call(
        pack_body,
        out_shape=jax.ShapeDtypeStruct((count, TILE, TILE), integrals.dtype),
        in_specs=[
            pl.BlockSpec(memory_space=pltpu.SMEM),
            pl.BlockSpec(memory_space=pltpu.SMEM),
            pl.BlockSpec(memory_space=pltpu.HBM),
        ],
        out_specs=pl.BlockSpec(memory_space=pltpu.VMEM),
        scratch_shapes=[pltpu.SemaphoreType.DMA],
        compiler_params=params(),
        name="pack_tiles",
    )(row, lists, integrals)


def partial_body(steps_of, scalars, table, *refs):
    lhs_count, slot_count, has_acc, final, has_whole = steps_of
    refs = list(refs)
    lhs = [[refs.pop(0) for _ in range(slot_count)] for _ in range(lhs_count)]
    packed = [refs.pop(0) for _ in range(slot_count)]
    acc = refs.pop(0) if has_acc else None
    if has_whole:
        refs.pop(0)
    outs, lhs_all, rhs_all = refs[:-2], refs[-2], refs[-1]
    step = pl.program_id(0)
    capacity, depth = lhs[0][0].shape[1:]
    width = rhs_all.shape[1]
    count = packed[0].shape[0]
    col_tiles = table.shape[1] // (depth // TILE)

    @pl.when(step == 0)
    def _():
        for t in range(lhs_count):
            for s in range(slot_count):
                lhs_all[t * capacity : (t + 1) * capacity, s * depth : (s + 1) * depth] = lhs[t][s][0]

    for s in range(slot_count):
        row = scalars[lhs_count + s]
        for k in range(depth // TILE):
            for n in range(width // TILE):
                e = table[row, k * col_tiles + step * (width // TILE) + n]
                tile = packed[s][jnp.minimum(e, count - 1)]
                rhs_all[s * depth + k * TILE : s * depth + (k + 1) * TILE, n * TILE : (n + 1) * TILE] = jnp.where(
                    e < count, tile, jnp.zeros_like(tile)
                )
    total = jnp.dot(lhs_all[...], rhs_all[...], preferred_element_type=jnp.float32)
    if has_acc:
        total = acc[...] + total
    if final:
        for t in range(lhs_count):
            outs[t][...] = total[t * capacity : (t + 1) * capacity].astype(outs[t].dtype)
    else:
        outs[0][...] = total


def partial(lhs, picks, table, slots, slot_rows, int_cols, acc=None, whole_cols=None, whole=None, place=None):
    _, capacity, _ = lhs.shape
    lhs_count, slot_count = len(picks), len(slots)
    m = lhs_count * capacity
    depth = table.shape[1] // (int_cols // TILE) * TILE
    width = min(MM_COLS, int_cols)
    steps = int_cols // width
    final = whole_cols is not None
    scalars = jnp.stack([*picks, *slot_rows, jnp.int32(0) if place is None else place]).astype(jnp.int32)
    last = lhs_count + slot_count

    def lhs_at(t, s):
        return lambda i, sc, tab: (sc[t], 0, sc[lhs_count + s])

    in_specs = [
        pl.BlockSpec((1, capacity, depth), lhs_at(t, s)) for t in range(lhs_count) for s in range(slot_count)
    ]
    in_specs += [pl.BlockSpec(slot.shape, lambda i, sc, tab: (0, 0, 0)) for slot in slots]
    operands = [scalars, table] + [lhs] * (lhs_count * slot_count) + list(slots)
    aliases = {}
    if acc is not None:
        in_specs.append(pl.BlockSpec((m, width), lambda i, sc, tab: (0, i)))
        operands.append(acc)
        if not final:
            aliases = {len(operands) - 1: 0}
    if whole is not None:
        in_specs.append(pl.BlockSpec(memory_space=pltpu.HBM))
        operands.append(whole)
        aliases = {len(operands) - 1: 0}
    if final:
        out_specs = [pl.BlockSpec((capacity, width), lambda i, sc, tab: (0, sc[last] * steps + i))]
        out_shape = [jax.ShapeDtypeStruct((capacity, whole_cols), lhs.dtype)]
        for _ in range(lhs_count - 1):
            out_specs.append(pl.BlockSpec((capacity, width), lambda i, sc, tab: (0, i)))
            out_shape.append(jax.ShapeDtypeStruct((capacity, int_cols), lhs.dtype))
    else:
        out_specs = [pl.BlockSpec((m, width), lambda i, sc, tab: (0, i))]
        out_shape = [jax.ShapeDtypeStruct((m, int_cols), jnp.float32)]
    k = slot_count * depth
    return pl.pallas_call(
        functools.partial(partial_body, (lhs_count, slot_count, acc is not None, final, whole is not None)),
        out_shape=out_shape,
        grid_spec=pltpu.PrefetchScalarGridSpec(
            num_scalar_prefetch=2,
            grid=(steps,),
            in_specs=in_specs,
            out_specs=out_specs,
            scratch_shapes=[pltpu.VMEM((m, k), lhs.dtype), pltpu.VMEM((k, width), lhs.dtype)],
        ),
        input_output_aliases=aliases,
        compiler_params=params(),
        cost_estimate=pl.CostEstimate(
            flops=4 * m * k * int_cols, bytes_accessed=8 * m * int_cols + k * int_cols, transcendentals=0
        ),
        name="last_blocks" if final else "first_blocks",
    )(*operands)


def tie_body(*refs):
    pass


def tie(value, *others):
    return pl.pallas_call(
        tie_body,
        out_shape=jax.ShapeDtypeStruct(value.shape, value.dtype),
        in_specs=[pl.BlockSpec(memory_space=pltpu.HBM)] * (1 + len(others)),
        out_specs=pl.BlockSpec(memory_space=pltpu.HBM),
        input_output_aliases={0: 0},
        compiler_params=params(),
        name="tie",
    )(value, *others)


def choose_body(flag, a_ref, b_ref, out_ref, sem):
    @pl.when(flag[0] != 0)
    def _():
        pltpu.make_async_copy(a_ref, out_ref, sem).start()

    @pl.when(flag[0] == 0)
    def _():
        pltpu.make_async_copy(b_ref, out_ref, sem).start()

    pltpu.make_async_copy(a_ref, out_ref, sem).wait()


def choose(here, a, b):
    return pl.pallas_call(
        choose_body,
        out_shape=jax.ShapeDtypeStruct(a.shape, a.dtype),
        in_specs=[
            pl.BlockSpec(memory_space=pltpu.SMEM),
            pl.BlockSpec(memory_space=pltpu.HBM),
            pl.BlockSpec(memory_space=pltpu.HBM),
        ],
        out_specs=pl.BlockSpec(memory_space=pltpu.VMEM),
        scratch_shapes=[pltpu.SemaphoreType.DMA],
        compiler_params=params(),
        name="choose",
    )(here.astype(jnp.int32).reshape(1), a, b)


def place_body(place_ref, piece_ref, whole_ref, out_ref):
    out_ref[...] = piece_ref[...]


def put(piece, whole, place):
    m, n = piece.shape
    width = min(2 * MM_COLS, n)
    steps = n // width
    return pl.pallas_call(
        place_body,
        out_shape=jax.ShapeDtypeStruct(whole.shape, whole.dtype),
        grid_spec=pltpu.PrefetchScalarGridSpec(
            num_scalar_prefetch=1,
            grid=(steps,),
            in_specs=[pl.BlockSpec((m, width), lambda i, s: (0, i)), pl.BlockSpec(memory_space=pltpu.HBM)],
            out_specs=pl.BlockSpec((m, width), lambda i, s: (0, s[0] * steps + i)),
        ),
        input_output_aliases={2: 0},
        compiler_params=params(),
        cost_estimate=pl.CostEstimate(flops=0, bytes_accessed=4 * m * n, transcendentals=0),
        name="put",
    )(place.astype(jnp.int32).reshape(1), piece, whole)


def col_index(ie, ia, ib, core):
    return ((ie * 2 + ia) * 2 + ib) * 2 + core


def on_device(amplitudes, amp_mask, integrals, int_tiles, pair_dest):
    rows = lax.axis_size("row")
    cols = lax.axis_size("col")
    extra = cols // 8
    pair_rows, amp_cols = amplitudes.shape
    int_rows, int_cols = integrals.shape
    capacity = 2 * pair_rows // cols
    z = lax.axis_index("row")
    me = lax.axis_index("col")
    core = lax.rem(me, 2)
    ib = lax.rem(lax.div(me, 2), 2)
    ia = lax.rem(lax.div(me, 4), 2)
    ie = lax.div(me, 8)
    every = [(e, a, b, c) for e in range(extra) for a in range(2) for b in range(2) for c in range(2)]

    amp_scale = amp_mask.astype(jnp.bfloat16)
    amp_used = (
        amplitudes.reshape(amp_mask.shape[0], TILE, amp_mask.shape[1], TILE) * amp_scale[:, None, :, None]
    ).reshape(pair_rows, amp_cols)
    amp_all = lax.all_gather(amp_used, "col", axis=1, tiled=True)

    own_lists = int_tiles[:, 0, :]
    count = own_lists.shape[1]
    tiles = (int_rows // TILE) * (int_cols // TILE)
    found = own_lists[:, None, :] == jnp.arange(tiles, dtype=jnp.int32)[None, :, None]
    own_table = jnp.min(jnp.where(found, jnp.arange(count, dtype=jnp.int32), count), axis=2)

    along = [
        (col_index(e, a, b, c), col_index(e, a ^ (c == 1), b ^ (c == 0), c)) for e, a, b, c in every
    ]
    across = [(col_index(e, a, b, c), col_index(e, a, b, 1 - c)) for e, a, b, c in every]
    table_next = lax.ppermute(own_table, "col", along)
    pair_tables = lax.ppermute(jnp.concatenate([own_table, table_next], axis=0), "col", across)
    tables = [own_table, table_next, pair_tables[:rows], pair_tables[rows:]]
    blocks = [[], [], [], []]

    def spread(slot):
        mine_next = lax.ppermute(slot, "col", along)
        theirs = lax.ppermute(slot, "col", across)
        theirs_next = lax.ppermute(mine_next, "col", across)
        for q, block in enumerate((slot, mine_next, theirs, theirs_next)):
            blocks[q].append(block)

    col_ids = jnp.arange(cols, dtype=jnp.int32)
    onehot = (pair_dest[:, None] == col_ids[None, :]).astype(jnp.int32)
    before = jnp.cumsum(onehot, axis=0) - onehot
    target = pair_dest * capacity + jnp.sum(before * onehot, axis=1)
    turns = [(de, da, db) for de in range(extra) for da, db in ((0, 0), (1, 0), (0, 1))]
    wanted = jnp.stack(
        [col_index(lax.rem(ie + de, extra), ia ^ da, ib ^ db, core) for de, da, db in turns]
    ).astype(jnp.int32)
    row_ids = (wanted[:, None] * capacity + jnp.arange(capacity, dtype=jnp.int32)[None, :]).reshape(-1)
    picker = (row_ids[:, None] == target[None, :]).astype(jnp.bfloat16)
    lhs = jnp.dot(picker, amp_all, preferred_element_type=jnp.bfloat16).reshape(len(turns), capacity, -1)

    panels = (0, 2, 1, 3)
    early = max(rows - 2, 1)
    hops = [(de, turn) for de in range(extra) for turn in (0, 1)]
    picks_of = {}
    for q in panels:
        kind = core if q < 2 else 1 - core
        picks_of[q] = [jnp.int32(3 * de) + turn * (1 + kind) for de, turn in hops]

    def first_sums():
        return {
            q: partial(lhs, picks_of[q], tables[q], blocks[q][:early], slot_rows[:early], int_cols)[0]
            for q in panels
        }

    packed = pack(z.astype(jnp.int32).reshape(1), own_lists, integrals)
    spread(packed)
    partner = ({}, {})
    for i in range(rows):
        if i ^ 1 < rows:
            partner[0][i] = i ^ 1
        if 0 <= ((i + 1) ^ 1) - 1 < rows:
            partner[1][i] = ((i + 1) ^ 1) - 1
    held = ({i: i for i in range(rows)}, {i: i for i in range(rows)})
    values = (packed, packed)
    history = []
    order = [[] for _ in range(rows)]
    slot_rows = [z.astype(jnp.int32)]
    filled = 1
    sums = None
    while filled < rows:
        moved, fresh = ({}, {}), []
        for side in (0, 1):
            passed = held[0] if not history else held[1 - side]
            pairs = [(p, i) for i, p in partner[side].items() if p in passed]
            moved[side].update({i: passed[p] for p, i in pairs})
            source = values[1 - side]
            fresh.append(lax.ppermute(source, "row", pairs) if pairs else None)
        if len(blocks[0]) == rows - 1 and sums is None:
            sums = first_sums()
            waited = tuple(sums.values())
        else:
            waited = (blocks[1][-1],)
        fresh = [value if value is None else tie(value, *waited) for value in fresh]
        history.append(fresh)
        for i in range(rows):
            for side in (0, 1):
                if i in moved[side]:
                    order[i].append((len(history) - 1, side, moved[side][i]))
        held, values = moved, tuple(fresh)
        while filled < rows and all(len(o) >= filled for o in order):
            kinds = sorted({order[i][filled - 1][:2] for i in range(rows)})
            slot = None
            for kind in kinds:
                here = functools.reduce(
                    jnp.logical_or, [z == i for i in range(rows) if order[i][filled - 1][:2] == kind]
                )
                value = history[kind[0]][kind[1]]
                slot = value if slot is None else choose(here, value, slot)
            origin = jnp.array([order[i][filled - 1][2] for i in range(rows)], jnp.int32)
            slot_rows.append(origin[z])
            spread(slot)
            filled += 1

    out = None
    arrived = []
    for q in panels:
        kind = core if q < 2 else 1 - core
        second = q % 2
        a_own = jnp.where(kind == 0, ia, ia ^ second)
        b_own = jnp.where(kind == 0, ib ^ second, ib)
        out, *pieces = partial(
            lhs,
            picks_of[q],
            tables[q],
            blocks[q][early:],
            slot_rows[early:],
            int_cols,
            acc=sums[q],
            whole_cols=cols * int_cols,
            whole=out,
            place=col_index(ie, a_own, b_own, kind),
        )
        for (de, turn), piece in zip(hops[1:], pieces):
            pairs = []
            for e, a, b, c in every:
                to_kind = c if q < 2 else 1 - c
                flip_a = turn if to_kind == 0 else 0
                flip_b = turn if to_kind == 1 else 0
                pairs.append((col_index(e, a, b, c), col_index((e + de) % extra, a ^ flip_a, b ^ flip_b, c)))
            got = lax.ppermute(piece, "col", pairs)
            from_e = lax.rem(ie - de + extra, extra)
            a_of = jnp.where(kind == 0, ia ^ turn, ia ^ second)
            b_of = jnp.where(kind == 0, ib ^ second, ib ^ turn)
            arrived.append((got, col_index(from_e, a_of, b_of, kind)))
    for got, place in arrived:
        out = put(got, out, place)
    return out


def solution(mesh):
    in_specs = (P("row", "col"), P("row", "col"), P("row", "col"), P(None, "col", None), P("row"))
    out_specs = P(("row", "col"), None)
    return jax.shard_map(
        on_device, mesh=mesh, in_specs=in_specs, out_specs=out_specs, check_vma=False
    )
```

time: 278 us -> 196 us (0.71)
  Pallas kernels: 123 us -> 76.8 us
  waiting for transfers between devices: 97.1 us -> 58.5 us
  local copies, waits for them, and re-layouts: 3.34 us -> 13 us
  other arithmetic: 9.23 us -> 5.4 us
  starting transfers between devices: 24.1 us -> 20.5 us
    ppermute x20 -> x19, waiting for transfers between devices: 97.1 us -> 43.8 us  [the longest x4 29.6 us: spread(): mine_next = lax.ppermute(slot, 'col', along)]
    pallas_call x24 -> x15, Pallas kernels: 113 us -> 65.4 us  [the longest x8 60.9 us: partial(): pl.pallas_call(functools.partial(partial_body, (lhs_count, slot_count, ac...]
    ppermute x4, waiting for transfers between devices: 0.01 us -> 14.7 us  [on_device(): got = lax.ppermute(piece, 'col', pairs)]
    another operation x0 -> x6, local copies, waits for them, and re-layouts: none -> 9.86 us  [partial(): jnp.stack([*picks, *slot_rows, jnp.int32(0) if place is None else place])]
    ppermute x20 -> x19, starting transfers between devices: 20 us -> 16.5 us  [the longest x4 7.66 us: spread(): mine_next = lax.ppermute(slot, 'col', along)]
    select_n x1 -> x0, other arithmetic: 2.81 us -> none  [on_device(): value = source if value is None else jnp.where(here, source, value)]
  transfers between devices with their start and end apart: 25 -> 24, of which waited for: 8 -> 8; matrix products, arithmetic and copies ran while one was open for 3% -> 12% of each run, Pallas kernels for 41% -> 38%
where the time goes in v2:
time: 196 us; the launch traced here: 195 us
  Pallas kernels  76.8 us (39%)
  waiting for transfers between devices  58.5 us (30%)
  starting transfers between devices  20.5 us (10%)
  between operations  13.6 us (7%)
  local copies, waits for them, and re-layouts  13 us (7%)
  matrix products  7.11 us (4%)
  other arithmetic  5.4 us (3%)
    pallas_call x8, Pallas kernels, partial(): pl.pallas_call(functools.partial(partial_body, (lhs_count, slot_count, ac...  60.9 us
    ppermute x4, waiting for transfers between devices, spread(): mine_next = lax.ppermute(slot, 'col', along)  29.6 us
    ppermute x4, waiting for transfers between devices, on_device(): got = lax.ppermute(piece, 'col', pairs)  14.7 us
    ppermute x5, waiting for transfers between devices, on_device(): fresh.append(lax.ppermute(source, 'row', pairs) if pairs else None)  14.1 us
    another operation x6, local copies, waits for them, and re-layouts, partial(): jnp.stack([*picks, *slot_rows, jnp.int32(0) if place is None else place])  9.86 us
    pallas_call x4, Pallas kernels, put(): pl.pallas_call(place_body, out_shape=jax.ShapeDtypeStruct(whole.shape, wh...  8.17 us
    ppermute x4, starting transfers between devices, spread(): mine_next = lax.ppermute(slot, 'col', along)  7.66 us
    dot_general x1, matrix products, on_device(): jnp.dot(picker, amp_all, preferred_element_type=jnp.bfloat16)  7.11 us
  transfers between devices with their start and end apart: 24, of which 8 were waited for; matrix products, arithmetic and copies ran while one was open for 12% of the time, Pallas kernels for 38%

profile of v2, /device:TPU:0, one launch (start us, length us, event | category | flops | bytes accessed | tf_op | source)
XLA Modules:
  0.0 194.9 jit_solution(5065821819392469702)
XLA Ops:
  6.5 0.7 convert_element_type.15
  7.7 1.9 bitcast_multiply_fusion
  9.6 3.2 %pack_tiles.1.refs_4_ = bf16[32,128,128]{2,1,0:T(8,128)(2,1)} custom-call(s32[1]{0:T(128)} %bitcast.11.row_ref, s32[4,32]{1,0:T(4,128)} %bitcast.77, bf16[512,2048]{1,0:T(8,128)(2,1)} %src_ref.1), custom_call_target="tpu_custom_call" | custom-call | tf_op jit(solution)/shard_map/pack_tiles/pallas_call | solution.py:32
  12.8 4.1 %collective-permute-start.3 = (bf16[32,128,128]{2,1,0:T(8,128)(2,1)}, bf16[32,128,128]{2,1,0:T(8,128)(2,1)}, u32[]{:S(2)}, u32[]{:S(2)}) collective-permute-start(bf16[32,128,128]{2,1,0:T(8,128)(2,1)} %pack_tiles.1.refs_4_), channel_id=1, source_target_pairs={{0,2},{1,5},{2,0},{3,7},{4,6},{5,1},{6,4},{7,3},{8,10},{9,13},{10,... | collective-permute-start | bytes 3145736 | tf_op jit(solution)/shard_map/ppermute | solution.py:254
  17.3 1.7 collective-permute-start.2
  19.1 1.1 collective-permute-start
  20.2 2.3 %reduce-window.6 = s32[8,8,128]{2,1,0:T(8,128)S(1)} reduce-window(s32[8,8,128]{2,1,0:T(8,128)S(1)} %fusion.7, s32[]{:T(128)} %constant.47.clone.1), window={size=1x1x128 pad=0_0x0_0x127_0}, to_apply=%region_1.2 | reduce-window | flops 1040384 | bytes 65540 | tf_op jit(solution)/shard_map/reduce-window
  22.9 12.7 %collective-permute-done.3.refs_1_.refs_4_ = bf16[32,128,128]{2,1,0:T(8,128)(2,1)} collective-permute-done((bf16[32,128,128]{2,1,0:T(8,128)(2,1)}, bf16[32,128,128]{2,1,0:T(8,128)(2,1)}, u32[]{:S(2)}, u32[]{:S(2)}) %collective-permute-start.3) | collective-permute-done | bytes 1048608 | tf_op jit(solution)/shard_map/ppermute | solution.py:254
  35.6 5.7 %collective-permute-done.5.refs_0_ = bf16[32,128,128]{2,1,0:T(8,128)(2,1)} collective-permute-done((bf16[32,128,128]{2,1,0:T(8,128)(2,1)}, bf16[32,128,128]{2,1,0:T(8,128)(2,1)}, u32[]{:S(2)}, u32[]{:S(2)}) %collective-permute-start.5) | collective-permute-done | bytes 1048608 | tf_op jit(solution)/shard_map/ppermute | solution.py:308
  41.3 1.5 collective-permute-start.6
  42.8 1.7 collective-permute-start.9
  44.5 1.3 collective-permute-start.4
  46.1 0.6 dynamic_slice.11
  46.8 1.3 stack.69.scalars
  48.1 1.2 stack.68.scalars
  49.3 0.6 fusion.8
  50.4 11.2 %collective-permute-done.6.refs_1_.refs_5_ = bf16[32,128,128]{2,1,0:T(8,128)(2,1)} collective-permute-done((bf16[32,128,128]{2,1,0:T(8,128)(2,1)}, bf16[32,128,128]{2,1,0:T(8,128)(2,1)}, u32[]{:S(2)}, u32[]{:S(2)}) %collective-permute-start.6) | collective-permute-done | bytes 1048608 | tf_op jit(solution)/shard_map/ppermute | solution.py:254
  61.7 1.5 collective-permute-start.10
  63.2 8.4 %collective-permute-done.4.refs_0_ = bf16[32,128,128]{2,1,0:T(8,128)(2,1)} collective-permute-done((bf16[32,128,128]{2,1,0:T(8,128)(2,1)}, bf16[32,128,128]{2,1,0:T(8,128)(2,1)}, u32[]{:S(2)}, u32[]{:S(2)}) %collective-permute-start.4) | collective-permute-done | bytes 1048608 | tf_op jit(solution)/shard_map/ppermute | solution.py:308
  71.6 2.2 %choose.2.refs_4_ = bf16[32,128,128]{2,1,0:T(8,128)(2,1)} custom-call(s32[1]{0:T(128)} %bitcast.10.flag, bf16[32,128,128]{2,1,0:T(8,128)(2,1)} %tie.7.a_ref, bf16[32,128,128]{2,1,0:T(8,128)(2,1)} %tie.5.b_ref), custom_call_target="tpu_custom_call" | custom-call | tf_op jit(solution)/shard_map/choose/pallas_call | solution.py:174
  74.0 7.1 %fusion = bf16[768,2048]{1,0:T(8,128)(2,1)} fusion(bf16[1024,2048]{1,0:T(8,128)(2,1)} %all-gather.2.cloned.1.call-done, s32[1024]{0:T(1024)S(1)} %multiply_add_fusion, s32[768]{0:T(1024)S(1)} %add.136), kind=kOutput, calls=%fused_computation | convolution fusion | flops 3222011904 | bytes 7347200 | tf_op jit(solution)/shard_map/dot_general | solution.py:270
  81.1 7.4 %first_blocks.4.refs_1_.refs_6_ = f32[512,2048]{1,0:T(8,128)} custom-call(s32[5]{0:T(128)} %stack.68.scalars, s32[4,64]{1,0:T(4,128)} %copy-done.1, bf16[3,256,2048]{2,1,0:T(8,128)(2,1)} %bitcast.42, bf16[3,256,2048]{2,1,0:T(8,128)(2,1)} %bitcast.43, bf16[3,256,2048]{2,1,0:T(8,128)(2,1)} %bitcast.44, bf16[3,256,2048]{2,1,0:T(8,128)(2,1)} %bitcast.45, ...), custom_call_target="tpu_custom_call" | custom-call | flops 4294967296 | bytes 10485760 | tf_op jit(solution)/shard_map/first_blocks/pallas_call | solution.py:126
  88.5 7.5 %first_blocks.6.refs_3_.refs_6_ = f32[512,2048]{1,0:T(8,128)} custom-call(s32[5]{0:T(128)} %stack.68.scalars, s32[4,64]{1,0:T(4,128)} %copy-done.2, bf16[3,256,2048]{2,1,0:T(8,128)(2,1)} %bitcast.46, bf16[3,256,2048]{2,1,0:T(8,128)(2,1)} %bitcast.47, bf16[3,256,2048]{2,1,0:T(8,128)(2,1)} %bitcast.48, bf16[3,256,2048]{2,1,0:T(8,128)(2,1)} %bitcast.49, ...), custom_call_target="tpu_custom_call" | custom-call | flops 4294967296 | bytes 10485760 | tf_op jit(solution)/shard_map/first_blocks/pallas_call | solution.py:126
  95.9 1.6 collective-permute-start.7
  97.6 7.4 %first_blocks.7.refs_4_.refs_6_ = f32[512,2048]{1,0:T(8,128)} custom-call(s32[5]{0:T(128)} %stack.69.scalars, s32[4,64]{1,0:T(4,128)} %get-tuple-element.22.table, bf16[3,256,2048]{2,1,0:T(8,128)(2,1)} %bitcast.50, bf16[3,256,2048]{2,1,0:T(8,128)(2,1)} %bitcast.51, bf16[3,256,2048]{2,1,0:T(8,128)(2,1)} %bitcast.52, bf16[3,256,2048]{2,1,0:T(8,128)(2,1)} %bitcast.53, ...), custom_call_target="tpu_custom_call" | custom-call | flops 4294967296 | bytes 10485760 | tf_op jit(solution)/shard_map/first_blocks/pallas_call | solution.py:126
  105.0 7.4 %first_blocks.5.refs_2_.refs_6_ = f32[512,2048]{1,0:T(8,128)} custom-call(s32[5]{0:T(128)} %stack.69.scalars, s32[4,64]{1,0:T(4,128)} %get-tuple-element.21.table, bf16[3,256,2048]{2,1,0:T(8,128)(2,1)} %bitcast.57, bf16[3,256,2048]{2,1,0:T(8,128)(2,1)} %bitcast.55, bf16[3,256,2048]{2,1,0:T(8,128)(2,1)} %bitcast.56, bf16[3,256,2048]{2,1,0:T(8,128)(2,1)} %bitcast.54, ...), custom_call_target="tpu_custom_call" | custom-call | flops 4294967296 | bytes 10485760 | tf_op jit(solution)/shard_map/first_blocks/pallas_call | solution.py:126
  112.4 2.3 %choose.3.refs_5_ = bf16[32,128,128]{2,1,0:T(8,128)(2,1)} custom-call(s32[1]{0:T(128)} %bitcast.10.flag, bf16[32,128,128]{2,1,0:T(8,128)(2,1)} %tie.9.a_ref, bf16[32,128,128]{2,1,0:T(8,128)(2,1)} %tie.8.b_ref), custom_call_target="tpu_custom_call" | custom-call | tf_op jit(solution)/shard_map/choose/pallas_call | solution.py:174
  115.7 0.6 dynamic_slice.10
  116.3 0.6 dynamic_slice.9
  116.8 1.8 stack.75.scalars
  118.7 1.9 stack.73.scalars
  120.5 1.8 stack.71.scalars
  122.3 1.9 stack.62.scalars
  124.2 5.7 %collective-permute-done.15.refs_5_ = bf16[32,128,128]{2,1,0:T(8,128)(2,1)} collective-permute-done((bf16[32,128,128]{2,1,0:T(8,128)(2,1)}, bf16[32,128,128]{2,1,0:T(8,128)(2,1)}, u32[]{:S(2)}, u32[]{:S(2)}) %collective-permute-start.15) | collective-permute-done | bytes 1048608 | tf_op jit(solution)/shard_map/ppermute | solution.py:254
  129.9 7.8 %last_blocks.4 = (bf16[256,16384]{1,0:T(8,128)(2,1)}, bf16[256,2048]{1,0:T(8,128)(2,1)}) custom-call(s32[5]{0:T(128)} %stack.75.scalars, s32[4,64]{1,0:T(4,128)} %copy-done.1, bf16[3,256,2048]{2,1,0:T(8,128)(2,1)} %bitcast.58, bf16[3,256,2048]{2,1,0:T(8,128)(2,1)} %bitcast.59, bf16[3,256,2048]{2,1,0:T(8,128)(2,1)} %bitcast.60, ...), custom_call_target="tpu_custom_call" | custom-call | flops 4294967296 | bytes 10485760 | tf_op jit(solution)/shard_map/last_blocks/pallas_call | solution.py:126
  138.1 7.8 %last_blocks.5 = (bf16[256,16384]{1,0:T(8,128)(2,1)}, bf16[256,2048]{1,0:T(8,128)(2,1)}) custom-call(s32[5]{0:T(128)} %stack.73.scalars, s32[4,64]{1,0:T(4,128)} %get-tuple-element.21.table, bf16[3,256,2048]{2,1,0:T(8,128)(2,1)} %bitcast.62, bf16[3,256,2048]{2,1,0:T(8,128)(2,1)} %bitcast.63, ...), custom_call_target="tpu_custom_call", output_to_operand_aliasing={{0}: (9, {})} | custom-call | flops 4294967296 | bytes 10485760 | tf_op jit(solution)/shard_map/last_blocks/pallas_call | solution.py:126
  145.9 1.3 collective-permute-start.21
  147.2 7.8 %last_blocks.6 = (bf16[256,16384]{1,0:T(8,128)(2,1)}, bf16[256,2048]{1,0:T(8,128)(2,1)}) custom-call(s32[5]{0:T(128)} %stack.71.scalars, s32[4,64]{1,0:T(4,128)} %copy-done.2, bf16[3,256,2048]{2,1,0:T(8,128)(2,1)} %bitcast.66, bf16[3,256,2048]{2,1,0:T(8,128)(2,1)} %bitcast.67, bf16[3,256,2048]{2,1,0:T(8,128)(2,1)} %bitcast.68, ...), custom_call_target="tpu_custom_call", output_to_operand_aliasing={{0}: (9, {})} | custom-call | flops 4294967296 | bytes 10485760 | tf_op jit(solution)/shard_map/last_blocks/pallas_call | solution.py:126
  155.0 0.7 collective-permute-start.20
  155.8 7.8 %last_blocks.7 = (bf16[256,16384]{1,0:T(8,128)(2,1)}, bf16[256,2048]{1,0:T(8,128)(2,1)}) custom-call(s32[5]{0:T(128)} %stack.62.scalars, s32[4,64]{1,0:T(4,128)} %get-tuple-element.22.table, bf16[3,256,2048]{2,1,0:T(8,128)(2,1)} %bitcast.70, bf16[3,256,2048]{2,1,0:T(8,128)(2,1)} %bitcast.71, ...), custom_call_target="tpu_custom_call", output_to_operand_aliasing={{0}: (9, {})} | custom-call | flops 4294967296 | bytes 10485760 | tf_op jit(solution)/shard_map/last_blocks/pallas_call | solution.py:126
  163.6 1.6 collective-permute-start.19
  165.2 2.0 %put.4.whole_ref = bf16[256,16384]{1,0:T(8,128)(2,1)} custom-call(s32[1]{0:T(128)} %bitcast.18.place_ref, bf16[256,2048]{1,0:T(8,128)(2,1)} %collective-permute-done.22.piece_ref, bf16[256,16384]{1,0:T(8,128)(2,1)} %get-tuple-element.20.whole_ref), custom_call_target="tpu_custom_call", output_to_operand_aliasing={{}: (2, {})} | custom-call | bytes 2097152 | tf_op jit(solution)/shard_map/put/pallas_call | solution.py:197
  167.2 1.9 collective-permute-done.21.piece_ref
  169.2 2.0 %put.5.whole_ref = bf16[256,16384]{1,0:T(8,128)(2,1)} custom-call(s32[1]{0:T(128)} %bitcast.17.place_ref, bf16[256,2048]{1,0:T(8,128)(2,1)} %collective-permute-done.21.piece_ref, bf16[256,16384]{1,0:T(8,128)(2,1)} %put.4.whole_ref), custom_call_target="tpu_custom_call", output_to_operand_aliasing={{}: (2, {})} | custom-call | bytes 2097152 | tf_op jit(solution)/shard_map/put/pallas_call | solution.py:197
  171.2 10.2 %collective-permute-done.20.piece_ref = bf16[256,2048]{1,0:T(8,128)(2,1)} collective-permute-done((bf16[256,2048]{1,0:T(8,128)(2,1)}, bf16[256,2048]{1,0:T(8,128)(2,1)}, u32[]{:S(2)}, u32[]{:S(2)}) %collective-permute-start.20) | collective-permute-done | bytes 1048608 | tf_op jit(solution)/shard_map/ppermute | solution.py:361
  181.4 2.0 %put.6.whole_ref = bf16[256,16384]{1,0:T(8,128)(2,1)} custom-call(s32[1]{0:T(128)} %bitcast.16.place_ref, bf16[256,2048]{1,0:T(8,128)(2,1)} %collective-permute-done.20.piece_ref, bf16[256,16384]{1,0:T(8,128)(2,1)} %put.5.whole_ref), custom_call_target="tpu_custom_call", output_to_operand_aliasing={{}: (2, {})} | custom-call | bytes 2097152 | tf_op jit(solution)/shard_map/put/pallas_call | solution.py:197
  183.5 2.5 %collective-permute-done.19.piece_ref = bf16[256,2048]{1,0:T(8,128)(2,1)} collective-permute-done((bf16[256,2048]{1,0:T(8,128)(2,1)}, bf16[256,2048]{1,0:T(8,128)(2,1)}, u32[]{:S(2)}, u32[]{:S(2)}) %collective-permute-start.19) | collective-permute-done | bytes 1048608 | tf_op jit(solution)/shard_map/ppermute | solution.py:361
  186.0 2.0 %put.7 = bf16[256,16384]{1,0:T(8,128)(2,1)} custom-call(s32[1]{0:T(128)} %bitcast.place_ref, bf16[256,2048]{1,0:T(8,128)(2,1)} %collective-permute-done.19.piece_ref, bf16[256,16384]{1,0:T(8,128)(2,1)} %put.6.whole_ref), custom_call_target="tpu_custom_call", output_to_operand_aliasing={{}: (2, {})} | custom-call | bytes 2097152 | tf_op jit(solution)/shard_map/put/pallas_call | solution.py:197
  (62 shorter events, 3.9 us)
Async XLA Ops:
  6.5 12.5 %copy-start.3 = (s32[4,1,32]{2,1,0:T(1,128)S(1)}, s32[4,1,32]{2,1,0:T(1,128)}, u32[]{:S(2)}) copy-start(s32[4,1,32]{2,1,0:T(1,128)} %param.11) | copy-start | bytes 1540
  6.5 13.6 %copy-start = (s32[1024]{0:T(1024)S(1)}, s32[1024]{0:T(1024)}, u32[]{:S(2)}) copy-start(s32[1024]{0:T(1024)} %param.12) | copy-start | bytes 12292
  6.5 67.4 %all-gather.2.cloned.1.call-start = ((), (), s32[]{:S(2)}) async-start(), calls=%async_computation | async-start | bytes 4718592 | tf_op jit(solution)/shard_map/all_gather | solution.py:236
  9.6 36.5 %copy-start.6 = (s32[4]{0:T(128)S(1)}, s32[4]{0:T(128)}, u32[]{:S(2)}) copy-start(s32[4]{0:T(128)} %constant.57.clone) | copy-start | bytes 52
  12.8 22.8 %collective-permute-start.3 = (bf16[32,128,128]{2,1,0:T(8,128)(2,1)}, bf16[32,128,128]{2,1,0:T(8,128)(2,1)}, u32[]{:S(2)}, u32[]{:S(2)}) collective-permute-start(bf16[32,128,128]{2,1,0:T(8,128)(2,1)} %pack_tiles.1.refs_4_), channel_id=1, source_target_pairs={{0,2},{1,5},{2,0},{3,7},{4,6},{5,1},{6,4},{7,3},{8,10},{9,13},{10,... | collective-permute-start | bytes 3145736 | tf_op jit(solution)/shard_map/ppermute | solution.py:254
  16.9 24.4 %collective-permute-start.5 = (bf16[32,128,128]{2,1,0:T(8,128)(2,1)}, bf16[32,128,128]{2,1,0:T(8,128)(2,1)}, u32[]{:S(2)}, u32[]{:S(2)}) collective-permute-start(bf16[32,128,128]{2,1,0:T(8,128)(2,1)} %pack_tiles.1.refs_4_), channel_id=1, source_target_pairs={{8,0},{0,8},{24,16},{16,24},{9,1},{1,9},{25,17},{17,25},{10,2},{2,... | collective-permute-start | bytes 3145736 | tf_op jit(solution)/shard_map/ppermute | solution.py:308
  17.3 27.2 %collective-permute-start.2 = (bf16[32,128,128]{2,1,0:T(8,128)(2,1)}, bf16[32,128,128]{2,1,0:T(8,128)(2,1)}, u32[]{:S(2)}, u32[]{:S(2)}) collective-permute-start(bf16[32,128,128]{2,1,0:T(8,128)(2,1)} %pack_tiles.1.refs_4_), channel_id=1, source_target_pairs={{16,8},{8,16},{17,9},{9,17},{18,10},{10,18},{19,11},{11,19},{20,12... | collective-permute-start | bytes 3145736 | tf_op jit(solution)/shard_map/ppermute | solution.py:308
  18.9 86.0 %collective-permute-start.11 = (bf16[32,128,128]{2,1,0:T(8,128)(2,1)}, bf16[32,128,128]{2,1,0:T(8,128)(2,1)}, u32[]{:S(2)}, u32[]{:S(2)}) collective-permute-start(bf16[32,128,128]{2,1,0:T(8,128)(2,1)} %pack_tiles.1.refs_4_), channel_id=1, source_target_pairs={{0,1},{1,0},{2,3},{3,2},{4,5},{5,4},{6,7},{7,6},{8,9},{9,8},{10,11... | collective-permute-start | bytes 3145736 | tf_op jit(solution)/shard_map/ppermute | solution.py:255
  19.1 42.6 %copy-start.1 = (s32[4,64]{1,0:T(4,128)}, s32[4,64]{1,0:T(4,128)S(1)}, u32[]{:S(2)}) copy-start(s32[4,64]{1,0:T(4,128)S(1)} %select_reduce_fusion.table) | copy-start | bytes 3076
  19.1 26.8 %collective-permute-start = (s32[4,64]{1,0:T(4,128)S(1)}, s32[4,64]{1,0:T(4,128)S(1)}, u32[]{:S(2)}, u32[]{:S(2)}) collective-permute-start(s32[4,64]{1,0:T(4,128)S(1)} %select_reduce_fusion.table), channel_id=1, source_target_pairs={{0,2},{1,5},{2,0},{3,7},{4,6},{5,1},{6,4},{7,3},{8,10},{9,13},{10,... | collective-permute-start | bytes 3080 | tf_op jit(solution)/shard_map/ppermute | solution.py:248
  41.3 20.3 %collective-permute-start.6 = (bf16[32,128,128]{2,1,0:T(8,128)(2,1)}, bf16[32,128,128]{2,1,0:T(8,128)(2,1)}, u32[]{:S(2)}, u32[]{:S(2)}) collective-permute-start(bf16[32,128,128]{2,1,0:T(8,128)(2,1)} %tie.6.refs_5_), channel_id=1, source_target_pairs={{0,2},{1,5},{2,0},{3,7},{4,6},{5,1},{6,4},{7,3},{8,10},{9,13},{10,... | collective-permute-start | bytes 3145736 | tf_op jit(solution)/shard_map/ppermute | solution.py:254
  42.8 18.9 %collective-permute-start.9 = (bf16[32,128,128]{2,1,0:T(8,128)(2,1)}, bf16[32,128,128]{2,1,0:T(8,128)(2,1)}, u32[]{:S(2)}, u32[]{:S(2)}) collective-permute-start(bf16[32,128,128]{2,1,0:T(8,128)(2,1)} %tie.6.refs_5_), channel_id=1, source_target_pairs={{16,8},{8,16},{17,9},{9,17},{18,10},{10,18},{19,11},{11,19},{20,12... | collective-permute-start | bytes 3145736 | tf_op jit(solution)/shard_map/ppermute | solution.py:308
  44.5 27.1 %collective-permute-start.4 = (bf16[32,128,128]{2,1,0:T(8,128)(2,1)}, bf16[32,128,128]{2,1,0:T(8,128)(2,1)}, u32[]{:S(2)}, u32[]{:S(2)}) collective-permute-start(bf16[32,128,128]{2,1,0:T(8,128)(2,1)} %tie.5.b_ref), channel_id=1, source_target_pairs={{8,0},{16,24},{9,1},{17,25},{10,2},{18,26},{11,3},{19,27},{12,4},{... | collective-permute-start | bytes 3145736 | tf_op jit(solution)/shard_map/ppermute | solution.py:308
  46.0 27.9 %copy-start.2 = (s32[4,64]{1,0:T(4,128)}, s32[4,64]{1,0:T(4,128)S(1)}, u32[]{:S(2)}) copy-start(s32[4,64]{1,0:T(4,128)S(1)} %collective-permute-done.table) | copy-start | bytes 3076
  46.0 3.3 %collective-permute-start.1 = (s32[8,64]{1,0:T(8,128)S(1)}, s32[8,64]{1,0:T(8,128)S(1)}, u32[]{:S(2)}, u32[]{:S(2)}) collective-permute-start(s32[8,64]{1,0:T(8,128)S(1)} %pad_add_fusion), channel_id=1, source_target_pairs={{0,1},{1,0},{2,3},{3,2},{4,5},{5,4},{6,7},{7,6},{8,9},{9,8},{10,11... | collective-permute-start | bytes 6152 | tf_op jit(solution)/shard_map/ppermute | solution.py:249
  49.9 55.1 %collective-permute-start.12 = (bf16[32,128,128]{2,1,0:T(8,128)(2,1)}, bf16[32,128,128]{2,1,0:T(8,128)(2,1)}, u32[]{:S(2)}, u32[]{:S(2)}) collective-permute-start(bf16[32,128,128]{2,1,0:T(8,128)(2,1)} %tie.6.refs_5_), channel_id=1, source_target_pairs={{0,1},{1,0},{2,3},{3,2},{4,5},{5,4},{6,7},{7,6},{8,9},{9,8},{10,11... | collective-permute-start | bytes 3145736 | tf_op jit(solution)/shard_map/ppermute | solution.py:255
  61.6 34.3 %collective-permute-start.13 = (bf16[32,128,128]{2,1,0:T(8,128)(2,1)}, bf16[32,128,128]{2,1,0:T(8,128)(2,1)}, u32[]{:S(2)}, u32[]{:S(2)}) collective-permute-start(bf16[32,128,128]{2,1,0:T(8,128)(2,1)} %collective-permute-done.3.refs_1_.refs_4_), channel_id=1, source_target_pairs={{0,1},{1,0},{2,3},{3,2},{4,5},{5,4},{6,7},{7,6},{8,9},{9,8},{10,11... | collective-permute-start | bytes 3145736 | tf_op jit(solution)/shard_map/ppermute | solution.py:256
  61.7 50.7 %collective-permute-start.10 = (bf16[32,128,128]{2,1,0:T(8,128)(2,1)}, bf16[32,128,128]{2,1,0:T(8,128)(2,1)}, u32[]{:S(2)}, u32[]{:S(2)}) collective-permute-start(bf16[32,128,128]{2,1,0:T(8,128)(2,1)} %tie.8.b_ref), channel_id=1, source_target_pairs={{8,0},{16,24},{9,1},{17,25},{10,2},{18,26},{11,3},{19,27},{12,4},{... | collective-permute-start | bytes 3145736 | tf_op jit(solution)/shard_map/ppermute | solution.py:308
  73.8 23.7 %collective-permute-start.14 = (bf16[32,128,128]{2,1,0:T(8,128)(2,1)}, bf16[32,128,128]{2,1,0:T(8,128)(2,1)}, u32[]{:S(2)}, u32[]{:S(2)}) collective-permute-start(bf16[32,128,128]{2,1,0:T(8,128)(2,1)} %collective-permute-done.6.refs_1_.refs_5_), channel_id=1, source_target_pairs={{0,1},{1,0},{2,3},{3,2},{4,5},{5,4},{6,7},{7,6},{8,9},{9,8},{10,11... | collective-permute-start | bytes 3145736 | tf_op jit(solution)/shard_map/ppermute | solution.py:256
  95.9 28.3 %collective-permute-start.7 = (bf16[32,128,128]{2,1,0:T(8,128)(2,1)}, bf16[32,128,128]{2,1,0:T(8,128)(2,1)}, u32[]{:S(2)}, u32[]{:S(2)}) collective-permute-start(bf16[32,128,128]{2,1,0:T(8,128)(2,1)} %choose.2.refs_4_), channel_id=1, source_target_pairs={{0,2},{1,5},{2,0},{3,7},{4,6},{5,1},{6,4},{7,3},{8,10},{9,13},{10,... | collective-permute-start | bytes 3145736 | tf_op jit(solution)/shard_map/ppermute | solution.py:254
  112.4 3.3 %copy-start.5 = (s32[4]{0:T(128)S(1)}, s32[4]{0:T(128)}, u32[]{:S(2)}) copy-start(s32[4]{0:T(128)} %constant.59.clone) | copy-start | bytes 52
  112.4 3.9 %copy-start.4 = (s32[4]{0:T(128)S(1)}, s32[4]{0:T(128)}, u32[]{:S(2)}) copy-start(s32[4]{0:T(128)} %constant.58.clone) | copy-start | bytes 52
  114.7 15.2 %collective-permute-start.15 = (bf16[32,128,128]{2,1,0:T(8,128)(2,1)}, bf16[32,128,128]{2,1,0:T(8,128)(2,1)}, u32[]{:S(2)}, u32[]{:S(2)}) collective-permute-start(bf16[32,128,128]{2,1,0:T(8,128)(2,1)} %choose.3.refs_5_), channel_id=1, source_target_pairs={{0,2},{1,5},{2,0},{3,7},{4,6},{5,1},{6,4},{7,3},{8,10},{9,13},{10,... | collective-permute-start | bytes 3145736 | tf_op jit(solution)/shard_map/ppermute | solution.py:254
  115.2 22.9 %collective-permute-start.17 = (bf16[32,128,128]{2,1,0:T(8,128)(2,1)}, bf16[32,128,128]{2,1,0:T(8,128)(2,1)}, u32[]{:S(2)}, u32[]{:S(2)}) collective-permute-start(bf16[32,128,128]{2,1,0:T(8,128)(2,1)} %choose.2.refs_4_), channel_id=1, source_target_pairs={{0,1},{1,0},{2,3},{3,2},{4,5},{5,4},{6,7},{7,6},{8,9},{9,8},{10,11... | collective-permute-start | bytes 3145736 | tf_op jit(solution)/shard_map/ppermute | solution.py:255
  115.2 22.9 %collective-permute-start.18 = (bf16[32,128,128]{2,1,0:T(8,128)(2,1)}, bf16[32,128,128]{2,1,0:T(8,128)(2,1)}, u32[]{:S(2)}, u32[]{:S(2)}) collective-permute-start(bf16[32,128,128]{2,1,0:T(8,128)(2,1)} %choose.3.refs_5_), channel_id=1, source_target_pairs={{0,1},{1,0},{2,3},{3,2},{4,5},{5,4},{6,7},{7,6},{8,9},{9,8},{10,11... | collective-permute-start | bytes 3145736 | tf_op jit(solution)/shard_map/ppermute | solution.py:255
  124.2 31.6 %collective-permute-start.8 = (bf16[32,128,128]{2,1,0:T(8,128)(2,1)}, bf16[32,128,128]{2,1,0:T(8,128)(2,1)}, u32[]{:S(2)}, u32[]{:S(2)}) collective-permute-start(bf16[32,128,128]{2,1,0:T(8,128)(2,1)} %collective-permute-done.7.refs_4_), channel_id=1, source_target_pairs={{0,1},{1,0},{2,3},{3,2},{4,5},{5,4},{6,7},{7,6},{8,9},{9,8},{10,11... | collective-permute-start | bytes 3145736 | tf_op jit(solution)/shard_map/ppermute | solution.py:256
  129.9 25.9 %collective-permute-start.16 = (bf16[32,128,128]{2,1,0:T(8,128)(2,1)}, bf16[32,128,128]{2,1,0:T(8,128)(2,1)}, u32[]{:S(2)}, u32[]{:S(2)}) collective-permute-start(bf16[32,128,128]{2,1,0:T(8,128)(2,1)} %collective-permute-done.15.refs_5_), channel_id=1, source_target_pairs={{0,1},{1,0},{2,3},{3,2},{4,5},{5,4},{6,7},{7,6},{8,9},{9,8},{10,11... | collective-permute-start | bytes 3145736 | tf_op jit(solution)/shard_map/ppermute | solution.py:256
  137.7 27.5 %collective-permute-start.22 = (bf16[256,2048]{1,0:T(8,128)(2,1)}, bf16[256,2048]{1,0:T(8,128)(2,1)}, u32[]{:S(2)}, u32[]{:S(2)}) collective-permute-start(bf16[256,2048]{1,0:T(8,128)(2,1)} %get-tuple-element.19), channel_id=1, source_target_pairs={{0,4},{1,3},{2,6},{3,1},{4,0},{5,7},{6,2},{7,5},{8,12},{9,11},{10,... | collective-permute-start | bytes 3145736 | tf_op jit(solution)/shard_map/ppermute | solution.py:361
  145.9 23.2 %collective-permute-start.21 = (bf16[256,2048]{1,0:T(8,128)(2,1)}, bf16[256,2048]{1,0:T(8,128)(2,1)}, u32[]{:S(2)}, u32[]{:S(2)}) collective-permute-start(bf16[256,2048]{1,0:T(8,128)(2,1)} %get-tuple-element.18), channel_id=1, source_target_pairs={{0,2},{1,5},{2,0},{3,7},{4,6},{5,1},{6,4},{7,3},{8,10},{9,13},{10,... | collective-permute-start | bytes 3145736 | tf_op jit(solution)/shard_map/ppermute | solution.py:361
  155.0 26.4 %collective-permute-start.20 = (bf16[256,2048]{1,0:T(8,128)(2,1)}, bf16[256,2048]{1,0:T(8,128)(2,1)}, u32[]{:S(2)}, u32[]{:S(2)}) collective-permute-start(bf16[256,2048]{1,0:T(8,128)(2,1)} %get-tuple-element.17), channel_id=1, source_target_pairs={{0,4},{1,3},{2,6},{3,1},{4,0},{5,7},{6,2},{7,5},{8,12},{9,11},{10,... | collective-permute-start | bytes 3145736 | tf_op jit(solution)/shard_map/ppermute | solution.py:361
  163.6 22.5 %collective-permute-start.19 = (bf16[256,2048]{1,0:T(8,128)(2,1)}, bf16[256,2048]{1,0:T(8,128)(2,1)}, u32[]{:S(2)}, u32[]{:S(2)}) collective-permute-start(bf16[256,2048]{1,0:T(8,128)(2,1)} %get-tuple-element.16), channel_id=1, source_target_pairs={{0,2},{1,5},{2,0},{3,7},{4,6},{5,1},{6,4},{7,3},{8,10},{9,13},{10,... | collective-permute-start | bytes 3145736 | tf_op jit(solution)/shard_map/ppermute | solution.py:361
Sparse Core Ops, SparseCore 0:
  9.8 46.8 all-gather.1

commit v3 on v0

v3 whole, which is shorter than its diff:
```python
import functools

import jax
import jax.numpy as jnp
import numpy as np
from jax import lax
from jax.experimental import pallas as pl
from jax.experimental.pallas import tpu as pltpu
from jax.sharding import PartitionSpec as P

TILE = 128
MM_COLS = 512
VMEM_LIMIT = (64 << 20) - (256 << 10)


def params():
    return pltpu.CompilerParams(vmem_limit_bytes=VMEM_LIMIT)


def pack_body(scalars, ids_ref, src_ref, out_ref):
    col_tiles = src_ref.shape[1] // TILE
    tiles = col_tiles * (src_ref.shape[0] // TILE)
    for e in range(out_ref.shape[0]):
        t = jnp.minimum(ids_ref[scalars[0], e], tiles - 1)
        k = pl.multiple_of(lax.div(t, col_tiles) * TILE, TILE)
        n = pl.multiple_of(lax.rem(t, col_tiles) * TILE, TILE)
        out_ref[e] = src_ref[pl.ds(k, TILE), pl.ds(n, TILE)]


def pack(scalars, lists, integrals):
    count = lists.shape[1]
    return pl.pallas_call(
        pack_body,
        out_shape=jax.ShapeDtypeStruct((count, TILE, TILE), integrals.dtype),
        in_specs=[
            pl.BlockSpec(memory_space=pltpu.SMEM),
            pl.BlockSpec(memory_space=pltpu.SMEM),
            pl.BlockSpec(memory_space=pltpu.VMEM),
        ],
        out_specs=pl.BlockSpec(memory_space=pltpu.VMEM),
        compiler_params=params(),
        name="pack_tiles",
    )(scalars, lists, integrals)


def mask_body(mask_ref, amp_ref, after_ref, out_ref):
    for a in range(mask_ref.shape[0]):
        for k in range(mask_ref.shape[1]):
            at = (slice(a * TILE, (a + 1) * TILE), slice(k * TILE, (k + 1) * TILE))
            scale = mask_ref[a, k].astype(jnp.float32)
            out_ref[at] = (amp_ref[at].astype(jnp.float32) * scale).astype(out_ref.dtype)


def mask_tiles(mask, amplitudes, after):
    return pl.pallas_call(
        mask_body,
        out_shape=jax.ShapeDtypeStruct(amplitudes.shape, amplitudes.dtype),
        in_specs=[
            pl.BlockSpec(memory_space=pltpu.SMEM),
            pl.BlockSpec(memory_space=pltpu.VMEM),
            pl.BlockSpec(memory_space=pltpu.HBM),
        ],
        out_specs=pl.BlockSpec(memory_space=pltpu.VMEM),
        compiler_params=params(),
        name="mask_tiles",
    )(mask, amplitudes, after)


def pick_body(first, capacity, scalars, target_ref, *refs):
    amps, (mine, theirs) = refs[:-2], refs[-2:]
    step = pl.program_id(0)
    half = pl.num_programs(0) // 2
    rows = scalars[first + step] * capacity + lax.broadcasted_iota(jnp.int32, (capacity, target_ref.shape[1]), 0)
    chosen = jnp.where(rows == target_ref[...], 1.0, 0.0).astype(mine.dtype)
    for at, amp in enumerate(amps):
        value = jnp.dot(chosen, amp[...], preferred_element_type=jnp.float32).astype(mine.dtype)

        @pl.when(step < half)
        def _():
            theirs[at, 0] = value

        @pl.when(step >= half)
        def _():
            mine[at, 0] = value


def pick_rows(scalars, first, count, target, amps, capacity):
    n, k = amps[0].shape
    shape = jax.ShapeDtypeStruct((len(amps), count, capacity, k), amps[0].dtype)
    block = (len(amps), 1, capacity, k)
    return pl.pallas_call(
        functools.partial(pick_body, first, capacity),
        out_shape=[shape, shape],
        grid_spec=pltpu.PrefetchScalarGridSpec(
            num_scalar_prefetch=1,
            grid=(2 * count,),
            in_specs=[pl.BlockSpec((1, n), lambda i, s: (0, 0))]
            + [pl.BlockSpec((n, k), lambda i, s: (0, 0)) for _ in amps],
            out_specs=[
                pl.BlockSpec(block, lambda i, s: (0, jnp.maximum(i - count, 0), 0, 0)),
                pl.BlockSpec(block, lambda i, s: (0, jnp.minimum(i, count - 1), 0, 0)),
            ],
        ),
        compiler_params=params(),
        cost_estimate=pl.CostEstimate(
            flops=4 * count * capacity * n * k * len(amps), bytes_accessed=8 * n * k * len(amps), transcendentals=0
        ),
        name="pick_rows",
    )(scalars, target.reshape(1, n), *amps)


def product_body(at, has_whole, scalars, table, mine, theirs, *refs):
    core_at, picks, rows_at, mine_at, theirs_at = at
    slot_count = len(rows_at)
    packed_hbm = refs[:slot_count]
    refs = refs[slot_count + has_whole :]
    outs, (lhs_all, rhs_all, packed, lhs_sem, sems) = refs[:-5], refs[-5:]
    step = pl.program_id(0)
    capacity, part = mine.shape[2:]
    depth = lhs_all.shape[1] // slot_count
    width = rhs_all.shape[1]
    count = packed.shape[1]
    col_tiles = table.shape[1] // (depth // TILE)

    @pl.when(step == 0)
    def _():
        for s in range(slot_count):
            pltpu.make_async_copy(packed_hbm[s], packed.at[s], sems.at[s]).start()
        for s in range(slot_count):
            for source, chip, side in (
                (mine, scalars[mine_at[s]], scalars[core_at]),
                (theirs, scalars[theirs_at[s]], 1 - scalars[core_at]),
            ):
                lanes = pl.ds(pl.multiple_of(s * depth + side * part, part), part)
                for t, pick in enumerate(picks):
                    pltpu.make_async_copy(
                        source.at[chip, scalars[pick]], lhs_all.at[pl.ds(t * capacity, capacity), lanes], lhs_sem
                    ).start()
        for s in range(slot_count):
            pltpu.make_async_copy(packed_hbm[s], packed.at[s], sems.at[s]).wait()
        pltpu.make_async_copy(lhs_all, lhs_all, lhs_sem).wait()

    for s in range(slot_count):
        row = scalars[rows_at[s]]
        for k in range(depth // TILE):
            for n in range(width // TILE):
                e = table[row, k * col_tiles + step * (width // TILE) + n]
                tile = packed[s, jnp.minimum(e, count - 1)]
                rhs_all[s * depth + k * TILE : s * depth + (k + 1) * TILE, n * TILE : (n + 1) * TILE] = jnp.where(
                    e < count, tile, jnp.zeros_like(tile)
                )
    total = jnp.dot(lhs_all[...], rhs_all[...], preferred_element_type=jnp.float32)
    for t in range(len(picks)):
        outs[t][...] = total[t * capacity : (t + 1) * capacity].astype(outs[t].dtype)


def product(scalars, table, mine, theirs, slots, int_cols, whole_cols, whole, at, place_at):
    core_at, picks, rows_at, mine_at, theirs_at = at
    capacity, part = mine.shape[2:]
    slot_count, m = len(slots), len(picks) * capacity
    depth = 2 * part
    width = min(MM_COLS, int_cols)
    steps = int_cols // width
    hbm = pl.BlockSpec(memory_space=pltpu.HBM)
    operands = [scalars, table, mine, theirs, *slots]
    aliases = {}
    if whole is not None:
        aliases = {len(operands): 0}
        operands.append(whole)
    out_specs = [pl.BlockSpec((capacity, width), lambda i, sc, tab: (0, sc[place_at] * steps + i))]
    out_shape = [jax.ShapeDtypeStruct((capacity, whole_cols), mine.dtype)]
    for _ in picks[1:]:
        out_specs.append(pl.BlockSpec((capacity, width), lambda i, sc, tab: (0, i)))
        out_shape.append(jax.ShapeDtypeStruct((capacity, int_cols), mine.dtype))
    k = slot_count * depth
    return pl.pallas_call(
        functools.partial(product_body, at, whole is not None),
        out_shape=out_shape,
        grid_spec=pltpu.PrefetchScalarGridSpec(
            num_scalar_prefetch=2,
            grid=(steps,),
            in_specs=[hbm] * (len(operands) - 2),
            out_specs=out_specs,
            scratch_shapes=[
                pltpu.VMEM((m, k), mine.dtype),
                pltpu.VMEM((k, width), mine.dtype),
                pltpu.VMEM((slot_count, *slots[0].shape), mine.dtype),
                pltpu.SemaphoreType.DMA,
                pltpu.SemaphoreType.DMA((slot_count,)),
            ],
        ),
        input_output_aliases=aliases,
        compiler_params=params(),
        cost_estimate=pl.CostEstimate(
            flops=4 * m * k * int_cols, bytes_accessed=2 * m * (k + int_cols) + k * int_cols, transcendentals=0
        ),
        name="product",
    )(*operands)


def tie_body(*refs):
    pass


def tie(value, *others):
    return pl.pallas_call(
        tie_body,
        out_shape=jax.ShapeDtypeStruct(value.shape, value.dtype),
        in_specs=[pl.BlockSpec(memory_space=pltpu.HBM)] * (1 + len(others)),
        out_specs=pl.BlockSpec(memory_space=pltpu.HBM),
        input_output_aliases={0: 0},
        compiler_params=params(),
        name="tie",
    )(value, *others)


def choose_body(at, scalars, into_ref, other_ref, out_ref, sem):
    @pl.when(scalars[at] != 0)
    def _():
        copy = pltpu.make_async_copy(other_ref, out_ref, sem)
        copy.start()
        copy.wait()


def choose(scalars, at, into, other):
    return pl.pallas_call(
        functools.partial(choose_body, at),
        out_shape=jax.ShapeDtypeStruct(into.shape, into.dtype),
        in_specs=[
            pl.BlockSpec(memory_space=pltpu.SMEM),
            pl.BlockSpec(memory_space=pltpu.HBM),
            pl.BlockSpec(memory_space=pltpu.HBM),
        ],
        out_specs=pl.BlockSpec(memory_space=pltpu.HBM),
        scratch_shapes=[pltpu.SemaphoreType.DMA],
        input_output_aliases={1: 0},
        compiler_params=params(),
        name="choose",
    )(scalars, into, other)


def place_body(place_ref, piece_ref, whole_ref, out_ref):
    out_ref[...] = piece_ref[...]


def put(piece, whole, scalars, at):
    m, n = piece.shape
    width = min(2 * MM_COLS, n)
    steps = n // width
    return pl.pallas_call(
        place_body,
        out_shape=jax.ShapeDtypeStruct(whole.shape, whole.dtype),
        grid_spec=pltpu.PrefetchScalarGridSpec(
            num_scalar_prefetch=1,
            grid=(steps,),
            in_specs=[pl.BlockSpec((m, width), lambda i, s: (0, i)), pl.BlockSpec(memory_space=pltpu.HBM)],
            out_specs=pl.BlockSpec((m, width), lambda i, s: (0, s[at] * steps + i)),
        ),
        input_output_aliases={2: 0},
        compiler_params=params(),
        cost_estimate=pl.CostEstimate(flops=0, bytes_accessed=4 * m * n, transcendentals=0),
        name="put",
    )(scalars, piece, whole)


def col_index(ie, ia, ib, core):
    return ((ie * 2 + ia) * 2 + ib) * 2 + core


class Scalars:
    def __init__(self, rows, cols):
        self.places = [(z, me // 8, me // 4 % 2, me // 2 % 2, me % 2) for z in range(rows) for me in range(cols)]
        self.columns = []

    def add(self, value_of):
        self.columns.append([int(value_of(*place)) for place in self.places])
        return len(self.columns) - 1

    def of_device(self, z, me, cols):
        table = np.array(self.columns, np.int32).T
        return lax.dynamic_slice(jnp.asarray(table), (z * cols + me, 0), (1, table.shape[1]))[0]


def line_schedule(rows):
    partner = ({}, {})
    for i in range(rows):
        if i ^ 1 < rows:
            partner[0][i] = i ^ 1
        if 0 <= ((i + 1) ^ 1) - 1 < rows:
            partner[1][i] = ((i + 1) ^ 1) - 1
    held = ({i: i for i in range(rows)}, {i: i for i in range(rows)})
    steps, order = [], [[] for _ in range(rows)]
    while min(len(o) for o in order) < rows - 1:
        moved, pairs = ({}, {}), []
        for side in (0, 1):
            passed = held[1 - side]
            pairs.append([(p, i) for i, p in partner[side].items() if p in passed])
            moved[side].update({i: passed[p] for p, i in pairs[side]})
        for i in range(rows):
            for side in (0, 1):
                if i in moved[side]:
                    order[i].append((len(steps), side, moved[side][i]))
        steps.append(pairs)
        held = moved
    return steps, order


def on_device(amplitudes, amp_mask, integrals, int_tiles, pair_dest):
    rows = lax.axis_size("row")
    cols = lax.axis_size("col")
    extra = cols // 8
    pair_rows, amp_cols = amplitudes.shape
    int_rows, int_cols = integrals.shape
    capacity = 2 * pair_rows // cols
    every = [(e, a, b, c) for e in range(extra) for a in range(2) for b in range(2) for c in range(2)]
    chips = [(e, a, b) for e in range(extra) for a in range(2) for b in range(2)]
    hops = [(de, turn) for de in range(extra) for turn in (0, 1)]
    turns = [(de, da, db) for de in range(extra) for da, db in ((0, 0), (1, 0), (0, 1))]
    steps, order = line_schedule(rows)

    def permute(value, moved_to):
        return lax.ppermute(value, "col", [(col_index(*at), col_index(*moved_to(*at))) for at in every])

    def along(e, a, b, c):
        return e, a ^ (c == 1), b ^ (c == 0), c

    def other(e, a, b, c):
        return e, a ^ (c == 0), b ^ (c == 1), c

    def across(e, a, b, c):
        return e, a, b, 1 - c

    consts = Scalars(rows, cols)
    consts.add(lambda z, e, a, b, c: z)
    core_at = consts.add(lambda z, e, a, b, c: c)
    wanted_at = len(consts.columns)
    for flip in (1, 0):
        for de, da, db in turns:
            consts.add(lambda z, e, a, b, c: col_index((e + de) % extra, a ^ da, b ^ db, c ^ flip))
    slot_rows = [lambda z: z] + [functools.partial(lambda j, z: order[z][j][2], j) for j in range(rows - 1)]
    rows_at = [consts.add(lambda z, e, a, b, c: row(z)) for row in slot_rows]
    gathered = [(de, p, q) for de in range(extra) for q in (0, 1) for p in (0, 1)]

    def arrival(chip, e, a, b, c):
        ce, ca, cb = chips[chip]
        p, q = (cb ^ b, ca ^ a) if c == 0 else (ca ^ a, cb ^ b)
        return gathered.index(((ce - e) % extra, p, q))

    mine_at = [consts.add(lambda z, e, a, b, c: arrival(row(z), e, a, b, c)) for row in slot_rows]
    theirs_at = [consts.add(lambda z, e, a, b, c: arrival(row(z), e, a, b, 1 - c)) for row in slot_rows]
    picks_at, place_at, arrive_at = {}, {}, {}
    for q in range(4):
        flip, second = int(q >= 2), q % 2
        picks_at[q] = [
            consts.add(lambda z, e, a, b, c: 3 * de + turn * (1 + (c ^ flip))) for de, turn in hops
        ]

        def block(e, a, b, kind, turn):
            return col_index(e, a ^ (second if kind else turn), b ^ (turn if kind else second), kind)

        place_at[q] = consts.add(lambda z, e, a, b, c: block(e, a, b, c ^ flip, 0))
        arrive_at[q] = [
            consts.add(lambda z, e, a, b, c: block((e - de) % extra, a, b, c ^ flip, turn)) for de, turn in hops[1:]
        ]
    flags_at = {}
    for j in range(rows - 1):
        kinds = sorted({order[i][j][:2] for i in range(rows)})
        for kind in kinds[:-1]:
            flags_at[j, kind] = consts.add(lambda z, e, a, b, c: order[z][j][:2] == kind)
    scalars = consts.of_device(lax.axis_index("row"), lax.axis_index("col"), cols)

    own_lists = int_tiles[:, 0, :]
    packed = pack(scalars, own_lists, integrals)

    def line_step(values, pairs):
        return [lax.ppermute(values[1 - side], "row", pairs[side]) if pairs[side] else None for side in (0, 1)]

    fresh = line_step((packed, packed), steps[0])
    amp_used = mask_tiles(amp_mask, amplitudes, packed)
    amp_next = permute(amp_used, along)
    amp_other = permute(amp_used, other)
    amp_far = permute(amp_next, other)
    amps = [amp_used, amp_next, amp_other, amp_far]
    for de in range(1, extra):
        amps += [permute(amp, lambda e, a, b, c: ((e - de) % extra, a, b, c)) for amp in amps[:4]]

    count = own_lists.shape[1]
    tiles = (int_rows // TILE) * (int_cols // TILE)
    found = own_lists[:, None, :] == jnp.arange(tiles, dtype=jnp.int32)[None, :, None]
    own_table = jnp.min(jnp.where(found, jnp.arange(count, dtype=jnp.int32), count), axis=2)
    table_next = permute(own_table, along)
    pair_tables = permute(jnp.concatenate([own_table, table_next], axis=0), across)
    tables = [own_table, table_next, pair_tables[:rows], pair_tables[rows:]]

    col_ids = jnp.arange(cols, dtype=jnp.int32)
    onehot = (pair_dest[:, None] == col_ids[None, :]).astype(jnp.int32)
    before = jnp.cumsum(onehot, axis=0) - onehot
    target = pair_dest * capacity + jnp.sum(before * onehot, axis=1)
    mine, for_them = pick_rows(scalars, wanted_at, len(turns), target, amps, capacity)
    theirs = permute(for_them, across)

    blocks = [[], [], [], []]

    def spread(slot, last):
        mine_next = permute(slot, along)
        blocks[0].append(slot)
        blocks[2].append(permute(slot, across))
        if not last:
            blocks[1].append(mine_next)
            blocks[3].append(permute(mine_next, across))
        return mine_next

    last_next = spread(packed, rows == 1)
    history = []
    for at in range(len(steps)):
        if at > 0:
            fresh = line_step(history[-1], steps[at])
        if at == 0:
            waited = (amp_far, amp_other, pair_tables)
        elif at < len(steps) - 1:
            waited = (*blocks[1], *blocks[2])
        else:
            waited = (theirs, *blocks[1][-1:], *blocks[2][-1:], *blocks[3][:-1])
        history.append([value if value is None else tie(value, *waited) for value in fresh])
        while len(blocks[0]) < rows and all(order[i][len(blocks[0]) - 1][0] <= at for i in range(rows)):
            j = len(blocks[0]) - 1
            kinds = sorted({order[i][j][:2] for i in range(rows)})
            slot = history[kinds[-1][0]][kinds[-1][1]]
            for kind in kinds[:-1]:
                slot = choose(scalars, flags_at[j, kind], slot, history[kind[0]][kind[1]])
            last_next = spread(slot, j == rows - 2)

    out = None
    arrived = []
    for q in (0, 2, 1, 3):
        out, *pieces = product(
            scalars,
            tables[q],
            mine,
            theirs,
            blocks[q],
            int_cols,
            cols * int_cols,
            out,
            (core_at, picks_at[q], rows_at, mine_at, theirs_at),
            place_at[q],
        )
        for (de, turn), piece, place in zip(hops[1:], pieces, arrive_at[q]):
            def sent_to(e, a, b, c):
                kind = c ^ int(q >= 2)
                return (e + de) % extra, a ^ (0 if kind else turn), b ^ (turn if kind else 0), c

            arrived.append((permute(piece, sent_to), place))
        if q == 0:
            last_next = tie(last_next, pieces[0])
            blocks[1].append(last_next)
            blocks[3].append(permute(last_next, across))
    for got, place in arrived:
        out = put(got, out, scalars, place)
    return out


def solution(mesh):
    in_specs = (P("row", "col"), P("row", "col"), P("row", "col"), P(None, "col", None), P("row"))
    out_specs = P(("row", "col"), None)
    return jax.shard_map(
        on_device, mesh=mesh, in_specs=in_specs, out_specs=out_specs, check_vma=False
    )
```

time: 295 us -> 235 us (0.80)
  the two profiles are of different devices: /device:TPU:0 before, /device:TPU:9 now
where the time goes in v3:
time: 235 us; the launch traced here: 234 us
  Pallas kernels  138 us (59%)
  waiting for transfers between devices  50.3 us (21%)
  starting transfers between devices  38.5 us (16%)
  other arithmetic  3.92 us (2%)
  local copies, waits for them, and re-layouts  3.51 us (1%)
    pallas_call x2, Pallas kernels, choose(): pl.pallas_call(functools.partial(choose_body, at), out_shape=jax.ShapeDty...  67.2 us
    pallas_call x4, Pallas kernels, product(): pl.pallas_call(functools.partial(product_body, at, whole is not None), ou...  41.2 us
    ppermute x22, waiting for transfers between devices, permute(): lax.ppermute(value, 'col', [(col_index(*at), col_index(*moved_to(*at))) f...  28 us
    ppermute x22, starting transfers between devices, permute(): lax.ppermute(value, 'col', [(col_index(*at), col_index(*moved_to(*at))) f...  26.9 us
    ppermute x5, waiting for transfers between devices, line_step(): lax.ppermute(values[1 - side], 'row', pairs[side])  22.3 us
    pallas_call x1, Pallas kernels, pick_rows(): pl.pallas_call(functools.partial(pick_body, first, capacity), out_shape=[...  13.7 us
    ppermute x5, starting transfers between devices, line_step(): lax.ppermute(values[1 - side], 'row', pairs[side])  11.6 us
    pallas_call x4, Pallas kernels, put(): pl.pallas_call(place_body, out_shape=jax.ShapeDtypeStruct(whole.shape, wh...  10.9 us
  transfers between devices with their start and end apart: 27, of which 6 were waited for; matrix products, arithmetic and copies ran while one was open for 2% of the time, Pallas kernels for 41%

profile of v3, /device:TPU:9, one launch (start us, length us, event | category | flops | bytes accessed | tf_op | source)
XLA Modules:
  0.0 234.3 jit_solution(6215939826131668890)
XLA Ops:
  0.0 1.4 copy.24.mask_ref
  1.4 1.3 dynamic-slice_bitcast_fusion.scalars.place_ref
  2.6 2.9 %pack_tiles.1.after_ref.refs_0_ = bf16[32,128,128]{2,1,0:T(8,128)(2,1)} custom-call(s32[38]{0:T(128)} %dynamic-slice_bitcast_fusion.scalars.place_ref, s32[4,32]{1,0:T(4,128)} %bitcast.26, bf16[512,2048]{1,0:T(8,128)(2,1)} %src_ref.1), custom_call_target="tpu_custom_call" | custom-call | tf_op jit(solution)/shard_map/pack_tiles/pallas_call | solution.py:32
  5.5 2.0 mask_tiles.1.refs_0_
  7.4 1.2 collective-permute-start.2
  8.7 0.2 collective-permute-start.8
  8.8 1.2 collective-permute-start.3
  10.1 8.5 %collective-permute-done.2.refs_1_ = bf16[1024,256]{1,0:T(8,128)(2,1)S(1)} collective-permute-done((bf16[1024,256]{1,0:T(8,128)(2,1)}, bf16[1024,256]{1,0:T(8,128)(2,1)S(1)}, u32[]{:S(2)}, u32[]{:S(2)}) %collective-permute-start.2) | collective-permute-done | bytes 524320 | tf_op jit(solution)/shard_map/ppermute | solution.py:322
  18.5 2.6 %collective-permute-start.4 = (bf16[1024,256]{1,0:T(8,128)(2,1)S(1)}, bf16[1024,256]{1,0:T(8,128)(2,1)}, u32[]{:S(2)}, u32[]{:S(2)}) collective-permute-start(bf16[1024,256]{1,0:T(8,128)(2,1)S(1)} %collective-permute-done.2.refs_1_), channel_id=1, source_target_pairs={{0,4},{1,3},{2,6},{3,1},{4,0},{5,7},{6,2},{7,5},{8,12},{9,11},{10,... | collective-permute-start | bytes 1572872 | tf_op jit(solution)/shard_map/ppermute | solution.py:322
  21.2 0.8 select_reduce_fusion.table
  22.0 0.8 collective-permute-start
  22.8 2.1 collective-permute-done.table
  24.9 3.5 %collective-permute-start.1 = (s32[8,64]{1,0:T(8,128)S(1)}, s32[8,64]{1,0:T(8,128)S(1)}, u32[]{:S(2)}, u32[]{:S(2)}) collective-permute-start(s32[8,64]{1,0:T(8,128)S(1)} %pad_add_fusion), channel_id=1, source_target_pairs={{0,1},{1,0},{2,3},{3,2},{4,5},{5,4},{6,7},{7,6},{8,9},{9,8},{10,11... | collective-permute-start | bytes 6152 | tf_op jit(solution)/shard_map/ppermute | solution.py:322
  28.3 3.7 %collective-permute-start.11 = (bf16[32,128,128]{2,1,0:T(8,128)(2,1)}, bf16[32,128,128]{2,1,0:T(8,128)(2,1)}, u32[]{:S(2)}, u32[]{:S(2)}) collective-permute-start(bf16[32,128,128]{2,1,0:T(8,128)(2,1)} %pack_tiles.1.after_ref.refs_0_), channel_id=1, source_target_pairs={{16,8},{8,16},{17,9},{9,17},{18,10},{10,18},{19,11},{11,19},{20,12... | collective-permute-start | bytes 3145736 | tf_op jit(solution)/shard_map/ppermute | solution.py:376
  32.2 1.8 collective-permute-start.13
  34.1 2.3 reduce-window.6
  36.4 0.3 slice_reduce_fusion
  36.6 0.2 reduce-window.9
  36.9 2.0 collective-permute-start.14
  39.0 16.9 %collective-permute-done.11.refs_0_ = bf16[32,128,128]{2,1,0:T(8,128)(2,1)} collective-permute-done((bf16[32,128,128]{2,1,0:T(8,128)(2,1)}, bf16[32,128,128]{2,1,0:T(8,128)(2,1)}, u32[]{:S(2)}, u32[]{:S(2)}) %collective-permute-start.11) | collective-permute-done | bytes 1048608 | tf_op jit(solution)/shard_map/ppermute | solution.py:376
  55.9 3.1 %collective-permute-start.17 = (bf16[32,128,128]{2,1,0:T(8,128)(2,1)}, bf16[32,128,128]{2,1,0:T(8,128)(2,1)}, u32[]{:S(2)}, u32[]{:S(2)}) collective-permute-start(bf16[32,128,128]{2,1,0:T(8,128)(2,1)} %tie.6.refs_1_), channel_id=1, source_target_pairs={{16,8},{8,16},{17,9},{9,17},{18,10},{10,18},{19,11},{11,19},{20,12... | collective-permute-start | bytes 3145736 | tf_op jit(solution)/shard_map/ppermute | solution.py:376
  59.0 2.3 collective-permute-start.12
  61.3 1.1 collective-permute-start.7
  62.4 0.6 multiply_add_fusion
  63.0 13.7 %pick_rows.1 = (bf16[4,3,256,256]{3,2,1,0:T(8,128)(2,1)}, bf16[4,3,256,256]{3,2,1,0:T(8,128)(2,1)}) custom-call(s32[38]{0:T(128)} %dynamic-slice_bitcast_fusion.scalars.place_ref, s32[1,1024]{1,0:T(1,128)} %bitcast.28, bf16[1024,256]{1,0:T(8,128)(2,1)} %mask_tiles.1.refs_0_, bf16[1024,256]{1,0:T(8,128)(2,1)} %copy-done.5, ...), custom_call_target="tpu_custom_call" | custom-call | flops 3221225472 | bytes 8388608 | tf_op jit(solution)/shard_map/pick_rows/pallas_call | solution.py:91
  76.8 5.4 %collective-permute-done.17.refs_0_ = bf16[32,128,128]{2,1,0:T(8,128)(2,1)} collective-permute-done((bf16[32,128,128]{2,1,0:T(8,128)(2,1)}, bf16[32,128,128]{2,1,0:T(8,128)(2,1)}, u32[]{:S(2)}, u32[]{:S(2)}) %collective-permute-start.17) | collective-permute-done | bytes 1048608 | tf_op jit(solution)/shard_map/ppermute | solution.py:376
  82.2 2.3 collective-permute-start.18
  84.5 33.7 %choose.2.refs_2_ = bf16[32,128,128]{2,1,0:T(8,128)(2,1)} custom-call(s32[38]{0:T(128)} %dynamic-slice_bitcast_fusion.scalars.place_ref, bf16[32,128,128]{2,1,0:T(8,128)(2,1)} %tie.8.into_ref, bf16[32,128,128]{2,1,0:T(8,128)(2,1)} %tie.7.other_ref), custom_call_target="tpu_custom_call", output_to_operand_aliasing={{}: (1, {})} | custom-call | tf_op jit(solution)/shard_map/choose/pallas_call | solution.py:226
  118.3 2.8 %collective-permute-start.19 = (bf16[32,128,128]{2,1,0:T(8,128)(2,1)}, bf16[32,128,128]{2,1,0:T(8,128)(2,1)}, u32[]{:S(2)}, u32[]{:S(2)}) collective-permute-start(bf16[32,128,128]{2,1,0:T(8,128)(2,1)} %choose.2.refs_2_), channel_id=1, source_target_pairs={{0,1},{1,0},{2,3},{3,2},{4,5},{5,4},{6,7},{7,6},{8,9},{9,8},{10,11... | collective-permute-start | bytes 3145736 | tf_op jit(solution)/shard_map/ppermute | solution.py:322
  121.1 11.3 %collective-permute-done.15.refs_2_ = bf16[32,128,128]{2,1,0:T(8,128)(2,1)} collective-permute-done((bf16[32,128,128]{2,1,0:T(8,128)(2,1)}, bf16[32,128,128]{2,1,0:T(8,128)(2,1)}, u32[]{:S(2)}, u32[]{:S(2)}) %collective-permute-start.15) | collective-permute-done | bytes 1048608 | tf_op jit(solution)/shard_map/ppermute | solution.py:322
  132.5 33.5 %choose.3.refs_3_ = bf16[32,128,128]{2,1,0:T(8,128)(2,1)} custom-call(s32[38]{0:T(128)} %dynamic-slice_bitcast_fusion.scalars.place_ref, bf16[32,128,128]{2,1,0:T(8,128)(2,1)} %tie.10.into_ref, bf16[32,128,128]{2,1,0:T(8,128)(2,1)} %tie.9.other_ref), custom_call_target="tpu_custom_call", output_to_operand_aliasing={{}: (1, {})} | custom-call | tf_op jit(solution)/shard_map/choose/pallas_call | solution.py:226
  166.2 3.7 %collective-permute-start.22 = (bf16[32,128,128]{2,1,0:T(8,128)(2,1)}, bf16[32,128,128]{2,1,0:T(8,128)(2,1)}, u32[]{:S(2)}, u32[]{:S(2)}) collective-permute-start(bf16[32,128,128]{2,1,0:T(8,128)(2,1)} %choose.3.refs_3_), channel_id=1, source_target_pairs={{0,1},{1,0},{2,3},{3,2},{4,5},{5,4},{6,7},{7,6},{8,9},{9,8},{10,11... | collective-permute-start | bytes 3145736 | tf_op jit(solution)/shard_map/ppermute | solution.py:322
  169.8 0.6 fusion.4
  170.4 10.3 %product.4 = (bf16[256,16384]{1,0:T(8,128)(2,1)}, bf16[256,2048]{1,0:T(8,128)(2,1)}) custom-call(s32[38]{0:T(128)} %dynamic-slice_bitcast_fusion.scalars.place_ref, s32[4,64]{1,0:T(4,128)} %copy-done.3, bf16[4,3,256,256]{3,2,1,0:T(8,128)(2,1)} %get-tuple-element.15.mine, bf16[4,3,256,256]{3,2,1,0:T(8,128)(2,1)} %collective-permute-done.5.refs_1_.theirs, ...), custom_call_target="tpu_custom_call" | custom-call | flops 8589934592 | bytes 8388608 | tf_op jit(solution)/shard_map/product/pallas_call | solution.py:176
  180.8 0.4 collective-permute-start.26
  181.2 0.3 collective-permute-start.16
  181.5 2.0 collective-permute-start.21
  183.5 10.3 %product.5 = (bf16[256,16384]{1,0:T(8,128)(2,1)}, bf16[256,2048]{1,0:T(8,128)(2,1)}) custom-call(s32[38]{0:T(128)} %dynamic-slice_bitcast_fusion.scalars.place_ref, s32[4,64]{1,0:T(4,128)} %get-tuple-element.25.table, bf16[4,3,256,256]{3,2,1,0:T(8,128)(2,1)} %get-tuple-element.15.mine, ...), custom_call_target="tpu_custom_call", output_to_operand_aliasing={{0}: (8, {})} | custom-call | flops 8589934592 | bytes 8388608 | tf_op jit(solution)/shard_map/product/pallas_call | solution.py:176
  193.9 0.4 collective-permute-start.25
  194.2 10.3 %product.6 = (bf16[256,16384]{1,0:T(8,128)(2,1)}, bf16[256,2048]{1,0:T(8,128)(2,1)}) custom-call(s32[38]{0:T(128)} %dynamic-slice_bitcast_fusion.scalars.place_ref, s32[4,64]{1,0:T(4,128)} %copy-done.4, bf16[4,3,256,256]{3,2,1,0:T(8,128)(2,1)} %get-tuple-element.15.mine, ...), custom_call_target="tpu_custom_call", output_to_operand_aliasing={{0}: (8, {})} | custom-call | flops 8589934592 | bytes 8388608 | tf_op jit(solution)/shard_map/product/pallas_call | solution.py:176
  204.5 1.3 collective-permute-start.24
  205.9 10.3 %product.7 = (bf16[256,16384]{1,0:T(8,128)(2,1)}, bf16[256,2048]{1,0:T(8,128)(2,1)}) custom-call(s32[38]{0:T(128)} %dynamic-slice_bitcast_fusion.scalars.place_ref, s32[4,64]{1,0:T(4,128)} %get-tuple-element.26.table, bf16[4,3,256,256]{3,2,1,0:T(8,128)(2,1)} %get-tuple-element.15.mine, ...), custom_call_target="tpu_custom_call", output_to_operand_aliasing={{0}: (8, {})} | custom-call | flops 8589934592 | bytes 8388608 | tf_op jit(solution)/shard_map/product/pallas_call | solution.py:176
  216.2 1.1 collective-permute-start.23
  217.3 2.7 %put.4.whole_ref = bf16[256,16384]{1,0:T(8,128)(2,1)} custom-call(s32[38]{0:T(128)} %dynamic-slice_bitcast_fusion.scalars.place_ref, bf16[256,2048]{1,0:T(8,128)(2,1)} %collective-permute-done.26.piece_ref, bf16[256,16384]{1,0:T(8,128)(2,1)} %get-tuple-element.24.whole_ref), custom_call_target="tpu_custom_call", output_to_operand_aliasing={{}: (2, {})} | custom-call | bytes 2097152 | tf_op jit(solution)/shard_map/put/pallas_call | solution.py:250
  220.0 2.7 %put.5.whole_ref = bf16[256,16384]{1,0:T(8,128)(2,1)} custom-call(s32[38]{0:T(128)} %dynamic-slice_bitcast_fusion.scalars.place_ref, bf16[256,2048]{1,0:T(8,128)(2,1)} %collective-permute-done.25.piece_ref, bf16[256,16384]{1,0:T(8,128)(2,1)} %put.4.whole_ref), custom_call_target="tpu_custom_call", output_to_operand_aliasing={{}: (2, {})} | custom-call | bytes 2097152 | tf_op jit(solution)/shard_map/put/pallas_call | solution.py:250
  222.8 2.7 %put.6.whole_ref = bf16[256,16384]{1,0:T(8,128)(2,1)} custom-call(s32[38]{0:T(128)} %dynamic-slice_bitcast_fusion.scalars.place_ref, bf16[256,2048]{1,0:T(8,128)(2,1)} %collective-permute-done.24.piece_ref, bf16[256,16384]{1,0:T(8,128)(2,1)} %put.5.whole_ref), custom_call_target="tpu_custom_call", output_to_operand_aliasing={{}: (2, {})} | custom-call | bytes 2097152 | tf_op jit(solution)/shard_map/put/pallas_call | solution.py:250
  225.5 6.1 %collective-permute-done.23.piece_ref = bf16[256,2048]{1,0:T(8,128)(2,1)} collective-permute-done((bf16[256,2048]{1,0:T(8,128)(2,1)}, bf16[256,2048]{1,0:T(8,128)(2,1)}, u32[]{:S(2)}, u32[]{:S(2)}) %collective-permute-start.23) | collective-permute-done | bytes 1048608 | tf_op jit(solution)/shard_map/ppermute | solution.py:322
  231.5 2.7 %put.7 = bf16[256,16384]{1,0:T(8,128)(2,1)} custom-call(s32[38]{0:T(128)} %dynamic-slice_bitcast_fusion.scalars.place_ref, bf16[256,2048]{1,0:T(8,128)(2,1)} %collective-permute-done.23.piece_ref, bf16[256,16384]{1,0:T(8,128)(2,1)} %put.6.whole_ref), custom_call_target="tpu_custom_call", output_to_operand_aliasing={{}: (2, {})} | custom-call | bytes 2097152 | tf_op jit(solution)/shard_map/put/pallas_call | solution.py:250
  (49 shorter events, 0.7 us)
Async XLA Ops:
  0.0 34.1 %copy-start.2 = (s32[1024]{0:T(1024)S(1)}, s32[1024]{0:T(1024)}, u32[]{:S(2)}) copy-start(s32[1024]{0:T(1024)} %param.10) | copy-start | bytes 12292
  7.4 11.1 %collective-permute-start.2 = (bf16[1024,256]{1,0:T(8,128)(2,1)}, bf16[1024,256]{1,0:T(8,128)(2,1)S(1)}, u32[]{:S(2)}, u32[]{:S(2)}) collective-permute-start(bf16[1024,256]{1,0:T(8,128)(2,1)} %mask_tiles.1.refs_0_), channel_id=1, source_target_pairs={{0,2},{1,5},{2,0},{3,7},{4,6},{5,1},{6,4},{7,3},{8,10},{9,13},{10,... | collective-permute-start | bytes 1572872 | tf_op jit(solution)/shard_map/ppermute | solution.py:322
  8.7 25.3 %collective-permute-start.8 = (bf16[32,128,128]{2,1,0:T(8,128)(2,1)}, bf16[32,128,128]{2,1,0:T(8,128)(2,1)}, u32[]{:S(2)}, u32[]{:S(2)}) collective-permute-start(bf16[32,128,128]{2,1,0:T(8,128)(2,1)} %pack_tiles.1.after_ref.refs_0_), channel_id=1, source_target_pairs={{8,0},{0,8},{24,16},{16,24},{9,1},{1,9},{25,17},{17,25},{10,2},{2,... | collective-permute-start | bytes 3145736 | tf_op jit(solution)/shard_map/ppermute | solution.py:376
  8.8 23.3 %collective-permute-start.3 = (bf16[1024,256]{1,0:T(8,128)(2,1)}, bf16[1024,256]{1,0:T(8,128)(2,1)}, u32[]{:S(2)}, u32[]{:S(2)}) collective-permute-start(bf16[1024,256]{1,0:T(8,128)(2,1)} %mask_tiles.1.refs_0_), channel_id=1, source_target_pairs={{0,4},{1,3},{2,6},{3,1},{4,0},{5,7},{6,2},{7,5},{8,12},{9,11},{10,... | collective-permute-start | bytes 1572872 | tf_op jit(solution)/shard_map/ppermute | solution.py:322
  18.5 13.5 %copy-start.5 = (bf16[1024,256]{1,0:T(8,128)(2,1)}, bf16[1024,256]{1,0:T(8,128)(2,1)S(1)}, u32[]{:S(2)}) copy-start(bf16[1024,256]{1,0:T(8,128)(2,1)S(1)} %collective-permute-done.2.refs_1_) | copy-start | bytes 1572868
  18.5 15.4 %collective-permute-start.4 = (bf16[1024,256]{1,0:T(8,128)(2,1)S(1)}, bf16[1024,256]{1,0:T(8,128)(2,1)}, u32[]{:S(2)}, u32[]{:S(2)}) collective-permute-start(bf16[1024,256]{1,0:T(8,128)(2,1)S(1)} %collective-permute-done.2.refs_1_), channel_id=1, source_target_pairs={{0,4},{1,3},{2,6},{3,1},{4,0},{5,7},{6,2},{7,5},{8,12},{9,11},{10,... | collective-permute-start | bytes 1572872 | tf_op jit(solution)/shard_map/ppermute | solution.py:322
  22.0 54.8 %copy-start.3 = (s32[4,64]{1,0:T(4,128)}, s32[4,64]{1,0:T(4,128)S(1)}, u32[]{:S(2)}) copy-start(s32[4,64]{1,0:T(4,128)S(1)} %select_reduce_fusion.table) | copy-start | bytes 3076
  22.0 2.9 %collective-permute-start = (s32[4,64]{1,0:T(4,128)S(1)}, s32[4,64]{1,0:T(4,128)S(1)}, u32[]{:S(2)}, u32[]{:S(2)}) collective-permute-start(s32[4,64]{1,0:T(4,128)S(1)} %select_reduce_fusion.table), channel_id=1, source_target_pairs={{0,2},{1,5},{2,0},{3,7},{4,6},{5,1},{6,4},{7,3},{8,10},{9,13},{10,... | collective-permute-start | bytes 3080 | tf_op jit(solution)/shard_map/ppermute | solution.py:322
  24.9 51.8 %copy-start.4 = (s32[4,64]{1,0:T(4,128)}, s32[4,64]{1,0:T(4,128)S(1)}, u32[]{:S(2)}) copy-start(s32[4,64]{1,0:T(4,128)S(1)} %collective-permute-done.table) | copy-start | bytes 3076
  24.9 7.2 %collective-permute-start.1 = (s32[8,64]{1,0:T(8,128)S(1)}, s32[8,64]{1,0:T(8,128)S(1)}, u32[]{:S(2)}, u32[]{:S(2)}) collective-permute-start(s32[8,64]{1,0:T(8,128)S(1)} %pad_add_fusion), channel_id=1, source_target_pairs={{0,1},{1,0},{2,3},{3,2},{4,5},{5,4},{6,7},{7,6},{8,9},{9,8},{10,11... | collective-permute-start | bytes 6152 | tf_op jit(solution)/shard_map/ppermute | solution.py:322
  28.3 27.5 %collective-permute-start.11 = (bf16[32,128,128]{2,1,0:T(8,128)(2,1)}, bf16[32,128,128]{2,1,0:T(8,128)(2,1)}, u32[]{:S(2)}, u32[]{:S(2)}) collective-permute-start(bf16[32,128,128]{2,1,0:T(8,128)(2,1)} %pack_tiles.1.after_ref.refs_0_), channel_id=1, source_target_pairs={{16,8},{8,16},{17,9},{9,17},{18,10},{10,18},{19,11},{11,19},{20,12... | collective-permute-start | bytes 3145736 | tf_op jit(solution)/shard_map/ppermute | solution.py:376
  32.1 1.9 copy-start
  32.1 26.9 %collective-permute-start.6 = (bf16[32,128,128]{2,1,0:T(8,128)(2,1)}, bf16[32,128,128]{2,1,0:T(8,128)(2,1)}, u32[]{:S(2)}, u32[]{:S(2)}) collective-permute-start(bf16[32,128,128]{2,1,0:T(8,128)(2,1)} %pack_tiles.1.after_ref.refs_0_), channel_id=1, source_target_pairs={{0,2},{1,5},{2,0},{3,7},{4,6},{5,1},{6,4},{7,3},{8,10},{9,13},{10,... | collective-permute-start | bytes 3145736 | tf_op jit(solution)/shard_map/ppermute | solution.py:322
  32.2 29.2 %collective-permute-start.13 = (bf16[32,128,128]{2,1,0:T(8,128)(2,1)}, bf16[32,128,128]{2,1,0:T(8,128)(2,1)}, u32[]{:S(2)}, u32[]{:S(2)}) collective-permute-start(bf16[32,128,128]{2,1,0:T(8,128)(2,1)} %pack_tiles.1.after_ref.refs_0_), channel_id=1, source_target_pairs={{0,1},{1,0},{2,3},{3,2},{4,5},{5,4},{6,7},{7,6},{8,9},{9,8},{10,11... | collective-permute-start | bytes 3145736 | tf_op jit(solution)/shard_map/ppermute | solution.py:322
  34.0 42.7 %collective-permute-start.9 = (bf16[32,128,128]{2,1,0:T(8,128)(2,1)}, bf16[32,128,128]{2,1,0:T(8,128)(2,1)}, u32[]{:S(2)}, u32[]{:S(2)}) collective-permute-start(bf16[32,128,128]{2,1,0:T(8,128)(2,1)} %tie.6.refs_1_), channel_id=1, source_target_pairs={{0,2},{1,5},{2,0},{3,7},{4,6},{5,1},{6,4},{7,3},{8,10},{9,13},{10,... | collective-permute-start | bytes 3145736 | tf_op jit(solution)/shard_map/ppermute | solution.py:322
  36.9 39.9 %collective-permute-start.14 = (bf16[32,128,128]{2,1,0:T(8,128)(2,1)}, bf16[32,128,128]{2,1,0:T(8,128)(2,1)}, u32[]{:S(2)}, u32[]{:S(2)}) collective-permute-start(bf16[32,128,128]{2,1,0:T(8,128)(2,1)} %tie.6.refs_1_), channel_id=1, source_target_pairs={{0,1},{1,0},{2,3},{3,2},{4,5},{5,4},{6,7},{7,6},{8,9},{9,8},{10,11... | collective-permute-start | bytes 3145736 | tf_op jit(solution)/shard_map/ppermute | solution.py:322
  55.9 26.3 %collective-permute-start.17 = (bf16[32,128,128]{2,1,0:T(8,128)(2,1)}, bf16[32,128,128]{2,1,0:T(8,128)(2,1)}, u32[]{:S(2)}, u32[]{:S(2)}) collective-permute-start(bf16[32,128,128]{2,1,0:T(8,128)(2,1)} %tie.6.refs_1_), channel_id=1, source_target_pairs={{16,8},{8,16},{17,9},{9,17},{18,10},{10,18},{19,11},{11,19},{20,12... | collective-permute-start | bytes 3145736 | tf_op jit(solution)/shard_map/ppermute | solution.py:376
  59.0 25.4 %collective-permute-start.12 = (bf16[32,128,128]{2,1,0:T(8,128)(2,1)}, bf16[32,128,128]{2,1,0:T(8,128)(2,1)}, u32[]{:S(2)}, u32[]{:S(2)}) collective-permute-start(bf16[32,128,128]{2,1,0:T(8,128)(2,1)} %tie.7.other_ref), channel_id=1, source_target_pairs={{8,0},{16,24},{9,1},{17,25},{10,2},{18,26},{11,3},{19,27},{12,4},{... | collective-permute-start | bytes 3145736 | tf_op jit(solution)/shard_map/ppermute | solution.py:376
  61.3 59.8 %collective-permute-start.7 = (bf16[32,128,128]{2,1,0:T(8,128)(2,1)}, bf16[32,128,128]{2,1,0:T(8,128)(2,1)}, u32[]{:S(2)}, u32[]{:S(2)}) collective-permute-start(bf16[32,128,128]{2,1,0:T(8,128)(2,1)} %collective-permute-done.6.refs_1_.refs_0_), channel_id=1, source_target_pairs={{0,1},{1,0},{2,3},{3,2},{4,5},{5,4},{6,7},{7,6},{8,9},{9,8},{10,11... | collective-permute-start | bytes 3145736 | tf_op jit(solution)/shard_map/ppermute | solution.py:322
  76.7 44.4 %collective-permute-start.5 = (bf16[4,3,256,256]{3,2,1,0:T(8,128)(2,1)}, bf16[4,3,256,256]{3,2,1,0:T(8,128)(2,1)}, u32[]{:S(2)}, u32[]{:S(2)}) collective-permute-start(bf16[4,3,256,256]{3,2,1,0:T(8,128)(2,1)} %get-tuple-element.16), channel_id=1, source_target_pairs={{0,1},{1,0},{2,3},{3,2},{4,5},{5,4},{6,7},{7,6},{8,9},{9,8},{10,11... | collective-permute-start | bytes 4718600 | tf_op jit(solution)/shard_map/ppermute | solution.py:322
  82.2 38.9 %collective-permute-start.18 = (bf16[32,128,128]{2,1,0:T(8,128)(2,1)}, bf16[32,128,128]{2,1,0:T(8,128)(2,1)}, u32[]{:S(2)}, u32[]{:S(2)}) collective-permute-start(bf16[32,128,128]{2,1,0:T(8,128)(2,1)} %tie.9.other_ref), channel_id=1, source_target_pairs={{8,0},{16,24},{9,1},{17,25},{10,2},{18,26},{11,3},{19,27},{12,4},{... | collective-permute-start | bytes 3145736 | tf_op jit(solution)/shard_map/ppermute | solution.py:376
  84.5 85.4 %copy-start.1 = (s32[8,64]{1,0:T(8,128)S(1)}, s32[8,64]{1,0:T(8,128)}, u32[]{:S(2)}) copy-start(s32[8,64]{1,0:T(8,128)} %copy-done) | copy-start | bytes 6148
  118.2 14.3 %collective-permute-start.15 = (bf16[32,128,128]{2,1,0:T(8,128)(2,1)}, bf16[32,128,128]{2,1,0:T(8,128)(2,1)}, u32[]{:S(2)}, u32[]{:S(2)}) collective-permute-start(bf16[32,128,128]{2,1,0:T(8,128)(2,1)} %choose.2.refs_2_), channel_id=1, source_target_pairs={{0,2},{1,5},{2,0},{3,7},{4,6},{5,1},{6,4},{7,3},{8,10},{9,13},{10,... | collective-permute-start | bytes 3145736 | tf_op jit(solution)/shard_map/ppermute | solution.py:322
  118.3 14.2 %collective-permute-start.19 = (bf16[32,128,128]{2,1,0:T(8,128)(2,1)}, bf16[32,128,128]{2,1,0:T(8,128)(2,1)}, u32[]{:S(2)}, u32[]{:S(2)}) collective-permute-start(bf16[32,128,128]{2,1,0:T(8,128)(2,1)} %choose.2.refs_2_), channel_id=1, source_target_pairs={{0,1},{1,0},{2,3},{3,2},{4,5},{5,4},{6,7},{7,6},{8,9},{9,8},{10,11... | collective-permute-start | bytes 3145736 | tf_op jit(solution)/shard_map/ppermute | solution.py:322
  121.1 11.4 %collective-permute-start.10 = (bf16[32,128,128]{2,1,0:T(8,128)(2,1)}, bf16[32,128,128]{2,1,0:T(8,128)(2,1)}, u32[]{:S(2)}, u32[]{:S(2)}) collective-permute-start(bf16[32,128,128]{2,1,0:T(8,128)(2,1)} %collective-permute-done.9.refs_2_.refs_1_), channel_id=1, source_target_pairs={{0,1},{1,0},{2,3},{3,2},{4,5},{5,4},{6,7},{7,6},{8,9},{9,8},{10,11... | collective-permute-start | bytes 3145736 | tf_op jit(solution)/shard_map/ppermute | solution.py:322
  166.0 15.5 %collective-permute-start.20 = (bf16[32,128,128]{2,1,0:T(8,128)(2,1)}, bf16[32,128,128]{2,1,0:T(8,128)(2,1)}, u32[]{:S(2)}, u32[]{:S(2)}) collective-permute-start(bf16[32,128,128]{2,1,0:T(8,128)(2,1)} %choose.3.refs_3_), channel_id=1, source_target_pairs={{0,2},{1,5},{2,0},{3,7},{4,6},{5,1},{6,4},{7,3},{8,10},{9,13},{10,... | collective-permute-start | bytes 3145736 | tf_op jit(solution)/shard_map/ppermute | solution.py:322
  166.2 17.4 %collective-permute-start.22 = (bf16[32,128,128]{2,1,0:T(8,128)(2,1)}, bf16[32,128,128]{2,1,0:T(8,128)(2,1)}, u32[]{:S(2)}, u32[]{:S(2)}) collective-permute-start(bf16[32,128,128]{2,1,0:T(8,128)(2,1)} %choose.3.refs_3_), channel_id=1, source_target_pairs={{0,1},{1,0},{2,3},{3,2},{4,5},{5,4},{6,7},{7,6},{8,9},{9,8},{10,11... | collective-permute-start | bytes 3145736 | tf_op jit(solution)/shard_map/ppermute | solution.py:322
  180.8 36.5 %collective-permute-start.26 = (bf16[256,2048]{1,0:T(8,128)(2,1)}, bf16[256,2048]{1,0:T(8,128)(2,1)}, u32[]{:S(2)}, u32[]{:S(2)}) collective-permute-start(bf16[256,2048]{1,0:T(8,128)(2,1)} %get-tuple-element.17.refs_1_), channel_id=1, source_target_pairs={{0,4},{1,3},{2,6},{3,1},{4,0},{5,7},{6,2},{7,5},{8,12},{9,11},{10,... | collective-permute-start | bytes 3145736 | tf_op jit(solution)/shard_map/ppermute | solution.py:322
  181.2 24.7 %collective-permute-start.16 = (bf16[32,128,128]{2,1,0:T(8,128)(2,1)}, bf16[32,128,128]{2,1,0:T(8,128)(2,1)}, u32[]{:S(2)}, u32[]{:S(2)}) collective-permute-start(bf16[32,128,128]{2,1,0:T(8,128)(2,1)} %collective-permute-done.15.refs_2_), channel_id=1, source_target_pairs={{0,1},{1,0},{2,3},{3,2},{4,5},{5,4},{6,7},{7,6},{8,9},{9,8},{10,11... | collective-permute-start | bytes 3145736 | tf_op jit(solution)/shard_map/ppermute | solution.py:322
  181.5 24.4 %collective-permute-start.21 = (bf16[32,128,128]{2,1,0:T(8,128)(2,1)}, bf16[32,128,128]{2,1,0:T(8,128)(2,1)}, u32[]{:S(2)}, u32[]{:S(2)}) collective-permute-start(bf16[32,128,128]{2,1,0:T(8,128)(2,1)} %tie.11.refs_3_), channel_id=1, source_target_pairs={{0,1},{1,0},{2,3},{3,2},{4,5},{5,4},{6,7},{7,6},{8,9},{9,8},{10,11... | collective-permute-start | bytes 3145736 | tf_op jit(solution)/shard_map/ppermute | solution.py:322
  193.9 26.2 %collective-permute-start.25 = (bf16[256,2048]{1,0:T(8,128)(2,1)}, bf16[256,2048]{1,0:T(8,128)(2,1)}, u32[]{:S(2)}, u32[]{:S(2)}) collective-permute-start(bf16[256,2048]{1,0:T(8,128)(2,1)} %get-tuple-element.23), channel_id=1, source_target_pairs={{0,2},{1,5},{2,0},{3,7},{4,6},{5,1},{6,4},{7,3},{8,10},{9,13},{10,... | collective-permute-start | bytes 3145736 | tf_op jit(solution)/shard_map/ppermute | solution.py:322
  204.5 18.2 %collective-permute-start.24 = (bf16[256,2048]{1,0:T(8,128)(2,1)}, bf16[256,2048]{1,0:T(8,128)(2,1)}, u32[]{:S(2)}, u32[]{:S(2)}) collective-permute-start(bf16[256,2048]{1,0:T(8,128)(2,1)} %get-tuple-element.22), channel_id=1, source_target_pairs={{0,4},{1,3},{2,6},{3,1},{4,0},{5,7},{6,2},{7,5},{8,12},{9,11},{10,... | collective-permute-start | bytes 3145736 | tf_op jit(solution)/shard_map/ppermute | solution.py:322
  216.2 15.4 %collective-permute-start.23 = (bf16[256,2048]{1,0:T(8,128)(2,1)}, bf16[256,2048]{1,0:T(8,128)(2,1)}, u32[]{:S(2)}, u32[]{:S(2)}) collective-permute-start(bf16[256,2048]{1,0:T(8,128)(2,1)} %get-tuple-element.21), channel_id=1, source_target_pairs={{0,2},{1,5},{2,0},{3,7},{4,6},{5,1},{6,4},{7,3},{8,10},{9,13},{10,... | collective-permute-start | bytes 3145736 | tf_op jit(solution)/shard_map/ppermute | solution.py:322

commit v4 on v3

--- a/solution.py
+++ b/solution.py
@@ -9,6 +9,7 @@
 from jax.sharding import PartitionSpec as P
 
 TILE = 128
+NOTHING = pl.CostEstimate(flops=0, bytes_accessed=0, transcendentals=0)
 MM_COLS = 512
 VMEM_LIMIT = (64 << 20) - (256 << 10)
 
@@ -17,53 +18,36 @@
     return pltpu.CompilerParams(vmem_limit_bytes=VMEM_LIMIT)
 
 
-def pack_body(scalars, ids_ref, src_ref, out_ref):
+def pack_body(row, ids_ref, mask_ref, src_ref, amp_ref, out_ref, used_ref):
     col_tiles = src_ref.shape[1] // TILE
     tiles = col_tiles * (src_ref.shape[0] // TILE)
     for e in range(out_ref.shape[0]):
-        t = jnp.minimum(ids_ref[scalars[0], e], tiles - 1)
+        t = jnp.minimum(ids_ref[row[0], e], tiles - 1)
         k = pl.multiple_of(lax.div(t, col_tiles) * TILE, TILE)
         n = pl.multiple_of(lax.rem(t, col_tiles) * TILE, TILE)
         out_ref[e] = src_ref[pl.ds(k, TILE), pl.ds(n, TILE)]
-
-
-def pack(scalars, lists, integrals):
+    for k in range(mask_ref.shape[0]):
+        for a in range(mask_ref.shape[1]):
+            at = (slice(a * TILE, (a + 1) * TILE), slice(k * TILE, (k + 1) * TILE))
+            scale = mask_ref[k, a].astype(jnp.float32)
+            used_ref[at] = (amp_ref[at].astype(jnp.float32) * scale).astype(used_ref.dtype)
+
+
+def pack(row, lists, mask, integrals, amplitudes):
     count = lists.shape[1]
+    smem, vmem = pl.BlockSpec(memory_space=pltpu.SMEM), pl.BlockSpec(memory_space=pltpu.VMEM)
     return pl.pallas_call(
         pack_body,
-        out_shape=jax.ShapeDtypeStruct((count, TILE, TILE), integrals.dtype),
-        in_specs=[
-            pl.BlockSpec(memory_space=pltpu.SMEM),
-            pl.BlockSpec(memory_space=pltpu.SMEM),
-            pl.BlockSpec(memory_space=pltpu.VMEM),
+        out_shape=[
+            jax.ShapeDtypeStruct((count, TILE, TILE), integrals.dtype),
+            jax.ShapeDtypeStruct(amplitudes.shape, amplitudes.dtype),
         ],
-        out_specs=pl.BlockSpec(memory_space=pltpu.VMEM),
-        compiler_params=params(),
+        in_specs=[smem, smem, smem, vmem, vmem],
+        out_specs=[vmem, vmem],
+        compiler_params=params(),
+        cost_estimate=NOTHING,
         name="pack_tiles",
-    )(scalars, lists, integrals)
-
-
-def mask_body(mask_ref, amp_ref, after_ref, out_ref):
-    for a in range(mask_ref.shape[0]):
-        for k in range(mask_ref.shape[1]):
-            at = (slice(a * TILE, (a + 1) * TILE), slice(k * TILE, (k + 1) * TILE))
-            scale = mask_ref[a, k].astype(jnp.float32)
-            out_ref[at] = (amp_ref[at].astype(jnp.float32) * scale).astype(out_ref.dtype)
-
-
-def mask_tiles(mask, amplitudes, after):
-    return pl.pallas_call(
-        mask_body,
-        out_shape=jax.ShapeDtypeStruct(amplitudes.shape, amplitudes.dtype),
-        in_specs=[
-            pl.BlockSpec(memory_space=pltpu.SMEM),
-            pl.BlockSpec(memory_space=pltpu.VMEM),
-            pl.BlockSpec(memory_space=pltpu.HBM),
-        ],
-        out_specs=pl.BlockSpec(memory_space=pltpu.VMEM),
-        compiler_params=params(),
-        name="mask_tiles",
-    )(mask, amplitudes, after)
+    )(row, lists, mask.T, integrals, amplitudes)
 
 
 def pick_body(first, capacity, scalars, target_ref, *refs):
@@ -102,9 +86,7 @@
             ],
         ),
         compiler_params=params(),
-        cost_estimate=pl.CostEstimate(
-            flops=4 * count * capacity * n * k * len(amps), bytes_accessed=8 * n * k * len(amps), transcendentals=0
-        ),
+        cost_estimate=NOTHING,
         name="pick_rows",
     )(scalars, target.reshape(1, n), *amps)
 
@@ -191,9 +173,7 @@
         ),
         input_output_aliases=aliases,
         compiler_params=params(),
-        cost_estimate=pl.CostEstimate(
-            flops=4 * m * k * int_cols, bytes_accessed=2 * m * (k + int_cols) + k * int_cols, transcendentals=0
-        ),
+        cost_estimate=NOTHING,
         name="product",
     )(*operands)
 
@@ -210,33 +190,38 @@
         out_specs=pl.BlockSpec(memory_space=pltpu.HBM),
         input_output_aliases={0: 0},
         compiler_params=params(),
+        cost_estimate=NOTHING,
         name="tie",
     )(value, *others)
 
 
-def choose_body(at, scalars, into_ref, other_ref, out_ref, sem):
+def choose_body(at, scalars, a_ref, b_ref, out_ref, sem):
     @pl.when(scalars[at] != 0)
     def _():
-        copy = pltpu.make_async_copy(other_ref, out_ref, sem)
-        copy.start()
-        copy.wait()
-
-
-def choose(scalars, at, into, other):
+        pltpu.make_async_copy(a_ref, out_ref, sem).start()
+
+    @pl.when(scalars[at] == 0)
+    def _():
+        pltpu.make_async_copy(b_ref, out_ref, sem).start()
+
+    pltpu.make_async_copy(a_ref, out_ref, sem).wait()
+
+
+def choose(scalars, at, a, b):
     return pl.pallas_call(
         functools.partial(choose_body, at),
-        out_shape=jax.ShapeDtypeStruct(into.shape, into.dtype),
+        out_shape=jax.ShapeDtypeStruct(a.shape, a.dtype),
         in_specs=[
             pl.BlockSpec(memory_space=pltpu.SMEM),
             pl.BlockSpec(memory_space=pltpu.HBM),
             pl.BlockSpec(memory_space=pltpu.HBM),
         ],
-        out_specs=pl.BlockSpec(memory_space=pltpu.HBM),
+        out_specs=pl.BlockSpec(memory_space=pltpu.VMEM),
         scratch_shapes=[pltpu.SemaphoreType.DMA],
-        input_output_aliases={1: 0},
-        compiler_params=params(),
+        compiler_params=params(),
+        cost_estimate=NOTHING,
         name="choose",
-    )(scalars, into, other)
+    )(scalars, a, b)
 
 
 def place_body(place_ref, piece_ref, whole_ref, out_ref):
@@ -331,7 +316,6 @@
         return e, a, b, 1 - c
 
     consts = Scalars(rows, cols)
-    consts.add(lambda z, e, a, b, c: z)
     core_at = consts.add(lambda z, e, a, b, c: c)
     wanted_at = len(consts.columns)
     for flip in (1, 0):
@@ -339,6 +323,7 @@
             consts.add(lambda z, e, a, b, c: col_index((e + de) % extra, a ^ da, b ^ db, c ^ flip))
     slot_rows = [lambda z: z] + [functools.partial(lambda j, z: order[z][j][2], j) for j in range(rows - 1)]
     rows_at = [consts.add(lambda z, e, a, b, c: row(z)) for row in slot_rows]
+    low_rows_at = [consts.add(lambda z, e, a, b, c: rows + row(z)) for row in slot_rows]
     gathered = [(de, p, q) for de in range(extra) for q in (0, 1) for p in (0, 1)]
 
     def arrival(chip, e, a, b, c):
@@ -370,93 +355,95 @@
     scalars = consts.of_device(lax.axis_index("row"), lax.axis_index("col"), cols)
 
     own_lists = int_tiles[:, 0, :]
-    packed = pack(scalars, own_lists, integrals)
+    row = lax.axis_index("row").astype(jnp.int32).reshape(1)
+    packed, amp_used = pack(row, own_lists, amp_mask, integrals, amplitudes)
 
     def line_step(values, pairs):
         return [lax.ppermute(values[1 - side], "row", pairs[side]) if pairs[side] else None for side in (0, 1)]
 
     fresh = line_step((packed, packed), steps[0])
-    amp_used = mask_tiles(amp_mask, amplitudes, packed)
     amp_next = permute(amp_used, along)
     amp_other = permute(amp_used, other)
-    amp_far = permute(amp_next, other)
-    amps = [amp_used, amp_next, amp_other, amp_far]
-    for de in range(1, extra):
-        amps += [permute(amp, lambda e, a, b, c: ((e - de) % extra, a, b, c)) for amp in amps[:4]]
 
     count = own_lists.shape[1]
     tiles = (int_rows // TILE) * (int_cols // TILE)
     found = own_lists[:, None, :] == jnp.arange(tiles, dtype=jnp.int32)[None, :, None]
     own_table = jnp.min(jnp.where(found, jnp.arange(count, dtype=jnp.int32), count), axis=2)
     table_next = permute(own_table, along)
-    pair_tables = permute(jnp.concatenate([own_table, table_next], axis=0), across)
-    tables = [own_table, table_next, pair_tables[:rows], pair_tables[rows:]]
 
     col_ids = jnp.arange(cols, dtype=jnp.int32)
     onehot = (pair_dest[:, None] == col_ids[None, :]).astype(jnp.int32)
     before = jnp.cumsum(onehot, axis=0) - onehot
     target = pair_dest * capacity + jnp.sum(before * onehot, axis=1)
-    mine, for_them = pick_rows(scalars, wanted_at, len(turns), target, amps, capacity)
-    theirs = permute(for_them, across)
-
-    blocks = [[], [], [], []]
-
-    def spread(slot, last):
-        mine_next = permute(slot, along)
-        blocks[0].append(slot)
-        blocks[2].append(permute(slot, across))
-        if not last:
-            blocks[1].append(mine_next)
-            blocks[3].append(permute(mine_next, across))
-        return mine_next
-
-    last_next = spread(packed, rows == 1)
+
+    slots, nexts, theirs_of, theirs_next = [packed], [permute(packed, along)], [permute(packed, across)], []
     history = []
     for at in range(len(steps)):
         if at > 0:
             fresh = line_step(history[-1], steps[at])
         if at == 0:
-            waited = (amp_far, amp_other, pair_tables)
-        elif at < len(steps) - 1:
-            waited = (*blocks[1], *blocks[2])
+            waited = (amp_next, amp_other, table_next, nexts[0], theirs_of[0], target, scalars)
+        elif at == 1:
+            amps = [amp_used, amp_next, amp_other, permute(amp_next, other)]
+            for de in range(1, extra):
+                amps += [permute(amp, lambda e, a, b, c: ((e - de) % extra, a, b, c)) for amp in amps[:4]]
+            pair_tables = permute(jnp.concatenate([own_table, table_next], axis=0), across)
+            waited = (*amps[3:], pair_tables, *nexts[1:], *theirs_of[1:])
+        elif at == 2:
+            mine, for_them = pick_rows(scalars, wanted_at, len(turns), target, amps, capacity)
+            theirs = permute(for_them, across)
+            waited = (theirs, *nexts[-1:], *theirs_of[-1:])
         else:
-            waited = (theirs, *blocks[1][-1:], *blocks[2][-1:], *blocks[3][:-1])
-        history.append([value if value is None else tie(value, *waited) for value in fresh])
-        while len(blocks[0]) < rows and all(order[i][len(blocks[0]) - 1][0] <= at for i in range(rows)):
-            j = len(blocks[0]) - 1
+            waited = (*nexts[-1:], *theirs_of[-1:])
+        if at > 0 and len(theirs_next) < len(nexts) - 1:
+            theirs_next.append(permute(nexts[len(theirs_next)], across))
+            waited = (*waited, theirs_next[-1])
+        both = [value for value in fresh if value is not None]
+        tied = [tie(both[0], *waited, *both[1:])]
+        tied += [tie(value, *tied) for value in both[1:]]
+        tied = iter(tied)
+        history.append([value if value is None else next(tied) for value in fresh])
+        while len(slots) < rows and all(order[i][len(slots) - 1][0] <= at for i in range(rows)):
+            j = len(slots) - 1
             kinds = sorted({order[i][j][:2] for i in range(rows)})
             slot = history[kinds[-1][0]][kinds[-1][1]]
             for kind in kinds[:-1]:
-                slot = choose(scalars, flags_at[j, kind], slot, history[kind[0]][kind[1]])
-            last_next = spread(slot, j == rows - 2)
+                slot = choose(scalars, flags_at[j, kind], history[kind[0]][kind[1]], slot)
+            slots.append(slot)
+            nexts.append(permute(slot, along))
+            theirs_of.append(permute(slot, across))
 
     out = None
     arrived = []
-    for q in (0, 2, 1, 3):
+    for turn_at, q in enumerate((0, 2, 1, 3)):
+        if turn_at >= 2:
+            out = tie(out, *arrived[turn_at - 2])
         out, *pieces = product(
             scalars,
-            tables[q],
+            (own_table, table_next, pair_tables, pair_tables)[q],
             mine,
             theirs,
-            blocks[q],
+            (slots, nexts, theirs_of, theirs_next)[q],
             int_cols,
             cols * int_cols,
             out,
-            (core_at, picks_at[q], rows_at, mine_at, theirs_at),
+            (core_at, picks_at[q], rows_at if q < 3 else low_rows_at, mine_at, theirs_at),
             place_at[q],
         )
-        for (de, turn), piece, place in zip(hops[1:], pieces, arrive_at[q]):
+        arrived.append([])
+        for (de, turn), piece in zip(hops[1:], pieces):
             def sent_to(e, a, b, c):
                 kind = c ^ int(q >= 2)
                 return (e + de) % extra, a ^ (0 if kind else turn), b ^ (turn if kind else 0), c
 
-            arrived.append((permute(piece, sent_to), place))
-        if q == 0:
-            last_next = tie(last_next, pieces[0])
-            blocks[1].append(last_next)
-            blocks[3].append(permute(last_next, across))
-    for got, place in arrived:
-        out = put(got, out, scalars, place)
+            arrived[-1].append(permute(piece, sent_to))
+        if q in (0, 2):
+            while len(theirs_next) < rows - (q == 0):
+                nexts[len(theirs_next)] = tie(nexts[len(theirs_next)], pieces[0])
+                theirs_next.append(permute(nexts[len(theirs_next)], across))
+    for got, q in zip(arrived, (0, 2, 1, 3)):
+        for piece, place in zip(got, arrive_at[q]):
+            out = put(piece, out, scalars, place)
     return out
 
 

time: 235 us -> 170 us (0.72)
  the two profiles are of different devices: /device:TPU:9 before, /device:TPU:0 now
where the time goes in v4:
time: 170 us; the launch traced here: 169 us
  Pallas kernels  75 us (44%)
  waiting for transfers between devices  61.8 us (36%)
  starting transfers between devices  23.7 us (14%)
  other arithmetic  6.6 us (4%)
    pallas_call x4, Pallas kernels, product(): pl.pallas_call(functools.partial(product_body, at, whole is not None), ou...  41.4 us
    ppermute x5, waiting for transfers between devices, line_step(): lax.ppermute(values[1 - side], 'row', pairs[side])  38.6 us
    ppermute x22, waiting for transfers between devices, permute(): lax.ppermute(value, 'col', [(col_index(*at), col_index(*moved_to(*at))) f...  23.1 us
    ppermute x22, starting transfers between devices, permute(): lax.ppermute(value, 'col', [(col_index(*at), col_index(*moved_to(*at))) f...  14.3 us
    pallas_call x1, Pallas kernels, pick_rows(): pl.pallas_call(functools.partial(pick_body, first, capacity), out_shape=[...  13.7 us
    pallas_call x4, Pallas kernels, put(): pl.pallas_call(place_body, out_shape=jax.ShapeDtypeStruct(whole.shape, wh...  10.9 us
    ppermute x5, starting transfers between devices, line_step(): lax.ppermute(values[1 - side], 'row', pairs[side])  9.42 us
    pallas_call x2, Pallas kernels, choose(): pl.pallas_call(functools.partial(choose_body, at), out_shape=jax.ShapeDty...  5.8 us
  transfers between devices with their start and end apart: 27, of which 8 were waited for; matrix products, arithmetic and copies ran while one was open for 5% of the time, Pallas kernels for 39%

profile of v4, /device:TPU:0, one launch (start us, length us, event | category | flops | bytes accessed | tf_op | source)
XLA Modules:
  0.0 168.8 jit_solution(3616809053276667284)
XLA Ops:
  0.0 3.2 %pack_tiles.1 = (bf16[32,128,128]{2,1,0:T(8,128)(2,1)}, bf16[1024,256]{1,0:T(8,128)(2,1)}) custom-call(s32[1]{0:T(128)} %bitcast.5.row, s32[4,32]{1,0:T(4,128)} %bitcast.29, s32[2,8]{1,0:T(2,128)} %bitcast.31, bf16[512,2048]{1,0:T(8,128)(2,1)} %src_ref.1, bf16[1024,256]{1,0:T(8,128)(2,1)} %amp_ref.1), custom_call_target="tpu_custom_call" | custom-call | tf_op jit(solution)/shard_map/pack_tiles/pallas_call | solution.py:39
  3.2 3.0 %collective-permute-start.3 = (bf16[1024,256]{1,0:T(8,128)(2,1)}, bf16[1024,256]{1,0:T(8,128)(2,1)}, u32[]{:S(2)}, u32[]{:S(2)}) collective-permute-start(bf16[1024,256]{1,0:T(8,128)(2,1)} %get-tuple-element.17.refs_0_), channel_id=1, source_target_pairs={{0,4},{1,3},{2,6},{3,1},{4,0},{5,7},{6,2},{7,5},{8,12},{9,11},{10,... | collective-permute-start | bytes 1572872 | tf_op jit(solution)/shard_map/ppermute | solution.py:307
  6.2 0.8 select_reduce_fusion.table
  7.0 1.6 collective-permute-start
  8.5 1.7 %collective-permute-start.10 = (bf16[32,128,128]{2,1,0:T(8,128)(2,1)}, bf16[32,128,128]{2,1,0:T(8,128)(2,1)}, u32[]{:S(2)}, u32[]{:S(2)}) collective-permute-start(bf16[32,128,128]{2,1,0:T(8,128)(2,1)} %get-tuple-element.20.refs_0_), channel_id=1, source_target_pairs={{16,8},{8,16},{17,9},{9,17},{18,10},{10,18},{19,11},{11,19},{20,12... | collective-permute-start | bytes 3145736 | tf_op jit(solution)/shard_map/ppermute | solution.py:362
  10.3 3.5 %collective-permute-start.8 = (bf16[32,128,128]{2,1,0:T(8,128)(2,1)}, bf16[32,128,128]{2,1,0:T(8,128)(2,1)}, u32[]{:S(2)}, u32[]{:S(2)}) collective-permute-start(bf16[32,128,128]{2,1,0:T(8,128)(2,1)} %get-tuple-element.20.refs_0_), channel_id=1, source_target_pairs={{8,0},{0,8},{24,16},{16,24},{9,1},{1,9},{25,17},{17,25},{10,2},{2,... | collective-permute-start | bytes 3145736 | tf_op jit(solution)/shard_map/ppermute | solution.py:362
  13.7 0.5 collective-permute-start.6
  14.3 0.7 fusion.3
  15.0 2.3 %reduce-window.6 = s32[8,8,128]{2,1,0:T(8,128)S(1)} reduce-window(s32[8,8,128]{2,1,0:T(8,128)S(1)} %fusion.3, s32[]{:T(128)} %constant.20.clone.1), window={size=1x1x128 pad=0_0x0_0x127_0}, to_apply=%region_1.2 | reduce-window | flops 1040384 | bytes 65540 | tf_op jit(solution)/shard_map/reduce-window
  17.2 0.3 slice_reduce_fusion
  17.5 0.2 reduce-window.9
  17.6 1.3 dynamic-slice_bitcast_fusion.scalars.refs_7_.place_ref
  18.9 1.5 collective-permute-start.2
  20.5 0.7 fusion.2
  21.2 1.3 multiply_add_fusion.refs_6_
  22.5 12.0 %collective-permute-done.2.refs_1_ = bf16[1024,256]{1,0:T(8,128)(2,1)} collective-permute-done((bf16[1024,256]{1,0:T(8,128)(2,1)}, bf16[1024,256]{1,0:T(8,128)(2,1)}, u32[]{:S(2)}, u32[]{:S(2)}) %collective-permute-start.2) | collective-permute-done | bytes 524320 | tf_op jit(solution)/shard_map/ppermute | solution.py:307
  34.5 0.5 collective-permute-start.4
  35.0 2.8 %collective-permute-done.8.refs_0_ = bf16[32,128,128]{2,1,0:T(8,128)(2,1)} collective-permute-done((bf16[32,128,128]{2,1,0:T(8,128)(2,1)}, bf16[32,128,128]{2,1,0:T(8,128)(2,1)}, u32[]{:S(2)}, u32[]{:S(2)}) %collective-permute-start.8) | collective-permute-done | bytes 1048608 | tf_op jit(solution)/shard_map/ppermute | solution.py:362
  37.8 1.3 collective-permute-start.13
  39.1 0.7 pad_add_fusion
  39.8 1.7 collective-permute-start.15
  41.4 0.5 collective-permute-start.14
  41.9 0.5 collective-permute-start.11
  42.5 1.5 collective-permute-done.4.refs_3_.refs_1_
  44.0 13.7 %pick_rows.1 = (bf16[4,3,256,256]{3,2,1,0:T(8,128)(2,1)}, bf16[4,3,256,256]{3,2,1,0:T(8,128)(2,1)}) custom-call(s32[41]{0:T(128)} %dynamic-slice_bitcast_fusion.scalars.refs_7_.place_ref, s32[1,1024]{1,0:T(1,128)} %bitcast.27, bf16[1024,256]{1,0:T(8,128)(2,1)} %get-tuple-element.17.refs_0_, bf16[1024,256]{1,0:T(8,128)(2,1)} %collective-permute-done.2.refs_1_, ...), custom_call_target="tpu_custom_call" | custom-call | tf_op jit(solution)/shard_map/pick_rows/pallas_call | solution.py:75
  57.7 7.3 %collective-permute-done.13.refs_0_ = bf16[32,128,128]{2,1,0:T(8,128)(2,1)} collective-permute-done((bf16[32,128,128]{2,1,0:T(8,128)(2,1)}, bf16[32,128,128]{2,1,0:T(8,128)(2,1)}, u32[]{:S(2)}, u32[]{:S(2)}) %collective-permute-start.13) | collective-permute-done | bytes 1048608 | tf_op jit(solution)/shard_map/ppermute | solution.py:362
  65.0 2.9 %choose.2.refs_2_ = bf16[32,128,128]{2,1,0:T(8,128)(2,1)} custom-call(s32[41]{0:T(128)} %dynamic-slice_bitcast_fusion.scalars.refs_7_.place_ref, bf16[32,128,128]{2,1,0:T(8,128)(2,1)} %tie.10.a_ref, bf16[32,128,128]{2,1,0:T(8,128)(2,1)} %tie.11.b_ref.refs_1_), custom_call_target="tpu_custom_call" | custom-call | tf_op jit(solution)/shard_map/choose/pallas_call | solution.py:211
  67.9 0.6 collective-permute-start.12
  68.4 1.3 collective-permute-start.17
  69.8 0.6 collective-permute-start.16
  70.4 0.7 collective-permute-done.12.refs_4_.refs_1_
  71.1 28.5 %collective-permute-done.17.refs_0_ = bf16[32,128,128]{2,1,0:T(8,128)(2,1)} collective-permute-done((bf16[32,128,128]{2,1,0:T(8,128)(2,1)}, bf16[32,128,128]{2,1,0:T(8,128)(2,1)}, u32[]{:S(2)}, u32[]{:S(2)}) %collective-permute-start.17) | collective-permute-done | bytes 1048608 | tf_op jit(solution)/shard_map/ppermute | solution.py:362
  99.6 2.9 %choose.3.refs_3_ = bf16[32,128,128]{2,1,0:T(8,128)(2,1)} custom-call(s32[41]{0:T(128)} %dynamic-slice_bitcast_fusion.scalars.refs_7_.place_ref, bf16[32,128,128]{2,1,0:T(8,128)(2,1)} %tie.12.a_ref, bf16[32,128,128]{2,1,0:T(8,128)(2,1)} %tie.13.b_ref), custom_call_target="tpu_custom_call" | custom-call | tf_op jit(solution)/shard_map/choose/pallas_call | solution.py:211
  102.6 0.6 collective-permute-start.20
  103.2 10.3 %product.4 = (bf16[256,16384]{1,0:T(8,128)(2,1)}, bf16[256,2048]{1,0:T(8,128)(2,1)}) custom-call(s32[41]{0:T(128)} %dynamic-slice_bitcast_fusion.scalars.refs_7_.place_ref, s32[4,64]{1,0:T(4,128)} %copy-done.2, bf16[4,3,256,256]{3,2,1,0:T(8,128)(2,1)} %get-tuple-element.18.mine, bf16[4,3,256,256]{3,2,1,0:T(8,128)(2,1)} %collective-permute-done.5.refs_1_.theirs, ...), custom_call_target="tpu_custom_call" | custom-call | tf_op jit(solution)/shard_map/product/pallas_call | solution.py:158
  113.6 0.6 collective-permute-start.23
  114.1 10.4 %product.5 = (bf16[256,16384]{1,0:T(8,128)(2,1)}, bf16[256,2048]{1,0:T(8,128)(2,1)}) custom-call(s32[41]{0:T(128)} %dynamic-slice_bitcast_fusion.scalars.refs_7_.place_ref, s32[8,64]{1,0:T(8,128)} %copy-done, bf16[4,3,256,256]{3,2,1,0:T(8,128)(2,1)} %get-tuple-element.18.mine, ...), custom_call_target="tpu_custom_call", output_to_operand_aliasing={{0}: (8, {})} | custom-call | tf_op jit(solution)/shard_map/product/pallas_call | solution.py:158
  124.5 1.6 collective-permute-start.24
  126.1 0.5 collective-permute-start.22
  126.6 3.5 %collective-permute-done.23.refs_1_.piece_ref = bf16[256,2048]{1,0:T(8,128)(2,1)} collective-permute-done((bf16[256,2048]{1,0:T(8,128)(2,1)}, bf16[256,2048]{1,0:T(8,128)(2,1)}, u32[]{:S(2)}, u32[]{:S(2)}) %collective-permute-start.23) | collective-permute-done | bytes 1048608 | tf_op jit(solution)/shard_map/ppermute | solution.py:307
  130.1 10.3 %product.6 = (bf16[256,16384]{1,0:T(8,128)(2,1)}, bf16[256,2048]{1,0:T(8,128)(2,1)}) custom-call(s32[41]{0:T(128)} %dynamic-slice_bitcast_fusion.scalars.refs_7_.place_ref, s32[4,64]{1,0:T(4,128)} %copy-done.1, bf16[4,3,256,256]{3,2,1,0:T(8,128)(2,1)} %get-tuple-element.18.mine, ...), custom_call_target="tpu_custom_call", output_to_operand_aliasing={{0}: (8, {})} | custom-call | tf_op jit(solution)/shard_map/product/pallas_call | solution.py:158
  140.5 10.4 %product.7 = (bf16[256,16384]{1,0:T(8,128)(2,1)}, bf16[256,2048]{1,0:T(8,128)(2,1)}) custom-call(s32[41]{0:T(128)} %dynamic-slice_bitcast_fusion.scalars.refs_7_.place_ref, s32[8,64]{1,0:T(8,128)} %copy-done, bf16[4,3,256,256]{3,2,1,0:T(8,128)(2,1)} %get-tuple-element.18.mine, ...), custom_call_target="tpu_custom_call", output_to_operand_aliasing={{0}: (8, {})} | custom-call | tf_op jit(solution)/shard_map/product/pallas_call | solution.py:158
  150.9 1.5 collective-permute-start.25
  152.5 2.7 %put.4.whole_ref = bf16[256,16384]{1,0:T(8,128)(2,1)} custom-call(s32[41]{0:T(128)} %dynamic-slice_bitcast_fusion.scalars.refs_7_.place_ref, bf16[256,2048]{1,0:T(8,128)(2,1)} %collective-permute-done.23.refs_1_.piece_ref, bf16[256,16384]{1,0:T(8,128)(2,1)} %get-tuple-element.28.whole_ref), custom_call_target="tpu_custom_call", output_to_operand_aliasing={{}: (2, {})} | custom-call | bytes 2097152 | tf_op jit(solution)/shard_map/put/pallas_call | solution.py:235
  155.2 2.7 %put.5.whole_ref = bf16[256,16384]{1,0:T(8,128)(2,1)} custom-call(s32[41]{0:T(128)} %dynamic-slice_bitcast_fusion.scalars.refs_7_.place_ref, bf16[256,2048]{1,0:T(8,128)(2,1)} %collective-permute-done.24.refs_1_.piece_ref, bf16[256,16384]{1,0:T(8,128)(2,1)} %put.4.whole_ref), custom_call_target="tpu_custom_call", output_to_operand_aliasing={{}: (2, {})} | custom-call | bytes 2097152 | tf_op jit(solution)/shard_map/put/pallas_call | solution.py:235
  157.9 2.7 %put.6.whole_ref = bf16[256,16384]{1,0:T(8,128)(2,1)} custom-call(s32[41]{0:T(128)} %dynamic-slice_bitcast_fusion.scalars.refs_7_.place_ref, bf16[256,2048]{1,0:T(8,128)(2,1)} %collective-permute-done.26.piece_ref, bf16[256,16384]{1,0:T(8,128)(2,1)} %put.5.whole_ref), custom_call_target="tpu_custom_call", output_to_operand_aliasing={{}: (2, {})} | custom-call | bytes 2097152 | tf_op jit(solution)/shard_map/put/pallas_call | solution.py:235
  160.6 5.5 %collective-permute-done.25.piece_ref = bf16[256,2048]{1,0:T(8,128)(2,1)} collective-permute-done((bf16[256,2048]{1,0:T(8,128)(2,1)}, bf16[256,2048]{1,0:T(8,128)(2,1)}, u32[]{:S(2)}, u32[]{:S(2)}) %collective-permute-start.25) | collective-permute-done | bytes 1048608 | tf_op jit(solution)/shard_map/ppermute | solution.py:307
  166.1 2.7 %put.7 = bf16[256,16384]{1,0:T(8,128)(2,1)} custom-call(s32[41]{0:T(128)} %dynamic-slice_bitcast_fusion.scalars.refs_7_.place_ref, bf16[256,2048]{1,0:T(8,128)(2,1)} %collective-permute-done.25.piece_ref, bf16[256,16384]{1,0:T(8,128)(2,1)} %put.6.whole_ref), custom_call_target="tpu_custom_call", output_to_operand_aliasing={{}: (2, {})} | custom-call | bytes 2097152 | tf_op jit(solution)/shard_map/put/pallas_call | solution.py:235
  (43 shorter events, 0.4 us)
Async XLA Ops:
  3.2 15.7 %collective-permute-start.3 = (bf16[1024,256]{1,0:T(8,128)(2,1)}, bf16[1024,256]{1,0:T(8,128)(2,1)}, u32[]{:S(2)}, u32[]{:S(2)}) collective-permute-start(bf16[1024,256]{1,0:T(8,128)(2,1)} %get-tuple-element.17.refs_0_), channel_id=1, source_target_pairs={{0,4},{1,3},{2,6},{3,1},{4,0},{5,7},{6,2},{7,5},{8,12},{9,11},{10,... | collective-permute-start | bytes 1572872 | tf_op jit(solution)/shard_map/ppermute | solution.py:307
  6.9 58.0 %copy-start.2 = (s32[4,64]{1,0:T(4,128)}, s32[4,64]{1,0:T(4,128)S(1)}, u32[]{:S(2)}) copy-start(s32[4,64]{1,0:T(4,128)S(1)} %select_reduce_fusion.table) | copy-start | bytes 3076
  7.0 6.8 %collective-permute-start = (s32[4,64]{1,0:T(4,128)S(1)}, s32[4,64]{1,0:T(4,128)S(1)}, u32[]{:S(2)}, u32[]{:S(2)}) collective-permute-start(s32[4,64]{1,0:T(4,128)S(1)} %select_reduce_fusion.table), channel_id=1, source_target_pairs={{0,2},{1,5},{2,0},{3,7},{4,6},{5,1},{6,4},{7,3},{8,10},{9,13},{10,... | collective-permute-start | bytes 3080 | tf_op jit(solution)/shard_map/ppermute | solution.py:307
  8.5 26.4 %collective-permute-start.10 = (bf16[32,128,128]{2,1,0:T(8,128)(2,1)}, bf16[32,128,128]{2,1,0:T(8,128)(2,1)}, u32[]{:S(2)}, u32[]{:S(2)}) collective-permute-start(bf16[32,128,128]{2,1,0:T(8,128)(2,1)} %get-tuple-element.20.refs_0_), channel_id=1, source_target_pairs={{16,8},{8,16},{17,9},{9,17},{18,10},{10,18},{19,11},{11,19},{20,12... | collective-permute-start | bytes 3145736 | tf_op jit(solution)/shard_map/ppermute | solution.py:362
  10.2 24.7 %collective-permute-start.9 = (bf16[32,128,128]{2,1,0:T(8,128)(2,1)}, bf16[32,128,128]{2,1,0:T(8,128)(2,1)}, u32[]{:S(2)}, u32[]{:S(2)}) collective-permute-start(bf16[32,128,128]{2,1,0:T(8,128)(2,1)} %get-tuple-element.20.refs_0_), channel_id=1, source_target_pairs={{0,1},{1,0},{2,3},{3,2},{4,5},{5,4},{6,7},{7,6},{8,9},{9,8},{10,11... | collective-permute-start | bytes 3145736 | tf_op jit(solution)/shard_map/ppermute | solution.py:307
  10.3 27.5 %collective-permute-start.8 = (bf16[32,128,128]{2,1,0:T(8,128)(2,1)}, bf16[32,128,128]{2,1,0:T(8,128)(2,1)}, u32[]{:S(2)}, u32[]{:S(2)}) collective-permute-start(bf16[32,128,128]{2,1,0:T(8,128)(2,1)} %get-tuple-element.20.refs_0_), channel_id=1, source_target_pairs={{8,0},{0,8},{24,16},{16,24},{9,1},{1,9},{25,17},{17,25},{10,2},{2,... | collective-permute-start | bytes 3145736 | tf_op jit(solution)/shard_map/ppermute | solution.py:362
  13.7 24.1 %copy-start.1 = (s32[4,64]{1,0:T(4,128)}, s32[4,64]{1,0:T(4,128)S(1)}, u32[]{:S(2)}) copy-start(s32[4,64]{1,0:T(4,128)S(1)} %collective-permute-done.refs_3_.table) | copy-start | bytes 3076
  13.7 24.1 %collective-permute-start.6 = (bf16[32,128,128]{2,1,0:T(8,128)(2,1)}, bf16[32,128,128]{2,1,0:T(8,128)(2,1)}, u32[]{:S(2)}, u32[]{:S(2)}) collective-permute-start(bf16[32,128,128]{2,1,0:T(8,128)(2,1)} %get-tuple-element.20.refs_0_), channel_id=1, source_target_pairs={{0,2},{1,5},{2,0},{3,7},{4,6},{5,1},{6,4},{7,3},{8,10},{9,13},{10,... | collective-permute-start | bytes 3145736 | tf_op jit(solution)/shard_map/ppermute | solution.py:307
  18.9 15.5 %collective-permute-start.2 = (bf16[1024,256]{1,0:T(8,128)(2,1)}, bf16[1024,256]{1,0:T(8,128)(2,1)}, u32[]{:S(2)}, u32[]{:S(2)}) collective-permute-start(bf16[1024,256]{1,0:T(8,128)(2,1)} %get-tuple-element.17.refs_0_), channel_id=1, source_target_pairs={{0,2},{1,5},{2,0},{3,7},{4,6},{5,1},{6,4},{7,3},{8,10},{9,13},{10,... | collective-permute-start | bytes 1572872 | tf_op jit(solution)/shard_map/ppermute | solution.py:307
  34.5 9.5 %collective-permute-start.4 = (bf16[1024,256]{1,0:T(8,128)(2,1)}, bf16[1024,256]{1,0:T(8,128)(2,1)}, u32[]{:S(2)}, u32[]{:S(2)}) collective-permute-start(bf16[1024,256]{1,0:T(8,128)(2,1)} %collective-permute-done.2.refs_1_), channel_id=1, source_target_pairs={{0,4},{1,3},{2,6},{3,1},{4,0},{5,7},{6,2},{7,5},{8,12},{9,11},{10,... | collective-permute-start | bytes 1572872 | tf_op jit(solution)/shard_map/ppermute | solution.py:307
  37.8 27.1 %collective-permute-start.13 = (bf16[32,128,128]{2,1,0:T(8,128)(2,1)}, bf16[32,128,128]{2,1,0:T(8,128)(2,1)}, u32[]{:S(2)}, u32[]{:S(2)}) collective-permute-start(bf16[32,128,128]{2,1,0:T(8,128)(2,1)} %tie.10.a_ref), channel_id=1, source_target_pairs={{8,0},{16,24},{9,1},{17,25},{10,2},{18,26},{11,3},{19,27},{12,4},{... | collective-permute-start | bytes 3145736 | tf_op jit(solution)/shard_map/ppermute | solution.py:362
  39.8 2.2 %collective-permute-start.1 = (s32[8,64]{1,0:T(8,128)S(1)}, s32[8,64]{1,0:T(8,128)S(1)}, u32[]{:S(2)}, u32[]{:S(2)}) collective-permute-start(s32[8,64]{1,0:T(8,128)S(1)} %pad_add_fusion), channel_id=1, source_target_pairs={{0,1},{1,0},{2,3},{3,2},{4,5},{5,4},{6,7},{7,6},{8,9},{9,8},{10,11... | collective-permute-start | bytes 6152 | tf_op jit(solution)/shard_map/ppermute | solution.py:307
  39.8 25.1 %collective-permute-start.15 = (bf16[32,128,128]{2,1,0:T(8,128)(2,1)}, bf16[32,128,128]{2,1,0:T(8,128)(2,1)}, u32[]{:S(2)}, u32[]{:S(2)}) collective-permute-start(bf16[32,128,128]{2,1,0:T(8,128)(2,1)} %tie.9.refs_1_), channel_id=1, source_target_pairs={{16,8},{8,16},{17,9},{9,17},{18,10},{10,18},{19,11},{11,19},{20,12... | collective-permute-start | bytes 3145736 | tf_op jit(solution)/shard_map/ppermute | solution.py:362
  41.4 23.5 %collective-permute-start.14 = (bf16[32,128,128]{2,1,0:T(8,128)(2,1)}, bf16[32,128,128]{2,1,0:T(8,128)(2,1)}, u32[]{:S(2)}, u32[]{:S(2)}) collective-permute-start(bf16[32,128,128]{2,1,0:T(8,128)(2,1)} %tie.9.refs_1_), channel_id=1, source_target_pairs={{0,1},{1,0},{2,3},{3,2},{4,5},{5,4},{6,7},{7,6},{8,9},{9,8},{10,11... | collective-permute-start | bytes 3145736 | tf_op jit(solution)/shard_map/ppermute | solution.py:307
  41.9 23.0 %copy-start = (s32[8,64]{1,0:T(8,128)}, s32[8,64]{1,0:T(8,128)S(1)}, u32[]{:S(2)}) copy-start(s32[8,64]{1,0:T(8,128)S(1)} %collective-permute-done.1.refs_2_.table) | copy-start | bytes 6148
  41.9 23.0 %collective-permute-start.11 = (bf16[32,128,128]{2,1,0:T(8,128)(2,1)}, bf16[32,128,128]{2,1,0:T(8,128)(2,1)}, u32[]{:S(2)}, u32[]{:S(2)}) collective-permute-start(bf16[32,128,128]{2,1,0:T(8,128)(2,1)} %tie.9.refs_1_), channel_id=1, source_target_pairs={{0,2},{1,5},{2,0},{3,7},{4,6},{5,1},{6,4},{7,3},{8,10},{9,13},{10,... | collective-permute-start | bytes 3145736 | tf_op jit(solution)/shard_map/ppermute | solution.py:307
  44.0 21.0 %collective-permute-start.7 = (bf16[32,128,128]{2,1,0:T(8,128)(2,1)}, bf16[32,128,128]{2,1,0:T(8,128)(2,1)}, u32[]{:S(2)}, u32[]{:S(2)}) collective-permute-start(bf16[32,128,128]{2,1,0:T(8,128)(2,1)} %collective-permute-done.6.refs_4_.refs_0_), channel_id=1, source_target_pairs={{0,1},{1,0},{2,3},{3,2},{4,5},{5,4},{6,7},{7,6},{8,9},{9,8},{10,11... | collective-permute-start | bytes 3145736 | tf_op jit(solution)/shard_map/ppermute | solution.py:307
  64.9 5.5 %collective-permute-start.5 = (bf16[4,3,256,256]{3,2,1,0:T(8,128)(2,1)}, bf16[4,3,256,256]{3,2,1,0:T(8,128)(2,1)}, u32[]{:S(2)}, u32[]{:S(2)}) collective-permute-start(bf16[4,3,256,256]{3,2,1,0:T(8,128)(2,1)} %get-tuple-element.19), channel_id=1, source_target_pairs={{0,1},{1,0},{2,3},{3,2},{4,5},{5,4},{6,7},{7,6},{8,9},{9,8},{10,11... | collective-permute-start | bytes 4718600 | tf_op jit(solution)/shard_map/ppermute | solution.py:307
  67.9 3.2 %collective-permute-start.12 = (bf16[32,128,128]{2,1,0:T(8,128)(2,1)}, bf16[32,128,128]{2,1,0:T(8,128)(2,1)}, u32[]{:S(2)}, u32[]{:S(2)}) collective-permute-start(bf16[32,128,128]{2,1,0:T(8,128)(2,1)} %collective-permute-done.11.refs_3_.refs_1_), channel_id=1, source_target_pairs={{0,1},{1,0},{2,3},{3,2},{4,5},{5,4},{6,7},{7,6},{8,9},{9,8},{10,11... | collective-permute-start | bytes 3145736 | tf_op jit(solution)/shard_map/ppermute | solution.py:307
  68.4 31.2 %collective-permute-start.17 = (bf16[32,128,128]{2,1,0:T(8,128)(2,1)}, bf16[32,128,128]{2,1,0:T(8,128)(2,1)}, u32[]{:S(2)}, u32[]{:S(2)}) collective-permute-start(bf16[32,128,128]{2,1,0:T(8,128)(2,1)} %tie.12.a_ref), channel_id=1, source_target_pairs={{8,0},{16,24},{9,1},{17,25},{10,2},{18,26},{11,3},{19,27},{12,4},{... | collective-permute-start | bytes 3145736 | tf_op jit(solution)/shard_map/ppermute | solution.py:362
  69.7 29.9 %collective-permute-start.18 = (bf16[32,128,128]{2,1,0:T(8,128)(2,1)}, bf16[32,128,128]{2,1,0:T(8,128)(2,1)}, u32[]{:S(2)}, u32[]{:S(2)}) collective-permute-start(bf16[32,128,128]{2,1,0:T(8,128)(2,1)} %choose.2.refs_2_), channel_id=1, source_target_pairs={{0,1},{1,0},{2,3},{3,2},{4,5},{5,4},{6,7},{7,6},{8,9},{9,8},{10,11... | collective-permute-start | bytes 3145736 | tf_op jit(solution)/shard_map/ppermute | solution.py:307
  69.8 29.8 %collective-permute-start.16 = (bf16[32,128,128]{2,1,0:T(8,128)(2,1)}, bf16[32,128,128]{2,1,0:T(8,128)(2,1)}, u32[]{:S(2)}, u32[]{:S(2)}) collective-permute-start(bf16[32,128,128]{2,1,0:T(8,128)(2,1)} %choose.2.refs_2_), channel_id=1, source_target_pairs={{0,2},{1,5},{2,0},{3,7},{4,6},{5,1},{6,4},{7,3},{8,10},{9,13},{10,... | collective-permute-start | bytes 3145736 | tf_op jit(solution)/shard_map/ppermute | solution.py:307
  102.5 11.6 %collective-permute-start.21 = (bf16[32,128,128]{2,1,0:T(8,128)(2,1)}, bf16[32,128,128]{2,1,0:T(8,128)(2,1)}, u32[]{:S(2)}, u32[]{:S(2)}) collective-permute-start(bf16[32,128,128]{2,1,0:T(8,128)(2,1)} %choose.3.refs_3_), channel_id=1, source_target_pairs={{0,1},{1,0},{2,3},{3,2},{4,5},{5,4},{6,7},{7,6},{8,9},{9,8},{10,11... | collective-permute-start | bytes 3145736 | tf_op jit(solution)/shard_map/ppermute | solution.py:307
  102.6 23.5 %collective-permute-start.20 = (bf16[32,128,128]{2,1,0:T(8,128)(2,1)}, bf16[32,128,128]{2,1,0:T(8,128)(2,1)}, u32[]{:S(2)}, u32[]{:S(2)}) collective-permute-start(bf16[32,128,128]{2,1,0:T(8,128)(2,1)} %choose.3.refs_3_), channel_id=1, source_target_pairs={{0,2},{1,5},{2,0},{3,7},{4,6},{5,1},{6,4},{7,3},{8,10},{9,13},{10,... | collective-permute-start | bytes 3145736 | tf_op jit(solution)/shard_map/ppermute | solution.py:307
  113.6 16.5 %collective-permute-start.23 = (bf16[256,2048]{1,0:T(8,128)(2,1)}, bf16[256,2048]{1,0:T(8,128)(2,1)}, u32[]{:S(2)}, u32[]{:S(2)}) collective-permute-start(bf16[256,2048]{1,0:T(8,128)(2,1)} %get-tuple-element.21.refs_1_), channel_id=1, source_target_pairs={{0,4},{1,3},{2,6},{3,1},{4,0},{5,7},{6,2},{7,5},{8,12},{9,11},{10,... | collective-permute-start | bytes 3145736 | tf_op jit(solution)/shard_map/ppermute | solution.py:307
  124.5 16.0 %collective-permute-start.24 = (bf16[256,2048]{1,0:T(8,128)(2,1)}, bf16[256,2048]{1,0:T(8,128)(2,1)}, u32[]{:S(2)}, u32[]{:S(2)}) collective-permute-start(bf16[256,2048]{1,0:T(8,128)(2,1)} %get-tuple-element.23.refs_1_), channel_id=1, source_target_pairs={{0,2},{1,5},{2,0},{3,7},{4,6},{5,1},{6,4},{7,3},{8,10},{9,13},{10,... | collective-permute-start | bytes 3145736 | tf_op jit(solution)/shard_map/ppermute | solution.py:307
  126.1 14.4 %collective-permute-start.19 = (bf16[32,128,128]{2,1,0:T(8,128)(2,1)}, bf16[32,128,128]{2,1,0:T(8,128)(2,1)}, u32[]{:S(2)}, u32[]{:S(2)}) collective-permute-start(bf16[32,128,128]{2,1,0:T(8,128)(2,1)} %tie.14.refs_2_), channel_id=1, source_target_pairs={{0,1},{1,0},{2,3},{3,2},{4,5},{5,4},{6,7},{7,6},{8,9},{9,8},{10,11... | collective-permute-start | bytes 3145736 | tf_op jit(solution)/shard_map/ppermute | solution.py:307
  126.1 14.4 %collective-permute-start.22 = (bf16[32,128,128]{2,1,0:T(8,128)(2,1)}, bf16[32,128,128]{2,1,0:T(8,128)(2,1)}, u32[]{:S(2)}, u32[]{:S(2)}) collective-permute-start(bf16[32,128,128]{2,1,0:T(8,128)(2,1)} %tie.15.refs_3_), channel_id=1, source_target_pairs={{0,1},{1,0},{2,3},{3,2},{4,5},{5,4},{6,7},{7,6},{8,9},{9,8},{10,11... | collective-permute-start | bytes 3145736 | tf_op jit(solution)/shard_map/ppermute | solution.py:307
  140.4 17.5 %collective-permute-start.26 = (bf16[256,2048]{1,0:T(8,128)(2,1)}, bf16[256,2048]{1,0:T(8,128)(2,1)}, u32[]{:S(2)}, u32[]{:S(2)}) collective-permute-start(bf16[256,2048]{1,0:T(8,128)(2,1)} %get-tuple-element.27), channel_id=1, source_target_pairs={{0,4},{1,3},{2,6},{3,1},{4,0},{5,7},{6,2},{7,5},{8,12},{9,11},{10,... | collective-permute-start | bytes 3145736 | tf_op jit(solution)/shard_map/ppermute | solution.py:307
  150.9 15.2 %collective-permute-start.25 = (bf16[256,2048]{1,0:T(8,128)(2,1)}, bf16[256,2048]{1,0:T(8,128)(2,1)}, u32[]{:S(2)}, u32[]{:S(2)}) collective-permute-start(bf16[256,2048]{1,0:T(8,128)(2,1)} %get-tuple-element.26), channel_id=1, source_target_pairs={{0,2},{1,5},{2,0},{3,7},{4,6},{5,1},{6,4},{7,3},{8,10},{9,13},{10,... | collective-permute-start | bytes 3145736 | tf_op jit(solution)/shard_map/ppermute | solution.py:307

commit v5 on v4

--- a/solution.py
+++ b/solution.py
@@ -9,6 +9,7 @@
 from jax.sharding import PartitionSpec as P
 
 TILE = 128
+PARTS = 8
 NOTHING = pl.CostEstimate(flops=0, bytes_accessed=0, transcendentals=0)
 MM_COLS = 512
 VMEM_LIMIT = (64 << 20) - (256 << 10)
@@ -18,14 +19,14 @@
     return pltpu.CompilerParams(vmem_limit_bytes=VMEM_LIMIT)
 
 
-def pack_body(row, ids_ref, mask_ref, src_ref, amp_ref, out_ref, used_ref):
+def pack_body(row, ids_ref, mask_ref, src_ref, amp_ref, out_ref, again_ref, used_ref):
     col_tiles = src_ref.shape[1] // TILE
     tiles = col_tiles * (src_ref.shape[0] // TILE)
     for e in range(out_ref.shape[0]):
         t = jnp.minimum(ids_ref[row[0], e], tiles - 1)
         k = pl.multiple_of(lax.div(t, col_tiles) * TILE, TILE)
         n = pl.multiple_of(lax.rem(t, col_tiles) * TILE, TILE)
-        out_ref[e] = src_ref[pl.ds(k, TILE), pl.ds(n, TILE)]
+        out_ref[e] = again_ref[e] = src_ref[pl.ds(k, TILE), pl.ds(n, TILE)]
     for k in range(mask_ref.shape[0]):
         for a in range(mask_ref.shape[1]):
             at = (slice(a * TILE, (a + 1) * TILE), slice(k * TILE, (k + 1) * TILE))
@@ -40,10 +41,11 @@
         pack_body,
         out_shape=[
             jax.ShapeDtypeStruct((count, TILE, TILE), integrals.dtype),
+            jax.ShapeDtypeStruct((count, TILE, TILE), integrals.dtype),
             jax.ShapeDtypeStruct(amplitudes.shape, amplitudes.dtype),
         ],
         in_specs=[smem, smem, smem, vmem, vmem],
-        out_specs=[vmem, vmem],
+        out_specs=[vmem, vmem, vmem],
         compiler_params=params(),
         cost_estimate=NOTHING,
         name="pack_tiles",
@@ -195,55 +197,81 @@
     )(value, *others)
 
 
-def choose_body(at, scalars, a_ref, b_ref, out_ref, sem):
+def choose_body(at, scalars, a_ref, b_ref, out_ref, held, in_sems, out_sems):
+    parts = in_sems.shape[0]
+    size = held.shape[0] // parts
+    spans = [pl.ds(p * size, size) for p in range(parts)]
+
     @pl.when(scalars[at] != 0)
     def _():
-        pltpu.make_async_copy(a_ref, out_ref, sem).start()
+        for p, span in enumerate(spans):
+            pltpu.make_async_copy(a_ref.at[span], held.at[span], in_sems.at[p]).start()
 
     @pl.when(scalars[at] == 0)
     def _():
-        pltpu.make_async_copy(b_ref, out_ref, sem).start()
-
-    pltpu.make_async_copy(a_ref, out_ref, sem).wait()
+        for p, span in enumerate(spans):
+            pltpu.make_async_copy(b_ref.at[span], held.at[span], in_sems.at[p]).start()
+
+    outs = [pltpu.make_async_copy(held.at[span], out_ref.at[span], out_sems.at[p]) for p, span in enumerate(spans)]
+    for p, span in enumerate(spans):
+        pltpu.make_async_copy(a_ref.at[span], held.at[span], in_sems.at[p]).wait()
+        outs[p].start()
+    for copy in outs:
+        copy.wait()
 
 
 def choose(scalars, at, a, b):
+    hbm = pl.BlockSpec(memory_space=pltpu.HBM)
     return pl.pallas_call(
         functools.partial(choose_body, at),
         out_shape=jax.ShapeDtypeStruct(a.shape, a.dtype),
-        in_specs=[
-            pl.BlockSpec(memory_space=pltpu.SMEM),
-            pl.BlockSpec(memory_space=pltpu.HBM),
-            pl.BlockSpec(memory_space=pltpu.HBM),
+        in_specs=[pl.BlockSpec(memory_space=pltpu.SMEM), hbm, hbm],
+        out_specs=hbm,
+        scratch_shapes=[
+            pltpu.VMEM(a.shape, a.dtype),
+            pltpu.SemaphoreType.DMA((PARTS,)),
+            pltpu.SemaphoreType.DMA((PARTS,)),
         ],
-        out_specs=pl.BlockSpec(memory_space=pltpu.VMEM),
-        scratch_shapes=[pltpu.SemaphoreType.DMA],
         compiler_params=params(),
         cost_estimate=NOTHING,
         name="choose",
     )(scalars, a, b)
 
 
-def place_body(place_ref, piece_ref, whole_ref, out_ref):
-    out_ref[...] = piece_ref[...]
+def put_body(at, scalars, piece_ref, whole_ref, out_ref, held, in_sems, out_sems):
+    parts = in_sems.shape[0]
+    m, n = held.shape
+    size = m // parts
+    columns = pl.ds(pl.multiple_of(scalars[at] * n, TILE), n)
+    spans = [pl.ds(p * size, size) for p in range(parts)]
+    ins = [pltpu.make_async_copy(piece_ref.at[span], held.at[span], in_sems.at[p]) for p, span in enumerate(spans)]
+    outs = [
+        pltpu.make_async_copy(held.at[span], out_ref.at[span, columns], out_sems.at[p]) for p, span in enumerate(spans)
+    ]
+    for copy in ins:
+        copy.start()
+    for before, after in zip(ins, outs):
+        before.wait()
+        after.start()
+    for copy in outs:
+        copy.wait()
 
 
 def put(piece, whole, scalars, at):
-    m, n = piece.shape
-    width = min(2 * MM_COLS, n)
-    steps = n // width
+    hbm = pl.BlockSpec(memory_space=pltpu.HBM)
     return pl.pallas_call(
-        place_body,
+        functools.partial(put_body, at),
         out_shape=jax.ShapeDtypeStruct(whole.shape, whole.dtype),
-        grid_spec=pltpu.PrefetchScalarGridSpec(
-            num_scalar_prefetch=1,
-            grid=(steps,),
-            in_specs=[pl.BlockSpec((m, width), lambda i, s: (0, i)), pl.BlockSpec(memory_space=pltpu.HBM)],
-            out_specs=pl.BlockSpec((m, width), lambda i, s: (0, s[at] * steps + i)),
-        ),
+        in_specs=[pl.BlockSpec(memory_space=pltpu.SMEM), hbm, hbm],
+        out_specs=hbm,
+        scratch_shapes=[
+            pltpu.VMEM(piece.shape, piece.dtype),
+            pltpu.SemaphoreType.DMA((PARTS,)),
+            pltpu.SemaphoreType.DMA((PARTS,)),
+        ],
         input_output_aliases={2: 0},
         compiler_params=params(),
-        cost_estimate=pl.CostEstimate(flops=0, bytes_accessed=4 * m * n, transcendentals=0),
+        cost_estimate=NOTHING,
         name="put",
     )(scalars, piece, whole)
 
@@ -267,27 +295,41 @@
 
 
 def line_schedule(rows):
-    partner = ({}, {})
-    for i in range(rows):
-        if i ^ 1 < rows:
-            partner[0][i] = i ^ 1
-        if 0 <= ((i + 1) ^ 1) - 1 < rows:
-            partner[1][i] = ((i + 1) ^ 1) - 1
-    held = ({i: i for i in range(rows)}, {i: i for i in range(rows)})
-    steps, order = [], [[] for _ in range(rows)]
-    while min(len(o) for o in order) < rows - 1:
-        moved, pairs = ({}, {}), []
-        for side in (0, 1):
-            passed = held[1 - side]
-            pairs.append([(p, i) for i, p in partner[side].items() if p in passed])
-            moved[side].update({i: passed[p] for p, i in pairs[side]})
+    if rows == 4:
+        phases = [
+            [(-1, [(0, 1), (1, 0), (2, 3), (3, 2)]), (-1, [(0, 2), (2, 0), (1, 3), (3, 1)])],
+            [(-1, [(1, 2), (2, 1)]), (1, [(1, 0), (2, 3)])],
+        ]
+    else:
+        partner = ({}, {})
         for i in range(rows):
+            if i ^ 1 < rows:
+                partner[0][i] = i ^ 1
+            if 0 <= ((i + 1) ^ 1) - 1 < rows:
+                partner[1][i] = ((i + 1) ^ 1) - 1
+        phases, reached, last, count = [], (set(range(rows)), set(range(rows))), (-1, -1), 0
+        while True:
+            moves, now, fresh = [], [-1, -1], (set(), set())
             for side in (0, 1):
-                if i in moved[side]:
-                    order[i].append((len(steps), side, moved[side][i]))
-        steps.append(pairs)
-        held = moved
-    return steps, order
+                pairs = [(p, i) for i, p in partner[side].items() if p in reached[1 - side]]
+                fresh[side].update(i for _, i in pairs)
+                if pairs:
+                    moves.append((last[1 - side], pairs))
+                    now[side] = count
+                    count += 1
+            if not moves:
+                break
+            phases.append(moves)
+            reached, last = fresh, tuple(now)
+    arrivals = [[] for _ in range(rows)]
+    blocks = []
+    for moves in phases:
+        for source, pairs in moves:
+            got = {b: a if source < 0 else blocks[source][a] for a, b in pairs}
+            blocks.append(got)
+            for i, block in got.items():
+                arrivals[i].append((len(blocks) - 1, block))
+    return phases, arrivals
 
 
 def on_device(amplitudes, amp_mask, integrals, int_tiles, pair_dest):
@@ -301,7 +343,7 @@
     chips = [(e, a, b) for e in range(extra) for a in range(2) for b in range(2)]
     hops = [(de, turn) for de in range(extra) for turn in (0, 1)]
     turns = [(de, da, db) for de in range(extra) for da, db in ((0, 0), (1, 0), (0, 1))]
-    steps, order = line_schedule(rows)
+    phases, order = line_schedule(rows)
 
     def permute(value, moved_to):
         return lax.ppermute(value, "col", [(col_index(*at), col_index(*moved_to(*at))) for at in every])
@@ -321,7 +363,7 @@
     for flip in (1, 0):
         for de, da, db in turns:
             consts.add(lambda z, e, a, b, c: col_index((e + de) % extra, a ^ da, b ^ db, c ^ flip))
-    slot_rows = [lambda z: z] + [functools.partial(lambda j, z: order[z][j][2], j) for j in range(rows - 1)]
+    slot_rows = [lambda z: z] + [functools.partial(lambda j, z: order[z][j][1], j) for j in range(rows - 1)]
     rows_at = [consts.add(lambda z, e, a, b, c: row(z)) for row in slot_rows]
     low_rows_at = [consts.add(lambda z, e, a, b, c: rows + row(z)) for row in slot_rows]
     gathered = [(de, p, q) for de in range(extra) for q in (0, 1) for p in (0, 1)]
@@ -349,66 +391,72 @@
         ]
     flags_at = {}
     for j in range(rows - 1):
-        kinds = sorted({order[i][j][:2] for i in range(rows)})
+        kinds = sorted({order[i][j][0] for i in range(rows)})
         for kind in kinds[:-1]:
-            flags_at[j, kind] = consts.add(lambda z, e, a, b, c: order[z][j][:2] == kind)
+            flags_at[j, kind] = consts.add(lambda z, e, a, b, c: order[z][j][0] == kind)
     scalars = consts.of_device(lax.axis_index("row"), lax.axis_index("col"), cols)
 
     own_lists = int_tiles[:, 0, :]
     row = lax.axis_index("row").astype(jnp.int32).reshape(1)
-    packed, amp_used = pack(row, own_lists, amp_mask, integrals, amplitudes)
-
-    def line_step(values, pairs):
-        return [lax.ppermute(values[1 - side], "row", pairs[side]) if pairs[side] else None for side in (0, 1)]
-
-    fresh = line_step((packed, packed), steps[0])
+    packed, packed_again, amp_used = pack(row, own_lists, amp_mask, integrals, amplitudes)
+
+    moved = []
+
+    def line_phase(moves, own):
+        return [lax.ppermute(own if source < 0 else moved[source], "row", pairs) for source, pairs in moves]
+
+    fresh = line_phase(phases[0], packed)
     amp_next = permute(amp_used, along)
     amp_other = permute(amp_used, other)
+    amps = [amp_used, amp_next, amp_other, permute(amp_next, other)]
+    for de in range(1, extra):
+        amps += [permute(amp, lambda e, a, b, c: ((e - de) % extra, a, b, c)) for amp in amps[:4]]
 
     count = own_lists.shape[1]
     tiles = (int_rows // TILE) * (int_cols // TILE)
     found = own_lists[:, None, :] == jnp.arange(tiles, dtype=jnp.int32)[None, :, None]
     own_table = jnp.min(jnp.where(found, jnp.arange(count, dtype=jnp.int32), count), axis=2)
-    table_next = permute(own_table, along)
 
     col_ids = jnp.arange(cols, dtype=jnp.int32)
     onehot = (pair_dest[:, None] == col_ids[None, :]).astype(jnp.int32)
     before = jnp.cumsum(onehot, axis=0) - onehot
     target = pair_dest * capacity + jnp.sum(before * onehot, axis=1)
 
+    mine, for_them = pick_rows(scalars, wanted_at, len(turns), target, amps, capacity)
     slots, nexts, theirs_of, theirs_next = [packed], [permute(packed, along)], [permute(packed, across)], []
-    history = []
-    for at in range(len(steps)):
+    for at, moves in enumerate(phases):
         if at > 0:
-            fresh = line_step(history[-1], steps[at])
+            fresh = line_phase(moves, packed_again)
         if at == 0:
-            waited = (amp_next, amp_other, table_next, nexts[0], theirs_of[0], target, scalars)
+            waited = (mine, nexts[0], theirs_of[0])
+            fresh[0] = tie(fresh[0], mine)
         elif at == 1:
-            amps = [amp_used, amp_next, amp_other, permute(amp_next, other)]
-            for de in range(1, extra):
-                amps += [permute(amp, lambda e, a, b, c: ((e - de) % extra, a, b, c)) for amp in amps[:4]]
+            theirs = permute(for_them, across)
+            own_table = tie(own_table, *nexts[1:])
+            table_next = permute(own_table, along)
             pair_tables = permute(jnp.concatenate([own_table, table_next], axis=0), across)
-            waited = (*amps[3:], pair_tables, *nexts[1:], *theirs_of[1:])
-        elif at == 2:
-            mine, for_them = pick_rows(scalars, wanted_at, len(turns), target, amps, capacity)
-            theirs = permute(for_them, across)
-            waited = (theirs, *nexts[-1:], *theirs_of[-1:])
+            waited = (theirs, table_next, *theirs_of[1:], *nexts[1:])
+            theirs_next.append(permute(nexts[0], across))
+            waited = (theirs, table_next, *nexts[1:], *theirs_of[1:], *theirs_next)
         else:
             waited = (*nexts[-1:], *theirs_of[-1:])
-        if at > 0 and len(theirs_next) < len(nexts) - 1:
-            theirs_next.append(permute(nexts[len(theirs_next)], across))
-            waited = (*waited, theirs_next[-1])
-        both = [value for value in fresh if value is not None]
-        tied = [tie(both[0], *waited, *both[1:])]
-        tied += [tie(value, *tied) for value in both[1:]]
-        tied = iter(tied)
-        history.append([value if value is None else next(tied) for value in fresh])
-        while len(slots) < rows and all(order[i][len(slots) - 1][0] <= at for i in range(rows)):
+            while len(theirs_next) < len(nexts) - 1:
+                theirs_next.append(permute(nexts[len(theirs_next)], across))
+                waited = (*waited, theirs_next[-1])
+        tied = []
+        for i, value in enumerate(fresh):
+            if at > 0 or i > 0:
+                value = tie(value, *waited, *fresh[i + 1 :], *(tied[:1] if at > 0 else ()))
+            tied.append(value)
+        moved += tied
+        if at == 0:
+            packed_again = tie(packed_again, moved[-1])
+        while len(slots) < rows and all(order[i][len(slots) - 1][0] < len(moved) for i in range(rows)):
             j = len(slots) - 1
-            kinds = sorted({order[i][j][:2] for i in range(rows)})
-            slot = history[kinds[-1][0]][kinds[-1][1]]
+            kinds = sorted({order[i][j][0] for i in range(rows)})
+            slot = moved[kinds[-1]]
             for kind in kinds[:-1]:
-                slot = choose(scalars, flags_at[j, kind], history[kind[0]][kind[1]], slot)
+                slot = choose(scalars, flags_at[j, kind], moved[kind], slot)
             slots.append(slot)
             nexts.append(permute(slot, along))
             theirs_of.append(permute(slot, across))

time: 170 us -> 167 us (0.982)
  waiting for transfers between devices: 61.8 us -> 57.3 us
  starting transfers between devices: 23.7 us -> 26.5 us
  local copies, waits for them, and re-layouts: 1.56 us -> 4.24 us
  Pallas kernels: 75 us -> 72.7 us
    ppermute x5 -> x4, waiting for transfers between devices: 38.6 us -> 19.1 us  [line_phase(): lax.ppermute(own if source < 0 else moved[source], 'row', pairs)]
    ppermute x22, waiting for transfers between devices: 23.1 us -> 38.3 us  [permute(): lax.ppermute(value, 'col', [(col_index(*at), col_index(*moved_to(*at))) f...]
    ppermute x22, starting transfers between devices: 14.3 us -> 18.5 us  [permute(): lax.ppermute(value, 'col', [(col_index(*at), col_index(*moved_to(*at))) f...]
    pallas_call x2 -> x1, Pallas kernels: 5.8 us -> 2.91 us  [choose(): pl.pallas_call(functools.partial(choose_body, at), out_shape=jax.ShapeDty...]
    unnamed x6 -> x14, local copies, waits for them, and re-layouts: 0.01 us -> 2.74 us
    ppermute x5 -> x4, starting transfers between devices: 9.42 us -> 8.02 us  [line_phase(): lax.ppermute(own if source < 0 else moved[source], 'row', pairs)]
  transfers between devices with their start and end apart: 27 -> 26, of which waited for: 8 -> 11; matrix products, arithmetic and copies ran while one was open for 5% -> 4% of each run, Pallas kernels for 39% -> 38%
where the time goes in v5:
time: 167 us
  Pallas kernels  72.7 us (44%)
  waiting for transfers between devices  57.3 us (34%)
  starting transfers between devices  26.5 us (16%)
  other arithmetic  5.87 us (4%)
  local copies, waits for them, and re-layouts  4.24 us (3%)
    pallas_call x4, Pallas kernels, product(): pl.pallas_call(functools.partial(product_body, at, whole is not None), ou...  41.4 us
    ppermute x22, waiting for transfers between devices, permute(): lax.ppermute(value, 'col', [(col_index(*at), col_index(*moved_to(*at))) f...  38.3 us
    ppermute x4, waiting for transfers between devices, line_phase(): lax.ppermute(own if source < 0 else moved[source], 'row', pairs)  19.1 us
    ppermute x22, starting transfers between devices, permute(): lax.ppermute(value, 'col', [(col_index(*at), col_index(*moved_to(*at))) f...  18.5 us
    pallas_call x1, Pallas kernels, pick_rows(): pl.pallas_call(functools.partial(pick_body, first, capacity), out_shape=[...  13.7 us
    pallas_call x4, Pallas kernels, put(): pl.pallas_call(functools.partial(put_body, at), out_shape=jax.ShapeDtypeS...  11 us
    ppermute x4, starting transfers between devices, line_phase(): lax.ppermute(own if source < 0 else moved[source], 'row', pairs)  8.02 us
    pallas_call x1, Pallas kernels, pack(): pl.pallas_call(pack_body, out_shape=[jax.ShapeDtypeStruct((count, TILE, T...  3.67 us
  transfers between devices with their start and end apart: 26, of which 11 were waited for; matrix products, arithmetic and copies ran while one was open for 4% of the time, Pallas kernels for 38%

profile of v5, /device:TPU:0, one launch (start us, length us, event | category | flops | bytes accessed | tf_op | source)
XLA Modules:
  0.0 166.8 jit_solution(12722761267388116969)
XLA Ops:
  0.0 3.7 %pack_tiles.1 = (bf16[32,128,128]{2,1,0:T(8,128)(2,1)}, bf16[32,128,128]{2,1,0:T(8,128)(2,1)}, bf16[1024,256]{1,0:T(8,128)(2,1)}) custom-call(s32[1]{0:T(128)} %bitcast.2.row, s32[4,32]{1,0:T(4,128)} %bitcast.29, s32[2,8]{1,0:T(2,128)} %bitcast.31, bf16[512,2048]{1,0:T(8,128)(2,1)} %src_ref.1, bf16[1024,256]{1,0:T(8,128)(2,1)} %amp_ref.1), custom_call_target="tpu_custom_call" | custom-call | tf_op jit(solution)/shard_map/pack_tiles/pallas_call | solution.py:40
  3.7 3.0 %collective-permute-start.2 = (bf16[1024,256]{1,0:T(8,128)(2,1)}, bf16[1024,256]{1,0:T(8,128)(2,1)}, u32[]{:S(2)}, u32[]{:S(2)}) collective-permute-start(bf16[1024,256]{1,0:T(8,128)(2,1)} %get-tuple-element.19.refs_0_), channel_id=1, source_target_pairs={{0,4},{1,3},{2,6},{3,1},{4,0},{5,7},{6,2},{7,5},{8,12},{9,11},{10,... | collective-permute-start | bytes 1572872 | tf_op jit(solution)/shard_map/ppermute | solution.py:349
  6.6 1.5 collective-permute-start.1
  8.1 0.5 collective-permute-start.6
  8.7 2.6 %collective-permute-start.5 = (bf16[32,128,128]{2,1,0:T(8,128)(2,1)}, bf16[32,128,128]{2,1,0:T(8,128)(2,1)}, u32[]{:S(2)}, u32[]{:S(2)}) collective-permute-start(bf16[32,128,128]{2,1,0:T(8,128)(2,1)} %get-tuple-element.18.refs_0_), channel_id=1, source_target_pairs={{0,16},{16,0},{8,24},{24,8},{1,17},{17,1},{9,25},{25,9},{2,18},{18... | collective-permute-start | bytes 3145736 | tf_op jit(solution)/shard_map/ppermute | solution.py:406
  11.3 8.0 %collective-permute-done.2.refs_2_ = bf16[1024,256]{1,0:T(8,128)(2,1)} collective-permute-done((bf16[1024,256]{1,0:T(8,128)(2,1)}, bf16[1024,256]{1,0:T(8,128)(2,1)}, u32[]{:S(2)}, u32[]{:S(2)}) %collective-permute-start.2) | collective-permute-done | bytes 524320 | tf_op jit(solution)/shard_map/ppermute | solution.py:349
  19.2 2.5 %collective-permute-start = (bf16[32,128,128]{2,1,0:T(8,128)(2,1)}, bf16[32,128,128]{2,1,0:T(8,128)(2,1)}, u32[]{:S(2)}, u32[]{:S(2)}) collective-permute-start(bf16[32,128,128]{2,1,0:T(8,128)(2,1)} %get-tuple-element.18.refs_0_), channel_id=1, source_target_pairs={{0,8},{8,0},{16,24},{24,16},{1,9},{9,1},{17,25},{25,17},{2,10},{10... | collective-permute-start | bytes 3145736 | tf_op jit(solution)/shard_map/ppermute | solution.py:406
  21.7 0.7 fusion.3
  22.4 2.3 %reduce-window.6 = s32[8,8,128]{2,1,0:T(8,128)S(1)} reduce-window(s32[8,8,128]{2,1,0:T(8,128)S(1)} %fusion.3, s32[]{:T(128)} %constant.20.clone.1), window={size=1x1x128 pad=0_0x0_0x127_0}, to_apply=%region_1.2 | reduce-window | flops 1040384 | bytes 65540 | tf_op jit(solution)/shard_map/reduce-window
  25.1 1.2 dynamic-slice_bitcast_fusion.scalars
  26.3 0.8 copy-done
  27.1 1.5 collective-permute-start.3
  28.7 0.7 fusion.2
  29.4 1.3 multiply_add_fusion
  30.7 3.5 %collective-permute-done.6.refs_2_.refs_0_ = bf16[32,128,128]{2,1,0:T(8,128)(2,1)} collective-permute-done((bf16[32,128,128]{2,1,0:T(8,128)(2,1)}, bf16[32,128,128]{2,1,0:T(8,128)(2,1)}, u32[]{:S(2)}, u32[]{:S(2)}) %collective-permute-start.6) | collective-permute-done | bytes 1048608 | tf_op jit(solution)/shard_map/ppermute | solution.py:349
  34.2 2.3 %collective-permute-done.3.refs_3_ = bf16[1024,256]{1,0:T(8,128)(2,1)S(1)} collective-permute-done((bf16[1024,256]{1,0:T(8,128)(2,1)S(1)}, bf16[1024,256]{1,0:T(8,128)(2,1)S(1)}, u32[]{:S(2)}, u32[]{:S(2)}) %collective-permute-start.3) | collective-permute-done | bytes 524320 | tf_op jit(solution)/shard_map/ppermute | solution.py:349
  36.5 0.8 copy-done.1
  37.3 13.7 %pick_rows.1 = (bf16[4,3,256,256]{3,2,1,0:T(8,128)(2,1)}, bf16[4,3,256,256]{3,2,1,0:T(8,128)(2,1)}) custom-call(s32[40]{0:T(128)} %dynamic-slice_bitcast_fusion.scalars, s32[1,1024]{1,0:T(1,128)} %bitcast.27, bf16[1024,256]{1,0:T(8,128)(2,1)} %get-tuple-element.19.refs_0_, bf16[1024,256]{1,0:T(8,128)(2,1)} %copy-done, ...), custom_call_target="tpu_custom_call" | custom-call | tf_op jit(solution)/shard_map/pick_rows/pallas_call | solution.py:77
  51.0 7.1 %collective-permute-done.5.refs_0_ = bf16[32,128,128]{2,1,0:T(8,128)(2,1)} collective-permute-done((bf16[32,128,128]{2,1,0:T(8,128)(2,1)}, bf16[32,128,128]{2,1,0:T(8,128)(2,1)}, u32[]{:S(2)}, u32[]{:S(2)}) %collective-permute-start.5) | collective-permute-done | bytes 1048608 | tf_op jit(solution)/shard_map/ppermute | solution.py:406
  58.0 1.5 collective-permute-start.8
  59.5 3.5 %collective-permute-done.refs_0_ = bf16[32,128,128]{2,1,0:T(8,128)(2,1)} collective-permute-done((bf16[32,128,128]{2,1,0:T(8,128)(2,1)}, bf16[32,128,128]{2,1,0:T(8,128)(2,1)}, u32[]{:S(2)}, u32[]{:S(2)}) %collective-permute-start) | collective-permute-done | bytes 1048608 | tf_op jit(solution)/shard_map/ppermute | solution.py:406
  63.1 1.7 collective-permute-start.4
  64.7 1.6 collective-permute-start.13
  66.4 1.3 collective-permute-start.16
  67.7 5.5 %collective-permute-done.8.refs_2_.refs_4_.refs_0_ = bf16[32,128,128]{2,1,0:T(8,128)(2,1)} collective-permute-done((bf16[32,128,128]{2,1,0:T(8,128)(2,1)}, bf16[32,128,128]{2,1,0:T(8,128)(2,1)}, u32[]{:S(2)}, u32[]{:S(2)}) %collective-permute-start.8) | collective-permute-done | bytes 1048608 | tf_op jit(solution)/shard_map/ppermute | solution.py:349
  73.2 11.2 %collective-permute-done.4.refs_1_.refs_3_.refs_0_ = bf16[32,128,128]{2,1,0:T(8,128)(2,1)} collective-permute-done((bf16[32,128,128]{2,1,0:T(8,128)(2,1)}, bf16[32,128,128]{2,1,0:T(8,128)(2,1)}, u32[]{:S(2)}, u32[]{:S(2)}) %collective-permute-start.4) | collective-permute-done | bytes 1048608 | tf_op jit(solution)/shard_map/ppermute | solution.py:349
  84.4 0.7 select_reduce_fusion.refs_0_
  85.1 1.5 collective-permute-start.9
  86.6 8.5 %collective-permute-done.16.refs_8_.refs_0_ = bf16[32,128,128]{2,1,0:T(8,128)(2,1)} collective-permute-done((bf16[32,128,128]{2,1,0:T(8,128)(2,1)}, bf16[32,128,128]{2,1,0:T(8,128)(2,1)}, u32[]{:S(2)}, u32[]{:S(2)}) %collective-permute-start.16) | collective-permute-done | bytes 1048608 | tf_op jit(solution)/shard_map/ppermute | solution.py:406
  95.1 0.6 copy-done.3
  95.7 2.9 %choose.1.refs_3_ = bf16[32,128,128]{2,1,0:T(8,128)(2,1)} custom-call(s32[40]{0:T(128)} %dynamic-slice_bitcast_fusion.scalars, bf16[32,128,128]{2,1,0:T(8,128)(2,1)} %tie.15.refs_8_.a_ref, bf16[32,128,128]{2,1,0:T(8,128)(2,1)} %tie.16.b_ref), custom_call_target="tpu_custom_call" | custom-call | tf_op jit(solution)/shard_map/choose/pallas_call | solution.py:225
  98.7 0.6 collective-permute-start.19
  99.3 2.2 %collective-permute-start.10 = (s32[8,64]{1,0:T(8,128)S(1)}, s32[8,64]{1,0:T(8,128)S(1)}, u32[]{:S(2)}, u32[]{:S(2)}) collective-permute-start(s32[8,64]{1,0:T(8,128)S(1)} %pad_add_fusion), channel_id=1, source_target_pairs={{0,1},{1,0},{2,3},{3,2},{4,5},{5,4},{6,7},{7,6},{8,9},{9,8},{10,11... | collective-permute-start | bytes 6152 | tf_op jit(solution)/shard_map/ppermute | solution.py:349
  101.5 10.3 %product.4 = (bf16[256,16384]{1,0:T(8,128)(2,1)}, bf16[256,2048]{1,0:T(8,128)(2,1)}) custom-call(s32[40]{0:T(128)} %dynamic-slice_bitcast_fusion.scalars, s32[4,64]{1,0:T(4,128)} %tie.13.table, bf16[4,3,256,256]{3,2,1,0:T(8,128)(2,1)} %get-tuple-element.20.refs_1_.mine, bf16[4,3,256,256]{3,2,1,0:T(8,128)(2,1)} %collective-permute-done.11.refs_1_.theirs, ...), custom_call_target="tpu_custom_call" | custom-call | tf_op jit(solution)/shard_map/product/pallas_call | solution.py:160
  111.8 0.5 collective-permute-start.22
  112.3 0.6 copy-done.5
  112.9 10.4 %product.5 = (bf16[256,16384]{1,0:T(8,128)(2,1)}, bf16[256,2048]{1,0:T(8,128)(2,1)}) custom-call(s32[40]{0:T(128)} %dynamic-slice_bitcast_fusion.scalars, s32[8,64]{1,0:T(8,128)} %copy-done.5, bf16[4,3,256,256]{3,2,1,0:T(8,128)(2,1)} %get-tuple-element.20.refs_1_.mine, ...), custom_call_target="tpu_custom_call", output_to_operand_aliasing={{0}: (8, {})} | custom-call | tf_op jit(solution)/shard_map/product/pallas_call | solution.py:160
  123.3 1.6 collective-permute-start.23
  125.3 1.8 %collective-permute-done.22.refs_1_.piece_ref = bf16[256,2048]{1,0:T(8,128)(2,1)} collective-permute-done((bf16[256,2048]{1,0:T(8,128)(2,1)}, bf16[256,2048]{1,0:T(8,128)(2,1)}, u32[]{:S(2)}, u32[]{:S(2)}) %collective-permute-start.22) | collective-permute-done | bytes 1048608 | tf_op jit(solution)/shard_map/ppermute | solution.py:349
  127.1 10.3 %product.6 = (bf16[256,16384]{1,0:T(8,128)(2,1)}, bf16[256,2048]{1,0:T(8,128)(2,1)}) custom-call(s32[40]{0:T(128)} %dynamic-slice_bitcast_fusion.scalars, s32[4,64]{1,0:T(4,128)} %copy-done.3, bf16[4,3,256,256]{3,2,1,0:T(8,128)(2,1)} %get-tuple-element.20.refs_1_.mine, ...), custom_call_target="tpu_custom_call", output_to_operand_aliasing={{0}: (8, {})} | custom-call | tf_op jit(solution)/shard_map/product/pallas_call | solution.py:160
  137.8 0.7 collective-permute-done.23.refs_1_.piece_ref
  138.5 10.4 %product.7 = (bf16[256,16384]{1,0:T(8,128)(2,1)}, bf16[256,2048]{1,0:T(8,128)(2,1)}) custom-call(s32[40]{0:T(128)} %dynamic-slice_bitcast_fusion.scalars, s32[8,64]{1,0:T(8,128)} %copy-done.5, bf16[4,3,256,256]{3,2,1,0:T(8,128)(2,1)} %get-tuple-element.20.refs_1_.mine, ...), custom_call_target="tpu_custom_call", output_to_operand_aliasing={{0}: (8, {})} | custom-call | tf_op jit(solution)/shard_map/product/pallas_call | solution.py:160
  148.8 1.6 collective-permute-start.24
  150.4 2.7 %put.4.whole_ref = bf16[256,16384]{1,0:T(8,128)(2,1)} custom-call(s32[40]{0:T(128)} %dynamic-slice_bitcast_fusion.scalars, bf16[256,2048]{1,0:T(8,128)(2,1)} %collective-permute-done.22.refs_1_.piece_ref, bf16[256,16384]{1,0:T(8,128)(2,1)} %get-tuple-element.30.whole_ref), custom_call_target="tpu_custom_call", output_to_operand_aliasing={{}: (2, {})} | custom-call | tf_op jit(solution)/shard_map/put/pallas_call | solution.py:262
  153.2 2.8 %put.5.whole_ref = bf16[256,16384]{1,0:T(8,128)(2,1)} custom-call(s32[40]{0:T(128)} %dynamic-slice_bitcast_fusion.scalars, bf16[256,2048]{1,0:T(8,128)(2,1)} %collective-permute-done.23.refs_1_.piece_ref, bf16[256,16384]{1,0:T(8,128)(2,1)} %put.4.whole_ref), custom_call_target="tpu_custom_call", output_to_operand_aliasing={{}: (2, {})} | custom-call | tf_op jit(solution)/shard_map/put/pallas_call | solution.py:262
  155.9 2.8 %put.6.whole_ref = bf16[256,16384]{1,0:T(8,128)(2,1)} custom-call(s32[40]{0:T(128)} %dynamic-slice_bitcast_fusion.scalars, bf16[256,2048]{1,0:T(8,128)(2,1)} %collective-permute-done.25.piece_ref, bf16[256,16384]{1,0:T(8,128)(2,1)} %put.5.whole_ref), custom_call_target="tpu_custom_call", output_to_operand_aliasing={{}: (2, {})} | custom-call | tf_op jit(solution)/shard_map/put/pallas_call | solution.py:262
  158.7 5.3 %collective-permute-done.24.piece_ref = bf16[256,2048]{1,0:T(8,128)(2,1)} collective-permute-done((bf16[256,2048]{1,0:T(8,128)(2,1)}, bf16[256,2048]{1,0:T(8,128)(2,1)}, u32[]{:S(2)}, u32[]{:S(2)}) %collective-permute-start.24) | collective-permute-done | bytes 1048608 | tf_op jit(solution)/shard_map/ppermute | solution.py:349
  164.0 2.7 %put.7 = bf16[256,16384]{1,0:T(8,128)(2,1)} custom-call(s32[40]{0:T(128)} %dynamic-slice_bitcast_fusion.scalars, bf16[256,2048]{1,0:T(8,128)(2,1)} %collective-permute-done.24.piece_ref, bf16[256,16384]{1,0:T(8,128)(2,1)} %put.6.whole_ref), custom_call_target="tpu_custom_call", output_to_operand_aliasing={{}: (2, {})} | custom-call | tf_op jit(solution)/shard_map/put/pallas_call | solution.py:262
  (50 shorter events, 1.5 us)
Async XLA Ops:
  0.0 84.4 %copy-start.6 = (s32[4,1,32]{2,1,0:T(1,128)S(1)}, s32[4,1,32]{2,1,0:T(1,128)}, u32[]{:S(2)}) copy-start(s32[4,1,32]{2,1,0:T(1,128)} %param.9) | copy-start | bytes 1540
  3.7 15.5 %collective-permute-start.2 = (bf16[1024,256]{1,0:T(8,128)(2,1)}, bf16[1024,256]{1,0:T(8,128)(2,1)}, u32[]{:S(2)}, u32[]{:S(2)}) collective-permute-start(bf16[1024,256]{1,0:T(8,128)(2,1)} %get-tuple-element.19.refs_0_), channel_id=1, source_target_pairs={{0,4},{1,3},{2,6},{3,1},{4,0},{5,7},{6,2},{7,5},{8,12},{9,11},{10,... | collective-permute-start | bytes 1572872 | tf_op jit(solution)/shard_map/ppermute | solution.py:349
  6.6 19.7 %collective-permute-start.1 = (bf16[1024,256]{1,0:T(8,128)(2,1)}, bf16[1024,256]{1,0:T(8,128)(2,1)S(1)}, u32[]{:S(2)}, u32[]{:S(2)}) collective-permute-start(bf16[1024,256]{1,0:T(8,128)(2,1)} %get-tuple-element.19.refs_0_), channel_id=1, source_target_pairs={{0,2},{1,5},{2,0},{3,7},{4,6},{5,1},{6,4},{7,3},{8,10},{9,13},{10,... | collective-permute-start | bytes 1572872 | tf_op jit(solution)/shard_map/ppermute | solution.py:349
  8.1 26.1 %collective-permute-start.6 = (bf16[32,128,128]{2,1,0:T(8,128)(2,1)}, bf16[32,128,128]{2,1,0:T(8,128)(2,1)}, u32[]{:S(2)}, u32[]{:S(2)}) collective-permute-start(bf16[32,128,128]{2,1,0:T(8,128)(2,1)} %get-tuple-element.18.refs_0_), channel_id=1, source_target_pairs={{0,2},{1,5},{2,0},{3,7},{4,6},{5,1},{6,4},{7,3},{8,10},{9,13},{10,... | collective-permute-start | bytes 3145736 | tf_op jit(solution)/shard_map/ppermute | solution.py:349
  8.7 42.3 %collective-permute-start.7 = (bf16[32,128,128]{2,1,0:T(8,128)(2,1)}, bf16[32,128,128]{2,1,0:T(8,128)(2,1)}, u32[]{:S(2)}, u32[]{:S(2)}) collective-permute-start(bf16[32,128,128]{2,1,0:T(8,128)(2,1)} %get-tuple-element.18.refs_0_), channel_id=1, source_target_pairs={{0,1},{1,0},{2,3},{3,2},{4,5},{5,4},{6,7},{7,6},{8,9},{9,8},{10,11... | collective-permute-start | bytes 3145736 | tf_op jit(solution)/shard_map/ppermute | solution.py:349
  8.7 49.4 %collective-permute-start.5 = (bf16[32,128,128]{2,1,0:T(8,128)(2,1)}, bf16[32,128,128]{2,1,0:T(8,128)(2,1)}, u32[]{:S(2)}, u32[]{:S(2)}) collective-permute-start(bf16[32,128,128]{2,1,0:T(8,128)(2,1)} %get-tuple-element.18.refs_0_), channel_id=1, source_target_pairs={{0,16},{16,0},{8,24},{24,8},{1,17},{17,1},{9,25},{25,9},{2,18},{18... | collective-permute-start | bytes 3145736 | tf_op jit(solution)/shard_map/ppermute | solution.py:406
  19.2 43.8 %collective-permute-start = (bf16[32,128,128]{2,1,0:T(8,128)(2,1)}, bf16[32,128,128]{2,1,0:T(8,128)(2,1)}, u32[]{:S(2)}, u32[]{:S(2)}) collective-permute-start(bf16[32,128,128]{2,1,0:T(8,128)(2,1)} %get-tuple-element.18.refs_0_), channel_id=1, source_target_pairs={{0,8},{8,0},{16,24},{24,16},{1,9},{9,1},{17,25},{25,17},{2,10},{10... | collective-permute-start | bytes 3145736 | tf_op jit(solution)/shard_map/ppermute | solution.py:406
  26.3 0.8 copy-start
  27.1 9.4 %collective-permute-start.3 = (bf16[1024,256]{1,0:T(8,128)(2,1)S(1)}, bf16[1024,256]{1,0:T(8,128)(2,1)S(1)}, u32[]{:S(2)}, u32[]{:S(2)}) collective-permute-start(bf16[1024,256]{1,0:T(8,128)(2,1)S(1)} %collective-permute-done.1.refs_1_), channel_id=1, source_target_pairs={{0,4},{1,3},{2,6},{3,1},{4,0},{5,7},{6,2},{7,5},{8,12},{9,11},{10,... | collective-permute-start | bytes 1572872 | tf_op jit(solution)/shard_map/ppermute | solution.py:349
  34.2 32.1 %collective-permute-start.12 = (bf16[32,128,128]{2,1,0:T(8,128)(2,1)}, bf16[32,128,128]{2,1,0:T(8,128)(2,1)}, u32[]{:S(2)}, u32[]{:S(2)}) collective-permute-start(bf16[32,128,128]{2,1,0:T(8,128)(2,1)} %collective-permute-done.6.refs_2_.refs_0_), channel_id=1, source_target_pairs={{0,1},{1,0},{2,3},{3,2},{4,5},{5,4},{6,7},{7,6},{8,9},{9,8},{10,11... | collective-permute-start | bytes 3145736 | tf_op jit(solution)/shard_map/ppermute | solution.py:349
  36.5 0.8 copy-start.1
  58.0 15.1 %collective-permute-start.8 = (bf16[32,128,128]{2,1,0:T(8,128)(2,1)}, bf16[32,128,128]{2,1,0:T(8,128)(2,1)}, u32[]{:S(2)}, u32[]{:S(2)}) collective-permute-start(bf16[32,128,128]{2,1,0:T(8,128)(2,1)} %tie.12.refs_1_.refs_2_), channel_id=1, source_target_pairs={{0,2},{1,5},{2,0},{3,7},{4,6},{5,1},{6,4},{7,3},{8,10},{9,13},{10,... | collective-permute-start | bytes 3145736 | tf_op jit(solution)/shard_map/ppermute | solution.py:349
  63.1 21.3 %collective-permute-start.4 = (bf16[32,128,128]{2,1,0:T(8,128)(2,1)}, bf16[32,128,128]{2,1,0:T(8,128)(2,1)}, u32[]{:S(2)}, u32[]{:S(2)}) collective-permute-start(bf16[32,128,128]{2,1,0:T(8,128)(2,1)} %tie.11.refs_1_), channel_id=1, source_target_pairs={{0,2},{1,5},{2,0},{3,7},{4,6},{5,1},{6,4},{7,3},{8,10},{9,13},{10,... | collective-permute-start | bytes 3145736 | tf_op jit(solution)/shard_map/ppermute | solution.py:349
  64.7 30.3 %collective-permute-start.11 = (bf16[4,3,256,256]{3,2,1,0:T(8,128)(2,1)}, bf16[4,3,256,256]{3,2,1,0:T(8,128)(2,1)}, u32[]{:S(2)}, u32[]{:S(2)}) collective-permute-start(bf16[4,3,256,256]{3,2,1,0:T(8,128)(2,1)} %get-tuple-element.21), channel_id=1, source_target_pairs={{0,1},{1,0},{2,3},{3,2},{4,5},{5,4},{6,7},{7,6},{8,9},{9,8},{10,11... | collective-permute-start | bytes 4718600 | tf_op jit(solution)/shard_map/ppermute | solution.py:349
  64.7 20.4 %collective-permute-start.13 = (bf16[32,128,128]{2,1,0:T(8,128)(2,1)}, bf16[32,128,128]{2,1,0:T(8,128)(2,1)}, u32[]{:S(2)}, u32[]{:S(2)}) collective-permute-start(bf16[32,128,128]{2,1,0:T(8,128)(2,1)} %tie.14), channel_id=1, source_target_pairs={{8,16},{16,8},{9,17},{17,9},{10,18},{18,10},{11,19},{19,11},{12,20... | collective-permute-start | bytes 3145736 | tf_op jit(solution)/shard_map/ppermute | solution.py:406
  66.4 28.7 %collective-permute-start.16 = (bf16[32,128,128]{2,1,0:T(8,128)(2,1)}, bf16[32,128,128]{2,1,0:T(8,128)(2,1)}, u32[]{:S(2)}, u32[]{:S(2)}) collective-permute-start(bf16[32,128,128]{2,1,0:T(8,128)(2,1)} %tie.12.refs_1_.refs_2_), channel_id=1, source_target_pairs={{8,0},{16,24},{9,1},{17,25},{10,2},{18,26},{11,3},{19,27},{12,4},{... | collective-permute-start | bytes 3145736 | tf_op jit(solution)/shard_map/ppermute | solution.py:406
  73.2 21.9 %collective-permute-start.15 = (bf16[32,128,128]{2,1,0:T(8,128)(2,1)}, bf16[32,128,128]{2,1,0:T(8,128)(2,1)}, u32[]{:S(2)}, u32[]{:S(2)}) collective-permute-start(bf16[32,128,128]{2,1,0:T(8,128)(2,1)} %tie.12.refs_1_.refs_2_), channel_id=1, source_target_pairs={{0,1},{1,0},{2,3},{3,2},{4,5},{5,4},{6,7},{7,6},{8,9},{9,8},{10,11... | collective-permute-start | bytes 3145736 | tf_op jit(solution)/shard_map/ppermute | solution.py:349
  84.4 10.7 %collective-permute-start.14 = (bf16[32,128,128]{2,1,0:T(8,128)(2,1)}, bf16[32,128,128]{2,1,0:T(8,128)(2,1)}, u32[]{:S(2)}, u32[]{:S(2)}) collective-permute-start(bf16[32,128,128]{2,1,0:T(8,128)(2,1)} %tie.11.refs_1_), channel_id=1, source_target_pairs={{0,1},{1,0},{2,3},{3,2},{4,5},{5,4},{6,7},{7,6},{8,9},{9,8},{10,11... | collective-permute-start | bytes 3145736 | tf_op jit(solution)/shard_map/ppermute | solution.py:349
  85.1 10.0 %collective-permute-start.9 = (s32[4,64]{1,0:T(4,128)}, s32[4,64]{1,0:T(4,128)S(1)}, u32[]{:S(2)}, u32[]{:S(2)}) collective-permute-start(s32[4,64]{1,0:T(4,128)} %tie.13.table), channel_id=1, source_target_pairs={{0,2},{1,5},{2,0},{3,7},{4,6},{5,1},{6,4},{7,3},{8,10},{9,13},{10,... | collective-permute-start | bytes 3080 | tf_op jit(solution)/shard_map/ppermute | solution.py:349
  95.1 0.6 copy-start.3
  95.6 3.6 %copy-start.2 = (s32[4,64]{1,0:T(4,128)S(1)}, s32[4,64]{1,0:T(4,128)}, u32[]{:S(2)}) copy-start(s32[4,64]{1,0:T(4,128)} %tie.13.table) | copy-start | bytes 3076
  95.7 3.6 %copy-start.4 = (s32[4,64]{1,0:T(4,128)S(1)}, s32[4,64]{1,0:T(4,128)}, u32[]{:S(2)}) copy-start(s32[4,64]{1,0:T(4,128)} %copy-done.3) | copy-start | bytes 3076
  98.6 13.7 %collective-permute-start.20 = (bf16[32,128,128]{2,1,0:T(8,128)(2,1)}, bf16[32,128,128]{2,1,0:T(8,128)(2,1)}, u32[]{:S(2)}, u32[]{:S(2)}) collective-permute-start(bf16[32,128,128]{2,1,0:T(8,128)(2,1)} %choose.1.refs_3_), channel_id=1, source_target_pairs={{0,1},{1,0},{2,3},{3,2},{4,5},{5,4},{6,7},{7,6},{8,9},{9,8},{10,11... | collective-permute-start | bytes 3145736 | tf_op jit(solution)/shard_map/ppermute | solution.py:349
  98.7 26.5 %collective-permute-start.19 = (bf16[32,128,128]{2,1,0:T(8,128)(2,1)}, bf16[32,128,128]{2,1,0:T(8,128)(2,1)}, u32[]{:S(2)}, u32[]{:S(2)}) collective-permute-start(bf16[32,128,128]{2,1,0:T(8,128)(2,1)} %choose.1.refs_3_), channel_id=1, source_target_pairs={{0,2},{1,5},{2,0},{3,7},{4,6},{5,1},{6,4},{7,3},{8,10},{9,13},{10,... | collective-permute-start | bytes 3145736 | tf_op jit(solution)/shard_map/ppermute | solution.py:349
  99.3 13.0 %collective-permute-start.10 = (s32[8,64]{1,0:T(8,128)S(1)}, s32[8,64]{1,0:T(8,128)S(1)}, u32[]{:S(2)}, u32[]{:S(2)}) collective-permute-start(s32[8,64]{1,0:T(8,128)S(1)} %pad_add_fusion), channel_id=1, source_target_pairs={{0,1},{1,0},{2,3},{3,2},{4,5},{5,4},{6,7},{7,6},{8,9},{9,8},{10,11... | collective-permute-start | bytes 6152 | tf_op jit(solution)/shard_map/ppermute | solution.py:349
  111.8 15.3 %collective-permute-start.22 = (bf16[256,2048]{1,0:T(8,128)(2,1)}, bf16[256,2048]{1,0:T(8,128)(2,1)}, u32[]{:S(2)}, u32[]{:S(2)}) collective-permute-start(bf16[256,2048]{1,0:T(8,128)(2,1)} %get-tuple-element.23.refs_1_), channel_id=1, source_target_pairs={{0,4},{1,3},{2,6},{3,1},{4,0},{5,7},{6,2},{7,5},{8,12},{9,11},{10,... | collective-permute-start | bytes 3145736 | tf_op jit(solution)/shard_map/ppermute | solution.py:349
  112.3 26.2 %collective-permute-start.17 = (bf16[32,128,128]{2,1,0:T(8,128)(2,1)}, bf16[32,128,128]{2,1,0:T(8,128)(2,1)}, u32[]{:S(2)}, u32[]{:S(2)}) collective-permute-start(bf16[32,128,128]{2,1,0:T(8,128)(2,1)} %tie.17.refs_1_), channel_id=1, source_target_pairs={{0,1},{1,0},{2,3},{3,2},{4,5},{5,4},{6,7},{7,6},{8,9},{9,8},{10,11... | collective-permute-start | bytes 3145736 | tf_op jit(solution)/shard_map/ppermute | solution.py:349
  112.3 0.6 copy-start.5
  123.3 15.2 %collective-permute-start.23 = (bf16[256,2048]{1,0:T(8,128)(2,1)}, bf16[256,2048]{1,0:T(8,128)(2,1)}, u32[]{:S(2)}, u32[]{:S(2)}) collective-permute-start(bf16[256,2048]{1,0:T(8,128)(2,1)} %get-tuple-element.25.refs_1_), channel_id=1, source_target_pairs={{0,2},{1,5},{2,0},{3,7},{4,6},{5,1},{6,4},{7,3},{8,10},{9,13},{10,... | collective-permute-start | bytes 3145736 | tf_op jit(solution)/shard_map/ppermute | solution.py:349
  124.8 13.6 %collective-permute-start.18 = (bf16[32,128,128]{2,1,0:T(8,128)(2,1)}, bf16[32,128,128]{2,1,0:T(8,128)(2,1)}, u32[]{:S(2)}, u32[]{:S(2)}) collective-permute-start(bf16[32,128,128]{2,1,0:T(8,128)(2,1)} %tie.18.refs_2_), channel_id=1, source_target_pairs={{0,1},{1,0},{2,3},{3,2},{4,5},{5,4},{6,7},{7,6},{8,9},{9,8},{10,11... | collective-permute-start | bytes 3145736 | tf_op jit(solution)/shard_map/ppermute | solution.py:349
  125.2 13.3 %collective-permute-start.21 = (bf16[32,128,128]{2,1,0:T(8,128)(2,1)}, bf16[32,128,128]{2,1,0:T(8,128)(2,1)}, u32[]{:S(2)}, u32[]{:S(2)}) collective-permute-start(bf16[32,128,128]{2,1,0:T(8,128)(2,1)} %tie.19.refs_3_), channel_id=1, source_target_pairs={{0,1},{1,0},{2,3},{3,2},{4,5},{5,4},{6,7},{7,6},{8,9},{9,8},{10,11... | collective-permute-start | bytes 3145736 | tf_op jit(solution)/shard_map/ppermute | solution.py:349
  137.5 18.5 %collective-permute-start.25 = (bf16[256,2048]{1,0:T(8,128)(2,1)}, bf16[256,2048]{1,0:T(8,128)(2,1)}, u32[]{:S(2)}, u32[]{:S(2)}) collective-permute-start(bf16[256,2048]{1,0:T(8,128)(2,1)} %get-tuple-element.29), channel_id=1, source_target_pairs={{0,4},{1,3},{2,6},{3,1},{4,0},{5,7},{6,2},{7,5},{8,12},{9,11},{10,... | collective-permute-start | bytes 3145736 | tf_op jit(solution)/shard_map/ppermute | solution.py:349
  148.8 15.2 %collective-permute-start.24 = (bf16[256,2048]{1,0:T(8,128)(2,1)}, bf16[256,2048]{1,0:T(8,128)(2,1)}, u32[]{:S(2)}, u32[]{:S(2)}) collective-permute-start(bf16[256,2048]{1,0:T(8,128)(2,1)} %get-tuple-element.28), channel_id=1, source_target_pairs={{0,2},{1,5},{2,0},{3,7},{4,6},{5,1},{6,4},{7,3},{8,10},{9,13},{10,... | collective-permute-start | bytes 3145736 | tf_op jit(solution)/shard_map/ppermute | solution.py:349

commit v6 on v5

--- a/solution.py
+++ b/solution.py
@@ -9,7 +9,6 @@
 from jax.sharding import PartitionSpec as P
 
 TILE = 128
-PARTS = 8
 NOTHING = pl.CostEstimate(flops=0, bytes_accessed=0, transcendentals=0)
 MM_COLS = 512
 VMEM_LIMIT = (64 << 20) - (256 << 10)
@@ -93,11 +92,12 @@
     )(scalars, target.reshape(1, n), *amps)
 
 
-def product_body(at, has_whole, scalars, table, mine, theirs, *refs):
+def product_body(at, has_acc, has_whole, final, scalars, table, mine, theirs, *refs):
     core_at, picks, rows_at, mine_at, theirs_at = at
     slot_count = len(rows_at)
     packed_hbm = refs[:slot_count]
-    refs = refs[slot_count + has_whole :]
+    acc = refs[slot_count] if has_acc else None
+    refs = refs[slot_count + has_acc + has_whole :]
     outs, (lhs_all, rhs_all, packed, lhs_sem, sems) = refs[:-5], refs[-5:]
     step = pl.program_id(0)
     capacity, part = mine.shape[2:]
@@ -134,11 +134,16 @@
                     e < count, tile, jnp.zeros_like(tile)
                 )
     total = jnp.dot(lhs_all[...], rhs_all[...], preferred_element_type=jnp.float32)
+    if has_acc:
+        total = acc[...] + total
+    if not final:
+        outs[0][...] = total
+        return
     for t in range(len(picks)):
         outs[t][...] = total[t * capacity : (t + 1) * capacity].astype(outs[t].dtype)
 
 
-def product(scalars, table, mine, theirs, slots, int_cols, whole_cols, whole, at, place_at):
+def product(scalars, table, mine, theirs, slots, int_cols, at, acc=None, whole_cols=None, whole=None, place_at=None):
     core_at, picks, rows_at, mine_at, theirs_at = at
     capacity, part = mine.shape[2:]
     slot_count, m = len(slots), len(picks) * capacity
@@ -147,23 +152,33 @@
     steps = int_cols // width
     hbm = pl.BlockSpec(memory_space=pltpu.HBM)
     operands = [scalars, table, mine, theirs, *slots]
+    in_specs = [hbm] * (len(operands) - 2)
     aliases = {}
+    chunk = pl.BlockSpec((m, width), lambda i, sc, tab: (0, i))
+    if acc is not None:
+        in_specs.append(chunk)
+        operands.append(acc)
     if whole is not None:
         aliases = {len(operands): 0}
+        in_specs.append(hbm)
         operands.append(whole)
-    out_specs = [pl.BlockSpec((capacity, width), lambda i, sc, tab: (0, sc[place_at] * steps + i))]
-    out_shape = [jax.ShapeDtypeStruct((capacity, whole_cols), mine.dtype)]
-    for _ in picks[1:]:
+    final = whole_cols is not None
+    out_specs = [chunk]
+    out_shape = [jax.ShapeDtypeStruct((m, int_cols), jnp.float32)]
+    if final:
+        out_specs = [pl.BlockSpec((capacity, width), lambda i, sc, tab: (0, sc[place_at] * steps + i))]
+        out_shape = [jax.ShapeDtypeStruct((capacity, whole_cols), mine.dtype)]
+    for _ in picks[1:] if final else ():
         out_specs.append(pl.BlockSpec((capacity, width), lambda i, sc, tab: (0, i)))
         out_shape.append(jax.ShapeDtypeStruct((capacity, int_cols), mine.dtype))
     k = slot_count * depth
     return pl.pallas_call(
-        functools.partial(product_body, at, whole is not None),
+        functools.partial(product_body, at, acc is not None, whole is not None, final),
         out_shape=out_shape,
         grid_spec=pltpu.PrefetchScalarGridSpec(
             num_scalar_prefetch=2,
             grid=(steps,),
-            in_specs=[hbm] * (len(operands) - 2),
+            in_specs=in_specs,
             out_specs=out_specs,
             scratch_shapes=[
                 pltpu.VMEM((m, k), mine.dtype),
@@ -197,27 +212,16 @@
     )(value, *others)
 
 
-def choose_body(at, scalars, a_ref, b_ref, out_ref, held, in_sems, out_sems):
-    parts = in_sems.shape[0]
-    size = held.shape[0] // parts
-    spans = [pl.ds(p * size, size) for p in range(parts)]
-
+def choose_body(at, scalars, a_ref, b_ref, out_ref, sem):
     @pl.when(scalars[at] != 0)
     def _():
-        for p, span in enumerate(spans):
-            pltpu.make_async_copy(a_ref.at[span], held.at[span], in_sems.at[p]).start()
+        pltpu.make_async_copy(a_ref, out_ref, sem).start()
 
     @pl.when(scalars[at] == 0)
     def _():
-        for p, span in enumerate(spans):
-            pltpu.make_async_copy(b_ref.at[span], held.at[span], in_sems.at[p]).start()
-
-    outs = [pltpu.make_async_copy(held.at[span], out_ref.at[span], out_sems.at[p]) for p, span in enumerate(spans)]
-    for p, span in enumerate(spans):
-        pltpu.make_async_copy(a_ref.at[span], held.at[span], in_sems.at[p]).wait()
-        outs[p].start()
-    for copy in outs:
-        copy.wait()
+        pltpu.make_async_copy(b_ref, out_ref, sem).start()
+
+    pltpu.make_async_copy(a_ref, out_ref, sem).wait()
 
 
 def choose(scalars, at, a, b):
@@ -226,49 +230,31 @@
         functools.partial(choose_body, at),
         out_shape=jax.ShapeDtypeStruct(a.shape, a.dtype),
         in_specs=[pl.BlockSpec(memory_space=pltpu.SMEM), hbm, hbm],
-        out_specs=hbm,
-        scratch_shapes=[
-            pltpu.VMEM(a.shape, a.dtype),
-            pltpu.SemaphoreType.DMA((PARTS,)),
-            pltpu.SemaphoreType.DMA((PARTS,)),
-        ],
+        out_specs=pl.BlockSpec(memory_space=pltpu.VMEM),
+        scratch_shapes=[pltpu.SemaphoreType.DMA],
         compiler_params=params(),
         cost_estimate=NOTHING,
         name="choose",
     )(scalars, a, b)
 
 
-def put_body(at, scalars, piece_ref, whole_ref, out_ref, held, in_sems, out_sems):
-    parts = in_sems.shape[0]
-    m, n = held.shape
-    size = m // parts
-    columns = pl.ds(pl.multiple_of(scalars[at] * n, TILE), n)
-    spans = [pl.ds(p * size, size) for p in range(parts)]
-    ins = [pltpu.make_async_copy(piece_ref.at[span], held.at[span], in_sems.at[p]) for p, span in enumerate(spans)]
-    outs = [
-        pltpu.make_async_copy(held.at[span], out_ref.at[span, columns], out_sems.at[p]) for p, span in enumerate(spans)
-    ]
-    for copy in ins:
-        copy.start()
-    for before, after in zip(ins, outs):
-        before.wait()
-        after.start()
-    for copy in outs:
-        copy.wait()
+def put_body(scalars, piece_ref, whole_ref, out_ref):
+    out_ref[...] = piece_ref[...]
 
 
 def put(piece, whole, scalars, at):
-    hbm = pl.BlockSpec(memory_space=pltpu.HBM)
-    return pl.pallas_call(
-        functools.partial(put_body, at),
+    m, n = piece.shape
+    width = min(2 * MM_COLS, n)
+    steps = n // width
+    return pl.pallas_call(
+        put_body,
         out_shape=jax.ShapeDtypeStruct(whole.shape, whole.dtype),
-        in_specs=[pl.BlockSpec(memory_space=pltpu.SMEM), hbm, hbm],
-        out_specs=hbm,
-        scratch_shapes=[
-            pltpu.VMEM(piece.shape, piece.dtype),
-            pltpu.SemaphoreType.DMA((PARTS,)),
-            pltpu.SemaphoreType.DMA((PARTS,)),
-        ],
+        grid_spec=pltpu.PrefetchScalarGridSpec(
+            num_scalar_prefetch=1,
+            grid=(steps,),
+            in_specs=[pl.BlockSpec((m, width), lambda i, s: (0, i)), pl.BlockSpec(memory_space=pltpu.HBM)],
+            out_specs=pl.BlockSpec((m, width), lambda i, s: (0, s[at] * steps + i)),
+        ),
         input_output_aliases={2: 0},
         compiler_params=params(),
         cost_estimate=NOTHING,
@@ -423,26 +409,29 @@
     target = pair_dest * capacity + jnp.sum(before * onehot, axis=1)
 
     mine, for_them = pick_rows(scalars, wanted_at, len(turns), target, amps, capacity)
+    sums = None
     slots, nexts, theirs_of, theirs_next = [packed], [permute(packed, along)], [permute(packed, across)], []
     for at, moves in enumerate(phases):
         if at > 0:
             fresh = line_phase(moves, packed_again)
         if at == 0:
-            waited = (mine, nexts[0], theirs_of[0])
-            fresh[0] = tie(fresh[0], mine)
+            own_table = tie(own_table, amp_next)
+            table_next = permute(own_table, along)
+            pair_tables = permute(jnp.concatenate([own_table, table_next], axis=0), across)
+            waited = (mine, nexts[0], theirs_of[0], pair_tables)
+            fresh[0] = tie(fresh[0], mine, fresh[1])
         elif at == 1:
             theirs = permute(for_them, across)
-            own_table = tie(own_table, *nexts[1:])
-            table_next = permute(own_table, along)
-            pair_tables = permute(jnp.concatenate([own_table, table_next], axis=0), across)
-            waited = (theirs, table_next, *theirs_of[1:], *nexts[1:])
-            theirs_next.append(permute(nexts[0], across))
-            waited = (theirs, table_next, *nexts[1:], *theirs_of[1:], *theirs_next)
+            waited = (theirs, *nexts[1:])
         else:
             waited = (*nexts[-1:], *theirs_of[-1:])
             while len(theirs_next) < len(nexts) - 1:
                 theirs_next.append(permute(nexts[len(theirs_next)], across))
                 waited = (*waited, theirs_next[-1])
+        if at == len(phases) - 1:
+            parts = (core_at, picks_at[0], *(places[: rows - 1] for places in (rows_at, mine_at, theirs_at)))
+            (sums,) = product(scalars, own_table, mine, theirs, slots, int_cols, parts)
+            waited = (*waited, sums)
         tied = []
         for i, value in enumerate(fresh):
             if at > 0 or i > 0:
@@ -466,17 +455,22 @@
     for turn_at, q in enumerate((0, 2, 1, 3)):
         if turn_at >= 2:
             out = tie(out, *arrived[turn_at - 2])
+        parts = (core_at, picks_at[q], rows_at if q < 3 else low_rows_at, mine_at, theirs_at)
+        blocks = (slots, nexts, theirs_of, theirs_next)[q]
+        if q == 0 and rows > 1:
+            blocks, parts = blocks[-1:], (*parts[:2], *(places[-1:] for places in parts[2:]))
         out, *pieces = product(
             scalars,
             (own_table, table_next, pair_tables, pair_tables)[q],
             mine,
             theirs,
-            (slots, nexts, theirs_of, theirs_next)[q],
+            blocks,
             int_cols,
-            cols * int_cols,
-            out,
-            (core_at, picks_at[q], rows_at if q < 3 else low_rows_at, mine_at, theirs_at),
-            place_at[q],
+            parts,
+            acc=sums if q == 0 else None,
+            whole_cols=cols * int_cols,
+            whole=out,
+            place_at=place_at[q],
         )
         arrived.append([])
         for (de, turn), piece in zip(hops[1:], pieces):

time: 167 us -> 161 us (0.964)
  waiting for transfers between devices: 57.3 us -> 46.6 us
  Pallas kernels: 72.7 us -> 78.1 us
  local copies, waits for them, and re-layouts: 4.24 us -> 2.15 us
    ppermute x22, waiting for transfers between devices: 38.3 us -> 30.1 us  [permute(): lax.ppermute(value, 'col', [(col_index(*at), col_index(*moved_to(*at))) f...]
    pallas_call x8 -> x9, Pallas kernels: 52.4 us -> 57.9 us  [the longest x5 47 us: product(): pl.pallas_call(functools.partial(product_body, at, acc is not None, whole...]
    ppermute x4, waiting for transfers between devices: 19.1 us -> 16.5 us  [line_phase(): lax.ppermute(own if source < 0 else moved[source], 'row', pairs)]
    unnamed x14 -> x4, local copies, waits for them, and re-layouts: 2.74 us -> 0.59 us
  transfers between devices with their start and end apart: 26 -> 26, of which waited for: 11 -> 10; matrix products, arithmetic and copies ran while one was open for 4% -> 5% of each run, Pallas kernels for 38% -> 45%
where the time goes in v6:
time: 161 us
  Pallas kernels  78.1 us (49%)
  waiting for transfers between devices  46.6 us (29%)
  starting transfers between devices  26.4 us (16%)
  other arithmetic  7.18 us (4%)
  local copies, waits for them, and re-layouts  2.15 us (1%)
    pallas_call x5, Pallas kernels, product(): pl.pallas_call(functools.partial(product_body, at, acc is not None, whole...  47 us
    ppermute x22, waiting for transfers between devices, permute(): lax.ppermute(value, 'col', [(col_index(*at), col_index(*moved_to(*at))) f...  30.1 us
    ppermute x22, starting transfers between devices, permute(): lax.ppermute(value, 'col', [(col_index(*at), col_index(*moved_to(*at))) f...  19.4 us
    ppermute x4, waiting for transfers between devices, line_phase(): lax.ppermute(own if source < 0 else moved[source], 'row', pairs)  16.5 us
    pallas_call x1, Pallas kernels, pick_rows(): pl.pallas_call(functools.partial(pick_body, first, capacity), out_shape=[...  13.7 us
    pallas_call x4, Pallas kernels, put(): pl.pallas_call(put_body, out_shape=jax.ShapeDtypeStruct(whole.shape, whol...  10.9 us
    ppermute x4, starting transfers between devices, line_phase(): lax.ppermute(own if source < 0 else moved[source], 'row', pairs)  7.09 us
    pallas_call x1, Pallas kernels, pack(): pl.pallas_call(pack_body, out_shape=[jax.ShapeDtypeStruct((count, TILE, T...  3.64 us
  transfers between devices with their start and end apart: 26, of which 10 were waited for; matrix products, arithmetic and copies ran while one was open for 5% of the time, Pallas kernels for 45%

profile of v6, /device:TPU:0, one launch (start us, length us, event | category | flops | bytes accessed | tf_op | source)
XLA Modules:
  0.0 160.7 jit_solution(8481735365727197544)
XLA Ops:
  0.0 3.6 %pack_tiles.1 = (bf16[32,128,128]{2,1,0:T(8,128)(2,1)}, bf16[32,128,128]{2,1,0:T(8,128)(2,1)}, bf16[1024,256]{1,0:T(8,128)(2,1)}) custom-call(s32[1]{0:T(128)} %bitcast.2.row, s32[4,32]{1,0:T(4,128)} %bitcast.29, s32[2,8]{1,0:T(2,128)} %bitcast.31, bf16[512,2048]{1,0:T(8,128)(2,1)} %src_ref.1, bf16[1024,256]{1,0:T(8,128)(2,1)} %amp_ref.1), custom_call_target="tpu_custom_call" | custom-call | tf_op jit(solution)/shard_map/pack_tiles/pallas_call | solution.py:39
  3.6 2.9 %collective-permute-start = (bf16[1024,256]{1,0:T(8,128)(2,1)}, bf16[1024,256]{1,0:T(8,128)(2,1)}, u32[]{:S(2)}, u32[]{:S(2)}) collective-permute-start(bf16[1024,256]{1,0:T(8,128)(2,1)} %get-tuple-element.18.refs_0_), channel_id=1, source_target_pairs={{0,2},{1,5},{2,0},{3,7},{4,6},{5,1},{6,4},{7,3},{8,10},{9,13},{10,... | collective-permute-start | bytes 1572872 | tf_op jit(solution)/shard_map/ppermute | solution.py:335
  6.6 1.5 collective-permute-start.3
  8.1 2.6 %collective-permute-start.7 = (bf16[32,128,128]{2,1,0:T(8,128)(2,1)}, bf16[32,128,128]{2,1,0:T(8,128)(2,1)}, u32[]{:S(2)}, u32[]{:S(2)}) collective-permute-start(bf16[32,128,128]{2,1,0:T(8,128)(2,1)} %get-tuple-element.21.refs_0_), channel_id=1, source_target_pairs={{0,16},{16,0},{8,24},{24,8},{1,17},{17,1},{9,25},{25,9},{2,18},{18... | collective-permute-start | bytes 3145736 | tf_op jit(solution)/shard_map/ppermute | solution.py:392
  10.7 1.6 collective-permute-start.10
  12.3 0.5 collective-permute-start.6
  12.8 0.7 fusion.3
  13.5 2.3 %reduce-window.6 = s32[8,8,128]{2,1,0:T(8,128)S(1)} reduce-window(s32[8,8,128]{2,1,0:T(8,128)S(1)} %fusion.3, s32[]{:T(128)} %constant.20.clone.1), window={size=1x1x128 pad=0_0x0_0x127_0}, to_apply=%region_1.2 | reduce-window | flops 1040384 | bytes 65540 | tf_op jit(solution)/shard_map/reduce-window
  15.7 0.3 slice_reduce_fusion
  16.2 2.9 %collective-permute-done.refs_1_ = bf16[1024,256]{1,0:T(8,128)(2,1)} collective-permute-done((bf16[1024,256]{1,0:T(8,128)(2,1)}, bf16[1024,256]{1,0:T(8,128)(2,1)}, u32[]{:S(2)}, u32[]{:S(2)}) %collective-permute-start) | collective-permute-done | bytes 524320 | tf_op jit(solution)/shard_map/ppermute | solution.py:335
  19.1 1.5 collective-permute-start.4
  20.7 1.1 collective-permute-done.3.refs_2_
  21.8 1.3 select_reduce_fusion.refs_0_
  23.1 0.7 fusion.2
  23.8 1.3 multiply_add_fusion
  25.1 9.2 %collective-permute-done.4.refs_3_ = bf16[1024,256]{1,0:T(8,128)(2,1)} collective-permute-done((bf16[1024,256]{1,0:T(8,128)(2,1)}, bf16[1024,256]{1,0:T(8,128)(2,1)}, u32[]{:S(2)}, u32[]{:S(2)}) %collective-permute-start.4) | collective-permute-done | bytes 524320 | tf_op jit(solution)/shard_map/ppermute | solution.py:335
  34.3 2.5 %collective-permute-start.1 = (s32[4,64]{1,0:T(4,128)}, s32[4,64]{1,0:T(4,128)S(1)}, u32[]{:S(2)}, u32[]{:S(2)}) collective-permute-start(s32[4,64]{1,0:T(4,128)} %tie.12.table), channel_id=1, source_target_pairs={{0,2},{1,5},{2,0},{3,7},{4,6},{5,1},{6,4},{7,3},{8,10},{9,13},{10,... | collective-permute-start | bytes 3080 | tf_op jit(solution)/shard_map/ppermute | solution.py:335
  36.8 1.3 dynamic-slice_bitcast_fusion.scalars
  38.0 13.7 %pick_rows.1 = (bf16[4,3,256,256]{3,2,1,0:T(8,128)(2,1)}, bf16[4,3,256,256]{3,2,1,0:T(8,128)(2,1)}) custom-call(s32[40]{0:T(128)} %dynamic-slice_bitcast_fusion.scalars, s32[1,1024]{1,0:T(1,128)} %bitcast.27, bf16[1024,256]{1,0:T(8,128)(2,1)} %get-tuple-element.18.refs_0_, bf16[1024,256]{1,0:T(8,128)(2,1)} %collective-permute-done.refs_1_, ...), custom_call_target="tpu_custom_call" | custom-call | tf_op jit(solution)/shard_map/pick_rows/pallas_call | solution.py:76
  51.8 0.7 pad_add_fusion
  52.5 3.7 %collective-permute-done.7.refs_0_.refs_2_ = bf16[32,128,128]{2,1,0:T(8,128)(2,1)} collective-permute-done((bf16[32,128,128]{2,1,0:T(8,128)(2,1)}, bf16[32,128,128]{2,1,0:T(8,128)(2,1)}, u32[]{:S(2)}, u32[]{:S(2)}) %collective-permute-start.7) | collective-permute-done | bytes 1048608 | tf_op jit(solution)/shard_map/ppermute | solution.py:392
  56.4 1.0 collective-permute-done.2.refs_4_.table
  57.4 0.6 copy-done
  58.0 1.6 %collective-permute-start.9 = (bf16[32,128,128]{2,1,0:T(8,128)(2,1)}, bf16[32,128,128]{2,1,0:T(8,128)(2,1)}, u32[]{:S(2)}, u32[]{:S(2)}) collective-permute-start(bf16[32,128,128]{2,1,0:T(8,128)(2,1)} %tie.14), channel_id=1, source_target_pairs={{8,16},{16,8},{9,17},{17,9},{10,18},{18,10},{11,19},{19,11},{12,20... | collective-permute-start | bytes 3145736 | tf_op jit(solution)/shard_map/ppermute | solution.py:392
  59.6 0.5 collective-permute-start.12
  60.2 1.3 collective-permute-start.13
  61.5 1.6 collective-permute-start.11
  63.0 8.8 %product.5.refs_4_.refs_1_ = f32[512,2048]{1,0:T(8,128)} custom-call(s32[40]{0:T(128)} %dynamic-slice_bitcast_fusion.scalars, s32[4,64]{1,0:T(4,128)} %tie.12.table, bf16[4,3,256,256]{3,2,1,0:T(8,128)(2,1)} %get-tuple-element.19.refs_1_.mine, bf16[4,3,256,256]{3,2,1,0:T(8,128)(2,1)} %collective-permute-done.5.theirs.refs_1_, ...), custom_call_target="tpu_custom_call" | custom-call | tf_op jit(solution)/shard_map/product/pallas_call | solution.py:175
  71.8 0.6 collective-permute-start.18
  72.4 2.4 %collective-permute-done.12.refs_3_.refs_0_ = bf16[32,128,128]{2,1,0:T(8,128)(2,1)} collective-permute-done((bf16[32,128,128]{2,1,0:T(8,128)(2,1)}, bf16[32,128,128]{2,1,0:T(8,128)(2,1)}, u32[]{:S(2)}, u32[]{:S(2)}) %collective-permute-start.12) | collective-permute-done | bytes 1048608 | tf_op jit(solution)/shard_map/ppermute | solution.py:335
  74.8 12.5 %collective-permute-done.13.refs_5_.refs_0_ = bf16[32,128,128]{2,1,0:T(8,128)(2,1)} collective-permute-done((bf16[32,128,128]{2,1,0:T(8,128)(2,1)}, bf16[32,128,128]{2,1,0:T(8,128)(2,1)}, u32[]{:S(2)}, u32[]{:S(2)}) %collective-permute-start.13) | collective-permute-done | bytes 1048608 | tf_op jit(solution)/shard_map/ppermute | solution.py:392
  87.3 2.9 %choose.1.refs_0_ = bf16[32,128,128]{2,1,0:T(8,128)(2,1)} custom-call(s32[40]{0:T(128)} %dynamic-slice_bitcast_fusion.scalars, bf16[32,128,128]{2,1,0:T(8,128)(2,1)} %tie.16.refs_5_.a_ref, bf16[32,128,128]{2,1,0:T(8,128)(2,1)} %tie.17.b_ref), custom_call_target="tpu_custom_call" | custom-call | tf_op jit(solution)/shard_map/choose/pallas_call | solution.py:229
  90.3 0.5 collective-permute-start.17
  90.8 7.2 %product.6 = (bf16[256,16384]{1,0:T(8,128)(2,1)}, bf16[256,2048]{1,0:T(8,128)(2,1)}) custom-call(s32[40]{0:T(128)} %dynamic-slice_bitcast_fusion.scalars, s32[4,64]{1,0:T(4,128)} %tie.12.table, bf16[4,3,256,256]{3,2,1,0:T(8,128)(2,1)} %get-tuple-element.19.refs_1_.mine, bf16[4,3,256,256]{3,2,1,0:T(8,128)(2,1)} %collective-permute-done.5.theirs.refs_1_, ...), custom_call_target="tpu_custom_call" | custom-call | tf_op jit(solution)/shard_map/product/pallas_call | solution.py:175
  98.1 1.6 %collective-permute-start.22 = (bf16[256,2048]{1,0:T(8,128)(2,1)}, bf16[256,2048]{1,0:T(8,128)(2,1)}, u32[]{:S(2)}, u32[]{:S(2)}) collective-permute-start(bf16[256,2048]{1,0:T(8,128)(2,1)} %get-tuple-element.23.refs_1_), channel_id=1, source_target_pairs={{0,4},{1,3},{2,6},{3,1},{4,0},{5,7},{6,2},{7,5},{8,12},{9,11},{10,... | collective-permute-start | bytes 3145736 | tf_op jit(solution)/shard_map/ppermute | solution.py:335
  99.7 10.3 %product.7 = (bf16[256,16384]{1,0:T(8,128)(2,1)}, bf16[256,2048]{1,0:T(8,128)(2,1)}) custom-call(s32[40]{0:T(128)} %dynamic-slice_bitcast_fusion.scalars, s32[8,64]{1,0:T(8,128)} %copy-done, bf16[4,3,256,256]{3,2,1,0:T(8,128)(2,1)} %get-tuple-element.19.refs_1_.mine, ...), custom_call_target="tpu_custom_call", output_to_operand_aliasing={{0}: (8, {})} | custom-call | tf_op jit(solution)/shard_map/product/pallas_call | solution.py:175
  110.1 1.6 collective-permute-start.23
  111.6 0.5 collective-permute-start.14
  112.2 6.6 %collective-permute-done.22.refs_1_.piece_ref = bf16[256,2048]{1,0:T(8,128)(2,1)} collective-permute-done((bf16[256,2048]{1,0:T(8,128)(2,1)}, bf16[256,2048]{1,0:T(8,128)(2,1)}, u32[]{:S(2)}, u32[]{:S(2)}) %collective-permute-start.22) | collective-permute-done | bytes 1048608 | tf_op jit(solution)/shard_map/ppermute | solution.py:335
  118.8 0.6 collective-permute-start.21
  119.4 10.3 %product.8 = (bf16[256,16384]{1,0:T(8,128)(2,1)}, bf16[256,2048]{1,0:T(8,128)(2,1)}) custom-call(s32[40]{0:T(128)} %dynamic-slice_bitcast_fusion.scalars, s32[4,64]{1,0:T(4,128)} %copy-done.1, bf16[4,3,256,256]{3,2,1,0:T(8,128)(2,1)} %get-tuple-element.19.refs_1_.mine, ...), custom_call_target="tpu_custom_call", output_to_operand_aliasing={{0}: (8, {})} | custom-call | tf_op jit(solution)/shard_map/product/pallas_call | solution.py:175
  129.7 2.6 %collective-permute-start.25 = (bf16[256,2048]{1,0:T(8,128)(2,1)}, bf16[256,2048]{1,0:T(8,128)(2,1)}, u32[]{:S(2)}, u32[]{:S(2)}) collective-permute-start(bf16[256,2048]{1,0:T(8,128)(2,1)} %get-tuple-element.29), channel_id=1, source_target_pairs={{0,4},{1,3},{2,6},{3,1},{4,0},{5,7},{6,2},{7,5},{8,12},{9,11},{10,... | collective-permute-start | bytes 3145736 | tf_op jit(solution)/shard_map/ppermute | solution.py:335
  132.4 10.4 %product.9 = (bf16[256,16384]{1,0:T(8,128)(2,1)}, bf16[256,2048]{1,0:T(8,128)(2,1)}) custom-call(s32[40]{0:T(128)} %dynamic-slice_bitcast_fusion.scalars, s32[8,64]{1,0:T(8,128)} %copy-done, bf16[4,3,256,256]{3,2,1,0:T(8,128)(2,1)} %get-tuple-element.19.refs_1_.mine, ...), custom_call_target="tpu_custom_call", output_to_operand_aliasing={{0}: (8, {})} | custom-call | tf_op jit(solution)/shard_map/product/pallas_call | solution.py:175
  142.8 2.7 %put.4.whole_ref = bf16[256,16384]{1,0:T(8,128)(2,1)} custom-call(s32[40]{0:T(128)} %dynamic-slice_bitcast_fusion.scalars, bf16[256,2048]{1,0:T(8,128)(2,1)} %collective-permute-done.22.refs_1_.piece_ref, bf16[256,16384]{1,0:T(8,128)(2,1)} %get-tuple-element.30.whole_ref), custom_call_target="tpu_custom_call", output_to_operand_aliasing={{}: (2, {})} | custom-call | tf_op jit(solution)/shard_map/put/pallas_call | solution.py:249
  145.6 2.7 %put.5.whole_ref = bf16[256,16384]{1,0:T(8,128)(2,1)} custom-call(s32[40]{0:T(128)} %dynamic-slice_bitcast_fusion.scalars, bf16[256,2048]{1,0:T(8,128)(2,1)} %collective-permute-done.23.refs_1_.piece_ref, bf16[256,16384]{1,0:T(8,128)(2,1)} %put.4.whole_ref), custom_call_target="tpu_custom_call", output_to_operand_aliasing={{}: (2, {})} | custom-call | tf_op jit(solution)/shard_map/put/pallas_call | solution.py:249
  148.3 2.7 %put.6.whole_ref = bf16[256,16384]{1,0:T(8,128)(2,1)} custom-call(s32[40]{0:T(128)} %dynamic-slice_bitcast_fusion.scalars, bf16[256,2048]{1,0:T(8,128)(2,1)} %collective-permute-done.25.piece_ref, bf16[256,16384]{1,0:T(8,128)(2,1)} %put.5.whole_ref), custom_call_target="tpu_custom_call", output_to_operand_aliasing={{}: (2, {})} | custom-call | tf_op jit(solution)/shard_map/put/pallas_call | solution.py:249
  151.0 6.9 %collective-permute-done.24.piece_ref = bf16[256,2048]{1,0:T(8,128)(2,1)} collective-permute-done((bf16[256,2048]{1,0:T(8,128)(2,1)}, bf16[256,2048]{1,0:T(8,128)(2,1)}, u32[]{:S(2)}, u32[]{:S(2)}) %collective-permute-start.24) | collective-permute-done | bytes 1048608 | tf_op jit(solution)/shard_map/ppermute | solution.py:335
  157.9 2.7 %put.7 = bf16[256,16384]{1,0:T(8,128)(2,1)} custom-call(s32[40]{0:T(128)} %dynamic-slice_bitcast_fusion.scalars, bf16[256,2048]{1,0:T(8,128)(2,1)} %collective-permute-done.24.piece_ref, bf16[256,16384]{1,0:T(8,128)(2,1)} %put.6.whole_ref), custom_call_target="tpu_custom_call", output_to_operand_aliasing={{}: (2, {})} | custom-call | tf_op jit(solution)/shard_map/put/pallas_call | solution.py:249
  (42 shorter events, 0.7 us)
Async XLA Ops:
  3.6 15.5 %collective-permute-start = (bf16[1024,256]{1,0:T(8,128)(2,1)}, bf16[1024,256]{1,0:T(8,128)(2,1)}, u32[]{:S(2)}, u32[]{:S(2)}) collective-permute-start(bf16[1024,256]{1,0:T(8,128)(2,1)} %get-tuple-element.18.refs_0_), channel_id=1, source_target_pairs={{0,2},{1,5},{2,0},{3,7},{4,6},{5,1},{6,4},{7,3},{8,10},{9,13},{10,... | collective-permute-start | bytes 1572872 | tf_op jit(solution)/shard_map/ppermute | solution.py:335
  6.6 15.2 %collective-permute-start.3 = (bf16[1024,256]{1,0:T(8,128)(2,1)}, bf16[1024,256]{1,0:T(8,128)(2,1)}, u32[]{:S(2)}, u32[]{:S(2)}) collective-permute-start(bf16[1024,256]{1,0:T(8,128)(2,1)} %get-tuple-element.18.refs_0_), channel_id=1, source_target_pairs={{0,4},{1,3},{2,6},{3,1},{4,0},{5,7},{6,2},{7,5},{8,12},{9,11},{10,... | collective-permute-start | bytes 1572872 | tf_op jit(solution)/shard_map/ppermute | solution.py:335
  8.1 48.1 %collective-permute-start.7 = (bf16[32,128,128]{2,1,0:T(8,128)(2,1)}, bf16[32,128,128]{2,1,0:T(8,128)(2,1)}, u32[]{:S(2)}, u32[]{:S(2)}) collective-permute-start(bf16[32,128,128]{2,1,0:T(8,128)(2,1)} %get-tuple-element.21.refs_0_), channel_id=1, source_target_pairs={{0,16},{16,0},{8,24},{24,8},{1,17},{17,1},{9,25},{25,9},{2,18},{18... | collective-permute-start | bytes 3145736 | tf_op jit(solution)/shard_map/ppermute | solution.py:392
  10.7 45.7 %collective-permute-start.10 = (bf16[32,128,128]{2,1,0:T(8,128)(2,1)}, bf16[32,128,128]{2,1,0:T(8,128)(2,1)}, u32[]{:S(2)}, u32[]{:S(2)}) collective-permute-start(bf16[32,128,128]{2,1,0:T(8,128)(2,1)} %get-tuple-element.21.refs_0_), channel_id=1, source_target_pairs={{0,8},{8,0},{16,24},{24,16},{1,9},{9,1},{17,25},{25,17},{2,10},{10... | collective-permute-start | bytes 3145736 | tf_op jit(solution)/shard_map/ppermute | solution.py:392
  12.3 45.1 %collective-permute-start.6 = (bf16[32,128,128]{2,1,0:T(8,128)(2,1)}, bf16[32,128,128]{2,1,0:T(8,128)(2,1)}, u32[]{:S(2)}, u32[]{:S(2)}) collective-permute-start(bf16[32,128,128]{2,1,0:T(8,128)(2,1)} %get-tuple-element.21.refs_0_), channel_id=1, source_target_pairs={{0,2},{1,5},{2,0},{3,7},{4,6},{5,1},{6,4},{7,3},{8,10},{9,13},{10,... | collective-permute-start | bytes 3145736 | tf_op jit(solution)/shard_map/ppermute | solution.py:335
  19.1 15.2 %collective-permute-start.4 = (bf16[1024,256]{1,0:T(8,128)(2,1)}, bf16[1024,256]{1,0:T(8,128)(2,1)}, u32[]{:S(2)}, u32[]{:S(2)}) collective-permute-start(bf16[1024,256]{1,0:T(8,128)(2,1)} %collective-permute-done.refs_1_), channel_id=1, source_target_pairs={{0,4},{1,3},{2,6},{3,1},{4,0},{5,7},{6,2},{7,5},{8,12},{9,11},{10,... | collective-permute-start | bytes 1572872 | tf_op jit(solution)/shard_map/ppermute | solution.py:335
  21.8 35.6 %collective-permute-start.8 = (bf16[32,128,128]{2,1,0:T(8,128)(2,1)}, bf16[32,128,128]{2,1,0:T(8,128)(2,1)}, u32[]{:S(2)}, u32[]{:S(2)}) collective-permute-start(bf16[32,128,128]{2,1,0:T(8,128)(2,1)} %get-tuple-element.21.refs_0_), channel_id=1, source_target_pairs={{0,1},{1,0},{2,3},{3,2},{4,5},{5,4},{6,7},{7,6},{8,9},{9,8},{10,11... | collective-permute-start | bytes 3145736 | tf_op jit(solution)/shard_map/ppermute | solution.py:335
  34.3 17.5 %collective-permute-start.1 = (s32[4,64]{1,0:T(4,128)}, s32[4,64]{1,0:T(4,128)S(1)}, u32[]{:S(2)}, u32[]{:S(2)}) collective-permute-start(s32[4,64]{1,0:T(4,128)} %tie.12.table), channel_id=1, source_target_pairs={{0,2},{1,5},{2,0},{3,7},{4,6},{5,1},{6,4},{7,3},{8,10},{9,13},{10,... | collective-permute-start | bytes 3080 | tf_op jit(solution)/shard_map/ppermute | solution.py:335
  51.7 20.1 %copy-start.1 = (s32[4,64]{1,0:T(4,128)}, s32[4,64]{1,0:T(4,128)S(1)}, u32[]{:S(2)}) copy-start(s32[4,64]{1,0:T(4,128)S(1)} %collective-permute-done.1.table) | copy-start | bytes 3076
  51.7 11.3 %collective-permute-start.5 = (bf16[4,3,256,256]{3,2,1,0:T(8,128)(2,1)}, bf16[4,3,256,256]{3,2,1,0:T(8,128)(2,1)}, u32[]{:S(2)}, u32[]{:S(2)}) collective-permute-start(bf16[4,3,256,256]{3,2,1,0:T(8,128)(2,1)} %get-tuple-element.20), channel_id=1, source_target_pairs={{0,1},{1,0},{2,3},{3,2},{4,5},{5,4},{6,7},{7,6},{8,9},{9,8},{10,11... | collective-permute-start | bytes 4718600 | tf_op jit(solution)/shard_map/ppermute | solution.py:335
  56.2 1.2 collective-permute-start.2
  57.4 0.6 copy-start
  58.0 13.8 %collective-permute-start.9 = (bf16[32,128,128]{2,1,0:T(8,128)(2,1)}, bf16[32,128,128]{2,1,0:T(8,128)(2,1)}, u32[]{:S(2)}, u32[]{:S(2)}) collective-permute-start(bf16[32,128,128]{2,1,0:T(8,128)(2,1)} %tie.14), channel_id=1, source_target_pairs={{8,16},{16,8},{9,17},{17,9},{10,18},{18,10},{11,19},{19,11},{12,20... | collective-permute-start | bytes 3145736 | tf_op jit(solution)/shard_map/ppermute | solution.py:392
  59.6 15.1 %collective-permute-start.12 = (bf16[32,128,128]{2,1,0:T(8,128)(2,1)}, bf16[32,128,128]{2,1,0:T(8,128)(2,1)}, u32[]{:S(2)}, u32[]{:S(2)}) collective-permute-start(bf16[32,128,128]{2,1,0:T(8,128)(2,1)} %tie.13.refs_1_.refs_2_), channel_id=1, source_target_pairs={{0,2},{1,5},{2,0},{3,7},{4,6},{5,1},{6,4},{7,3},{8,10},{9,13},{10,... | collective-permute-start | bytes 3145736 | tf_op jit(solution)/shard_map/ppermute | solution.py:335
  60.2 27.1 %collective-permute-start.13 = (bf16[32,128,128]{2,1,0:T(8,128)(2,1)}, bf16[32,128,128]{2,1,0:T(8,128)(2,1)}, u32[]{:S(2)}, u32[]{:S(2)}) collective-permute-start(bf16[32,128,128]{2,1,0:T(8,128)(2,1)} %tie.13.refs_1_.refs_2_), channel_id=1, source_target_pairs={{8,0},{16,24},{9,1},{17,25},{10,2},{18,26},{11,3},{19,27},{12,4},{... | collective-permute-start | bytes 3145736 | tf_op jit(solution)/shard_map/ppermute | solution.py:392
  61.5 25.8 %collective-permute-start.11 = (bf16[32,128,128]{2,1,0:T(8,128)(2,1)}, bf16[32,128,128]{2,1,0:T(8,128)(2,1)}, u32[]{:S(2)}, u32[]{:S(2)}) collective-permute-start(bf16[32,128,128]{2,1,0:T(8,128)(2,1)} %tie.15.refs_1_), channel_id=1, source_target_pairs={{0,2},{1,5},{2,0},{3,7},{4,6},{5,1},{6,4},{7,3},{8,10},{9,13},{10,... | collective-permute-start | bytes 3145736 | tf_op jit(solution)/shard_map/ppermute | solution.py:335
  63.0 36.7 %collective-permute-start.19 = (bf16[32,128,128]{2,1,0:T(8,128)(2,1)}, bf16[32,128,128]{2,1,0:T(8,128)(2,1)}, u32[]{:S(2)}, u32[]{:S(2)}) collective-permute-start(bf16[32,128,128]{2,1,0:T(8,128)(2,1)} %tie.13.refs_1_.refs_2_), channel_id=1, source_target_pairs={{0,1},{1,0},{2,3},{3,2},{4,5},{5,4},{6,7},{7,6},{8,9},{9,8},{10,11... | collective-permute-start | bytes 3145736 | tf_op jit(solution)/shard_map/ppermute | solution.py:335
  71.8 27.9 %collective-permute-start.18 = (bf16[32,128,128]{2,1,0:T(8,128)(2,1)}, bf16[32,128,128]{2,1,0:T(8,128)(2,1)}, u32[]{:S(2)}, u32[]{:S(2)}) collective-permute-start(bf16[32,128,128]{2,1,0:T(8,128)(2,1)} %tie.15.refs_1_), channel_id=1, source_target_pairs={{0,1},{1,0},{2,3},{3,2},{4,5},{5,4},{6,7},{7,6},{8,9},{9,8},{10,11... | collective-permute-start | bytes 3145736 | tf_op jit(solution)/shard_map/ppermute | solution.py:335
  90.2 9.5 %collective-permute-start.20 = (bf16[32,128,128]{2,1,0:T(8,128)(2,1)}, bf16[32,128,128]{2,1,0:T(8,128)(2,1)}, u32[]{:S(2)}, u32[]{:S(2)}) collective-permute-start(bf16[32,128,128]{2,1,0:T(8,128)(2,1)} %choose.1.refs_0_), channel_id=1, source_target_pairs={{0,1},{1,0},{2,3},{3,2},{4,5},{5,4},{6,7},{7,6},{8,9},{9,8},{10,11... | collective-permute-start | bytes 3145736 | tf_op jit(solution)/shard_map/ppermute | solution.py:335
  90.3 21.4 %collective-permute-start.17 = (bf16[32,128,128]{2,1,0:T(8,128)(2,1)}, bf16[32,128,128]{2,1,0:T(8,128)(2,1)}, u32[]{:S(2)}, u32[]{:S(2)}) collective-permute-start(bf16[32,128,128]{2,1,0:T(8,128)(2,1)} %choose.1.refs_0_), channel_id=1, source_target_pairs={{0,2},{1,5},{2,0},{3,7},{4,6},{5,1},{6,4},{7,3},{8,10},{9,13},{10,... | collective-permute-start | bytes 3145736 | tf_op jit(solution)/shard_map/ppermute | solution.py:335
  98.1 20.7 %collective-permute-start.22 = (bf16[256,2048]{1,0:T(8,128)(2,1)}, bf16[256,2048]{1,0:T(8,128)(2,1)}, u32[]{:S(2)}, u32[]{:S(2)}) collective-permute-start(bf16[256,2048]{1,0:T(8,128)(2,1)} %get-tuple-element.23.refs_1_), channel_id=1, source_target_pairs={{0,4},{1,3},{2,6},{3,1},{4,0},{5,7},{6,2},{7,5},{8,12},{9,11},{10,... | collective-permute-start | bytes 3145736 | tf_op jit(solution)/shard_map/ppermute | solution.py:335
  99.7 32.7 %collective-permute-start.16 = (bf16[32,128,128]{2,1,0:T(8,128)(2,1)}, bf16[32,128,128]{2,1,0:T(8,128)(2,1)}, u32[]{:S(2)}, u32[]{:S(2)}) collective-permute-start(bf16[32,128,128]{2,1,0:T(8,128)(2,1)} %tie.20.refs_2_), channel_id=1, source_target_pairs={{0,1},{1,0},{2,3},{3,2},{4,5},{5,4},{6,7},{7,6},{8,9},{9,8},{10,11... | collective-permute-start | bytes 3145736 | tf_op jit(solution)/shard_map/ppermute | solution.py:335
  110.1 19.6 %collective-permute-start.23 = (bf16[256,2048]{1,0:T(8,128)(2,1)}, bf16[256,2048]{1,0:T(8,128)(2,1)}, u32[]{:S(2)}, u32[]{:S(2)}) collective-permute-start(bf16[256,2048]{1,0:T(8,128)(2,1)} %get-tuple-element.25.refs_1_), channel_id=1, source_target_pairs={{0,2},{1,5},{2,0},{3,7},{4,6},{5,1},{6,4},{7,3},{8,10},{9,13},{10,... | collective-permute-start | bytes 3145736 | tf_op jit(solution)/shard_map/ppermute | solution.py:335
  111.6 20.7 %collective-permute-start.15 = (bf16[32,128,128]{2,1,0:T(8,128)(2,1)}, bf16[32,128,128]{2,1,0:T(8,128)(2,1)}, u32[]{:S(2)}, u32[]{:S(2)}) collective-permute-start(bf16[32,128,128]{2,1,0:T(8,128)(2,1)} %tie.19.refs_1_), channel_id=1, source_target_pairs={{0,1},{1,0},{2,3},{3,2},{4,5},{5,4},{6,7},{7,6},{8,9},{9,8},{10,11... | collective-permute-start | bytes 3145736 | tf_op jit(solution)/shard_map/ppermute | solution.py:335
  111.6 20.7 %collective-permute-start.14 = (bf16[32,128,128]{2,1,0:T(8,128)(2,1)}, bf16[32,128,128]{2,1,0:T(8,128)(2,1)}, u32[]{:S(2)}, u32[]{:S(2)}) collective-permute-start(bf16[32,128,128]{2,1,0:T(8,128)(2,1)} %tie.18.refs_0_), channel_id=1, source_target_pairs={{0,1},{1,0},{2,3},{3,2},{4,5},{5,4},{6,7},{7,6},{8,9},{9,8},{10,11... | collective-permute-start | bytes 3145736 | tf_op jit(solution)/shard_map/ppermute | solution.py:335
  118.8 13.6 %collective-permute-start.21 = (bf16[32,128,128]{2,1,0:T(8,128)(2,1)}, bf16[32,128,128]{2,1,0:T(8,128)(2,1)}, u32[]{:S(2)}, u32[]{:S(2)}) collective-permute-start(bf16[32,128,128]{2,1,0:T(8,128)(2,1)} %tie.21.refs_3_), channel_id=1, source_target_pairs={{0,1},{1,0},{2,3},{3,2},{4,5},{5,4},{6,7},{7,6},{8,9},{9,8},{10,11... | collective-permute-start | bytes 3145736 | tf_op jit(solution)/shard_map/ppermute | solution.py:335
  129.7 18.6 %collective-permute-start.25 = (bf16[256,2048]{1,0:T(8,128)(2,1)}, bf16[256,2048]{1,0:T(8,128)(2,1)}, u32[]{:S(2)}, u32[]{:S(2)}) collective-permute-start(bf16[256,2048]{1,0:T(8,128)(2,1)} %get-tuple-element.29), channel_id=1, source_target_pairs={{0,4},{1,3},{2,6},{3,1},{4,0},{5,7},{6,2},{7,5},{8,12},{9,11},{10,... | collective-permute-start | bytes 3145736 | tf_op jit(solution)/shard_map/ppermute | solution.py:335
  142.8 15.2 %collective-permute-start.24 = (bf16[256,2048]{1,0:T(8,128)(2,1)}, bf16[256,2048]{1,0:T(8,128)(2,1)}, u32[]{:S(2)}, u32[]{:S(2)}) collective-permute-start(bf16[256,2048]{1,0:T(8,128)(2,1)} %get-tuple-element.28), channel_id=1, source_target_pairs={{0,2},{1,5},{2,0},{3,7},{4,6},{5,1},{6,4},{7,3},{8,10},{9,13},{10,... | collective-permute-start | bytes 3145736 | tf_op jit(solution)/shard_map/ppermute | solution.py:335

commit v7 on v6

--- a/solution.py
+++ b/solution.py
@@ -51,40 +51,40 @@
     )(row, lists, mask.T, integrals, amplitudes)
 
 
-def pick_body(first, capacity, scalars, target_ref, *refs):
-    amps, (mine, theirs) = refs[:-2], refs[-2:]
+def pick_body(first, count, capacity, scalars, target_ref, *refs):
+    amps, (mine, theirs, chosen) = refs[:-3], refs[-3:]
     step = pl.program_id(0)
-    half = pl.num_programs(0) // 2
-    rows = scalars[first + step] * capacity + lax.broadcasted_iota(jnp.int32, (capacity, target_ref.shape[1]), 0)
-    chosen = jnp.where(rows == target_ref[...], 1.0, 0.0).astype(mine.dtype)
+    slot = lax.broadcasted_iota(jnp.int32, (capacity, target_ref.shape[1]), 0)
+    for d in range(count):
+        wanted = scalars[first + step * count + d] * capacity + slot
+        chosen[d * capacity : (d + 1) * capacity] = jnp.where(wanted == target_ref[...], 1.0, 0.0).astype(chosen.dtype)
     for at, amp in enumerate(amps):
-        value = jnp.dot(chosen, amp[...], preferred_element_type=jnp.float32).astype(mine.dtype)
-
-        @pl.when(step < half)
+        value = jnp.dot(chosen[...], amp[...], preferred_element_type=jnp.float32).astype(mine.dtype)
+        value = value.reshape(count, capacity, amp.shape[1])
+
+        @pl.when(step == 0)
         def _():
-            theirs[at, 0] = value
-
-        @pl.when(step >= half)
+            theirs[at] = value
+
+        @pl.when(step == 1)
         def _():
-            mine[at, 0] = value
+            mine[at] = value
 
 
 def pick_rows(scalars, first, count, target, amps, capacity):
     n, k = amps[0].shape
     shape = jax.ShapeDtypeStruct((len(amps), count, capacity, k), amps[0].dtype)
-    block = (len(amps), 1, capacity, k)
+    whole = pl.BlockSpec(shape.shape, lambda i, s: (0, 0, 0, 0))
     return pl.pallas_call(
-        functools.partial(pick_body, first, capacity),
+        functools.partial(pick_body, first, count, capacity),
         out_shape=[shape, shape],
         grid_spec=pltpu.PrefetchScalarGridSpec(
             num_scalar_prefetch=1,
-            grid=(2 * count,),
+            grid=(2,),
             in_specs=[pl.BlockSpec((1, n), lambda i, s: (0, 0))]
             + [pl.BlockSpec((n, k), lambda i, s: (0, 0)) for _ in amps],
-            out_specs=[
-                pl.BlockSpec(block, lambda i, s: (0, jnp.maximum(i - count, 0), 0, 0)),
-                pl.BlockSpec(block, lambda i, s: (0, jnp.minimum(i, count - 1), 0, 0)),
-            ],
+            out_specs=[whole, whole],
+            scratch_shapes=[pltpu.VMEM((count * capacity, n), amps[0].dtype)],
         ),
         compiler_params=params(),
         cost_estimate=NOTHING,
@@ -92,9 +92,19 @@
     )(scalars, target.reshape(1, n), *amps)
 
 
-def product_body(at, has_acc, has_whole, final, scalars, table, mine, theirs, *refs):
-    core_at, picks, rows_at, mine_at, theirs_at = at
+class Numbers:
+    def __init__(self, ref, base):
+        self.ref, self.base = ref, base
+
+    def __getitem__(self, at):
+        width = self.ref.shape[1]
+        return self.ref[self.base + at // width, at % width]
+
+
+def product_body(at, has_acc, has_whole, final, numbers, mine, theirs, *refs):
+    core_at, picks, rows_at, mine_at, theirs_at, tiles, base = at
     slot_count = len(rows_at)
+    scalars = Numbers(numbers, base)
     packed_hbm = refs[:slot_count]
     acc = refs[slot_count] if has_acc else None
     refs = refs[slot_count + has_acc + has_whole :]
@@ -104,7 +114,7 @@
     depth = lhs_all.shape[1] // slot_count
     width = rhs_all.shape[1]
     count = packed.shape[1]
-    col_tiles = table.shape[1] // (depth // TILE)
+    col_tiles = tiles // (depth // TILE)
 
     @pl.when(step == 0)
     def _():
@@ -120,19 +130,24 @@
                     pltpu.make_async_copy(
                         source.at[chip, scalars[pick]], lhs_all.at[pl.ds(t * capacity, capacity), lanes], lhs_sem
                     ).start()
-        for s in range(slot_count):
+    for s in range(slot_count):
+        @pl.when(step == 0)
+        def _():
             pltpu.make_async_copy(packed_hbm[s], packed.at[s], sems.at[s]).wait()
-        pltpu.make_async_copy(lhs_all, lhs_all, lhs_sem).wait()
-
-    for s in range(slot_count):
+
         row = scalars[rows_at[s]]
         for k in range(depth // TILE):
             for n in range(width // TILE):
-                e = table[row, k * col_tiles + step * (width // TILE) + n]
+                e = numbers[row, k * col_tiles + step * (width // TILE) + n]
                 tile = packed[s, jnp.minimum(e, count - 1)]
                 rhs_all[s * depth + k * TILE : s * depth + (k + 1) * TILE, n * TILE : (n + 1) * TILE] = jnp.where(
                     e < count, tile, jnp.zeros_like(tile)
                 )
+
+    @pl.when(step == 0)
+    def _():
+        pltpu.make_async_copy(lhs_all, lhs_all, lhs_sem).wait()
+
     total = jnp.dot(lhs_all[...], rhs_all[...], preferred_element_type=jnp.float32)
     if has_acc:
         total = acc[...] + total
@@ -143,18 +158,18 @@
         outs[t][...] = total[t * capacity : (t + 1) * capacity].astype(outs[t].dtype)
 
 
-def product(scalars, table, mine, theirs, slots, int_cols, at, acc=None, whole_cols=None, whole=None, place_at=None):
-    core_at, picks, rows_at, mine_at, theirs_at = at
+def product(numbers, mine, theirs, slots, int_cols, at, acc=None, whole_cols=None, whole=None, place_at=None):
+    picks, base = at[1], at[-1]
     capacity, part = mine.shape[2:]
     slot_count, m = len(slots), len(picks) * capacity
     depth = 2 * part
     width = min(MM_COLS, int_cols)
     steps = int_cols // width
     hbm = pl.BlockSpec(memory_space=pltpu.HBM)
-    operands = [scalars, table, mine, theirs, *slots]
-    in_specs = [hbm] * (len(operands) - 2)
+    operands = [numbers, mine, theirs, *slots]
+    in_specs = [hbm] * (len(operands) - 1)
     aliases = {}
-    chunk = pl.BlockSpec((m, width), lambda i, sc, tab: (0, i))
+    chunk = pl.BlockSpec((m, width), lambda i, numbers: (0, i))
     if acc is not None:
         in_specs.append(chunk)
         operands.append(acc)
@@ -166,17 +181,17 @@
     out_specs = [chunk]
     out_shape = [jax.ShapeDtypeStruct((m, int_cols), jnp.float32)]
     if final:
-        out_specs = [pl.BlockSpec((capacity, width), lambda i, sc, tab: (0, sc[place_at] * steps + i))]
+        out_specs = [pl.BlockSpec((capacity, width), lambda i, numbers: (0, Numbers(numbers, base)[place_at] * steps + i))]
         out_shape = [jax.ShapeDtypeStruct((capacity, whole_cols), mine.dtype)]
     for _ in picks[1:] if final else ():
-        out_specs.append(pl.BlockSpec((capacity, width), lambda i, sc, tab: (0, i)))
+        out_specs.append(pl.BlockSpec((capacity, width), lambda i, numbers: (0, i)))
         out_shape.append(jax.ShapeDtypeStruct((capacity, int_cols), mine.dtype))
     k = slot_count * depth
     return pl.pallas_call(
         functools.partial(product_body, at, acc is not None, whole is not None, final),
         out_shape=out_shape,
         grid_spec=pltpu.PrefetchScalarGridSpec(
-            num_scalar_prefetch=2,
+            num_scalar_prefetch=1,
             grid=(steps,),
             in_specs=in_specs,
             out_specs=out_specs,
@@ -350,8 +365,9 @@
         for de, da, db in turns:
             consts.add(lambda z, e, a, b, c: col_index((e + de) % extra, a ^ da, b ^ db, c ^ flip))
     slot_rows = [lambda z: z] + [functools.partial(lambda j, z: order[z][j][1], j) for j in range(rows - 1)]
-    rows_at = [consts.add(lambda z, e, a, b, c: row(z)) for row in slot_rows]
-    low_rows_at = [consts.add(lambda z, e, a, b, c: rows + row(z)) for row in slot_rows]
+    rows_at = {
+        q: [consts.add(lambda z, e, a, b, c: q * rows + row(z)) for row in slot_rows] for q in range(4)
+    }
     gathered = [(de, p, q) for de in range(extra) for q in (0, 1) for p in (0, 1)]
 
     def arrival(chip, e, a, b, c):
@@ -408,30 +424,37 @@
     before = jnp.cumsum(onehot, axis=0) - onehot
     target = pair_dest * capacity + jnp.sum(before * onehot, axis=1)
 
-    mine, for_them = pick_rows(scalars, wanted_at, len(turns), target, amps, capacity)
+    table_next = permute(own_table, along)
+    pair_tables = permute(jnp.concatenate([own_table, table_next], axis=0), across)
     sums = None
     slots, nexts, theirs_of, theirs_next = [packed], [permute(packed, along)], [permute(packed, across)], []
+    target = tie(target, pair_tables)
+    mine, for_them = pick_rows(scalars, wanted_at, len(turns), target, amps, capacity)
     for at, moves in enumerate(phases):
         if at > 0:
             fresh = line_phase(moves, packed_again)
         if at == 0:
-            own_table = tie(own_table, amp_next)
-            table_next = permute(own_table, along)
-            pair_tables = permute(jnp.concatenate([own_table, table_next], axis=0), across)
-            waited = (mine, nexts[0], theirs_of[0], pair_tables)
+            width = own_table.shape[1]
+            tail = jnp.pad(scalars, (0, -scalars.shape[0] % width)).reshape(-1, width)
+            numbers = jnp.concatenate([own_table, table_next, pair_tables, tail], axis=0)
+            waited = (mine, nexts[0], theirs_of[0])
             fresh[0] = tie(fresh[0], mine, fresh[1])
         elif at == 1:
             theirs = permute(for_them, across)
-            waited = (theirs, *nexts[1:])
+            waited = (theirs, nexts[-1])
         else:
             waited = (*nexts[-1:], *theirs_of[-1:])
             while len(theirs_next) < len(nexts) - 1:
                 theirs_next.append(permute(nexts[len(theirs_next)], across))
                 waited = (*waited, theirs_next[-1])
         if at == len(phases) - 1:
-            parts = (core_at, picks_at[0], *(places[: rows - 1] for places in (rows_at, mine_at, theirs_at)))
-            (sums,) = product(scalars, own_table, mine, theirs, slots, int_cols, parts)
+            parts = (core_at, picks_at[0], *(places[: rows - 1] for places in (rows_at[0], mine_at, theirs_at)), tiles, 4 * rows)
+            (sums,) = product(numbers, mine, theirs, slots, int_cols, parts)
             waited = (*waited, sums)
+            for j in range(len(theirs_next), len(nexts) - 1):
+                nexts[j] = tie(nexts[j], sums)
+                theirs_next.append(permute(nexts[j], across))
+                waited = (*waited, theirs_next[j])
         tied = []
         for i, value in enumerate(fresh):
             if at > 0 or i > 0:
@@ -453,20 +476,19 @@
     out = None
     arrived = []
     for turn_at, q in enumerate((0, 2, 1, 3)):
-        if turn_at >= 2:
-            out = tie(out, *arrived[turn_at - 2])
-        parts = (core_at, picks_at[q], rows_at if q < 3 else low_rows_at, mine_at, theirs_at)
+        if turn_at == 3:
+            out = tie(out, *arrived[0], *arrived[1])
+        places = (rows_at[q], mine_at, theirs_at)
         blocks = (slots, nexts, theirs_of, theirs_next)[q]
         if q == 0 and rows > 1:
-            blocks, parts = blocks[-1:], (*parts[:2], *(places[-1:] for places in parts[2:]))
+            blocks, places = blocks[-1:], [place[-1:] for place in places]
         out, *pieces = product(
-            scalars,
-            (own_table, table_next, pair_tables, pair_tables)[q],
+            numbers,
             mine,
             theirs,
             blocks,
             int_cols,
-            parts,
+            (core_at, picks_at[q], *places, tiles, 4 * rows),
             acc=sums if q == 0 else None,
             whole_cols=cols * int_cols,
             whole=out,

time: 161 us -> 162 us (level)
  the two profiles are of different devices: /device:TPU:0 before, /device:TPU:16 now
where the time goes in v7:
time: 162 us; the launch traced here: 161 us
  Pallas kernels  81.7 us (50%)
  waiting for transfers between devices  44.3 us (27%)
  starting transfers between devices  24.5 us (15%)
  other arithmetic  7.25 us (4%)
  local copies, waits for them, and re-layouts  2.69 us (2%)
    pallas_call x5, Pallas kernels, product(): pl.pallas_call(functools.partial(product_body, at, acc is not None, whole...  52.4 us
    ppermute x4, waiting for transfers between devices, line_phase(): lax.ppermute(own if source < 0 else moved[source], 'row', pairs)  26.9 us
    ppermute x22, waiting for transfers between devices, permute(): lax.ppermute(value, 'col', [(col_index(*at), col_index(*moved_to(*at))) f...  17.4 us
    ppermute x22, starting transfers between devices, permute(): lax.ppermute(value, 'col', [(col_index(*at), col_index(*moved_to(*at))) f...  15.4 us
    pallas_call x1, Pallas kernels, pick_rows(): pl.pallas_call(functools.partial(pick_body, first, count, capacity), out_...  11.8 us
    pallas_call x4, Pallas kernels, put(): pl.pallas_call(put_body, out_shape=jax.ShapeDtypeStruct(whole.shape, whol...  10.9 us
    ppermute x4, starting transfers between devices, line_phase(): lax.ppermute(own if source < 0 else moved[source], 'row', pairs)  9.15 us
    pallas_call x1, Pallas kernels, pack(): pl.pallas_call(pack_body, out_shape=[jax.ShapeDtypeStruct((count, TILE, T...  3.67 us
  transfers between devices with their start and end apart: 26, of which 7 were waited for; matrix products, arithmetic and copies ran while one was open for 6% of the time, Pallas kernels for 47%

profile of v7, /device:TPU:16, one launch (start us, length us, event | category | flops | bytes accessed | tf_op | source)
XLA Modules:
  0.0 160.6 jit_solution(11503279515046566315)
XLA Ops:
  0.0 3.7 %pack_tiles.1 = (bf16[32,128,128]{2,1,0:T(8,128)(2,1)}, bf16[32,128,128]{2,1,0:T(8,128)(2,1)}, bf16[1024,256]{1,0:T(8,128)(2,1)}) custom-call(s32[1]{0:T(128)} %bitcast.6.row, s32[4,32]{1,0:T(4,128)} %bitcast.31, s32[2,8]{1,0:T(2,128)} %bitcast.33, bf16[512,2048]{1,0:T(8,128)(2,1)} %src_ref.1, bf16[1024,256]{1,0:T(8,128)(2,1)} %amp_ref.1), custom_call_target="tpu_custom_call" | custom-call | tf_op jit(solution)/shard_map/pack_tiles/pallas_call | solution.py:39
  3.7 1.5 collective-permute-start.3
  5.2 1.5 collective-permute-start.2
  6.7 0.3 collective-permute-start.8
  7.0 1.6 collective-permute-start.7
  8.6 0.8 select_reduce_fusion
  9.4 0.6 collective-permute-start
  10.0 0.7 fusion.3
  10.7 2.3 %reduce-window.6 = s32[8,8,128]{2,1,0:T(8,128)S(1)} reduce-window(s32[8,8,128]{2,1,0:T(8,128)S(1)} %fusion.3, s32[]{:T(128)} %constant.20.clone.1), window={size=1x1x128 pad=0_0x0_0x127_0}, to_apply=%region_1.2 | reduce-window | flops 1040384 | bytes 65540 | tf_op jit(solution)/shard_map/reduce-window
  12.9 0.3 slice_reduce_fusion
  13.4 4.2 %collective-permute-done.2.refs_1_ = bf16[1024,256]{1,0:T(8,128)(2,1)} collective-permute-done((bf16[1024,256]{1,0:T(8,128)(2,1)}, bf16[1024,256]{1,0:T(8,128)(2,1)}, u32[]{:S(2)}, u32[]{:S(2)}) %collective-permute-start.2) | collective-permute-done | bytes 524320 | tf_op jit(solution)/shard_map/ppermute | solution.py:350
  17.7 1.5 collective-permute-start.4
  19.2 0.7 fusion.2
  19.9 1.3 multiply_add_fusion.refs_0_
  21.3 1.2 dynamic-slice_bitcast_fusion.scalars
  22.5 0.6 copy-done
  23.1 4.1 %collective-permute-done.4.refs_3_ = bf16[1024,256]{1,0:T(8,128)(2,1)} collective-permute-done((bf16[1024,256]{1,0:T(8,128)(2,1)}, bf16[1024,256]{1,0:T(8,128)(2,1)}, u32[]{:S(2)}, u32[]{:S(2)}) %collective-permute-start.4) | collective-permute-done | bytes 524320 | tf_op jit(solution)/shard_map/ppermute | solution.py:350
  27.2 11.8 %pick_rows.1 = (bf16[4,3,256,256]{3,2,1,0:T(8,128)(2,1)}, bf16[4,3,256,256]{3,2,1,0:T(8,128)(2,1)}) custom-call(s32[48]{0:T(128)} %dynamic-slice_bitcast_fusion.scalars, s32[1,1024]{1,0:T(1,128)} %bitcast.28, bf16[1024,256]{1,0:T(8,128)(2,1)} %get-tuple-element.18.refs_0_, bf16[1024,256]{1,0:T(8,128)(2,1)} %collective-permute-done.2.refs_1_, ...), custom_call_target="tpu_custom_call" | custom-call | tf_op jit(solution)/shard_map/pick_rows/pallas_call | solution.py:78
  39.0 0.4 collective-permute-start.5
  39.5 1.5 collective-permute-start.6
  41.0 10.8 %collective-permute-done.8.refs_2_.refs_0_ = bf16[32,128,128]{2,1,0:T(8,128)(2,1)} collective-permute-done((bf16[32,128,128]{2,1,0:T(8,128)(2,1)}, bf16[32,128,128]{2,1,0:T(8,128)(2,1)}, u32[]{:S(2)}, u32[]{:S(2)}) %collective-permute-start.8) | collective-permute-done | bytes 1048608 | tf_op jit(solution)/shard_map/ppermute | solution.py:408
  51.7 2.0 %collective-permute-done.7.refs_0_ = bf16[32,128,128]{2,1,0:T(8,128)(2,1)} collective-permute-done((bf16[32,128,128]{2,1,0:T(8,128)(2,1)}, bf16[32,128,128]{2,1,0:T(8,128)(2,1)}, u32[]{:S(2)}, u32[]{:S(2)}) %collective-permute-start.7) | collective-permute-done | bytes 1048608 | tf_op jit(solution)/shard_map/ppermute | solution.py:408
  53.7 0.5 collective-permute-start.11
  54.3 0.6 pad_bitcast_fusion
  54.9 1.3 pad_add_fusion.numbers
  56.2 5.3 %collective-permute-start.15 = (bf16[32,128,128]{2,1,0:T(8,128)(2,1)}, bf16[32,128,128]{2,1,0:T(8,128)(2,1)}, u32[]{:S(2)}, u32[]{:S(2)}) collective-permute-start(bf16[32,128,128]{2,1,0:T(8,128)(2,1)} %tie.13.refs_2_.refs_1_), channel_id=1, source_target_pairs={{8,0},{16,24},{9,1},{17,25},{10,2},{18,26},{11,3},{19,27},{12,4},{... | collective-permute-start | bytes 3145736 | tf_op jit(solution)/shard_map/ppermute | solution.py:408
  61.5 1.5 collective-permute-start.13
  63.0 1.9 %collective-permute-start.14 = (bf16[32,128,128]{2,1,0:T(8,128)(2,1)}, bf16[32,128,128]{2,1,0:T(8,128)(2,1)}, u32[]{:S(2)}, u32[]{:S(2)}) collective-permute-start(bf16[32,128,128]{2,1,0:T(8,128)(2,1)} %tie.16), channel_id=1, source_target_pairs={{8,16},{16,8},{9,17},{17,9},{10,18},{18,10},{11,19},{19,11},{12,20... | collective-permute-start | bytes 3145736 | tf_op jit(solution)/shard_map/ppermute | solution.py:408
  64.9 9.8 %product.5.refs_1_.refs_3_ = f32[512,2048]{1,0:T(8,128)} custom-call(s32[17,64]{1,0:T(8,128)} %pad_add_fusion.numbers, bf16[4,3,256,256]{3,2,1,0:T(8,128)(2,1)} %get-tuple-element.19.refs_1_.mine, bf16[4,3,256,256]{3,2,1,0:T(8,128)(2,1)} %collective-permute-done.5.theirs.refs_1_, bf16[32,128,128]{2,1,0:T(8,128)(2,1)} %get-tuple-element.21.refs_0_, ...), custom_call_target="tpu_custom_call" | custom-call | tf_op jit(solution)/shard_map/product/pallas_call | solution.py:190
  74.9 0.5 collective-permute-start.12
  75.4 14.1 %collective-permute-done.14.refs_0_ = bf16[32,128,128]{2,1,0:T(8,128)(2,1)} collective-permute-done((bf16[32,128,128]{2,1,0:T(8,128)(2,1)}, bf16[32,128,128]{2,1,0:T(8,128)(2,1)}, u32[]{:S(2)}, u32[]{:S(2)}) %collective-permute-start.14) | collective-permute-done | bytes 1048608 | tf_op jit(solution)/shard_map/ppermute | solution.py:408
  89.5 0.5 collective-permute-start.19
  90.0 2.9 %choose.1.refs_0_ = bf16[32,128,128]{2,1,0:T(8,128)(2,1)} custom-call(s32[48]{0:T(128)} %dynamic-slice_bitcast_fusion.scalars, bf16[32,128,128]{2,1,0:T(8,128)(2,1)} %tie.17.refs_6_.a_ref, bf16[32,128,128]{2,1,0:T(8,128)(2,1)} %tie.18.b_ref), custom_call_target="tpu_custom_call" | custom-call | tf_op jit(solution)/shard_map/choose/pallas_call | solution.py:244
  93.0 0.6 collective-permute-start.17
  93.6 7.5 %product.6 = (bf16[256,16384]{1,0:T(8,128)(2,1)}, bf16[256,2048]{1,0:T(8,128)(2,1)}) custom-call(s32[17,64]{1,0:T(8,128)} %pad_add_fusion.numbers, bf16[4,3,256,256]{3,2,1,0:T(8,128)(2,1)} %get-tuple-element.19.refs_1_.mine, bf16[4,3,256,256]{3,2,1,0:T(8,128)(2,1)} %collective-permute-done.5.theirs.refs_1_, bf16[32,128,128]{2,1,0:T(8,128)(2,1)} %choose.1.refs_0_, ...), custom_call_target="tpu_custom_call" | custom-call | tf_op jit(solution)/shard_map/product/pallas_call | solution.py:190
  101.1 0.6 collective-permute-start.22
  101.7 11.7 %product.7 = (bf16[256,16384]{1,0:T(8,128)(2,1)}, bf16[256,2048]{1,0:T(8,128)(2,1)}) custom-call(s32[17,64]{1,0:T(8,128)} %pad_add_fusion.numbers, bf16[4,3,256,256]{3,2,1,0:T(8,128)(2,1)} %get-tuple-element.19.refs_1_.mine, bf16[4,3,256,256]{3,2,1,0:T(8,128)(2,1)} %collective-permute-done.5.theirs.refs_1_, ...), custom_call_target="tpu_custom_call", output_to_operand_aliasing={{0}: (7, {})} | custom-call | tf_op jit(solution)/shard_map/product/pallas_call | solution.py:190
  113.4 1.6 collective-permute-start.23
  115.0 0.5 collective-permute-start.21
  115.5 11.7 %product.8 = (bf16[256,16384]{1,0:T(8,128)(2,1)}, bf16[256,2048]{1,0:T(8,128)(2,1)}) custom-call(s32[17,64]{1,0:T(8,128)} %pad_add_fusion.numbers, bf16[4,3,256,256]{3,2,1,0:T(8,128)(2,1)} %get-tuple-element.19.refs_1_.mine, bf16[4,3,256,256]{3,2,1,0:T(8,128)(2,1)} %collective-permute-done.5.theirs.refs_1_, ...), custom_call_target="tpu_custom_call", output_to_operand_aliasing={{0}: (7, {})} | custom-call | tf_op jit(solution)/shard_map/product/pallas_call | solution.py:190
  127.2 1.6 collective-permute-start.25
  128.8 2.3 %collective-permute-done.23.refs_2_.piece_ref = bf16[256,2048]{1,0:T(8,128)(2,1)} collective-permute-done((bf16[256,2048]{1,0:T(8,128)(2,1)}, bf16[256,2048]{1,0:T(8,128)(2,1)}, u32[]{:S(2)}, u32[]{:S(2)}) %collective-permute-start.23) | collective-permute-done | bytes 1048608 | tf_op jit(solution)/shard_map/ppermute | solution.py:350
  131.0 11.7 %product.9 = (bf16[256,16384]{1,0:T(8,128)(2,1)}, bf16[256,2048]{1,0:T(8,128)(2,1)}) custom-call(s32[17,64]{1,0:T(8,128)} %pad_add_fusion.numbers, bf16[4,3,256,256]{3,2,1,0:T(8,128)(2,1)} %get-tuple-element.19.refs_1_.mine, bf16[4,3,256,256]{3,2,1,0:T(8,128)(2,1)} %collective-permute-done.5.theirs.refs_1_, ...), custom_call_target="tpu_custom_call", output_to_operand_aliasing={{0}: (7, {})} | custom-call | tf_op jit(solution)/shard_map/product/pallas_call | solution.py:190
  142.9 2.7 %put.4.whole_ref = bf16[256,16384]{1,0:T(8,128)(2,1)} custom-call(s32[48]{0:T(128)} %dynamic-slice_bitcast_fusion.scalars, bf16[256,2048]{1,0:T(8,128)(2,1)} %collective-permute-done.22.refs_1_.piece_ref, bf16[256,16384]{1,0:T(8,128)(2,1)} %get-tuple-element.30.whole_ref), custom_call_target="tpu_custom_call", output_to_operand_aliasing={{}: (2, {})} | custom-call | tf_op jit(solution)/shard_map/put/pallas_call | solution.py:264
  145.7 2.7 %put.5.whole_ref = bf16[256,16384]{1,0:T(8,128)(2,1)} custom-call(s32[48]{0:T(128)} %dynamic-slice_bitcast_fusion.scalars, bf16[256,2048]{1,0:T(8,128)(2,1)} %collective-permute-done.23.refs_2_.piece_ref, bf16[256,16384]{1,0:T(8,128)(2,1)} %put.4.whole_ref), custom_call_target="tpu_custom_call", output_to_operand_aliasing={{}: (2, {})} | custom-call | tf_op jit(solution)/shard_map/put/pallas_call | solution.py:264
  148.4 2.7 %put.6.whole_ref = bf16[256,16384]{1,0:T(8,128)(2,1)} custom-call(s32[48]{0:T(128)} %dynamic-slice_bitcast_fusion.scalars, bf16[256,2048]{1,0:T(8,128)(2,1)} %collective-permute-done.25.piece_ref, bf16[256,16384]{1,0:T(8,128)(2,1)} %put.5.whole_ref), custom_call_target="tpu_custom_call", output_to_operand_aliasing={{}: (2, {})} | custom-call | tf_op jit(solution)/shard_map/put/pallas_call | solution.py:264
  151.1 6.8 %collective-permute-done.24.piece_ref = bf16[256,2048]{1,0:T(8,128)(2,1)} collective-permute-done((bf16[256,2048]{1,0:T(8,128)(2,1)}, bf16[256,2048]{1,0:T(8,128)(2,1)}, u32[]{:S(2)}, u32[]{:S(2)}) %collective-permute-start.24) | collective-permute-done | bytes 1048608 | tf_op jit(solution)/shard_map/ppermute | solution.py:350
  157.9 2.7 %put.7 = bf16[256,16384]{1,0:T(8,128)(2,1)} custom-call(s32[48]{0:T(128)} %dynamic-slice_bitcast_fusion.scalars, bf16[256,2048]{1,0:T(8,128)(2,1)} %collective-permute-done.24.piece_ref, bf16[256,16384]{1,0:T(8,128)(2,1)} %put.6.whole_ref), custom_call_target="tpu_custom_call", output_to_operand_aliasing={{}: (2, {})} | custom-call | tf_op jit(solution)/shard_map/put/pallas_call | solution.py:264
  (41 shorter events, 0.8 us)
Async XLA Ops:
  3.7 19.4 %collective-permute-start.3 = (bf16[1024,256]{1,0:T(8,128)(2,1)}, bf16[1024,256]{1,0:T(8,128)(2,1)}, u32[]{:S(2)}, u32[]{:S(2)}) collective-permute-start(bf16[1024,256]{1,0:T(8,128)(2,1)} %get-tuple-element.18.refs_0_), channel_id=1, source_target_pairs={{0,4},{1,3},{2,6},{3,1},{4,0},{5,7},{6,2},{7,5},{8,12},{9,11},{10,... | collective-permute-start | bytes 1572872 | tf_op jit(solution)/shard_map/ppermute | solution.py:350
  5.2 12.5 %collective-permute-start.2 = (bf16[1024,256]{1,0:T(8,128)(2,1)}, bf16[1024,256]{1,0:T(8,128)(2,1)}, u32[]{:S(2)}, u32[]{:S(2)}) collective-permute-start(bf16[1024,256]{1,0:T(8,128)(2,1)} %get-tuple-element.18.refs_0_), channel_id=1, source_target_pairs={{0,2},{1,5},{2,0},{3,7},{4,6},{5,1},{6,4},{7,3},{8,10},{9,13},{10,... | collective-permute-start | bytes 1572872 | tf_op jit(solution)/shard_map/ppermute | solution.py:350
  6.7 45.0 %collective-permute-start.8 = (bf16[32,128,128]{2,1,0:T(8,128)(2,1)}, bf16[32,128,128]{2,1,0:T(8,128)(2,1)}, u32[]{:S(2)}, u32[]{:S(2)}) collective-permute-start(bf16[32,128,128]{2,1,0:T(8,128)(2,1)} %get-tuple-element.21.refs_0_), channel_id=1, source_target_pairs={{0,16},{16,0},{8,24},{24,8},{1,17},{17,1},{9,25},{25,9},{2,18},{18... | collective-permute-start | bytes 3145736 | tf_op jit(solution)/shard_map/ppermute | solution.py:408
  7.0 46.7 %collective-permute-start.7 = (bf16[32,128,128]{2,1,0:T(8,128)(2,1)}, bf16[32,128,128]{2,1,0:T(8,128)(2,1)}, u32[]{:S(2)}, u32[]{:S(2)}) collective-permute-start(bf16[32,128,128]{2,1,0:T(8,128)(2,1)} %get-tuple-element.21.refs_0_), channel_id=1, source_target_pairs={{0,8},{8,0},{16,24},{24,16},{1,9},{9,1},{17,25},{25,17},{2,10},{10... | collective-permute-start | bytes 3145736 | tf_op jit(solution)/shard_map/ppermute | solution.py:408
  9.4 11.8 %collective-permute-start = (s32[4,64]{1,0:T(4,128)S(1)}, s32[4,64]{1,0:T(4,128)S(1)}, u32[]{:S(2)}, u32[]{:S(2)}) collective-permute-start(s32[4,64]{1,0:T(4,128)S(1)} %select_reduce_fusion), channel_id=1, source_target_pairs={{0,2},{1,5},{2,0},{3,7},{4,6},{5,1},{6,4},{7,3},{8,10},{9,13},{10,... | collective-permute-start | bytes 3080 | tf_op jit(solution)/shard_map/ppermute | solution.py:350
  17.7 9.5 %collective-permute-start.4 = (bf16[1024,256]{1,0:T(8,128)(2,1)}, bf16[1024,256]{1,0:T(8,128)(2,1)}, u32[]{:S(2)}, u32[]{:S(2)}) collective-permute-start(bf16[1024,256]{1,0:T(8,128)(2,1)} %collective-permute-done.2.refs_1_), channel_id=1, source_target_pairs={{0,4},{1,3},{2,6},{3,1},{4,0},{5,7},{6,2},{7,5},{8,12},{9,11},{10,... | collective-permute-start | bytes 1572872 | tf_op jit(solution)/shard_map/ppermute | solution.py:350
  21.2 1.3 collective-permute-start.1
  22.5 0.6 copy-start
  39.0 26.0 %collective-permute-start.5 = (bf16[4,3,256,256]{3,2,1,0:T(8,128)(2,1)}, bf16[4,3,256,256]{3,2,1,0:T(8,128)(2,1)}, u32[]{:S(2)}, u32[]{:S(2)}) collective-permute-start(bf16[4,3,256,256]{3,2,1,0:T(8,128)(2,1)} %get-tuple-element.20), channel_id=1, source_target_pairs={{0,1},{1,0},{2,3},{3,2},{4,5},{5,4},{6,7},{7,6},{8,9},{9,8},{10,11... | collective-permute-start | bytes 4718600 | tf_op jit(solution)/shard_map/ppermute | solution.py:350
  39.4 16.8 %collective-permute-start.9 = (bf16[32,128,128]{2,1,0:T(8,128)(2,1)}, bf16[32,128,128]{2,1,0:T(8,128)(2,1)}, u32[]{:S(2)}, u32[]{:S(2)}) collective-permute-start(bf16[32,128,128]{2,1,0:T(8,128)(2,1)} %get-tuple-element.21.refs_0_), channel_id=1, source_target_pairs={{0,1},{1,0},{2,3},{3,2},{4,5},{5,4},{6,7},{7,6},{8,9},{9,8},{10,11... | collective-permute-start | bytes 3145736 | tf_op jit(solution)/shard_map/ppermute | solution.py:350
  39.5 16.7 %collective-permute-start.6 = (bf16[32,128,128]{2,1,0:T(8,128)(2,1)}, bf16[32,128,128]{2,1,0:T(8,128)(2,1)}, u32[]{:S(2)}, u32[]{:S(2)}) collective-permute-start(bf16[32,128,128]{2,1,0:T(8,128)(2,1)} %get-tuple-element.21.refs_0_), channel_id=1, source_target_pairs={{0,2},{1,5},{2,0},{3,7},{4,6},{5,1},{6,4},{7,3},{8,10},{9,13},{10,... | collective-permute-start | bytes 3145736 | tf_op jit(solution)/shard_map/ppermute | solution.py:350
  53.7 21.1 %collective-permute-start.11 = (bf16[32,128,128]{2,1,0:T(8,128)(2,1)}, bf16[32,128,128]{2,1,0:T(8,128)(2,1)}, u32[]{:S(2)}, u32[]{:S(2)}) collective-permute-start(bf16[32,128,128]{2,1,0:T(8,128)(2,1)} %tie.12.refs_1_), channel_id=1, source_target_pairs={{0,2},{1,5},{2,0},{3,7},{4,6},{5,1},{6,4},{7,3},{8,10},{9,13},{10,... | collective-permute-start | bytes 3145736 | tf_op jit(solution)/shard_map/ppermute | solution.py:350
  56.2 33.3 %collective-permute-start.15 = (bf16[32,128,128]{2,1,0:T(8,128)(2,1)}, bf16[32,128,128]{2,1,0:T(8,128)(2,1)}, u32[]{:S(2)}, u32[]{:S(2)}) collective-permute-start(bf16[32,128,128]{2,1,0:T(8,128)(2,1)} %tie.13.refs_2_.refs_1_), channel_id=1, source_target_pairs={{8,0},{16,24},{9,1},{17,25},{10,2},{18,26},{11,3},{19,27},{12,4},{... | collective-permute-start | bytes 3145736 | tf_op jit(solution)/shard_map/ppermute | solution.py:408
  61.5 28.4 %collective-permute-start.13 = (bf16[32,128,128]{2,1,0:T(8,128)(2,1)}, bf16[32,128,128]{2,1,0:T(8,128)(2,1)}, u32[]{:S(2)}, u32[]{:S(2)}) collective-permute-start(bf16[32,128,128]{2,1,0:T(8,128)(2,1)} %tie.13.refs_2_.refs_1_), channel_id=1, source_target_pairs={{0,2},{1,5},{2,0},{3,7},{4,6},{5,1},{6,4},{7,3},{8,10},{9,13},{10,... | collective-permute-start | bytes 3145736 | tf_op jit(solution)/shard_map/ppermute | solution.py:350
  63.0 26.4 %collective-permute-start.14 = (bf16[32,128,128]{2,1,0:T(8,128)(2,1)}, bf16[32,128,128]{2,1,0:T(8,128)(2,1)}, u32[]{:S(2)}, u32[]{:S(2)}) collective-permute-start(bf16[32,128,128]{2,1,0:T(8,128)(2,1)} %tie.16), channel_id=1, source_target_pairs={{8,16},{16,8},{9,17},{17,9},{10,18},{18,10},{11,19},{19,11},{12,20... | collective-permute-start | bytes 3145736 | tf_op jit(solution)/shard_map/ppermute | solution.py:408
  74.8 15.2 %collective-permute-start.10 = (bf16[32,128,128]{2,1,0:T(8,128)(2,1)}, bf16[32,128,128]{2,1,0:T(8,128)(2,1)}, u32[]{:S(2)}, u32[]{:S(2)}) collective-permute-start(bf16[32,128,128]{2,1,0:T(8,128)(2,1)} %tie.14.refs_0_), channel_id=1, source_target_pairs={{0,1},{1,0},{2,3},{3,2},{4,5},{5,4},{6,7},{7,6},{8,9},{9,8},{10,11... | collective-permute-start | bytes 3145736 | tf_op jit(solution)/shard_map/ppermute | solution.py:350
  74.9 15.1 %collective-permute-start.12 = (bf16[32,128,128]{2,1,0:T(8,128)(2,1)}, bf16[32,128,128]{2,1,0:T(8,128)(2,1)}, u32[]{:S(2)}, u32[]{:S(2)}) collective-permute-start(bf16[32,128,128]{2,1,0:T(8,128)(2,1)} %tie.15.refs_1_), channel_id=1, source_target_pairs={{0,1},{1,0},{2,3},{3,2},{4,5},{5,4},{6,7},{7,6},{8,9},{9,8},{10,11... | collective-permute-start | bytes 3145736 | tf_op jit(solution)/shard_map/ppermute | solution.py:350
  89.5 12.2 %collective-permute-start.18 = (bf16[32,128,128]{2,1,0:T(8,128)(2,1)}, bf16[32,128,128]{2,1,0:T(8,128)(2,1)}, u32[]{:S(2)}, u32[]{:S(2)}) collective-permute-start(bf16[32,128,128]{2,1,0:T(8,128)(2,1)} %tie.12.refs_1_), channel_id=1, source_target_pairs={{0,1},{1,0},{2,3},{3,2},{4,5},{5,4},{6,7},{7,6},{8,9},{9,8},{10,11... | collective-permute-start | bytes 3145736 | tf_op jit(solution)/shard_map/ppermute | solution.py:350
  89.5 12.2 %collective-permute-start.19 = (bf16[32,128,128]{2,1,0:T(8,128)(2,1)}, bf16[32,128,128]{2,1,0:T(8,128)(2,1)}, u32[]{:S(2)}, u32[]{:S(2)}) collective-permute-start(bf16[32,128,128]{2,1,0:T(8,128)(2,1)} %tie.13.refs_2_.refs_1_), channel_id=1, source_target_pairs={{0,1},{1,0},{2,3},{3,2},{4,5},{5,4},{6,7},{7,6},{8,9},{9,8},{10,11... | collective-permute-start | bytes 3145736 | tf_op jit(solution)/shard_map/ppermute | solution.py:350
  92.9 8.8 %collective-permute-start.20 = (bf16[32,128,128]{2,1,0:T(8,128)(2,1)}, bf16[32,128,128]{2,1,0:T(8,128)(2,1)}, u32[]{:S(2)}, u32[]{:S(2)}) collective-permute-start(bf16[32,128,128]{2,1,0:T(8,128)(2,1)} %choose.1.refs_0_), channel_id=1, source_target_pairs={{0,1},{1,0},{2,3},{3,2},{4,5},{5,4},{6,7},{7,6},{8,9},{9,8},{10,11... | collective-permute-start | bytes 3145736 | tf_op jit(solution)/shard_map/ppermute | solution.py:350
  93.0 22.0 %collective-permute-start.17 = (bf16[32,128,128]{2,1,0:T(8,128)(2,1)}, bf16[32,128,128]{2,1,0:T(8,128)(2,1)}, u32[]{:S(2)}, u32[]{:S(2)}) collective-permute-start(bf16[32,128,128]{2,1,0:T(8,128)(2,1)} %choose.1.refs_0_), channel_id=1, source_target_pairs={{0,2},{1,5},{2,0},{3,7},{4,6},{5,1},{6,4},{7,3},{8,10},{9,13},{10,... | collective-permute-start | bytes 3145736 | tf_op jit(solution)/shard_map/ppermute | solution.py:350
  101.1 27.6 %collective-permute-start.22 = (bf16[256,2048]{1,0:T(8,128)(2,1)}, bf16[256,2048]{1,0:T(8,128)(2,1)}, u32[]{:S(2)}, u32[]{:S(2)}) collective-permute-start(bf16[256,2048]{1,0:T(8,128)(2,1)} %get-tuple-element.23.refs_1_), channel_id=1, source_target_pairs={{0,4},{1,3},{2,6},{3,1},{4,0},{5,7},{6,2},{7,5},{8,12},{9,11},{10,... | collective-permute-start | bytes 3145736 | tf_op jit(solution)/shard_map/ppermute | solution.py:350
  113.4 17.6 %collective-permute-start.23 = (bf16[256,2048]{1,0:T(8,128)(2,1)}, bf16[256,2048]{1,0:T(8,128)(2,1)}, u32[]{:S(2)}, u32[]{:S(2)}) collective-permute-start(bf16[256,2048]{1,0:T(8,128)(2,1)} %get-tuple-element.25.refs_1_), channel_id=1, source_target_pairs={{0,2},{1,5},{2,0},{3,7},{4,6},{5,1},{6,4},{7,3},{8,10},{9,13},{10,... | collective-permute-start | bytes 3145736 | tf_op jit(solution)/shard_map/ppermute | solution.py:350
  114.9 16.1 %collective-permute-start.16 = (bf16[32,128,128]{2,1,0:T(8,128)(2,1)}, bf16[32,128,128]{2,1,0:T(8,128)(2,1)}, u32[]{:S(2)}, u32[]{:S(2)}) collective-permute-start(bf16[32,128,128]{2,1,0:T(8,128)(2,1)} %tie.19.refs_2_), channel_id=1, source_target_pairs={{0,1},{1,0},{2,3},{3,2},{4,5},{5,4},{6,7},{7,6},{8,9},{9,8},{10,11... | collective-permute-start | bytes 3145736 | tf_op jit(solution)/shard_map/ppermute | solution.py:350
  115.0 16.1 %collective-permute-start.21 = (bf16[32,128,128]{2,1,0:T(8,128)(2,1)}, bf16[32,128,128]{2,1,0:T(8,128)(2,1)}, u32[]{:S(2)}, u32[]{:S(2)}) collective-permute-start(bf16[32,128,128]{2,1,0:T(8,128)(2,1)} %tie.20.refs_3_), channel_id=1, source_target_pairs={{0,1},{1,0},{2,3},{3,2},{4,5},{5,4},{6,7},{7,6},{8,9},{9,8},{10,11... | collective-permute-start | bytes 3145736 | tf_op jit(solution)/shard_map/ppermute | solution.py:350
  127.2 21.2 %collective-permute-start.25 = (bf16[256,2048]{1,0:T(8,128)(2,1)}, bf16[256,2048]{1,0:T(8,128)(2,1)}, u32[]{:S(2)}, u32[]{:S(2)}) collective-permute-start(bf16[256,2048]{1,0:T(8,128)(2,1)} %get-tuple-element.29), channel_id=1, source_target_pairs={{0,4},{1,3},{2,6},{3,1},{4,0},{5,7},{6,2},{7,5},{8,12},{9,11},{10,... | collective-permute-start | bytes 3145736 | tf_op jit(solution)/shard_map/ppermute | solution.py:350
  142.7 15.2 %collective-permute-start.24 = (bf16[256,2048]{1,0:T(8,128)(2,1)}, bf16[256,2048]{1,0:T(8,128)(2,1)}, u32[]{:S(2)}, u32[]{:S(2)}) collective-permute-start(bf16[256,2048]{1,0:T(8,128)(2,1)} %get-tuple-element.28), channel_id=1, source_target_pairs={{0,2},{1,5},{2,0},{3,7},{4,6},{5,1},{6,4},{7,3},{8,10},{9,13},{10,... | collective-permute-start | bytes 3145736 | tf_op jit(solution)/shard_map/ppermute | solution.py:350

commit v8 on v7

--- a/solution.py
+++ b/solution.py
@@ -130,11 +130,11 @@
                     pltpu.make_async_copy(
                         source.at[chip, scalars[pick]], lhs_all.at[pl.ds(t * capacity, capacity), lanes], lhs_sem
                     ).start()
+        for s in range(slot_count):
+            pltpu.make_async_copy(packed_hbm[s], packed.at[s], sems.at[s]).wait()
+        pltpu.make_async_copy(lhs_all, lhs_all, lhs_sem).wait()
+
     for s in range(slot_count):
-        @pl.when(step == 0)
-        def _():
-            pltpu.make_async_copy(packed_hbm[s], packed.at[s], sems.at[s]).wait()
-
         row = scalars[rows_at[s]]
         for k in range(depth // TILE):
             for n in range(width // TILE):
@@ -143,11 +143,6 @@
                 rhs_all[s * depth + k * TILE : s * depth + (k + 1) * TILE, n * TILE : (n + 1) * TILE] = jnp.where(
                     e < count, tile, jnp.zeros_like(tile)
                 )
-
-    @pl.when(step == 0)
-    def _():
-        pltpu.make_async_copy(lhs_all, lhs_all, lhs_sem).wait()
-
     total = jnp.dot(lhs_all[...], rhs_all[...], preferred_element_type=jnp.float32)
     if has_acc:
         total = acc[...] + total
@@ -158,7 +153,8 @@
         outs[t][...] = total[t * capacity : (t + 1) * capacity].astype(outs[t].dtype)
 
 
-def product(numbers, mine, theirs, slots, int_cols, at, acc=None, whole_cols=None, whole=None, place_at=None):
+def product(numbers, mine, theirs, slots, int_cols, at, acc=None, whole_cols=None, whole=None, place_at=None,
+            pieces_only=False):
     picks, base = at[1], at[-1]
     capacity, part = mine.shape[2:]
     slot_count, m = len(slots), len(picks) * capacity
@@ -177,13 +173,15 @@
         aliases = {len(operands): 0}
         in_specs.append(hbm)
         operands.append(whole)
-    final = whole_cols is not None
+    final = pieces_only or whole_cols is not None
     out_specs = [chunk]
     out_shape = [jax.ShapeDtypeStruct((m, int_cols), jnp.float32)]
-    if final:
+    if pieces_only:
+        out_specs, out_shape = [], []
+    elif final:
         out_specs = [pl.BlockSpec((capacity, width), lambda i, numbers: (0, Numbers(numbers, base)[place_at] * steps + i))]
         out_shape = [jax.ShapeDtypeStruct((capacity, whole_cols), mine.dtype)]
-    for _ in picks[1:] if final else ():
+    for _ in picks if pieces_only else picks[1:] if final else ():
         out_specs.append(pl.BlockSpec((capacity, width), lambda i, numbers: (0, i)))
         out_shape.append(jax.ShapeDtypeStruct((capacity, int_cols), mine.dtype))
     k = slot_count * depth
@@ -428,15 +426,15 @@
     pair_tables = permute(jnp.concatenate([own_table, table_next], axis=0), across)
     sums = None
     slots, nexts, theirs_of, theirs_next = [packed], [permute(packed, along)], [permute(packed, across)], []
-    target = tie(target, pair_tables)
+    width = own_table.shape[1]
+    tail = jnp.pad(scalars, (0, -scalars.shape[0] % width)).reshape(-1, width)
+    numbers = jnp.concatenate([own_table, table_next, pair_tables, tail], axis=0)
+    target = tie(target, numbers)
     mine, for_them = pick_rows(scalars, wanted_at, len(turns), target, amps, capacity)
     for at, moves in enumerate(phases):
         if at > 0:
             fresh = line_phase(moves, packed_again)
         if at == 0:
-            width = own_table.shape[1]
-            tail = jnp.pad(scalars, (0, -scalars.shape[0] % width)).reshape(-1, width)
-            numbers = jnp.concatenate([own_table, table_next, pair_tables, tail], axis=0)
             waited = (mine, nexts[0], theirs_of[0])
             fresh[0] = tie(fresh[0], mine, fresh[1])
         elif at == 1:
@@ -462,7 +460,7 @@
             tied.append(value)
         moved += tied
         if at == 0:
-            packed_again = tie(packed_again, moved[-1])
+            packed_again = tie(packed_again, fresh[1])
         while len(slots) < rows and all(order[i][len(slots) - 1][0] < len(moved) for i in range(rows)):
             j = len(slots) - 1
             kinds = sorted({order[i][j][0] for i in range(rows)})
@@ -477,23 +475,19 @@
     arrived = []
     for turn_at, q in enumerate((0, 2, 1, 3)):
         if turn_at == 3:
-            out = tie(out, *arrived[0], *arrived[1])
+            theirs_next[-1] = tie(theirs_next[-1], *arrived[0], *arrived[1])
         places = (rows_at[q], mine_at, theirs_at)
         blocks = (slots, nexts, theirs_of, theirs_next)[q]
         if q == 0 and rows > 1:
             blocks, places = blocks[-1:], [place[-1:] for place in places]
-        out, *pieces = product(
-            numbers,
-            mine,
-            theirs,
-            blocks,
-            int_cols,
-            (core_at, picks_at[q], *places, tiles, 4 * rows),
-            acc=sums if q == 0 else None,
-            whole_cols=cols * int_cols,
-            whole=out,
-            place_at=place_at[q],
-        )
+        call = functools.partial(product, numbers, mine, theirs, blocks, int_cols)
+        own = dict(whole_cols=cols * int_cols, whole=out, place_at=place_at[q])
+        if turn_at < 3:
+            out, *pieces = call(
+                (core_at, picks_at[q], *places, tiles, 4 * rows), acc=sums if q == 0 else None, **own
+            )
+        else:
+            pieces = call((core_at, picks_at[q][1:], *places, tiles, 4 * rows), pieces_only=True)
         arrived.append([])
         for (de, turn), piece in zip(hops[1:], pieces):
             def sent_to(e, a, b, c):
@@ -505,6 +499,8 @@
             while len(theirs_next) < rows - (q == 0):
                 nexts[len(theirs_next)] = tie(nexts[len(theirs_next)], pieces[0])
                 theirs_next.append(permute(nexts[len(theirs_next)], across))
+    own["whole"] = tie(out, pieces[0])
+    (out,) = call((core_at, picks_at[q][:1], *places, tiles, 4 * rows), **own)
     for got, q in zip(arrived, (0, 2, 1, 3)):
         for piece, place in zip(got, arrive_at[q]):
             out = put(piece, out, scalars, place)

time: 162 us -> 156 us (0.963)
  the two profiles are of different devices: /device:TPU:16 before, /device:TPU:0 now
where the time goes in v8:
time: 156 us; the launch traced here: 155 us
  Pallas kernels  82.6 us (53%)
  waiting for transfers between devices  39.9 us (26%)
  starting transfers between devices  24.4 us (16%)
  other arithmetic  6.56 us (4%)
    pallas_call x6, Pallas kernels, product(): pl.pallas_call(functools.partial(product_body, at, acc is not None, whole...  53.4 us
    ppermute x4, waiting for transfers between devices, line_phase(): lax.ppermute(own if source < 0 else moved[source], 'row', pairs)  26.3 us
    ppermute x22, starting transfers between devices, permute(): lax.ppermute(value, 'col', [(col_index(*at), col_index(*moved_to(*at))) f...  17.3 us
    ppermute x22, waiting for transfers between devices, permute(): lax.ppermute(value, 'col', [(col_index(*at), col_index(*moved_to(*at))) f...  13.7 us
    pallas_call x1, Pallas kernels, pick_rows(): pl.pallas_call(functools.partial(pick_body, first, count, capacity), out_...  11.8 us
    pallas_call x4, Pallas kernels, put(): pl.pallas_call(put_body, out_shape=jax.ShapeDtypeStruct(whole.shape, whol...  10.9 us
    ppermute x4, starting transfers between devices, line_phase(): lax.ppermute(own if source < 0 else moved[source], 'row', pairs)  7.1 us
    pallas_call x1, Pallas kernels, pack(): pl.pallas_call(pack_body, out_shape=[jax.ShapeDtypeStruct((count, TILE, T...  3.67 us
  transfers between devices with their start and end apart: 26, of which 8 were waited for; matrix products, arithmetic and copies ran while one was open for 5% of the time, Pallas kernels for 49%

profile of v8, /device:TPU:0, one launch (start us, length us, event | category | flops | bytes accessed | tf_op | source)
XLA Modules:
  0.0 154.6 jit_solution(9278853348194544026)
XLA Ops:
  0.0 3.7 %pack_tiles.1 = (bf16[32,128,128]{2,1,0:T(8,128)(2,1)}, bf16[32,128,128]{2,1,0:T(8,128)(2,1)}, bf16[1024,256]{1,0:T(8,128)(2,1)}) custom-call(s32[1]{0:T(128)} %bitcast.6.row, s32[4,32]{1,0:T(4,128)} %bitcast.31, s32[2,8]{1,0:T(2,128)} %bitcast.33, bf16[512,2048]{1,0:T(8,128)(2,1)} %src_ref.1, bf16[1024,256]{1,0:T(8,128)(2,1)} %amp_ref.1), custom_call_target="tpu_custom_call" | custom-call | tf_op jit(solution)/shard_map/pack_tiles/pallas_call | solution.py:39
  3.7 3.0 %collective-permute-start.3 = (bf16[1024,256]{1,0:T(8,128)(2,1)}, bf16[1024,256]{1,0:T(8,128)(2,1)}, u32[]{:S(2)}, u32[]{:S(2)}) collective-permute-start(bf16[1024,256]{1,0:T(8,128)(2,1)} %get-tuple-element.16.refs_0_), channel_id=1, source_target_pairs={{0,4},{1,3},{2,6},{3,1},{4,0},{5,7},{6,2},{7,5},{8,12},{9,11},{10,... | collective-permute-start | bytes 1572872 | tf_op jit(solution)/shard_map/ppermute | solution.py:348
  6.6 1.5 collective-permute-start.2
  8.1 2.6 %collective-permute-start.8 = (bf16[32,128,128]{2,1,0:T(8,128)(2,1)}, bf16[32,128,128]{2,1,0:T(8,128)(2,1)}, u32[]{:S(2)}, u32[]{:S(2)}) collective-permute-start(bf16[32,128,128]{2,1,0:T(8,128)(2,1)} %get-tuple-element.19.refs_0_), channel_id=1, source_target_pairs={{0,16},{16,0},{8,24},{24,8},{1,17},{17,1},{9,25},{25,9},{2,18},{18... | collective-permute-start | bytes 3145736 | tf_op jit(solution)/shard_map/ppermute | solution.py:406
  10.7 1.6 %collective-permute-start.7 = (bf16[32,128,128]{2,1,0:T(8,128)(2,1)}, bf16[32,128,128]{2,1,0:T(8,128)(2,1)}, u32[]{:S(2)}, u32[]{:S(2)}) collective-permute-start(bf16[32,128,128]{2,1,0:T(8,128)(2,1)} %get-tuple-element.19.refs_0_), channel_id=1, source_target_pairs={{0,8},{8,0},{16,24},{24,16},{1,9},{9,1},{17,25},{25,17},{2,10},{10... | collective-permute-start | bytes 3145736 | tf_op jit(solution)/shard_map/ppermute | solution.py:406
  12.3 0.8 select_reduce_fusion
  13.1 0.6 collective-permute-start
  13.7 0.7 fusion.3
  14.4 2.3 %reduce-window.6 = s32[8,8,128]{2,1,0:T(8,128)S(1)} reduce-window(s32[8,8,128]{2,1,0:T(8,128)S(1)} %fusion.3, s32[]{:T(128)} %constant.20.clone.1), window={size=1x1x128 pad=0_0x0_0x127_0}, to_apply=%region_1.2 | reduce-window | flops 1040384 | bytes 65540 | tf_op jit(solution)/shard_map/reduce-window
  16.6 0.3 slice_reduce_fusion
  17.1 0.7 fusion.2
  17.9 1.0 collective-permute-done.2.refs_1_
  18.8 1.8 %collective-permute-start.4 = (bf16[1024,256]{1,0:T(8,128)(2,1)}, bf16[1024,256]{1,0:T(8,128)(2,1)}, u32[]{:S(2)}, u32[]{:S(2)}) collective-permute-start(bf16[1024,256]{1,0:T(8,128)(2,1)} %collective-permute-done.2.refs_1_), channel_id=1, source_target_pairs={{0,4},{1,3},{2,6},{3,1},{4,0},{5,7},{6,2},{7,5},{8,12},{9,11},{10,... | collective-permute-start | bytes 1572872 | tf_op jit(solution)/shard_map/ppermute | solution.py:348
  20.6 1.3 multiply_add_fusion.refs_0_
  21.9 0.7 dynamic-slice_bitcast_fusion.scalars
  22.7 1.1 collective-permute-done.1
  23.8 0.6 pad_add_fusion.refs_1_.numbers
  24.4 3.9 %collective-permute-done.4.refs_3_ = bf16[1024,256]{1,0:T(8,128)(2,1)} collective-permute-done((bf16[1024,256]{1,0:T(8,128)(2,1)}, bf16[1024,256]{1,0:T(8,128)(2,1)}, u32[]{:S(2)}, u32[]{:S(2)}) %collective-permute-start.4) | collective-permute-done | bytes 524320 | tf_op jit(solution)/shard_map/ppermute | solution.py:348
  28.3 11.8 %pick_rows.1 = (bf16[4,3,256,256]{3,2,1,0:T(8,128)(2,1)}, bf16[4,3,256,256]{3,2,1,0:T(8,128)(2,1)}) custom-call(s32[48]{0:T(128)} %copy-done, s32[1,1024]{1,0:T(1,128)} %bitcast.28, bf16[1024,256]{1,0:T(8,128)(2,1)} %get-tuple-element.16.refs_0_, bf16[1024,256]{1,0:T(8,128)(2,1)} %collective-permute-done.2.refs_1_, ...), custom_call_target="tpu_custom_call" | custom-call | tf_op jit(solution)/shard_map/pick_rows/pallas_call | solution.py:78
  40.3 0.4 collective-permute-start.9
  40.7 1.7 %collective-permute-start.6 = (bf16[32,128,128]{2,1,0:T(8,128)(2,1)}, bf16[32,128,128]{2,1,0:T(8,128)(2,1)}, u32[]{:S(2)}, u32[]{:S(2)}) collective-permute-start(bf16[32,128,128]{2,1,0:T(8,128)(2,1)} %get-tuple-element.19.refs_0_), channel_id=1, source_target_pairs={{0,2},{1,5},{2,0},{3,7},{4,6},{5,1},{6,4},{7,3},{8,10},{9,13},{10,... | collective-permute-start | bytes 3145736 | tf_op jit(solution)/shard_map/ppermute | solution.py:348
  42.4 13.9 %collective-permute-done.8.refs_2_.refs_0_.refs_1_ = bf16[32,128,128]{2,1,0:T(8,128)(2,1)} collective-permute-done((bf16[32,128,128]{2,1,0:T(8,128)(2,1)}, bf16[32,128,128]{2,1,0:T(8,128)(2,1)}, u32[]{:S(2)}, u32[]{:S(2)}) %collective-permute-start.8) | collective-permute-done | bytes 1048608 | tf_op jit(solution)/shard_map/ppermute | solution.py:406
  56.3 0.2 collective-permute-done.7.refs_0_
  56.4 0.5 collective-permute-start.11
  57.0 1.6 %collective-permute-start.14 = (bf16[32,128,128]{2,1,0:T(8,128)(2,1)}, bf16[32,128,128]{2,1,0:T(8,128)(2,1)}, u32[]{:S(2)}, u32[]{:S(2)}) collective-permute-start(bf16[32,128,128]{2,1,0:T(8,128)(2,1)} %tie.17), channel_id=1, source_target_pairs={{8,16},{16,8},{9,17},{17,9},{10,18},{18,10},{11,19},{19,11},{12,20... | collective-permute-start | bytes 3145736 | tf_op jit(solution)/shard_map/ppermute | solution.py:406
  58.6 1.3 collective-permute-start.15
  59.9 1.6 %collective-permute-start.13 = (bf16[32,128,128]{2,1,0:T(8,128)(2,1)}, bf16[32,128,128]{2,1,0:T(8,128)(2,1)}, u32[]{:S(2)}, u32[]{:S(2)}) collective-permute-start(bf16[32,128,128]{2,1,0:T(8,128)(2,1)} %tie.14.refs_2_), channel_id=1, source_target_pairs={{0,2},{1,5},{2,0},{3,7},{4,6},{5,1},{6,4},{7,3},{8,10},{9,13},{10,... | collective-permute-start | bytes 3145736 | tf_op jit(solution)/shard_map/ppermute | solution.py:348
  61.5 9.0 %product.6.refs_1_.refs_3_ = f32[512,2048]{1,0:T(8,128)} custom-call(s32[17,64]{1,0:T(8,128)} %pad_add_fusion.refs_1_.numbers, bf16[4,3,256,256]{3,2,1,0:T(8,128)(2,1)} %get-tuple-element.17.refs_1_.mine, bf16[4,3,256,256]{3,2,1,0:T(8,128)(2,1)} %collective-permute-done.5.theirs.refs_1_, bf16[32,128,128]{2,1,0:T(8,128)(2,1)} %get-tuple-element.19.refs_0_, ...), custom_call_target="tpu_custom_call" | custom-call | tf_op jit(solution)/shard_map/product/pallas_call | solution.py:188
  70.6 1.0 collective-permute-done.11.refs_0_
  71.6 0.5 collective-permute-start.18
  72.1 12.2 %collective-permute-done.15.refs_6_.refs_0_ = bf16[32,128,128]{2,1,0:T(8,128)(2,1)} collective-permute-done((bf16[32,128,128]{2,1,0:T(8,128)(2,1)}, bf16[32,128,128]{2,1,0:T(8,128)(2,1)}, u32[]{:S(2)}, u32[]{:S(2)}) %collective-permute-start.15) | collective-permute-done | bytes 1048608 | tf_op jit(solution)/shard_map/ppermute | solution.py:406
  84.3 2.9 %choose.1.refs_0_ = bf16[32,128,128]{2,1,0:T(8,128)(2,1)} custom-call(s32[48]{0:T(128)} %copy-done, bf16[32,128,128]{2,1,0:T(8,128)(2,1)} %tie.18.refs_6_.a_ref, bf16[32,128,128]{2,1,0:T(8,128)(2,1)} %tie.19.b_ref), custom_call_target="tpu_custom_call" | custom-call | tf_op jit(solution)/shard_map/choose/pallas_call | solution.py:242
  87.2 0.6 collective-permute-start.20
  87.8 0.4 collective-permute-start.17
  88.2 7.3 %product.7 = (bf16[256,16384]{1,0:T(8,128)(2,1)}, bf16[256,2048]{1,0:T(8,128)(2,1)}) custom-call(s32[17,64]{1,0:T(8,128)} %pad_add_fusion.refs_1_.numbers, bf16[4,3,256,256]{3,2,1,0:T(8,128)(2,1)} %get-tuple-element.17.refs_1_.mine, bf16[4,3,256,256]{3,2,1,0:T(8,128)(2,1)} %collective-permute-done.5.theirs.refs_1_, bf16[32,128,128]{2,1,0:T(8,128)(2,1)} %choose.1.refs_0_, ...), custom_call_target="tpu_custom_call" | custom-call | tf_op jit(solution)/shard_map/product/pallas_call | solution.py:188
  95.6 1.7 %collective-permute-start.22 = (bf16[256,2048]{1,0:T(8,128)(2,1)}, bf16[256,2048]{1,0:T(8,128)(2,1)}, u32[]{:S(2)}, u32[]{:S(2)}) collective-permute-start(bf16[256,2048]{1,0:T(8,128)(2,1)} %get-tuple-element.21.refs_1_), channel_id=1, source_target_pairs={{0,4},{1,3},{2,6},{3,1},{4,0},{5,7},{6,2},{7,5},{8,12},{9,11},{10,... | collective-permute-start | bytes 3145736 | tf_op jit(solution)/shard_map/ppermute | solution.py:348
  97.3 10.5 %product.8 = (bf16[256,16384]{1,0:T(8,128)(2,1)}, bf16[256,2048]{1,0:T(8,128)(2,1)}) custom-call(s32[17,64]{1,0:T(8,128)} %pad_add_fusion.refs_1_.numbers, bf16[4,3,256,256]{3,2,1,0:T(8,128)(2,1)} %get-tuple-element.17.refs_1_.mine, bf16[4,3,256,256]{3,2,1,0:T(8,128)(2,1)} %collective-permute-done.5.theirs.refs_1_, ...), custom_call_target="tpu_custom_call", output_to_operand_aliasing={{0}: (7, {})} | custom-call | tf_op jit(solution)/shard_map/product/pallas_call | solution.py:188
  107.8 1.6 %collective-permute-start.23 = (bf16[256,2048]{1,0:T(8,128)(2,1)}, bf16[256,2048]{1,0:T(8,128)(2,1)}, u32[]{:S(2)}, u32[]{:S(2)}) collective-permute-start(bf16[256,2048]{1,0:T(8,128)(2,1)} %get-tuple-element.23.refs_1_), channel_id=1, source_target_pairs={{0,2},{1,5},{2,0},{3,7},{4,6},{5,1},{6,4},{7,3},{8,10},{9,13},{10,... | collective-permute-start | bytes 3145736 | tf_op jit(solution)/shard_map/ppermute | solution.py:348
  109.4 10.5 %product.10 = (bf16[256,16384]{1,0:T(8,128)(2,1)}, bf16[256,2048]{1,0:T(8,128)(2,1)}) custom-call(s32[17,64]{1,0:T(8,128)} %pad_add_fusion.refs_1_.numbers, bf16[4,3,256,256]{3,2,1,0:T(8,128)(2,1)} %get-tuple-element.17.refs_1_.mine, bf16[4,3,256,256]{3,2,1,0:T(8,128)(2,1)} %collective-permute-done.5.theirs.refs_1_, ...), custom_call_target="tpu_custom_call", output_to_operand_aliasing={{0}: (7, {})} | custom-call | tf_op jit(solution)/shard_map/product/pallas_call | solution.py:188
  119.9 0.8 collective-permute-start.25
  120.7 6.6 %collective-permute-done.23.refs_2_.piece_ref = bf16[256,2048]{1,0:T(8,128)(2,1)} collective-permute-done((bf16[256,2048]{1,0:T(8,128)(2,1)}, bf16[256,2048]{1,0:T(8,128)(2,1)}, u32[]{:S(2)}, u32[]{:S(2)}) %collective-permute-start.23) | collective-permute-done | bytes 1048608 | tf_op jit(solution)/shard_map/ppermute | solution.py:348
  127.3 8.1 %product.9.refs_1_ = bf16[256,2048]{1,0:T(8,128)(2,1)} custom-call(s32[17,64]{1,0:T(8,128)} %pad_add_fusion.refs_1_.numbers, bf16[4,3,256,256]{3,2,1,0:T(8,128)(2,1)} %get-tuple-element.17.refs_1_.mine, bf16[4,3,256,256]{3,2,1,0:T(8,128)(2,1)} %collective-permute-done.5.theirs.refs_1_, bf16[32,128,128]{2,1,0:T(8,128)(2,1)} %collective-permute-done.10.refs_4_.refs_0_, ...), custom_call_target="tpu_custom_call" | custom-call | tf_op jit(solution)/shard_map/product/pallas_call | solution.py:188
  135.3 0.4 collective-permute-start.24
  135.7 8.0 %product.11.whole_ref = bf16[256,16384]{1,0:T(8,128)(2,1)} custom-call(s32[17,64]{1,0:T(8,128)} %pad_add_fusion.refs_1_.numbers, bf16[4,3,256,256]{3,2,1,0:T(8,128)(2,1)} %get-tuple-element.17.refs_1_.mine, bf16[4,3,256,256]{3,2,1,0:T(8,128)(2,1)} %collective-permute-done.5.theirs.refs_1_, ...), custom_call_target="tpu_custom_call", output_to_operand_aliasing={{}: (7, {})} | custom-call | tf_op jit(solution)/shard_map/product/pallas_call | solution.py:188
  143.8 2.7 %put.4.whole_ref = bf16[256,16384]{1,0:T(8,128)(2,1)} custom-call(s32[48]{0:T(128)} %copy-done, bf16[256,2048]{1,0:T(8,128)(2,1)} %collective-permute-done.22.refs_1_.piece_ref, bf16[256,16384]{1,0:T(8,128)(2,1)} %product.11.whole_ref), custom_call_target="tpu_custom_call", output_to_operand_aliasing={{}: (2, {})} | custom-call | tf_op jit(solution)/shard_map/put/pallas_call | solution.py:262
  146.5 2.7 %put.5.whole_ref = bf16[256,16384]{1,0:T(8,128)(2,1)} custom-call(s32[48]{0:T(128)} %copy-done, bf16[256,2048]{1,0:T(8,128)(2,1)} %collective-permute-done.23.refs_2_.piece_ref, bf16[256,16384]{1,0:T(8,128)(2,1)} %put.4.whole_ref), custom_call_target="tpu_custom_call", output_to_operand_aliasing={{}: (2, {})} | custom-call | tf_op jit(solution)/shard_map/put/pallas_call | solution.py:262
  149.2 2.7 %put.6.whole_ref = bf16[256,16384]{1,0:T(8,128)(2,1)} custom-call(s32[48]{0:T(128)} %copy-done, bf16[256,2048]{1,0:T(8,128)(2,1)} %collective-permute-done.25.piece_ref, bf16[256,16384]{1,0:T(8,128)(2,1)} %put.5.whole_ref), custom_call_target="tpu_custom_call", output_to_operand_aliasing={{}: (2, {})} | custom-call | tf_op jit(solution)/shard_map/put/pallas_call | solution.py:262
  151.9 2.7 %put.7 = bf16[256,16384]{1,0:T(8,128)(2,1)} custom-call(s32[48]{0:T(128)} %copy-done, bf16[256,2048]{1,0:T(8,128)(2,1)} %collective-permute-done.24.piece_ref, bf16[256,16384]{1,0:T(8,128)(2,1)} %put.6.whole_ref), custom_call_target="tpu_custom_call", output_to_operand_aliasing={{}: (2, {})} | custom-call | tf_op jit(solution)/shard_map/put/pallas_call | solution.py:262
  (43 shorter events, 0.7 us)
Async XLA Ops:
  3.7 20.8 %collective-permute-start.3 = (bf16[1024,256]{1,0:T(8,128)(2,1)}, bf16[1024,256]{1,0:T(8,128)(2,1)}, u32[]{:S(2)}, u32[]{:S(2)}) collective-permute-start(bf16[1024,256]{1,0:T(8,128)(2,1)} %get-tuple-element.16.refs_0_), channel_id=1, source_target_pairs={{0,4},{1,3},{2,6},{3,1},{4,0},{5,7},{6,2},{7,5},{8,12},{9,11},{10,... | collective-permute-start | bytes 1572872 | tf_op jit(solution)/shard_map/ppermute | solution.py:348
  6.6 12.2 %collective-permute-start.2 = (bf16[1024,256]{1,0:T(8,128)(2,1)}, bf16[1024,256]{1,0:T(8,128)(2,1)}, u32[]{:S(2)}, u32[]{:S(2)}) collective-permute-start(bf16[1024,256]{1,0:T(8,128)(2,1)} %get-tuple-element.16.refs_0_), channel_id=1, source_target_pairs={{0,2},{1,5},{2,0},{3,7},{4,6},{5,1},{6,4},{7,3},{8,10},{9,13},{10,... | collective-permute-start | bytes 1572872 | tf_op jit(solution)/shard_map/ppermute | solution.py:348
  8.1 48.1 %collective-permute-start.8 = (bf16[32,128,128]{2,1,0:T(8,128)(2,1)}, bf16[32,128,128]{2,1,0:T(8,128)(2,1)}, u32[]{:S(2)}, u32[]{:S(2)}) collective-permute-start(bf16[32,128,128]{2,1,0:T(8,128)(2,1)} %get-tuple-element.19.refs_0_), channel_id=1, source_target_pairs={{0,16},{16,0},{8,24},{24,8},{1,17},{17,1},{9,25},{25,9},{2,18},{18... | collective-permute-start | bytes 3145736 | tf_op jit(solution)/shard_map/ppermute | solution.py:406
  10.7 45.7 %collective-permute-start.7 = (bf16[32,128,128]{2,1,0:T(8,128)(2,1)}, bf16[32,128,128]{2,1,0:T(8,128)(2,1)}, u32[]{:S(2)}, u32[]{:S(2)}) collective-permute-start(bf16[32,128,128]{2,1,0:T(8,128)(2,1)} %get-tuple-element.19.refs_0_), channel_id=1, source_target_pairs={{0,8},{8,0},{16,24},{24,16},{1,9},{9,1},{17,25},{25,17},{2,10},{10... | collective-permute-start | bytes 3145736 | tf_op jit(solution)/shard_map/ppermute | solution.py:406
  13.1 9.5 %collective-permute-start = (s32[4,64]{1,0:T(4,128)S(1)}, s32[4,64]{1,0:T(4,128)S(1)}, u32[]{:S(2)}, u32[]{:S(2)}) collective-permute-start(s32[4,64]{1,0:T(4,128)S(1)} %select_reduce_fusion), channel_id=1, source_target_pairs={{0,2},{1,5},{2,0},{3,7},{4,6},{5,1},{6,4},{7,3},{8,10},{9,13},{10,... | collective-permute-start | bytes 3080 | tf_op jit(solution)/shard_map/ppermute | solution.py:348
  18.8 9.5 %collective-permute-start.4 = (bf16[1024,256]{1,0:T(8,128)(2,1)}, bf16[1024,256]{1,0:T(8,128)(2,1)}, u32[]{:S(2)}, u32[]{:S(2)}) collective-permute-start(bf16[1024,256]{1,0:T(8,128)(2,1)} %collective-permute-done.2.refs_1_), channel_id=1, source_target_pairs={{0,4},{1,3},{2,6},{3,1},{4,0},{5,7},{6,2},{7,5},{8,12},{9,11},{10,... | collective-permute-start | bytes 1572872 | tf_op jit(solution)/shard_map/ppermute | solution.py:348
  22.6 5.8 %copy-start = (s32[48]{0:T(128)}, s32[48]{0:T(128)S(1)}, u32[]{:S(2)}) copy-start(s32[48]{0:T(128)S(1)} %dynamic-slice_bitcast_fusion.scalars) | copy-start | bytes 580
  22.6 1.2 collective-permute-start.1
  40.2 21.3 %collective-permute-start.5 = (bf16[4,3,256,256]{3,2,1,0:T(8,128)(2,1)}, bf16[4,3,256,256]{3,2,1,0:T(8,128)(2,1)}, u32[]{:S(2)}, u32[]{:S(2)}) collective-permute-start(bf16[4,3,256,256]{3,2,1,0:T(8,128)(2,1)} %get-tuple-element.18), channel_id=1, source_target_pairs={{0,1},{1,0},{2,3},{3,2},{4,5},{5,4},{6,7},{7,6},{8,9},{9,8},{10,11... | collective-permute-start | bytes 4718600 | tf_op jit(solution)/shard_map/ppermute | solution.py:348
  40.3 18.3 %collective-permute-start.9 = (bf16[32,128,128]{2,1,0:T(8,128)(2,1)}, bf16[32,128,128]{2,1,0:T(8,128)(2,1)}, u32[]{:S(2)}, u32[]{:S(2)}) collective-permute-start(bf16[32,128,128]{2,1,0:T(8,128)(2,1)} %get-tuple-element.19.refs_0_), channel_id=1, source_target_pairs={{0,1},{1,0},{2,3},{3,2},{4,5},{5,4},{6,7},{7,6},{8,9},{9,8},{10,11... | collective-permute-start | bytes 3145736 | tf_op jit(solution)/shard_map/ppermute | solution.py:348
  40.7 18.0 %collective-permute-start.6 = (bf16[32,128,128]{2,1,0:T(8,128)(2,1)}, bf16[32,128,128]{2,1,0:T(8,128)(2,1)}, u32[]{:S(2)}, u32[]{:S(2)}) collective-permute-start(bf16[32,128,128]{2,1,0:T(8,128)(2,1)} %get-tuple-element.19.refs_0_), channel_id=1, source_target_pairs={{0,2},{1,5},{2,0},{3,7},{4,6},{5,1},{6,4},{7,3},{8,10},{9,13},{10,... | collective-permute-start | bytes 3145736 | tf_op jit(solution)/shard_map/ppermute | solution.py:348
  56.4 15.1 %collective-permute-start.11 = (bf16[32,128,128]{2,1,0:T(8,128)(2,1)}, bf16[32,128,128]{2,1,0:T(8,128)(2,1)}, u32[]{:S(2)}, u32[]{:S(2)}) collective-permute-start(bf16[32,128,128]{2,1,0:T(8,128)(2,1)} %tie.13.refs_1_), channel_id=1, source_target_pairs={{0,2},{1,5},{2,0},{3,7},{4,6},{5,1},{6,4},{7,3},{8,10},{9,13},{10,... | collective-permute-start | bytes 3145736 | tf_op jit(solution)/shard_map/ppermute | solution.py:348
  57.0 14.6 %collective-permute-start.14 = (bf16[32,128,128]{2,1,0:T(8,128)(2,1)}, bf16[32,128,128]{2,1,0:T(8,128)(2,1)}, u32[]{:S(2)}, u32[]{:S(2)}) collective-permute-start(bf16[32,128,128]{2,1,0:T(8,128)(2,1)} %tie.17), channel_id=1, source_target_pairs={{8,16},{16,8},{9,17},{17,9},{10,18},{18,10},{11,19},{19,11},{12,20... | collective-permute-start | bytes 3145736 | tf_op jit(solution)/shard_map/ppermute | solution.py:406
  58.6 25.6 %collective-permute-start.15 = (bf16[32,128,128]{2,1,0:T(8,128)(2,1)}, bf16[32,128,128]{2,1,0:T(8,128)(2,1)}, u32[]{:S(2)}, u32[]{:S(2)}) collective-permute-start(bf16[32,128,128]{2,1,0:T(8,128)(2,1)} %tie.14.refs_2_), channel_id=1, source_target_pairs={{8,0},{16,24},{9,1},{17,25},{10,2},{18,26},{11,3},{19,27},{12,4},{... | collective-permute-start | bytes 3145736 | tf_op jit(solution)/shard_map/ppermute | solution.py:406
  59.9 24.4 %collective-permute-start.13 = (bf16[32,128,128]{2,1,0:T(8,128)(2,1)}, bf16[32,128,128]{2,1,0:T(8,128)(2,1)}, u32[]{:S(2)}, u32[]{:S(2)}) collective-permute-start(bf16[32,128,128]{2,1,0:T(8,128)(2,1)} %tie.14.refs_2_), channel_id=1, source_target_pairs={{0,2},{1,5},{2,0},{3,7},{4,6},{5,1},{6,4},{7,3},{8,10},{9,13},{10,... | collective-permute-start | bytes 3145736 | tf_op jit(solution)/shard_map/ppermute | solution.py:348
  70.5 13.8 %collective-permute-start.10 = (bf16[32,128,128]{2,1,0:T(8,128)(2,1)}, bf16[32,128,128]{2,1,0:T(8,128)(2,1)}, u32[]{:S(2)}, u32[]{:S(2)}) collective-permute-start(bf16[32,128,128]{2,1,0:T(8,128)(2,1)} %tie.15.refs_0_), channel_id=1, source_target_pairs={{0,1},{1,0},{2,3},{3,2},{4,5},{5,4},{6,7},{7,6},{8,9},{9,8},{10,11... | collective-permute-start | bytes 3145736 | tf_op jit(solution)/shard_map/ppermute | solution.py:348
  71.6 12.7 %collective-permute-start.12 = (bf16[32,128,128]{2,1,0:T(8,128)(2,1)}, bf16[32,128,128]{2,1,0:T(8,128)(2,1)}, u32[]{:S(2)}, u32[]{:S(2)}) collective-permute-start(bf16[32,128,128]{2,1,0:T(8,128)(2,1)} %tie.16.refs_1_), channel_id=1, source_target_pairs={{0,1},{1,0},{2,3},{3,2},{4,5},{5,4},{6,7},{7,6},{8,9},{9,8},{10,11... | collective-permute-start | bytes 3145736 | tf_op jit(solution)/shard_map/ppermute | solution.py:348
  71.6 25.7 %collective-permute-start.18 = (bf16[32,128,128]{2,1,0:T(8,128)(2,1)}, bf16[32,128,128]{2,1,0:T(8,128)(2,1)}, u32[]{:S(2)}, u32[]{:S(2)}) collective-permute-start(bf16[32,128,128]{2,1,0:T(8,128)(2,1)} %tie.13.refs_1_), channel_id=1, source_target_pairs={{0,1},{1,0},{2,3},{3,2},{4,5},{5,4},{6,7},{7,6},{8,9},{9,8},{10,11... | collective-permute-start | bytes 3145736 | tf_op jit(solution)/shard_map/ppermute | solution.py:348
  84.3 13.0 %collective-permute-start.19 = (bf16[32,128,128]{2,1,0:T(8,128)(2,1)}, bf16[32,128,128]{2,1,0:T(8,128)(2,1)}, u32[]{:S(2)}, u32[]{:S(2)}) collective-permute-start(bf16[32,128,128]{2,1,0:T(8,128)(2,1)} %tie.14.refs_2_), channel_id=1, source_target_pairs={{0,1},{1,0},{2,3},{3,2},{4,5},{5,4},{6,7},{7,6},{8,9},{9,8},{10,11... | collective-permute-start | bytes 3145736 | tf_op jit(solution)/shard_map/ppermute | solution.py:348
  87.2 10.0 %collective-permute-start.20 = (bf16[32,128,128]{2,1,0:T(8,128)(2,1)}, bf16[32,128,128]{2,1,0:T(8,128)(2,1)}, u32[]{:S(2)}, u32[]{:S(2)}) collective-permute-start(bf16[32,128,128]{2,1,0:T(8,128)(2,1)} %choose.1.refs_0_), channel_id=1, source_target_pairs={{0,1},{1,0},{2,3},{3,2},{4,5},{5,4},{6,7},{7,6},{8,9},{9,8},{10,11... | collective-permute-start | bytes 3145736 | tf_op jit(solution)/shard_map/ppermute | solution.py:348
  87.8 20.0 %collective-permute-start.17 = (bf16[32,128,128]{2,1,0:T(8,128)(2,1)}, bf16[32,128,128]{2,1,0:T(8,128)(2,1)}, u32[]{:S(2)}, u32[]{:S(2)}) collective-permute-start(bf16[32,128,128]{2,1,0:T(8,128)(2,1)} %choose.1.refs_0_), channel_id=1, source_target_pairs={{0,2},{1,5},{2,0},{3,7},{4,6},{5,1},{6,4},{7,3},{8,10},{9,13},{10,... | collective-permute-start | bytes 3145736 | tf_op jit(solution)/shard_map/ppermute | solution.py:348
  95.6 25.1 %collective-permute-start.22 = (bf16[256,2048]{1,0:T(8,128)(2,1)}, bf16[256,2048]{1,0:T(8,128)(2,1)}, u32[]{:S(2)}, u32[]{:S(2)}) collective-permute-start(bf16[256,2048]{1,0:T(8,128)(2,1)} %get-tuple-element.21.refs_1_), channel_id=1, source_target_pairs={{0,4},{1,3},{2,6},{3,1},{4,0},{5,7},{6,2},{7,5},{8,12},{9,11},{10,... | collective-permute-start | bytes 3145736 | tf_op jit(solution)/shard_map/ppermute | solution.py:348
  107.8 12.9 %collective-permute-start.21 = (bf16[32,128,128]{2,1,0:T(8,128)(2,1)}, bf16[32,128,128]{2,1,0:T(8,128)(2,1)}, u32[]{:S(2)}, u32[]{:S(2)}) collective-permute-start(bf16[32,128,128]{2,1,0:T(8,128)(2,1)} %tie.21.refs_3_), channel_id=1, source_target_pairs={{0,1},{1,0},{2,3},{3,2},{4,5},{5,4},{6,7},{7,6},{8,9},{9,8},{10,11... | collective-permute-start | bytes 3145736 | tf_op jit(solution)/shard_map/ppermute | solution.py:348
  107.8 19.4 %collective-permute-start.23 = (bf16[256,2048]{1,0:T(8,128)(2,1)}, bf16[256,2048]{1,0:T(8,128)(2,1)}, u32[]{:S(2)}, u32[]{:S(2)}) collective-permute-start(bf16[256,2048]{1,0:T(8,128)(2,1)} %get-tuple-element.23.refs_1_), channel_id=1, source_target_pairs={{0,2},{1,5},{2,0},{3,7},{4,6},{5,1},{6,4},{7,3},{8,10},{9,13},{10,... | collective-permute-start | bytes 3145736 | tf_op jit(solution)/shard_map/ppermute | solution.py:348
  109.4 17.9 %collective-permute-start.16 = (bf16[32,128,128]{2,1,0:T(8,128)(2,1)}, bf16[32,128,128]{2,1,0:T(8,128)(2,1)}, u32[]{:S(2)}, u32[]{:S(2)}) collective-permute-start(bf16[32,128,128]{2,1,0:T(8,128)(2,1)} %tie.20.refs_2_), channel_id=1, source_target_pairs={{0,1},{1,0},{2,3},{3,2},{4,5},{5,4},{6,7},{7,6},{8,9},{9,8},{10,11... | collective-permute-start | bytes 3145736 | tf_op jit(solution)/shard_map/ppermute | solution.py:348
  119.9 29.3 %collective-permute-start.25 = (bf16[256,2048]{1,0:T(8,128)(2,1)}, bf16[256,2048]{1,0:T(8,128)(2,1)}, u32[]{:S(2)}, u32[]{:S(2)}) collective-permute-start(bf16[256,2048]{1,0:T(8,128)(2,1)} %get-tuple-element.25), channel_id=1, source_target_pairs={{0,4},{1,3},{2,6},{3,1},{4,0},{5,7},{6,2},{7,5},{8,12},{9,11},{10,... | collective-permute-start | bytes 3145736 | tf_op jit(solution)/shard_map/ppermute | solution.py:348
  135.3 16.6 %collective-permute-start.24 = (bf16[256,2048]{1,0:T(8,128)(2,1)}, bf16[256,2048]{1,0:T(8,128)(2,1)}, u32[]{:S(2)}, u32[]{:S(2)}) collective-permute-start(bf16[256,2048]{1,0:T(8,128)(2,1)} %product.9.refs_1_), channel_id=1, source_target_pairs={{0,2},{1,5},{2,0},{3,7},{4,6},{5,1},{6,4},{7,3},{8,10},{9,13},{10,... | collective-permute-start | bytes 3145736 | tf_op jit(solution)/shard_map/ppermute | solution.py:348

commit v9 on v7

--- a/solution.py
+++ b/solution.py
@@ -130,11 +130,11 @@
                     pltpu.make_async_copy(
                         source.at[chip, scalars[pick]], lhs_all.at[pl.ds(t * capacity, capacity), lanes], lhs_sem
                     ).start()
+        for s in range(slot_count):
+            pltpu.make_async_copy(packed_hbm[s], packed.at[s], sems.at[s]).wait()
+        pltpu.make_async_copy(lhs_all, lhs_all, lhs_sem).wait()
+
     for s in range(slot_count):
-        @pl.when(step == 0)
-        def _():
-            pltpu.make_async_copy(packed_hbm[s], packed.at[s], sems.at[s]).wait()
-
         row = scalars[rows_at[s]]
         for k in range(depth // TILE):
             for n in range(width // TILE):
@@ -143,11 +143,6 @@
                 rhs_all[s * depth + k * TILE : s * depth + (k + 1) * TILE, n * TILE : (n + 1) * TILE] = jnp.where(
                     e < count, tile, jnp.zeros_like(tile)
                 )
-
-    @pl.when(step == 0)
-    def _():
-        pltpu.make_async_copy(lhs_all, lhs_all, lhs_sem).wait()
-
     total = jnp.dot(lhs_all[...], rhs_all[...], preferred_element_type=jnp.float32)
     if has_acc:
         total = acc[...] + total
@@ -408,36 +403,36 @@
         return [lax.ppermute(own if source < 0 else moved[source], "row", pairs) for source, pairs in moves]
 
     fresh = line_phase(phases[0], packed)
+    count = own_lists.shape[1]
+    tiles = (int_rows // TILE) * (int_cols // TILE)
+    found = own_lists[:, None, :] == jnp.arange(tiles, dtype=jnp.int32)[None, :, None]
+    own_table = jnp.min(jnp.where(found, jnp.arange(count, dtype=jnp.int32), count), axis=2)
+
+    col_ids = jnp.arange(cols, dtype=jnp.int32)
+    onehot = (pair_dest[:, None] == col_ids[None, :]).astype(jnp.int32)
+    before = jnp.cumsum(onehot, axis=0) - onehot
+    target = pair_dest * capacity + jnp.sum(before * onehot, axis=1)
+
+    table_next = permute(own_table, along)
+    amp_used = tie(amp_used, table_next)
     amp_next = permute(amp_used, along)
     amp_other = permute(amp_used, other)
     amps = [amp_used, amp_next, amp_other, permute(amp_next, other)]
     for de in range(1, extra):
         amps += [permute(amp, lambda e, a, b, c: ((e - de) % extra, a, b, c)) for amp in amps[:4]]
-
-    count = own_lists.shape[1]
-    tiles = (int_rows // TILE) * (int_cols // TILE)
-    found = own_lists[:, None, :] == jnp.arange(tiles, dtype=jnp.int32)[None, :, None]
-    own_table = jnp.min(jnp.where(found, jnp.arange(count, dtype=jnp.int32), count), axis=2)
-
-    col_ids = jnp.arange(cols, dtype=jnp.int32)
-    onehot = (pair_dest[:, None] == col_ids[None, :]).astype(jnp.int32)
-    before = jnp.cumsum(onehot, axis=0) - onehot
-    target = pair_dest * capacity + jnp.sum(before * onehot, axis=1)
-
-    table_next = permute(own_table, along)
     pair_tables = permute(jnp.concatenate([own_table, table_next], axis=0), across)
     sums = None
     slots, nexts, theirs_of, theirs_next = [packed], [permute(packed, along)], [permute(packed, across)], []
-    target = tie(target, pair_tables)
+    width = own_table.shape[1]
+    tail = jnp.pad(scalars, (0, -scalars.shape[0] % width)).reshape(-1, width)
+    numbers = jnp.concatenate([own_table, table_next, pair_tables, tail], axis=0)
+    target = tie(target, numbers)
     mine, for_them = pick_rows(scalars, wanted_at, len(turns), target, amps, capacity)
     for at, moves in enumerate(phases):
         if at > 0:
             fresh = line_phase(moves, packed_again)
         if at == 0:
-            width = own_table.shape[1]
-            tail = jnp.pad(scalars, (0, -scalars.shape[0] % width)).reshape(-1, width)
-            numbers = jnp.concatenate([own_table, table_next, pair_tables, tail], axis=0)
-            waited = (mine, nexts[0], theirs_of[0])
+            waited = (mine, theirs_of[0])
             fresh[0] = tie(fresh[0], mine, fresh[1])
         elif at == 1:
             theirs = permute(for_them, across)
@@ -462,7 +457,7 @@
             tied.append(value)
         moved += tied
         if at == 0:
-            packed_again = tie(packed_again, moved[-1])
+            packed_again = tie(packed_again, fresh[1])
         while len(slots) < rows and all(order[i][len(slots) - 1][0] < len(moved) for i in range(rows)):
             j = len(slots) - 1
             kinds = sorted({order[i][j][0] for i in range(rows)})
@@ -477,7 +472,9 @@
     arrived = []
     for turn_at, q in enumerate((0, 2, 1, 3)):
         if turn_at == 3:
-            out = tie(out, *arrived[0], *arrived[1])
+            for piece, place in zip(arrived[0], arrive_at[0]):
+                out = put(piece, out, scalars, place)
+            out = tie(out, *arrived[1])
         places = (rows_at[q], mine_at, theirs_at)
         blocks = (slots, nexts, theirs_of, theirs_next)[q]
         if q == 0 and rows > 1:
@@ -505,7 +502,7 @@
             while len(theirs_next) < rows - (q == 0):
                 nexts[len(theirs_next)] = tie(nexts[len(theirs_next)], pieces[0])
                 theirs_next.append(permute(nexts[len(theirs_next)], across))
-    for got, q in zip(arrived, (0, 2, 1, 3)):
+    for got, q in zip(arrived[1:], (2, 1, 3)):
         for piece, place in zip(got, arrive_at[q]):
             out = put(piece, out, scalars, place)
     return out

time: 162 us -> 161 us (level)
  the two profiles are of different devices: /device:TPU:16 before, /device:TPU:0 now
where the time goes in v9:
time: 161 us; the launch traced here: 160 us
  Pallas kernels  76.9 us (48%)
  waiting for transfers between devices  52.1 us (32%)
  starting transfers between devices  21.8 us (14%)
  other arithmetic  7.91 us (5%)
    pallas_call x5, Pallas kernels, product(): pl.pallas_call(functools.partial(product_body, at, acc is not None, whole...  47.7 us
    ppermute x22, waiting for transfers between devices, permute(): lax.ppermute(value, 'col', [(col_index(*at), col_index(*moved_to(*at))) f...  44.6 us
    ppermute x22, starting transfers between devices, permute(): lax.ppermute(value, 'col', [(col_index(*at), col_index(*moved_to(*at))) f...  13.3 us
    pallas_call x1, Pallas kernels, pick_rows(): pl.pallas_call(functools.partial(pick_body, first, count, capacity), out_...  11.8 us
    pallas_call x4, Pallas kernels, put(): pl.pallas_call(put_body, out_shape=jax.ShapeDtypeStruct(whole.shape, whol...  10.9 us
    ppermute x4, starting transfers between devices, line_phase(): lax.ppermute(own if source < 0 else moved[source], 'row', pairs)  8.53 us
    ppermute x4, waiting for transfers between devices, line_phase(): lax.ppermute(own if source < 0 else moved[source], 'row', pairs)  7.42 us
    pallas_call x1, Pallas kernels, pack(): pl.pallas_call(pack_body, out_shape=[jax.ShapeDtypeStruct((count, TILE, T...  3.65 us
  transfers between devices with their start and end apart: 26, of which 10 were waited for; matrix products, arithmetic and copies ran while one was open for 6% of the time, Pallas kernels for 44%

profile of v9, /device:TPU:0, one launch (start us, length us, event | category | flops | bytes accessed | tf_op | source)
XLA Modules:
  0.0 160.4 jit_solution(17968441582222093186)
XLA Ops:
  0.0 3.6 %pack_tiles.1 = (bf16[32,128,128]{2,1,0:T(8,128)(2,1)}, bf16[32,128,128]{2,1,0:T(8,128)(2,1)}, bf16[1024,256]{1,0:T(8,128)(2,1)}) custom-call(s32[1]{0:T(128)} %bitcast.6.row, s32[4,32]{1,0:T(4,128)} %bitcast.31, s32[2,8]{1,0:T(2,128)} %bitcast.33, bf16[512,2048]{1,0:T(8,128)(2,1)} %src_ref.1, bf16[1024,256]{1,0:T(8,128)(2,1)} %amp_ref.1), custom_call_target="tpu_custom_call" | custom-call | tf_op jit(solution)/shard_map/pack_tiles/pallas_call | solution.py:39
  3.7 4.0 %collective-permute-start.8 = (bf16[32,128,128]{2,1,0:T(8,128)(2,1)}, bf16[32,128,128]{2,1,0:T(8,128)(2,1)}, u32[]{:S(2)}, u32[]{:S(2)}) collective-permute-start(bf16[32,128,128]{2,1,0:T(8,128)(2,1)} %get-tuple-element.21.refs_0_), channel_id=1, source_target_pairs={{0,16},{16,0},{8,24},{24,8},{1,17},{17,1},{9,25},{25,9},{2,18},{18... | collective-permute-start | bytes 3145736 | tf_op jit(solution)/shard_map/ppermute | solution.py:403
  7.7 1.6 collective-permute-start.7
  9.3 0.8 select_reduce_fusion
  10.0 1.6 collective-permute-start
  11.6 0.7 fusion.3
  12.3 2.3 %reduce-window.6 = s32[8,8,128]{2,1,0:T(8,128)S(1)} reduce-window(s32[8,8,128]{2,1,0:T(8,128)S(1)} %fusion.3, s32[]{:T(128)} %constant.20.clone.1), window={size=1x1x128 pad=0_0x0_0x127_0}, to_apply=%region_1.2 | reduce-window | flops 1040384 | bytes 65540 | tf_op jit(solution)/shard_map/reduce-window
  14.6 0.6 copy-done.1
  15.1 0.6 collective-permute-start.2
  15.8 0.3 slice_reduce_fusion
  16.2 0.7 dynamic-slice_bitcast_fusion.scalars
  17.0 0.7 fusion.2
  17.7 1.6 collective-permute-start.3
  19.3 10.7 %collective-permute-done.2.refs_1_ = bf16[1024,256]{1,0:T(8,128)(2,1)} collective-permute-done((bf16[1024,256]{1,0:T(8,128)(2,1)}, bf16[1024,256]{1,0:T(8,128)(2,1)}, u32[]{:S(2)}, u32[]{:S(2)}) %collective-permute-start.2) | collective-permute-done | bytes 524320 | tf_op jit(solution)/shard_map/ppermute | solution.py:345
  30.0 1.5 collective-permute-start.4
  31.5 1.3 multiply_add_fusion.refs_0_
  32.8 0.7 pad_add_fusion.1
  33.5 1.2 collective-permute-done.1
  34.6 1.3 pad_add_fusion.refs_1_.numbers
  35.9 3.5 %collective-permute-done.4.refs_3_ = bf16[1024,256]{1,0:T(8,128)(2,1)} collective-permute-done((bf16[1024,256]{1,0:T(8,128)(2,1)}, bf16[1024,256]{1,0:T(8,128)(2,1)}, u32[]{:S(2)}, u32[]{:S(2)}) %collective-permute-start.4) | collective-permute-done | bytes 524320 | tf_op jit(solution)/shard_map/ppermute | solution.py:345
  39.5 11.8 %pick_rows.1 = (bf16[4,3,256,256]{3,2,1,0:T(8,128)(2,1)}, bf16[4,3,256,256]{3,2,1,0:T(8,128)(2,1)}) custom-call(s32[48]{0:T(128)} %copy-done, s32[1,1024]{1,0:T(1,128)} %bitcast.28, bf16[1024,256]{1,0:T(8,128)(2,1)} %tie.13.refs_0_, bf16[1024,256]{1,0:T(8,128)(2,1)} %collective-permute-done.2.refs_1_, bf16[1024,256]{1,0:T(8,128)(2,1)} %collective-permute-done.3.refs_2_, ...), custom_call_target="tpu_custom_call" | custom-call | tf_op jit(solution)/shard_map/pick_rows/pallas_call | solution.py:78
  51.3 0.5 collective-permute-start.9
  51.8 2.0 %collective-permute-done.8.refs_2_.refs_0_.refs_1_ = bf16[32,128,128]{2,1,0:T(8,128)(2,1)} collective-permute-done((bf16[32,128,128]{2,1,0:T(8,128)(2,1)}, bf16[32,128,128]{2,1,0:T(8,128)(2,1)}, u32[]{:S(2)}, u32[]{:S(2)}) %collective-permute-start.8) | collective-permute-done | bytes 1048608 | tf_op jit(solution)/shard_map/ppermute | solution.py:403
  53.9 1.5 collective-permute-start.11
  55.5 1.6 %collective-permute-start.14 = (bf16[32,128,128]{2,1,0:T(8,128)(2,1)}, bf16[32,128,128]{2,1,0:T(8,128)(2,1)}, u32[]{:S(2)}, u32[]{:S(2)}) collective-permute-start(bf16[32,128,128]{2,1,0:T(8,128)(2,1)} %tie.18), channel_id=1, source_target_pairs={{8,16},{16,8},{9,17},{17,9},{10,18},{18,10},{11,19},{19,11},{12,20... | collective-permute-start | bytes 3145736 | tf_op jit(solution)/shard_map/ppermute | solution.py:403
  57.1 1.3 collective-permute-start.15
  58.4 0.5 collective-permute-start.13
  59.0 8.9 %product.5.refs_1_.refs_3_ = f32[512,2048]{1,0:T(8,128)} custom-call(s32[17,64]{1,0:T(8,128)} %pad_add_fusion.refs_1_.numbers, bf16[4,3,256,256]{3,2,1,0:T(8,128)(2,1)} %get-tuple-element.19.refs_1_.mine, bf16[4,3,256,256]{3,2,1,0:T(8,128)(2,1)} %collective-permute-done.5.theirs.refs_1_, bf16[32,128,128]{2,1,0:T(8,128)(2,1)} %get-tuple-element.21.refs_0_, ...), custom_call_target="tpu_custom_call" | custom-call | tf_op jit(solution)/shard_map/product/pallas_call | solution.py:185
  67.9 0.4 collective-permute-start.10
  68.3 9.9 %collective-permute-done.11.refs_0_ = bf16[32,128,128]{2,1,0:T(8,128)(2,1)} collective-permute-done((bf16[32,128,128]{2,1,0:T(8,128)(2,1)}, bf16[32,128,128]{2,1,0:T(8,128)(2,1)}, u32[]{:S(2)}, u32[]{:S(2)}) %collective-permute-start.11) | collective-permute-done | bytes 1048608 | tf_op jit(solution)/shard_map/ppermute | solution.py:345
  78.1 0.5 collective-permute-start.19
  78.6 5.3 %collective-permute-done.15.refs_6_.refs_0_ = bf16[32,128,128]{2,1,0:T(8,128)(2,1)} collective-permute-done((bf16[32,128,128]{2,1,0:T(8,128)(2,1)}, bf16[32,128,128]{2,1,0:T(8,128)(2,1)}, u32[]{:S(2)}, u32[]{:S(2)}) %collective-permute-start.15) | collective-permute-done | bytes 1048608 | tf_op jit(solution)/shard_map/ppermute | solution.py:403
  83.9 5.4 %collective-permute-done.13.refs_2_.refs_0_ = bf16[32,128,128]{2,1,0:T(8,128)(2,1)} collective-permute-done((bf16[32,128,128]{2,1,0:T(8,128)(2,1)}, bf16[32,128,128]{2,1,0:T(8,128)(2,1)}, u32[]{:S(2)}, u32[]{:S(2)}) %collective-permute-start.13) | collective-permute-done | bytes 1048608 | tf_op jit(solution)/shard_map/ppermute | solution.py:345
  89.4 2.9 %choose.1.refs_0_ = bf16[32,128,128]{2,1,0:T(8,128)(2,1)} custom-call(s32[48]{0:T(128)} %copy-done, bf16[32,128,128]{2,1,0:T(8,128)(2,1)} %tie.19.refs_6_.a_ref, bf16[32,128,128]{2,1,0:T(8,128)(2,1)} %tie.20.b_ref), custom_call_target="tpu_custom_call" | custom-call | tf_op jit(solution)/shard_map/choose/pallas_call | solution.py:239
  92.4 7.4 %product.6 = (bf16[256,16384]{1,0:T(8,128)(2,1)}, bf16[256,2048]{1,0:T(8,128)(2,1)}) custom-call(s32[17,64]{1,0:T(8,128)} %pad_add_fusion.refs_1_.numbers, bf16[4,3,256,256]{3,2,1,0:T(8,128)(2,1)} %get-tuple-element.19.refs_1_.mine, bf16[4,3,256,256]{3,2,1,0:T(8,128)(2,1)} %collective-permute-done.5.theirs.refs_1_, bf16[32,128,128]{2,1,0:T(8,128)(2,1)} %choose.1.refs_0_, ...), custom_call_target="tpu_custom_call" | custom-call | tf_op jit(solution)/shard_map/product/pallas_call | solution.py:185
  99.8 1.6 collective-permute-start.22
  101.4 0.2 collective-permute-start.16
  101.6 10.5 %product.7 = (bf16[256,16384]{1,0:T(8,128)(2,1)}, bf16[256,2048]{1,0:T(8,128)(2,1)}) custom-call(s32[17,64]{1,0:T(8,128)} %pad_add_fusion.refs_1_.numbers, bf16[4,3,256,256]{3,2,1,0:T(8,128)(2,1)} %get-tuple-element.19.refs_1_.mine, bf16[4,3,256,256]{3,2,1,0:T(8,128)(2,1)} %collective-permute-done.5.theirs.refs_1_, ...), custom_call_target="tpu_custom_call", output_to_operand_aliasing={{0}: (7, {})} | custom-call | tf_op jit(solution)/shard_map/product/pallas_call | solution.py:185
  112.1 1.9 %collective-permute-start.23 = (bf16[256,2048]{1,0:T(8,128)(2,1)}, bf16[256,2048]{1,0:T(8,128)(2,1)}, u32[]{:S(2)}, u32[]{:S(2)}) collective-permute-start(bf16[256,2048]{1,0:T(8,128)(2,1)} %get-tuple-element.25.refs_1_), channel_id=1, source_target_pairs={{0,2},{1,5},{2,0},{3,7},{4,6},{5,1},{6,4},{7,3},{8,10},{9,13},{10,... | collective-permute-start | bytes 3145736 | tf_op jit(solution)/shard_map/ppermute | solution.py:345
  114.0 10.5 %product.8 = (bf16[256,16384]{1,0:T(8,128)(2,1)}, bf16[256,2048]{1,0:T(8,128)(2,1)}) custom-call(s32[17,64]{1,0:T(8,128)} %pad_add_fusion.refs_1_.numbers, bf16[4,3,256,256]{3,2,1,0:T(8,128)(2,1)} %get-tuple-element.19.refs_1_.mine, bf16[4,3,256,256]{3,2,1,0:T(8,128)(2,1)} %collective-permute-done.5.theirs.refs_1_, ...), custom_call_target="tpu_custom_call", output_to_operand_aliasing={{0}: (7, {})} | custom-call | tf_op jit(solution)/shard_map/product/pallas_call | solution.py:185
  124.5 0.6 collective-permute-start.25
  125.0 2.7 %put.4.refs_0_ = bf16[256,16384]{1,0:T(8,128)(2,1)} custom-call(s32[48]{0:T(128)} %copy-done, bf16[256,2048]{1,0:T(8,128)(2,1)} %collective-permute-done.22.piece_ref, bf16[256,16384]{1,0:T(8,128)(2,1)} %get-tuple-element.27.whole_ref), custom_call_target="tpu_custom_call", output_to_operand_aliasing={{}: (2, {})} | custom-call | tf_op jit(solution)/shard_map/put/pallas_call | solution.py:259
  127.8 4.2 %collective-permute-done.23.refs_1_.piece_ref = bf16[256,2048]{1,0:T(8,128)(2,1)} collective-permute-done((bf16[256,2048]{1,0:T(8,128)(2,1)}, bf16[256,2048]{1,0:T(8,128)(2,1)}, u32[]{:S(2)}, u32[]{:S(2)}) %collective-permute-start.23) | collective-permute-done | bytes 1048608 | tf_op jit(solution)/shard_map/ppermute | solution.py:345
  132.0 10.5 %product.9 = (bf16[256,16384]{1,0:T(8,128)(2,1)}, bf16[256,2048]{1,0:T(8,128)(2,1)}) custom-call(s32[17,64]{1,0:T(8,128)} %pad_add_fusion.refs_1_.numbers, bf16[4,3,256,256]{3,2,1,0:T(8,128)(2,1)} %get-tuple-element.19.refs_1_.mine, bf16[4,3,256,256]{3,2,1,0:T(8,128)(2,1)} %collective-permute-done.5.theirs.refs_1_, ...), custom_call_target="tpu_custom_call", output_to_operand_aliasing={{0}: (7, {})} | custom-call | tf_op jit(solution)/shard_map/product/pallas_call | solution.py:185
  142.6 2.7 %put.5.whole_ref = bf16[256,16384]{1,0:T(8,128)(2,1)} custom-call(s32[48]{0:T(128)} %copy-done, bf16[256,2048]{1,0:T(8,128)(2,1)} %collective-permute-done.23.refs_1_.piece_ref, bf16[256,16384]{1,0:T(8,128)(2,1)} %get-tuple-element.30.whole_ref), custom_call_target="tpu_custom_call", output_to_operand_aliasing={{}: (2, {})} | custom-call | tf_op jit(solution)/shard_map/put/pallas_call | solution.py:259
  145.3 2.7 %put.6.whole_ref = bf16[256,16384]{1,0:T(8,128)(2,1)} custom-call(s32[48]{0:T(128)} %copy-done, bf16[256,2048]{1,0:T(8,128)(2,1)} %collective-permute-done.25.piece_ref, bf16[256,16384]{1,0:T(8,128)(2,1)} %put.5.whole_ref), custom_call_target="tpu_custom_call", output_to_operand_aliasing={{}: (2, {})} | custom-call | tf_op jit(solution)/shard_map/put/pallas_call | solution.py:259
  148.0 9.7 %collective-permute-done.24.piece_ref = bf16[256,2048]{1,0:T(8,128)(2,1)} collective-permute-done((bf16[256,2048]{1,0:T(8,128)(2,1)}, bf16[256,2048]{1,0:T(8,128)(2,1)}, u32[]{:S(2)}, u32[]{:S(2)}) %collective-permute-start.24) | collective-permute-done | bytes 1048608 | tf_op jit(solution)/shard_map/ppermute | solution.py:345
  157.7 2.7 %put.7 = bf16[256,16384]{1,0:T(8,128)(2,1)} custom-call(s32[48]{0:T(128)} %copy-done, bf16[256,2048]{1,0:T(8,128)(2,1)} %collective-permute-done.24.piece_ref, bf16[256,16384]{1,0:T(8,128)(2,1)} %put.6.whole_ref), custom_call_target="tpu_custom_call", output_to_operand_aliasing={{}: (2, {})} | custom-call | tf_op jit(solution)/shard_map/put/pallas_call | solution.py:259
  (44 shorter events, 0.7 us)
Async XLA Ops:
  3.7 50.1 %collective-permute-start.8 = (bf16[32,128,128]{2,1,0:T(8,128)(2,1)}, bf16[32,128,128]{2,1,0:T(8,128)(2,1)}, u32[]{:S(2)}, u32[]{:S(2)}) collective-permute-start(bf16[32,128,128]{2,1,0:T(8,128)(2,1)} %get-tuple-element.21.refs_0_), channel_id=1, source_target_pairs={{0,16},{16,0},{8,24},{24,8},{1,17},{17,1},{9,25},{25,9},{2,18},{18... | collective-permute-start | bytes 3145736 | tf_op jit(solution)/shard_map/ppermute | solution.py:403
  7.7 46.2 %collective-permute-start.7 = (bf16[32,128,128]{2,1,0:T(8,128)(2,1)}, bf16[32,128,128]{2,1,0:T(8,128)(2,1)}, u32[]{:S(2)}, u32[]{:S(2)}) collective-permute-start(bf16[32,128,128]{2,1,0:T(8,128)(2,1)} %get-tuple-element.21.refs_0_), channel_id=1, source_target_pairs={{0,8},{8,0},{16,24},{24,16},{1,9},{9,1},{17,25},{25,17},{2,10},{10... | collective-permute-start | bytes 3145736 | tf_op jit(solution)/shard_map/ppermute | solution.py:403
  10.0 4.5 %collective-permute-start = (s32[4,64]{1,0:T(4,128)S(1)}, s32[4,64]{1,0:T(4,128)S(1)}, u32[]{:S(2)}, u32[]{:S(2)}) collective-permute-start(s32[4,64]{1,0:T(4,128)S(1)} %select_reduce_fusion), channel_id=1, source_target_pairs={{0,2},{1,5},{2,0},{3,7},{4,6},{5,1},{6,4},{7,3},{8,10},{9,13},{10,... | collective-permute-start | bytes 3080 | tf_op jit(solution)/shard_map/ppermute | solution.py:345
  14.5 0.6 copy-start.1
  15.1 14.8 %collective-permute-start.2 = (bf16[1024,256]{1,0:T(8,128)(2,1)}, bf16[1024,256]{1,0:T(8,128)(2,1)}, u32[]{:S(2)}, u32[]{:S(2)}) collective-permute-start(bf16[1024,256]{1,0:T(8,128)(2,1)} %tie.13.refs_0_), channel_id=1, source_target_pairs={{0,2},{1,5},{2,0},{3,7},{4,6},{5,1},{6,4},{7,3},{8,10},{9,13},{10,... | collective-permute-start | bytes 1572872 | tf_op jit(solution)/shard_map/ppermute | solution.py:345
  16.9 22.6 %copy-start = (s32[48]{0:T(128)}, s32[48]{0:T(128)S(1)}, u32[]{:S(2)}) copy-start(s32[48]{0:T(128)S(1)} %dynamic-slice_bitcast_fusion.scalars) | copy-start | bytes 580
  17.7 18.2 %collective-permute-start.3 = (bf16[1024,256]{1,0:T(8,128)(2,1)}, bf16[1024,256]{1,0:T(8,128)(2,1)}, u32[]{:S(2)}, u32[]{:S(2)}) collective-permute-start(bf16[1024,256]{1,0:T(8,128)(2,1)} %tie.13.refs_0_), channel_id=1, source_target_pairs={{0,4},{1,3},{2,6},{3,1},{4,0},{5,7},{6,2},{7,5},{8,12},{9,11},{10,... | collective-permute-start | bytes 1572872 | tf_op jit(solution)/shard_map/ppermute | solution.py:345
  30.0 9.5 %collective-permute-start.4 = (bf16[1024,256]{1,0:T(8,128)(2,1)}, bf16[1024,256]{1,0:T(8,128)(2,1)}, u32[]{:S(2)}, u32[]{:S(2)}) collective-permute-start(bf16[1024,256]{1,0:T(8,128)(2,1)} %collective-permute-done.2.refs_1_), channel_id=1, source_target_pairs={{0,4},{1,3},{2,6},{3,1},{4,0},{5,7},{6,2},{7,5},{8,12},{9,11},{10,... | collective-permute-start | bytes 1572872 | tf_op jit(solution)/shard_map/ppermute | solution.py:345
  33.5 1.2 collective-permute-start.1
  51.3 7.1 %collective-permute-start.5 = (bf16[4,3,256,256]{3,2,1,0:T(8,128)(2,1)}, bf16[4,3,256,256]{3,2,1,0:T(8,128)(2,1)}, u32[]{:S(2)}, u32[]{:S(2)}) collective-permute-start(bf16[4,3,256,256]{3,2,1,0:T(8,128)(2,1)} %get-tuple-element.20), channel_id=1, source_target_pairs={{0,1},{1,0},{2,3},{3,2},{4,5},{5,4},{6,7},{7,6},{8,9},{9,8},{10,11... | collective-permute-start | bytes 4718600 | tf_op jit(solution)/shard_map/ppermute | solution.py:345
  51.3 5.8 %collective-permute-start.9 = (bf16[32,128,128]{2,1,0:T(8,128)(2,1)}, bf16[32,128,128]{2,1,0:T(8,128)(2,1)}, u32[]{:S(2)}, u32[]{:S(2)}) collective-permute-start(bf16[32,128,128]{2,1,0:T(8,128)(2,1)} %get-tuple-element.21.refs_0_), channel_id=1, source_target_pairs={{0,1},{1,0},{2,3},{3,2},{4,5},{5,4},{6,7},{7,6},{8,9},{9,8},{10,11... | collective-permute-start | bytes 3145736 | tf_op jit(solution)/shard_map/ppermute | solution.py:345
  51.8 16.1 %collective-permute-start.6 = (bf16[32,128,128]{2,1,0:T(8,128)(2,1)}, bf16[32,128,128]{2,1,0:T(8,128)(2,1)}, u32[]{:S(2)}, u32[]{:S(2)}) collective-permute-start(bf16[32,128,128]{2,1,0:T(8,128)(2,1)} %get-tuple-element.21.refs_0_), channel_id=1, source_target_pairs={{0,2},{1,5},{2,0},{3,7},{4,6},{5,1},{6,4},{7,3},{8,10},{9,13},{10,... | collective-permute-start | bytes 3145736 | tf_op jit(solution)/shard_map/ppermute | solution.py:345
  53.9 24.2 %collective-permute-start.11 = (bf16[32,128,128]{2,1,0:T(8,128)(2,1)}, bf16[32,128,128]{2,1,0:T(8,128)(2,1)}, u32[]{:S(2)}, u32[]{:S(2)}) collective-permute-start(bf16[32,128,128]{2,1,0:T(8,128)(2,1)} %tie.14.refs_1_), channel_id=1, source_target_pairs={{0,2},{1,5},{2,0},{3,7},{4,6},{5,1},{6,4},{7,3},{8,10},{9,13},{10,... | collective-permute-start | bytes 3145736 | tf_op jit(solution)/shard_map/ppermute | solution.py:345
  55.5 22.7 %collective-permute-start.14 = (bf16[32,128,128]{2,1,0:T(8,128)(2,1)}, bf16[32,128,128]{2,1,0:T(8,128)(2,1)}, u32[]{:S(2)}, u32[]{:S(2)}) collective-permute-start(bf16[32,128,128]{2,1,0:T(8,128)(2,1)} %tie.18), channel_id=1, source_target_pairs={{8,16},{16,8},{9,17},{17,9},{10,18},{18,10},{11,19},{19,11},{12,20... | collective-permute-start | bytes 3145736 | tf_op jit(solution)/shard_map/ppermute | solution.py:403
  57.1 26.8 %collective-permute-start.15 = (bf16[32,128,128]{2,1,0:T(8,128)(2,1)}, bf16[32,128,128]{2,1,0:T(8,128)(2,1)}, u32[]{:S(2)}, u32[]{:S(2)}) collective-permute-start(bf16[32,128,128]{2,1,0:T(8,128)(2,1)} %tie.15.refs_2_), channel_id=1, source_target_pairs={{8,0},{16,24},{9,1},{17,25},{10,2},{18,26},{11,3},{19,27},{12,4},{... | collective-permute-start | bytes 3145736 | tf_op jit(solution)/shard_map/ppermute | solution.py:403
  58.4 30.9 %collective-permute-start.13 = (bf16[32,128,128]{2,1,0:T(8,128)(2,1)}, bf16[32,128,128]{2,1,0:T(8,128)(2,1)}, u32[]{:S(2)}, u32[]{:S(2)}) collective-permute-start(bf16[32,128,128]{2,1,0:T(8,128)(2,1)} %tie.15.refs_2_), channel_id=1, source_target_pairs={{0,2},{1,5},{2,0},{3,7},{4,6},{5,1},{6,4},{7,3},{8,10},{9,13},{10,... | collective-permute-start | bytes 3145736 | tf_op jit(solution)/shard_map/ppermute | solution.py:345
  67.9 21.5 %collective-permute-start.10 = (bf16[32,128,128]{2,1,0:T(8,128)(2,1)}, bf16[32,128,128]{2,1,0:T(8,128)(2,1)}, u32[]{:S(2)}, u32[]{:S(2)}) collective-permute-start(bf16[32,128,128]{2,1,0:T(8,128)(2,1)} %tie.16.refs_0_), channel_id=1, source_target_pairs={{0,1},{1,0},{2,3},{3,2},{4,5},{5,4},{6,7},{7,6},{8,9},{9,8},{10,11... | collective-permute-start | bytes 3145736 | tf_op jit(solution)/shard_map/ppermute | solution.py:345
  78.1 11.2 %collective-permute-start.12 = (bf16[32,128,128]{2,1,0:T(8,128)(2,1)}, bf16[32,128,128]{2,1,0:T(8,128)(2,1)}, u32[]{:S(2)}, u32[]{:S(2)}) collective-permute-start(bf16[32,128,128]{2,1,0:T(8,128)(2,1)} %tie.17.refs_1_), channel_id=1, source_target_pairs={{0,1},{1,0},{2,3},{3,2},{4,5},{5,4},{6,7},{7,6},{8,9},{9,8},{10,11... | collective-permute-start | bytes 3145736 | tf_op jit(solution)/shard_map/ppermute | solution.py:345
  78.1 23.2 %collective-permute-start.19 = (bf16[32,128,128]{2,1,0:T(8,128)(2,1)}, bf16[32,128,128]{2,1,0:T(8,128)(2,1)}, u32[]{:S(2)}, u32[]{:S(2)}) collective-permute-start(bf16[32,128,128]{2,1,0:T(8,128)(2,1)} %tie.15.refs_2_), channel_id=1, source_target_pairs={{0,1},{1,0},{2,3},{3,2},{4,5},{5,4},{6,7},{7,6},{8,9},{9,8},{10,11... | collective-permute-start | bytes 3145736 | tf_op jit(solution)/shard_map/ppermute | solution.py:345
  83.9 17.7 %collective-permute-start.18 = (bf16[32,128,128]{2,1,0:T(8,128)(2,1)}, bf16[32,128,128]{2,1,0:T(8,128)(2,1)}, u32[]{:S(2)}, u32[]{:S(2)}) collective-permute-start(bf16[32,128,128]{2,1,0:T(8,128)(2,1)} %tie.14.refs_1_), channel_id=1, source_target_pairs={{0,1},{1,0},{2,3},{3,2},{4,5},{5,4},{6,7},{7,6},{8,9},{9,8},{10,11... | collective-permute-start | bytes 3145736 | tf_op jit(solution)/shard_map/ppermute | solution.py:345
  92.3 9.4 %collective-permute-start.20 = (bf16[32,128,128]{2,1,0:T(8,128)(2,1)}, bf16[32,128,128]{2,1,0:T(8,128)(2,1)}, u32[]{:S(2)}, u32[]{:S(2)}) collective-permute-start(bf16[32,128,128]{2,1,0:T(8,128)(2,1)} %choose.1.refs_0_), channel_id=1, source_target_pairs={{0,1},{1,0},{2,3},{3,2},{4,5},{5,4},{6,7},{7,6},{8,9},{9,8},{10,11... | collective-permute-start | bytes 3145736 | tf_op jit(solution)/shard_map/ppermute | solution.py:345
  92.3 21.6 %collective-permute-start.17 = (bf16[32,128,128]{2,1,0:T(8,128)(2,1)}, bf16[32,128,128]{2,1,0:T(8,128)(2,1)}, u32[]{:S(2)}, u32[]{:S(2)}) collective-permute-start(bf16[32,128,128]{2,1,0:T(8,128)(2,1)} %choose.1.refs_0_), channel_id=1, source_target_pairs={{0,2},{1,5},{2,0},{3,7},{4,6},{5,1},{6,4},{7,3},{8,10},{9,13},{10,... | collective-permute-start | bytes 3145736 | tf_op jit(solution)/shard_map/ppermute | solution.py:345
  99.8 25.2 %collective-permute-start.22 = (bf16[256,2048]{1,0:T(8,128)(2,1)}, bf16[256,2048]{1,0:T(8,128)(2,1)}, u32[]{:S(2)}, u32[]{:S(2)}) collective-permute-start(bf16[256,2048]{1,0:T(8,128)(2,1)} %get-tuple-element.23.refs_1_), channel_id=1, source_target_pairs={{0,4},{1,3},{2,6},{3,1},{4,0},{5,7},{6,2},{7,5},{8,12},{9,11},{10,... | collective-permute-start | bytes 3145736 | tf_op jit(solution)/shard_map/ppermute | solution.py:345
  101.4 30.6 %collective-permute-start.16 = (bf16[32,128,128]{2,1,0:T(8,128)(2,1)}, bf16[32,128,128]{2,1,0:T(8,128)(2,1)}, u32[]{:S(2)}, u32[]{:S(2)}) collective-permute-start(bf16[32,128,128]{2,1,0:T(8,128)(2,1)} %tie.21.refs_2_), channel_id=1, source_target_pairs={{0,1},{1,0},{2,3},{3,2},{4,5},{5,4},{6,7},{7,6},{8,9},{9,8},{10,11... | collective-permute-start | bytes 3145736 | tf_op jit(solution)/shard_map/ppermute | solution.py:345
  112.1 19.9 %collective-permute-start.23 = (bf16[256,2048]{1,0:T(8,128)(2,1)}, bf16[256,2048]{1,0:T(8,128)(2,1)}, u32[]{:S(2)}, u32[]{:S(2)}) collective-permute-start(bf16[256,2048]{1,0:T(8,128)(2,1)} %get-tuple-element.25.refs_1_), channel_id=1, source_target_pairs={{0,2},{1,5},{2,0},{3,7},{4,6},{5,1},{6,4},{7,3},{8,10},{9,13},{10,... | collective-permute-start | bytes 3145736 | tf_op jit(solution)/shard_map/ppermute | solution.py:345
  114.0 18.0 %collective-permute-start.21 = (bf16[32,128,128]{2,1,0:T(8,128)(2,1)}, bf16[32,128,128]{2,1,0:T(8,128)(2,1)}, u32[]{:S(2)}, u32[]{:S(2)}) collective-permute-start(bf16[32,128,128]{2,1,0:T(8,128)(2,1)} %tie.22.refs_3_), channel_id=1, source_target_pairs={{0,1},{1,0},{2,3},{3,2},{4,5},{5,4},{6,7},{7,6},{8,9},{9,8},{10,11... | collective-permute-start | bytes 3145736 | tf_op jit(solution)/shard_map/ppermute | solution.py:345
  124.5 20.8 %collective-permute-start.25 = (bf16[256,2048]{1,0:T(8,128)(2,1)}, bf16[256,2048]{1,0:T(8,128)(2,1)}, u32[]{:S(2)}, u32[]{:S(2)}) collective-permute-start(bf16[256,2048]{1,0:T(8,128)(2,1)} %get-tuple-element.29), channel_id=1, source_target_pairs={{0,4},{1,3},{2,6},{3,1},{4,0},{5,7},{6,2},{7,5},{8,12},{9,11},{10,... | collective-permute-start | bytes 3145736 | tf_op jit(solution)/shard_map/ppermute | solution.py:345
  142.5 15.2 %collective-permute-start.24 = (bf16[256,2048]{1,0:T(8,128)(2,1)}, bf16[256,2048]{1,0:T(8,128)(2,1)}, u32[]{:S(2)}, u32[]{:S(2)}) collective-permute-start(bf16[256,2048]{1,0:T(8,128)(2,1)} %get-tuple-element.28), channel_id=1, source_target_pairs={{0,2},{1,5},{2,0},{3,7},{4,6},{5,1},{6,4},{7,3},{8,10},{9,13},{10,... | collective-permute-start | bytes 3145736 | tf_op jit(solution)/shard_map/ppermute | solution.py:345

commit v10 on v8

--- a/solution.py
+++ b/solution.py
@@ -406,26 +406,26 @@
         return [lax.ppermute(own if source < 0 else moved[source], "row", pairs) for source, pairs in moves]
 
     fresh = line_phase(phases[0], packed)
+    count = own_lists.shape[1]
+    tiles = (int_rows // TILE) * (int_cols // TILE)
+    found = own_lists[:, None, :] == jnp.arange(tiles, dtype=jnp.int32)[None, :, None]
+    own_table = jnp.min(jnp.where(found, jnp.arange(count, dtype=jnp.int32), count), axis=2)
+
+    col_ids = jnp.arange(cols, dtype=jnp.int32)
+    onehot = (pair_dest[:, None] == col_ids[None, :]).astype(jnp.int32)
+    before = jnp.cumsum(onehot, axis=0) - onehot
+    target = pair_dest * capacity + jnp.sum(before * onehot, axis=1)
+
+    table_next = permute(own_table, along)
+    slots, nexts, theirs_of, theirs_next = [packed], [permute(packed, along)], [permute(packed, across)], []
+    amp_used = tie(amp_used, table_next, nexts[0])
     amp_next = permute(amp_used, along)
     amp_other = permute(amp_used, other)
     amps = [amp_used, amp_next, amp_other, permute(amp_next, other)]
     for de in range(1, extra):
         amps += [permute(amp, lambda e, a, b, c: ((e - de) % extra, a, b, c)) for amp in amps[:4]]
-
-    count = own_lists.shape[1]
-    tiles = (int_rows // TILE) * (int_cols // TILE)
-    found = own_lists[:, None, :] == jnp.arange(tiles, dtype=jnp.int32)[None, :, None]
-    own_table = jnp.min(jnp.where(found, jnp.arange(count, dtype=jnp.int32), count), axis=2)
-
-    col_ids = jnp.arange(cols, dtype=jnp.int32)
-    onehot = (pair_dest[:, None] == col_ids[None, :]).astype(jnp.int32)
-    before = jnp.cumsum(onehot, axis=0) - onehot
-    target = pair_dest * capacity + jnp.sum(before * onehot, axis=1)
-
-    table_next = permute(own_table, along)
     pair_tables = permute(jnp.concatenate([own_table, table_next], axis=0), across)
     sums = None
-    slots, nexts, theirs_of, theirs_next = [packed], [permute(packed, along)], [permute(packed, across)], []
     width = own_table.shape[1]
     tail = jnp.pad(scalars, (0, -scalars.shape[0] % width)).reshape(-1, width)
     numbers = jnp.concatenate([own_table, table_next, pair_tables, tail], axis=0)
@@ -435,7 +435,7 @@
         if at > 0:
             fresh = line_phase(moves, packed_again)
         if at == 0:
-            waited = (mine, nexts[0], theirs_of[0])
+            waited = (mine, theirs_of[0])
             fresh[0] = tie(fresh[0], mine, fresh[1])
         elif at == 1:
             theirs = permute(for_them, across)
@@ -475,7 +475,9 @@
     arrived = []
     for turn_at, q in enumerate((0, 2, 1, 3)):
         if turn_at == 3:
-            theirs_next[-1] = tie(theirs_next[-1], *arrived[0], *arrived[1])
+            for piece, place in zip(arrived[0], arrive_at[0]):
+                out = put(piece, out, scalars, place)
+            theirs_next[-1] = tie(theirs_next[-1], *arrived[1], out)
         places = (rows_at[q], mine_at, theirs_at)
         blocks = (slots, nexts, theirs_of, theirs_next)[q]
         if q == 0 and rows > 1:
@@ -501,7 +503,7 @@
                 theirs_next.append(permute(nexts[len(theirs_next)], across))
     own["whole"] = tie(out, pieces[0])
     (out,) = call((core_at, picks_at[q][:1], *places, tiles, 4 * rows), **own)
-    for got, q in zip(arrived, (0, 2, 1, 3)):
+    for got, q in zip(arrived[1:], (2, 1, 3)):
         for piece, place in zip(got, arrive_at[q]):
             out = put(piece, out, scalars, place)
     return out

time: 156 us -> 160 us (1.026)
  starting transfers between devices: 24.4 us -> 30 us
  waiting for transfers between devices: 39.9 us -> 35.6 us
    ppermute x4, waiting for transfers between devices: 26.3 us -> 14.7 us  [line_phase(): lax.ppermute(own if source < 0 else moved[source], 'row', pairs)]
    ppermute x22, waiting for transfers between devices: 13.7 us -> 21 us  [permute(): lax.ppermute(value, 'col', [(col_index(*at), col_index(*moved_to(*at))) f...]
    ppermute x22, starting transfers between devices: 17.3 us -> 22.9 us  [permute(): lax.ppermute(value, 'col', [(col_index(*at), col_index(*moved_to(*at))) f...]
  transfers between devices with their start and end apart: 26 -> 26, of which waited for: 8 -> 8; matrix products, arithmetic and copies ran while one was open for 5% -> 6% of each run, Pallas kernels for 49% -> 48%
where the time goes in v10:
time: 160 us; the launch traced here: 158 us
  Pallas kernels  82.6 us (52%)
  waiting for transfers between devices  35.6 us (22%)
  starting transfers between devices  30 us (19%)
  other arithmetic  7.93 us (5%)
    pallas_call x6, Pallas kernels, product(): pl.pallas_call(functools.partial(product_body, at, acc is not None, whole...  53.3 us
    ppermute x22, starting transfers between devices, permute(): lax.ppermute(value, 'col', [(col_index(*at), col_index(*moved_to(*at))) f...  22.9 us
    ppermute x22, waiting for transfers between devices, permute(): lax.ppermute(value, 'col', [(col_index(*at), col_index(*moved_to(*at))) f...  21 us
    ppermute x4, waiting for transfers between devices, line_phase(): lax.ppermute(own if source < 0 else moved[source], 'row', pairs)  14.7 us
    pallas_call x1, Pallas kernels, pick_rows(): pl.pallas_call(functools.partial(pick_body, first, count, capacity), out_...  11.8 us
    pallas_call x4, Pallas kernels, put(): pl.pallas_call(put_body, out_shape=jax.ShapeDtypeStruct(whole.shape, whol...  10.9 us
    ppermute x4, starting transfers between devices, line_phase(): lax.ppermute(own if source < 0 else moved[source], 'row', pairs)  7.1 us
    pallas_call x1, Pallas kernels, pack(): pl.pallas_call(pack_body, out_shape=[jax.ShapeDtypeStruct((count, TILE, T...  3.71 us
  transfers between devices with their start and end apart: 26, of which 8 were waited for; matrix products, arithmetic and copies ran while one was open for 6% of the time, Pallas kernels for 48%

profile of v10, /device:TPU:0, one launch (start us, length us, event | category | flops | bytes accessed | tf_op | source)
XLA Modules:
  0.0 157.9 jit_solution(1209318225542275592)
XLA Ops:
  0.0 3.7 %pack_tiles.1 = (bf16[32,128,128]{2,1,0:T(8,128)(2,1)}, bf16[32,128,128]{2,1,0:T(8,128)(2,1)}, bf16[1024,256]{1,0:T(8,128)(2,1)}) custom-call(s32[1]{0:T(128)} %bitcast.6.row, s32[4,32]{1,0:T(4,128)} %bitcast.31, s32[2,8]{1,0:T(2,128)} %bitcast.33, bf16[512,2048]{1,0:T(8,128)(2,1)} %src_ref.1, bf16[1024,256]{1,0:T(8,128)(2,1)} %amp_ref.1), custom_call_target="tpu_custom_call" | custom-call | tf_op jit(solution)/shard_map/pack_tiles/pallas_call | solution.py:39
  3.7 2.9 %collective-permute-start.2 = (bf16[32,128,128]{2,1,0:T(8,128)(2,1)}, bf16[32,128,128]{2,1,0:T(8,128)(2,1)}, u32[]{:S(2)}, u32[]{:S(2)}) collective-permute-start(bf16[32,128,128]{2,1,0:T(8,128)(2,1)} %get-tuple-element.17.refs_0_), channel_id=1, source_target_pairs={{0,2},{1,5},{2,0},{3,7},{4,6},{5,1},{6,4},{7,3},{8,10},{9,13},{10,... | collective-permute-start | bytes 3145736 | tf_op jit(solution)/shard_map/ppermute | solution.py:348
  6.7 2.6 %collective-permute-start.8 = (bf16[32,128,128]{2,1,0:T(8,128)(2,1)}, bf16[32,128,128]{2,1,0:T(8,128)(2,1)}, u32[]{:S(2)}, u32[]{:S(2)}) collective-permute-start(bf16[32,128,128]{2,1,0:T(8,128)(2,1)} %get-tuple-element.17.refs_0_), channel_id=1, source_target_pairs={{0,16},{16,0},{8,24},{24,8},{1,17},{17,1},{9,25},{25,9},{2,18},{18... | collective-permute-start | bytes 3145736 | tf_op jit(solution)/shard_map/ppermute | solution.py:406
  9.2 1.6 collective-permute-start.7
  10.8 0.8 select_reduce_fusion
  11.6 0.6 collective-permute-start
  12.2 0.7 fusion.3
  12.9 2.3 %reduce-window.6 = s32[8,8,128]{2,1,0:T(8,128)S(1)} reduce-window(s32[8,8,128]{2,1,0:T(8,128)S(1)} %fusion.3, s32[]{:T(128)} %constant.20.clone.1), window={size=1x1x128 pad=0_0x0_0x127_0}, to_apply=%region_1.2 | reduce-window | flops 1040384 | bytes 65540 | tf_op jit(solution)/shard_map/reduce-window
  15.1 4.6 %collective-permute-done.refs_1_ = s32[4,64]{1,0:T(4,128)S(1)} collective-permute-done((s32[4,64]{1,0:T(4,128)S(1)}, s32[4,64]{1,0:T(4,128)S(1)}, u32[]{:S(2)}, u32[]{:S(2)}) %collective-permute-start) | collective-permute-done | bytes 1056 | tf_op jit(solution)/shard_map/ppermute | solution.py:348
  19.8 0.6 copy-done.1
  20.3 2.0 %collective-permute-start.3 = (bf16[1024,256]{1,0:T(8,128)(2,1)}, bf16[1024,256]{1,0:T(8,128)(2,1)}, u32[]{:S(2)}, u32[]{:S(2)}) collective-permute-start(bf16[1024,256]{1,0:T(8,128)(2,1)} %tie.14.refs_0_), channel_id=1, source_target_pairs={{0,2},{1,5},{2,0},{3,7},{4,6},{5,1},{6,4},{7,3},{8,10},{9,13},{10,... | collective-permute-start | bytes 1572872 | tf_op jit(solution)/shard_map/ppermute | solution.py:348
  22.8 0.7 dynamic-slice_bitcast_fusion.scalars
  23.6 0.7 fusion.2
  24.3 1.6 %collective-permute-start.4 = (bf16[1024,256]{1,0:T(8,128)(2,1)}, bf16[1024,256]{1,0:T(8,128)(2,1)}, u32[]{:S(2)}, u32[]{:S(2)}) collective-permute-start(bf16[1024,256]{1,0:T(8,128)(2,1)} %tie.14.refs_0_), channel_id=1, source_target_pairs={{0,4},{1,3},{2,6},{3,1},{4,0},{5,7},{6,2},{7,5},{8,12},{9,11},{10,... | collective-permute-start | bytes 1572872 | tf_op jit(solution)/shard_map/ppermute | solution.py:348
  25.9 7.8 %collective-permute-done.3.refs_1_ = bf16[1024,256]{1,0:T(8,128)(2,1)} collective-permute-done((bf16[1024,256]{1,0:T(8,128)(2,1)}, bf16[1024,256]{1,0:T(8,128)(2,1)}, u32[]{:S(2)}, u32[]{:S(2)}) %collective-permute-start.3) | collective-permute-done | bytes 524320 | tf_op jit(solution)/shard_map/ppermute | solution.py:348
  33.7 3.8 %collective-permute-start.5 = (bf16[1024,256]{1,0:T(8,128)(2,1)}, bf16[1024,256]{1,0:T(8,128)(2,1)}, u32[]{:S(2)}, u32[]{:S(2)}) collective-permute-start(bf16[1024,256]{1,0:T(8,128)(2,1)} %collective-permute-done.3.refs_1_), channel_id=1, source_target_pairs={{0,4},{1,3},{2,6},{3,1},{4,0},{5,7},{6,2},{7,5},{8,12},{9,11},{10,... | collective-permute-start | bytes 1572872 | tf_op jit(solution)/shard_map/ppermute | solution.py:348
  37.5 1.3 multiply_add_fusion.refs_0_
  38.7 0.7 pad_add_fusion.1
  39.5 1.2 collective-permute-done.1
  40.6 1.3 pad_add_fusion.refs_1_.numbers
  41.9 3.0 %collective-permute-done.5.refs_3_ = bf16[1024,256]{1,0:T(8,128)(2,1)} collective-permute-done((bf16[1024,256]{1,0:T(8,128)(2,1)}, bf16[1024,256]{1,0:T(8,128)(2,1)}, u32[]{:S(2)}, u32[]{:S(2)}) %collective-permute-start.5) | collective-permute-done | bytes 524320 | tf_op jit(solution)/shard_map/ppermute | solution.py:348
  44.9 11.8 %pick_rows.1 = (bf16[4,3,256,256]{3,2,1,0:T(8,128)(2,1)}, bf16[4,3,256,256]{3,2,1,0:T(8,128)(2,1)}) custom-call(s32[48]{0:T(128)} %copy-done, s32[1,1024]{1,0:T(1,128)} %bitcast.28, bf16[1024,256]{1,0:T(8,128)(2,1)} %tie.14.refs_0_, bf16[1024,256]{1,0:T(8,128)(2,1)} %collective-permute-done.3.refs_1_, bf16[1024,256]{1,0:T(8,128)(2,1)} %collective-permute-done.4.refs_2_, ...), custom_call_target="tpu_custom_call" | custom-call | tf_op jit(solution)/shard_map/pick_rows/pallas_call | solution.py:78
  56.7 0.5 collective-permute-start.9
  57.3 1.3 collective-permute-start.11
  58.5 1.7 %collective-permute-start.14 = (bf16[32,128,128]{2,1,0:T(8,128)(2,1)}, bf16[32,128,128]{2,1,0:T(8,128)(2,1)}, u32[]{:S(2)}, u32[]{:S(2)}) collective-permute-start(bf16[32,128,128]{2,1,0:T(8,128)(2,1)} %tie.19), channel_id=1, source_target_pairs={{8,16},{16,8},{9,17},{17,9},{10,18},{18,10},{11,19},{19,11},{12,20... | collective-permute-start | bytes 3145736 | tf_op jit(solution)/shard_map/ppermute | solution.py:406
  60.2 1.8 %collective-permute-done.9.refs_2_.refs_0_ = bf16[32,128,128]{2,1,0:T(8,128)(2,1)} collective-permute-done((bf16[32,128,128]{2,1,0:T(8,128)(2,1)}, bf16[32,128,128]{2,1,0:T(8,128)(2,1)}, u32[]{:S(2)}, u32[]{:S(2)}) %collective-permute-start.9) | collective-permute-done | bytes 1048608 | tf_op jit(solution)/shard_map/ppermute | solution.py:348
  62.0 1.3 collective-permute-start.15
  63.3 1.3 collective-permute-start.13
  64.6 8.9 %product.6.refs_1_.refs_3_ = f32[512,2048]{1,0:T(8,128)} custom-call(s32[17,64]{1,0:T(8,128)} %pad_add_fusion.refs_1_.numbers, bf16[4,3,256,256]{3,2,1,0:T(8,128)(2,1)} %get-tuple-element.18.refs_1_.mine, bf16[4,3,256,256]{3,2,1,0:T(8,128)(2,1)} %collective-permute-done.6.theirs.refs_1_, bf16[32,128,128]{2,1,0:T(8,128)(2,1)} %get-tuple-element.17.refs_0_, ...), custom_call_target="tpu_custom_call" | custom-call | tf_op jit(solution)/shard_map/product/pallas_call | solution.py:188
  73.5 0.7 collective-permute-start.10
  74.7 14.7 %collective-permute-done.15.refs_6_.refs_0_ = bf16[32,128,128]{2,1,0:T(8,128)(2,1)} collective-permute-done((bf16[32,128,128]{2,1,0:T(8,128)(2,1)}, bf16[32,128,128]{2,1,0:T(8,128)(2,1)}, u32[]{:S(2)}, u32[]{:S(2)}) %collective-permute-start.15) | collective-permute-done | bytes 1048608 | tf_op jit(solution)/shard_map/ppermute | solution.py:406
  89.4 2.9 %choose.1.refs_0_ = bf16[32,128,128]{2,1,0:T(8,128)(2,1)} custom-call(s32[48]{0:T(128)} %copy-done, bf16[32,128,128]{2,1,0:T(8,128)(2,1)} %tie.20.refs_6_.a_ref, bf16[32,128,128]{2,1,0:T(8,128)(2,1)} %tie.21.b_ref), custom_call_target="tpu_custom_call" | custom-call | tf_op jit(solution)/shard_map/choose/pallas_call | solution.py:242
  92.4 0.6 collective-permute-start.20
  92.9 1.3 collective-permute-start.17
  94.2 7.3 %product.7 = (bf16[256,16384]{1,0:T(8,128)(2,1)}, bf16[256,2048]{1,0:T(8,128)(2,1)}) custom-call(s32[17,64]{1,0:T(8,128)} %pad_add_fusion.refs_1_.numbers, bf16[4,3,256,256]{3,2,1,0:T(8,128)(2,1)} %get-tuple-element.18.refs_1_.mine, bf16[4,3,256,256]{3,2,1,0:T(8,128)(2,1)} %collective-permute-done.6.theirs.refs_1_, bf16[32,128,128]{2,1,0:T(8,128)(2,1)} %choose.1.refs_0_, ...), custom_call_target="tpu_custom_call" | custom-call | tf_op jit(solution)/shard_map/product/pallas_call | solution.py:188
  101.5 2.1 %collective-permute-start.23 = (bf16[256,2048]{1,0:T(8,128)(2,1)}, bf16[256,2048]{1,0:T(8,128)(2,1)}, u32[]{:S(2)}, u32[]{:S(2)}) collective-permute-start(bf16[256,2048]{1,0:T(8,128)(2,1)} %get-tuple-element.21.refs_1_), channel_id=1, source_target_pairs={{0,4},{1,3},{2,6},{3,1},{4,0},{5,7},{6,2},{7,5},{8,12},{9,11},{10,... | collective-permute-start | bytes 3145736 | tf_op jit(solution)/shard_map/ppermute | solution.py:348
  103.6 10.5 %product.8 = (bf16[256,16384]{1,0:T(8,128)(2,1)}, bf16[256,2048]{1,0:T(8,128)(2,1)}) custom-call(s32[17,64]{1,0:T(8,128)} %pad_add_fusion.refs_1_.numbers, bf16[4,3,256,256]{3,2,1,0:T(8,128)(2,1)} %get-tuple-element.18.refs_1_.mine, bf16[4,3,256,256]{3,2,1,0:T(8,128)(2,1)} %collective-permute-done.6.theirs.refs_1_, ...), custom_call_target="tpu_custom_call", output_to_operand_aliasing={{0}: (7, {})} | custom-call | tf_op jit(solution)/shard_map/product/pallas_call | solution.py:188
  114.2 0.8 collective-permute-start.22
  115.1 10.5 %product.9 = (bf16[256,16384]{1,0:T(8,128)(2,1)}, bf16[256,2048]{1,0:T(8,128)(2,1)}) custom-call(s32[17,64]{1,0:T(8,128)} %pad_add_fusion.refs_1_.numbers, bf16[4,3,256,256]{3,2,1,0:T(8,128)(2,1)} %get-tuple-element.18.refs_1_.mine, bf16[4,3,256,256]{3,2,1,0:T(8,128)(2,1)} %collective-permute-done.6.theirs.refs_1_, ...), custom_call_target="tpu_custom_call", output_to_operand_aliasing={{0}: (7, {})} | custom-call | tf_op jit(solution)/shard_map/product/pallas_call | solution.py:188
  125.6 1.5 collective-permute-start.25
  127.0 2.7 %put.4.refs_2_.refs_0_ = bf16[256,16384]{1,0:T(8,128)(2,1)} custom-call(s32[48]{0:T(128)} %copy-done, bf16[256,2048]{1,0:T(8,128)(2,1)} %collective-permute-done.23.piece_ref, bf16[256,16384]{1,0:T(8,128)(2,1)} %get-tuple-element.25.whole_ref), custom_call_target="tpu_custom_call", output_to_operand_aliasing={{}: (2, {})} | custom-call | tf_op jit(solution)/shard_map/put/pallas_call | solution.py:262
  129.8 2.1 %collective-permute-done.22.refs_1_.piece_ref = bf16[256,2048]{1,0:T(8,128)(2,1)} collective-permute-done((bf16[256,2048]{1,0:T(8,128)(2,1)}, bf16[256,2048]{1,0:T(8,128)(2,1)}, u32[]{:S(2)}, u32[]{:S(2)}) %collective-permute-start.22) | collective-permute-done | bytes 1048608 | tf_op jit(solution)/shard_map/ppermute | solution.py:348
  131.9 8.1 %product.10.refs_1_ = bf16[256,2048]{1,0:T(8,128)(2,1)} custom-call(s32[17,64]{1,0:T(8,128)} %pad_add_fusion.refs_1_.numbers, bf16[4,3,256,256]{3,2,1,0:T(8,128)(2,1)} %get-tuple-element.18.refs_1_.mine, bf16[4,3,256,256]{3,2,1,0:T(8,128)(2,1)} %collective-permute-done.6.theirs.refs_1_, bf16[32,128,128]{2,1,0:T(8,128)(2,1)} %collective-permute-done.10.refs_4_.refs_0_, ...), custom_call_target="tpu_custom_call" | custom-call | tf_op jit(solution)/shard_map/product/pallas_call | solution.py:188
  140.0 1.3 collective-permute-start.24
  141.3 8.0 %product.11.whole_ref = bf16[256,16384]{1,0:T(8,128)(2,1)} custom-call(s32[17,64]{1,0:T(8,128)} %pad_add_fusion.refs_1_.numbers, bf16[4,3,256,256]{3,2,1,0:T(8,128)(2,1)} %get-tuple-element.18.refs_1_.mine, bf16[4,3,256,256]{3,2,1,0:T(8,128)(2,1)} %collective-permute-done.6.theirs.refs_1_, ...), custom_call_target="tpu_custom_call", output_to_operand_aliasing={{}: (7, {})} | custom-call | tf_op jit(solution)/shard_map/product/pallas_call | solution.py:188
  149.3 2.7 %put.5.whole_ref = bf16[256,16384]{1,0:T(8,128)(2,1)} custom-call(s32[48]{0:T(128)} %copy-done, bf16[256,2048]{1,0:T(8,128)(2,1)} %collective-permute-done.22.refs_1_.piece_ref, bf16[256,16384]{1,0:T(8,128)(2,1)} %product.11.whole_ref), custom_call_target="tpu_custom_call", output_to_operand_aliasing={{}: (2, {})} | custom-call | tf_op jit(solution)/shard_map/put/pallas_call | solution.py:262
  152.1 2.7 %put.6.whole_ref = bf16[256,16384]{1,0:T(8,128)(2,1)} custom-call(s32[48]{0:T(128)} %copy-done, bf16[256,2048]{1,0:T(8,128)(2,1)} %collective-permute-done.25.piece_ref, bf16[256,16384]{1,0:T(8,128)(2,1)} %put.5.whole_ref), custom_call_target="tpu_custom_call", output_to_operand_aliasing={{}: (2, {})} | custom-call | tf_op jit(solution)/shard_map/put/pallas_call | solution.py:262
  155.2 2.7 %put.7 = bf16[256,16384]{1,0:T(8,128)(2,1)} custom-call(s32[48]{0:T(128)} %copy-done, bf16[256,2048]{1,0:T(8,128)(2,1)} %collective-permute-done.24.piece_ref, bf16[256,16384]{1,0:T(8,128)(2,1)} %put.6.whole_ref), custom_call_target="tpu_custom_call", output_to_operand_aliasing={{}: (2, {})} | custom-call | tf_op jit(solution)/shard_map/put/pallas_call | solution.py:262
  (46 shorter events, 1.5 us)
Async XLA Ops:
  3.7 16.0 %collective-permute-start.2 = (bf16[32,128,128]{2,1,0:T(8,128)(2,1)}, bf16[32,128,128]{2,1,0:T(8,128)(2,1)}, u32[]{:S(2)}, u32[]{:S(2)}) collective-permute-start(bf16[32,128,128]{2,1,0:T(8,128)(2,1)} %get-tuple-element.17.refs_0_), channel_id=1, source_target_pairs={{0,2},{1,5},{2,0},{3,7},{4,6},{5,1},{6,4},{7,3},{8,10},{9,13},{10,... | collective-permute-start | bytes 3145736 | tf_op jit(solution)/shard_map/ppermute | solution.py:348
  6.7 50.6 %collective-permute-start.8 = (bf16[32,128,128]{2,1,0:T(8,128)(2,1)}, bf16[32,128,128]{2,1,0:T(8,128)(2,1)}, u32[]{:S(2)}, u32[]{:S(2)}) collective-permute-start(bf16[32,128,128]{2,1,0:T(8,128)(2,1)} %get-tuple-element.17.refs_0_), channel_id=1, source_target_pairs={{0,16},{16,0},{8,24},{24,8},{1,17},{17,1},{9,25},{25,9},{2,18},{18... | collective-permute-start | bytes 3145736 | tf_op jit(solution)/shard_map/ppermute | solution.py:406
  9.2 48.0 %collective-permute-start.7 = (bf16[32,128,128]{2,1,0:T(8,128)(2,1)}, bf16[32,128,128]{2,1,0:T(8,128)(2,1)}, u32[]{:S(2)}, u32[]{:S(2)}) collective-permute-start(bf16[32,128,128]{2,1,0:T(8,128)(2,1)} %get-tuple-element.17.refs_0_), channel_id=1, source_target_pairs={{0,8},{8,0},{16,24},{24,16},{1,9},{9,1},{17,25},{25,17},{2,10},{10... | collective-permute-start | bytes 3145736 | tf_op jit(solution)/shard_map/ppermute | solution.py:406
  11.6 8.1 %collective-permute-start = (s32[4,64]{1,0:T(4,128)S(1)}, s32[4,64]{1,0:T(4,128)S(1)}, u32[]{:S(2)}, u32[]{:S(2)}) collective-permute-start(s32[4,64]{1,0:T(4,128)S(1)} %select_reduce_fusion), channel_id=1, source_target_pairs={{0,2},{1,5},{2,0},{3,7},{4,6},{5,1},{6,4},{7,3},{8,10},{9,13},{10,... | collective-permute-start | bytes 3080 | tf_op jit(solution)/shard_map/ppermute | solution.py:348
  19.7 0.6 copy-start.1
  20.3 13.4 %collective-permute-start.3 = (bf16[1024,256]{1,0:T(8,128)(2,1)}, bf16[1024,256]{1,0:T(8,128)(2,1)}, u32[]{:S(2)}, u32[]{:S(2)}) collective-permute-start(bf16[1024,256]{1,0:T(8,128)(2,1)} %tie.14.refs_0_), channel_id=1, source_target_pairs={{0,2},{1,5},{2,0},{3,7},{4,6},{5,1},{6,4},{7,3},{8,10},{9,13},{10,... | collective-permute-start | bytes 1572872 | tf_op jit(solution)/shard_map/ppermute | solution.py:348
  23.5 21.5 %copy-start = (s32[48]{0:T(128)}, s32[48]{0:T(128)S(1)}, u32[]{:S(2)}) copy-start(s32[48]{0:T(128)S(1)} %dynamic-slice_bitcast_fusion.scalars) | copy-start | bytes 580
  24.3 17.6 %collective-permute-start.4 = (bf16[1024,256]{1,0:T(8,128)(2,1)}, bf16[1024,256]{1,0:T(8,128)(2,1)}, u32[]{:S(2)}, u32[]{:S(2)}) collective-permute-start(bf16[1024,256]{1,0:T(8,128)(2,1)} %tie.14.refs_0_), channel_id=1, source_target_pairs={{0,4},{1,3},{2,6},{3,1},{4,0},{5,7},{6,2},{7,5},{8,12},{9,11},{10,... | collective-permute-start | bytes 1572872 | tf_op jit(solution)/shard_map/ppermute | solution.py:348
  33.7 11.3 %collective-permute-start.5 = (bf16[1024,256]{1,0:T(8,128)(2,1)}, bf16[1024,256]{1,0:T(8,128)(2,1)}, u32[]{:S(2)}, u32[]{:S(2)}) collective-permute-start(bf16[1024,256]{1,0:T(8,128)(2,1)} %collective-permute-done.3.refs_1_), channel_id=1, source_target_pairs={{0,4},{1,3},{2,6},{3,1},{4,0},{5,7},{6,2},{7,5},{8,12},{9,11},{10,... | collective-permute-start | bytes 1572872 | tf_op jit(solution)/shard_map/ppermute | solution.py:348
  39.4 1.2 collective-permute-start.1
  56.7 7.9 %collective-permute-start.6 = (bf16[4,3,256,256]{3,2,1,0:T(8,128)(2,1)}, bf16[4,3,256,256]{3,2,1,0:T(8,128)(2,1)}, u32[]{:S(2)}, u32[]{:S(2)}) collective-permute-start(bf16[4,3,256,256]{3,2,1,0:T(8,128)(2,1)} %get-tuple-element.19), channel_id=1, source_target_pairs={{0,1},{1,0},{2,3},{3,2},{4,5},{5,4},{6,7},{7,6},{8,9},{9,8},{10,11... | collective-permute-start | bytes 4718600 | tf_op jit(solution)/shard_map/ppermute | solution.py:348
  56.7 5.2 %collective-permute-start.9 = (bf16[32,128,128]{2,1,0:T(8,128)(2,1)}, bf16[32,128,128]{2,1,0:T(8,128)(2,1)}, u32[]{:S(2)}, u32[]{:S(2)}) collective-permute-start(bf16[32,128,128]{2,1,0:T(8,128)(2,1)} %get-tuple-element.17.refs_0_), channel_id=1, source_target_pairs={{0,1},{1,0},{2,3},{3,2},{4,5},{5,4},{6,7},{7,6},{8,9},{9,8},{10,11... | collective-permute-start | bytes 3145736 | tf_op jit(solution)/shard_map/ppermute | solution.py:348
  57.3 17.0 %collective-permute-start.11 = (bf16[32,128,128]{2,1,0:T(8,128)(2,1)}, bf16[32,128,128]{2,1,0:T(8,128)(2,1)}, u32[]{:S(2)}, u32[]{:S(2)}) collective-permute-start(bf16[32,128,128]{2,1,0:T(8,128)(2,1)} %tie.15.refs_1_), channel_id=1, source_target_pairs={{0,2},{1,5},{2,0},{3,7},{4,6},{5,1},{6,4},{7,3},{8,10},{9,13},{10,... | collective-permute-start | bytes 3145736 | tf_op jit(solution)/shard_map/ppermute | solution.py:348
  58.5 15.8 %collective-permute-start.14 = (bf16[32,128,128]{2,1,0:T(8,128)(2,1)}, bf16[32,128,128]{2,1,0:T(8,128)(2,1)}, u32[]{:S(2)}, u32[]{:S(2)}) collective-permute-start(bf16[32,128,128]{2,1,0:T(8,128)(2,1)} %tie.19), channel_id=1, source_target_pairs={{8,16},{16,8},{9,17},{17,9},{10,18},{18,10},{11,19},{19,11},{12,20... | collective-permute-start | bytes 3145736 | tf_op jit(solution)/shard_map/ppermute | solution.py:406
  62.0 27.4 %collective-permute-start.15 = (bf16[32,128,128]{2,1,0:T(8,128)(2,1)}, bf16[32,128,128]{2,1,0:T(8,128)(2,1)}, u32[]{:S(2)}, u32[]{:S(2)}) collective-permute-start(bf16[32,128,128]{2,1,0:T(8,128)(2,1)} %tie.16.refs_2_), channel_id=1, source_target_pairs={{8,0},{16,24},{9,1},{17,25},{10,2},{18,26},{11,3},{19,27},{12,4},{... | collective-permute-start | bytes 3145736 | tf_op jit(solution)/shard_map/ppermute | solution.py:406
  63.3 26.1 %collective-permute-start.13 = (bf16[32,128,128]{2,1,0:T(8,128)(2,1)}, bf16[32,128,128]{2,1,0:T(8,128)(2,1)}, u32[]{:S(2)}, u32[]{:S(2)}) collective-permute-start(bf16[32,128,128]{2,1,0:T(8,128)(2,1)} %tie.16.refs_2_), channel_id=1, source_target_pairs={{0,2},{1,5},{2,0},{3,7},{4,6},{5,1},{6,4},{7,3},{8,10},{9,13},{10,... | collective-permute-start | bytes 3145736 | tf_op jit(solution)/shard_map/ppermute | solution.py:348
  73.5 15.9 %collective-permute-start.10 = (bf16[32,128,128]{2,1,0:T(8,128)(2,1)}, bf16[32,128,128]{2,1,0:T(8,128)(2,1)}, u32[]{:S(2)}, u32[]{:S(2)}) collective-permute-start(bf16[32,128,128]{2,1,0:T(8,128)(2,1)} %tie.17.refs_0_), channel_id=1, source_target_pairs={{0,1},{1,0},{2,3},{3,2},{4,5},{5,4},{6,7},{7,6},{8,9},{9,8},{10,11... | collective-permute-start | bytes 3145736 | tf_op jit(solution)/shard_map/ppermute | solution.py:348
  74.2 15.2 %collective-permute-start.12 = (bf16[32,128,128]{2,1,0:T(8,128)(2,1)}, bf16[32,128,128]{2,1,0:T(8,128)(2,1)}, u32[]{:S(2)}, u32[]{:S(2)}) collective-permute-start(bf16[32,128,128]{2,1,0:T(8,128)(2,1)} %tie.18.refs_1_), channel_id=1, source_target_pairs={{0,1},{1,0},{2,3},{3,2},{4,5},{5,4},{6,7},{7,6},{8,9},{9,8},{10,11... | collective-permute-start | bytes 3145736 | tf_op jit(solution)/shard_map/ppermute | solution.py:348
  74.3 29.3 %collective-permute-start.19 = (bf16[32,128,128]{2,1,0:T(8,128)(2,1)}, bf16[32,128,128]{2,1,0:T(8,128)(2,1)}, u32[]{:S(2)}, u32[]{:S(2)}) collective-permute-start(bf16[32,128,128]{2,1,0:T(8,128)(2,1)} %tie.16.refs_2_), channel_id=1, source_target_pairs={{0,1},{1,0},{2,3},{3,2},{4,5},{5,4},{6,7},{7,6},{8,9},{9,8},{10,11... | collective-permute-start | bytes 3145736 | tf_op jit(solution)/shard_map/ppermute | solution.py:348
  89.4 14.2 %collective-permute-start.18 = (bf16[32,128,128]{2,1,0:T(8,128)(2,1)}, bf16[32,128,128]{2,1,0:T(8,128)(2,1)}, u32[]{:S(2)}, u32[]{:S(2)}) collective-permute-start(bf16[32,128,128]{2,1,0:T(8,128)(2,1)} %tie.15.refs_1_), channel_id=1, source_target_pairs={{0,1},{1,0},{2,3},{3,2},{4,5},{5,4},{6,7},{7,6},{8,9},{9,8},{10,11... | collective-permute-start | bytes 3145736 | tf_op jit(solution)/shard_map/ppermute | solution.py:348
  92.4 11.3 %collective-permute-start.20 = (bf16[32,128,128]{2,1,0:T(8,128)(2,1)}, bf16[32,128,128]{2,1,0:T(8,128)(2,1)}, u32[]{:S(2)}, u32[]{:S(2)}) collective-permute-start(bf16[32,128,128]{2,1,0:T(8,128)(2,1)} %choose.1.refs_0_), channel_id=1, source_target_pairs={{0,1},{1,0},{2,3},{3,2},{4,5},{5,4},{6,7},{7,6},{8,9},{9,8},{10,11... | collective-permute-start | bytes 3145736 | tf_op jit(solution)/shard_map/ppermute | solution.py:348
  92.9 21.2 %collective-permute-start.17 = (bf16[32,128,128]{2,1,0:T(8,128)(2,1)}, bf16[32,128,128]{2,1,0:T(8,128)(2,1)}, u32[]{:S(2)}, u32[]{:S(2)}) collective-permute-start(bf16[32,128,128]{2,1,0:T(8,128)(2,1)} %choose.1.refs_0_), channel_id=1, source_target_pairs={{0,2},{1,5},{2,0},{3,7},{4,6},{5,1},{6,4},{7,3},{8,10},{9,13},{10,... | collective-permute-start | bytes 3145736 | tf_op jit(solution)/shard_map/ppermute | solution.py:348
  101.5 25.5 %collective-permute-start.23 = (bf16[256,2048]{1,0:T(8,128)(2,1)}, bf16[256,2048]{1,0:T(8,128)(2,1)}, u32[]{:S(2)}, u32[]{:S(2)}) collective-permute-start(bf16[256,2048]{1,0:T(8,128)(2,1)} %get-tuple-element.21.refs_1_), channel_id=1, source_target_pairs={{0,4},{1,3},{2,6},{3,1},{4,0},{5,7},{6,2},{7,5},{8,12},{9,11},{10,... | collective-permute-start | bytes 3145736 | tf_op jit(solution)/shard_map/ppermute | solution.py:348
  114.2 15.6 %collective-permute-start.21 = (bf16[32,128,128]{2,1,0:T(8,128)(2,1)}, bf16[32,128,128]{2,1,0:T(8,128)(2,1)}, u32[]{:S(2)}, u32[]{:S(2)}) collective-permute-start(bf16[32,128,128]{2,1,0:T(8,128)(2,1)} %tie.23.refs_3_), channel_id=1, source_target_pairs={{0,1},{1,0},{2,3},{3,2},{4,5},{5,4},{6,7},{7,6},{8,9},{9,8},{10,11... | collective-permute-start | bytes 3145736 | tf_op jit(solution)/shard_map/ppermute | solution.py:348
  114.2 17.7 %collective-permute-start.22 = (bf16[256,2048]{1,0:T(8,128)(2,1)}, bf16[256,2048]{1,0:T(8,128)(2,1)}, u32[]{:S(2)}, u32[]{:S(2)}) collective-permute-start(bf16[256,2048]{1,0:T(8,128)(2,1)} %get-tuple-element.23.refs_1_), channel_id=1, source_target_pairs={{0,2},{1,5},{2,0},{3,7},{4,6},{5,1},{6,4},{7,3},{8,10},{9,13},{10,... | collective-permute-start | bytes 3145736 | tf_op jit(solution)/shard_map/ppermute | solution.py:348
  115.1 16.8 %collective-permute-start.16 = (bf16[32,128,128]{2,1,0:T(8,128)(2,1)}, bf16[32,128,128]{2,1,0:T(8,128)(2,1)}, u32[]{:S(2)}, u32[]{:S(2)}) collective-permute-start(bf16[32,128,128]{2,1,0:T(8,128)(2,1)} %tie.22.refs_2_), channel_id=1, source_target_pairs={{0,1},{1,0},{2,3},{3,2},{4,5},{5,4},{6,7},{7,6},{8,9},{9,8},{10,11... | collective-permute-start | bytes 3145736 | tf_op jit(solution)/shard_map/ppermute | solution.py:348
  125.6 26.5 %collective-permute-start.25 = (bf16[256,2048]{1,0:T(8,128)(2,1)}, bf16[256,2048]{1,0:T(8,128)(2,1)}, u32[]{:S(2)}, u32[]{:S(2)}) collective-permute-start(bf16[256,2048]{1,0:T(8,128)(2,1)} %get-tuple-element.26), channel_id=1, source_target_pairs={{0,4},{1,3},{2,6},{3,1},{4,0},{5,7},{6,2},{7,5},{8,12},{9,11},{10,... | collective-permute-start | bytes 3145736 | tf_op jit(solution)/shard_map/ppermute | solution.py:348
  140.0 15.2 %collective-permute-start.24 = (bf16[256,2048]{1,0:T(8,128)(2,1)}, bf16[256,2048]{1,0:T(8,128)(2,1)}, u32[]{:S(2)}, u32[]{:S(2)}) collective-permute-start(bf16[256,2048]{1,0:T(8,128)(2,1)} %product.10.refs_1_), channel_id=1, source_target_pairs={{0,2},{1,5},{2,0},{3,7},{4,6},{5,1},{6,4},{7,3},{8,10},{9,13},{10,... | collective-permute-start | bytes 3145736 | tf_op jit(solution)/shard_map/ppermute | solution.py:348

commit v11 on v8

--- a/solution.py
+++ b/solution.py
@@ -251,28 +251,44 @@
     )(scalars, a, b)
 
 
-def put_body(scalars, piece_ref, whole_ref, out_ref):
-    out_ref[...] = piece_ref[...]
-
-
-def put(piece, whole, scalars, at):
-    m, n = piece.shape
+def put_body(scalars, *refs):
+    pieces, out_ref = refs[:-2], refs[-1]
+    for p, piece in enumerate(pieces):
+
+        @pl.when(pl.program_id(0) == p)
+        def _():
+            out_ref[...] = piece[...]
+
+
+def put(pieces, whole, scalars, places):
+    m, n = pieces[0].shape
     width = min(2 * MM_COLS, n)
     steps = n // width
+
+    def piece_at(p):
+        return lambda i, j, s: (0, jnp.where(i == p, j, jnp.where(i < p, 0, steps - 1)))
+
+    def out_at(i, j, s):
+        place = s[places[0]]
+        for p in range(1, len(places)):
+            place = jnp.where(i == p, s[places[p]], place)
+        return (0, place * steps + j)
+
     return pl.pallas_call(
         put_body,
         out_shape=jax.ShapeDtypeStruct(whole.shape, whole.dtype),
         grid_spec=pltpu.PrefetchScalarGridSpec(
             num_scalar_prefetch=1,
-            grid=(steps,),
-            in_specs=[pl.BlockSpec((m, width), lambda i, s: (0, i)), pl.BlockSpec(memory_space=pltpu.HBM)],
-            out_specs=pl.BlockSpec((m, width), lambda i, s: (0, s[at] * steps + i)),
+            grid=(len(pieces), steps),
+            in_specs=[pl.BlockSpec((m, width), piece_at(p)) for p in range(len(pieces))]
+            + [pl.BlockSpec(memory_space=pltpu.HBM)],
+            out_specs=pl.BlockSpec((m, width), out_at),
         ),
-        input_output_aliases={2: 0},
+        input_output_aliases={1 + len(pieces): 0},
         compiler_params=params(),
         cost_estimate=NOTHING,
         name="put",
-    )(scalars, piece, whole)
+    )(scalars, *pieces, whole)
 
 
 def col_index(ie, ia, ib, core):
@@ -475,7 +491,8 @@
     arrived = []
     for turn_at, q in enumerate((0, 2, 1, 3)):
         if turn_at == 3:
-            theirs_next[-1] = tie(theirs_next[-1], *arrived[0], *arrived[1])
+            out = put(arrived[0], out, scalars, arrive_at[0])
+            theirs_next[-1] = tie(theirs_next[-1], *arrived[1], out)
         places = (rows_at[q], mine_at, theirs_at)
         blocks = (slots, nexts, theirs_of, theirs_next)[q]
         if q == 0 and rows > 1:
@@ -501,9 +518,8 @@
                 theirs_next.append(permute(nexts[len(theirs_next)], across))
     own["whole"] = tie(out, pieces[0])
     (out,) = call((core_at, picks_at[q][:1], *places, tiles, 4 * rows), **own)
-    for got, q in zip(arrived, (0, 2, 1, 3)):
-        for piece, place in zip(got, arrive_at[q]):
-            out = put(piece, out, scalars, place)
+    out = put(arrived[1] + arrived[2], out, scalars, arrive_at[2] + arrive_at[1])
+    out = put(arrived[3], out, scalars, arrive_at[3])
     return out
 
 

time: 156 us -> 155 us (level)
    pallas_call x4 -> x3, Pallas kernels: 10.9 us -> 10.2 us  [put(): pl.pallas_call(put_body, out_shape=jax.ShapeDtypeStruct(whole.shape, whol...]
  transfers between devices with their start and end apart: 26 -> 26, of which waited for: 8 -> 9; matrix products, arithmetic and copies ran while one was open for 5% -> 5% of each run, Pallas kernels for 49% -> 49%
where the time goes in v11:
time: 155 us; the launch traced here: 153 us
  Pallas kernels  82 us (53%)
  waiting for transfers between devices  39.1 us (25%)
  starting transfers between devices  24.4 us (16%)
  other arithmetic  6.56 us (4%)
    pallas_call x6, Pallas kernels, product(): pl.pallas_call(functools.partial(product_body, at, acc is not None, whole...  53.4 us
    ppermute x4, waiting for transfers between devices, line_phase(): lax.ppermute(own if source < 0 else moved[source], 'row', pairs)  26.3 us
    ppermute x22, starting transfers between devices, permute(): lax.ppermute(value, 'col', [(col_index(*at), col_index(*moved_to(*at))) f...  17.3 us
    ppermute x22, waiting for transfers between devices, permute(): lax.ppermute(value, 'col', [(col_index(*at), col_index(*moved_to(*at))) f...  12.9 us
    pallas_call x1, Pallas kernels, pick_rows(): pl.pallas_call(functools.partial(pick_body, first, count, capacity), out_...  11.8 us
    pallas_call x3, Pallas kernels, put(): pl.pallas_call(put_body, out_shape=jax.ShapeDtypeStruct(whole.shape, whol...  10.2 us
    ppermute x4, starting transfers between devices, line_phase(): lax.ppermute(own if source < 0 else moved[source], 'row', pairs)  7.1 us
    pallas_call x1, Pallas kernels, pack(): pl.pallas_call(pack_body, out_shape=[jax.ShapeDtypeStruct((count, TILE, T...  3.67 us
  transfers between devices with their start and end apart: 26, of which 9 were waited for; matrix products, arithmetic and copies ran while one was open for 5% of the time, Pallas kernels for 49%

profile of v11, /device:TPU:0, one launch (start us, length us, event | category | flops | bytes accessed | tf_op | source)
XLA Modules:
  0.0 153.2 jit_solution(14102775049465281311)
XLA Ops:
  0.0 3.7 %pack_tiles.1 = (bf16[32,128,128]{2,1,0:T(8,128)(2,1)}, bf16[32,128,128]{2,1,0:T(8,128)(2,1)}, bf16[1024,256]{1,0:T(8,128)(2,1)}) custom-call(s32[1]{0:T(128)} %bitcast.6.row, s32[4,32]{1,0:T(4,128)} %bitcast.31, s32[2,8]{1,0:T(2,128)} %bitcast.33, bf16[512,2048]{1,0:T(8,128)(2,1)} %src_ref.1, bf16[1024,256]{1,0:T(8,128)(2,1)} %amp_ref.1), custom_call_target="tpu_custom_call" | custom-call | tf_op jit(solution)/shard_map/pack_tiles/pallas_call | solution.py:39
  3.7 3.0 %collective-permute-start.3 = (bf16[1024,256]{1,0:T(8,128)(2,1)}, bf16[1024,256]{1,0:T(8,128)(2,1)}, u32[]{:S(2)}, u32[]{:S(2)}) collective-permute-start(bf16[1024,256]{1,0:T(8,128)(2,1)} %get-tuple-element.16.refs_0_), channel_id=1, source_target_pairs={{0,4},{1,3},{2,6},{3,1},{4,0},{5,7},{6,2},{7,5},{8,12},{9,11},{10,... | collective-permute-start | bytes 1572872 | tf_op jit(solution)/shard_map/ppermute | solution.py:364
  6.6 1.5 collective-permute-start.2
  8.1 2.6 %collective-permute-start.8 = (bf16[32,128,128]{2,1,0:T(8,128)(2,1)}, bf16[32,128,128]{2,1,0:T(8,128)(2,1)}, u32[]{:S(2)}, u32[]{:S(2)}) collective-permute-start(bf16[32,128,128]{2,1,0:T(8,128)(2,1)} %get-tuple-element.19.refs_0_), channel_id=1, source_target_pairs={{0,16},{16,0},{8,24},{24,8},{1,17},{17,1},{9,25},{25,9},{2,18},{18... | collective-permute-start | bytes 3145736 | tf_op jit(solution)/shard_map/ppermute | solution.py:422
  10.7 1.6 %collective-permute-start.7 = (bf16[32,128,128]{2,1,0:T(8,128)(2,1)}, bf16[32,128,128]{2,1,0:T(8,128)(2,1)}, u32[]{:S(2)}, u32[]{:S(2)}) collective-permute-start(bf16[32,128,128]{2,1,0:T(8,128)(2,1)} %get-tuple-element.19.refs_0_), channel_id=1, source_target_pairs={{0,8},{8,0},{16,24},{24,16},{1,9},{9,1},{17,25},{25,17},{2,10},{10... | collective-permute-start | bytes 3145736 | tf_op jit(solution)/shard_map/ppermute | solution.py:422
  12.3 0.8 select_reduce_fusion
  13.1 0.6 collective-permute-start
  13.7 0.7 fusion.3
  14.4 2.3 %reduce-window.6 = s32[8,8,128]{2,1,0:T(8,128)S(1)} reduce-window(s32[8,8,128]{2,1,0:T(8,128)S(1)} %fusion.3, s32[]{:T(128)} %constant.20.clone.1), window={size=1x1x128 pad=0_0x0_0x127_0}, to_apply=%region_1.2 | reduce-window | flops 1040384 | bytes 65540 | tf_op jit(solution)/shard_map/reduce-window
  16.6 0.3 slice_reduce_fusion
  17.1 0.7 fusion.2
  17.9 1.0 collective-permute-done.2.refs_1_
  18.8 1.8 %collective-permute-start.4 = (bf16[1024,256]{1,0:T(8,128)(2,1)}, bf16[1024,256]{1,0:T(8,128)(2,1)}, u32[]{:S(2)}, u32[]{:S(2)}) collective-permute-start(bf16[1024,256]{1,0:T(8,128)(2,1)} %collective-permute-done.2.refs_1_), channel_id=1, source_target_pairs={{0,4},{1,3},{2,6},{3,1},{4,0},{5,7},{6,2},{7,5},{8,12},{9,11},{10,... | collective-permute-start | bytes 1572872 | tf_op jit(solution)/shard_map/ppermute | solution.py:364
  20.6 1.3 multiply_add_fusion.refs_0_
  21.9 0.7 dynamic-slice_bitcast_fusion.scalars
  22.7 1.1 collective-permute-done.1
  23.8 0.6 pad_add_fusion.refs_1_.numbers
  24.4 3.9 %collective-permute-done.4.refs_3_ = bf16[1024,256]{1,0:T(8,128)(2,1)} collective-permute-done((bf16[1024,256]{1,0:T(8,128)(2,1)}, bf16[1024,256]{1,0:T(8,128)(2,1)}, u32[]{:S(2)}, u32[]{:S(2)}) %collective-permute-start.4) | collective-permute-done | bytes 524320 | tf_op jit(solution)/shard_map/ppermute | solution.py:364
  28.3 11.8 %pick_rows.1 = (bf16[4,3,256,256]{3,2,1,0:T(8,128)(2,1)}, bf16[4,3,256,256]{3,2,1,0:T(8,128)(2,1)}) custom-call(s32[48]{0:T(128)} %copy-done, s32[1,1024]{1,0:T(1,128)} %bitcast.28, bf16[1024,256]{1,0:T(8,128)(2,1)} %get-tuple-element.16.refs_0_, bf16[1024,256]{1,0:T(8,128)(2,1)} %collective-permute-done.2.refs_1_, ...), custom_call_target="tpu_custom_call" | custom-call | tf_op jit(solution)/shard_map/pick_rows/pallas_call | solution.py:78
  40.3 0.4 collective-permute-start.9
  40.7 1.7 %collective-permute-start.6 = (bf16[32,128,128]{2,1,0:T(8,128)(2,1)}, bf16[32,128,128]{2,1,0:T(8,128)(2,1)}, u32[]{:S(2)}, u32[]{:S(2)}) collective-permute-start(bf16[32,128,128]{2,1,0:T(8,128)(2,1)} %get-tuple-element.19.refs_0_), channel_id=1, source_target_pairs={{0,2},{1,5},{2,0},{3,7},{4,6},{5,1},{6,4},{7,3},{8,10},{9,13},{10,... | collective-permute-start | bytes 3145736 | tf_op jit(solution)/shard_map/ppermute | solution.py:364
  42.4 13.9 %collective-permute-done.8.refs_2_.refs_0_.refs_1_ = bf16[32,128,128]{2,1,0:T(8,128)(2,1)} collective-permute-done((bf16[32,128,128]{2,1,0:T(8,128)(2,1)}, bf16[32,128,128]{2,1,0:T(8,128)(2,1)}, u32[]{:S(2)}, u32[]{:S(2)}) %collective-permute-start.8) | collective-permute-done | bytes 1048608 | tf_op jit(solution)/shard_map/ppermute | solution.py:422
  56.3 0.2 collective-permute-done.7.refs_0_
  56.5 0.5 collective-permute-start.11
  57.0 1.6 %collective-permute-start.14 = (bf16[32,128,128]{2,1,0:T(8,128)(2,1)}, bf16[32,128,128]{2,1,0:T(8,128)(2,1)}, u32[]{:S(2)}, u32[]{:S(2)}) collective-permute-start(bf16[32,128,128]{2,1,0:T(8,128)(2,1)} %tie.17), channel_id=1, source_target_pairs={{8,16},{16,8},{9,17},{17,9},{10,18},{18,10},{11,19},{19,11},{12,20... | collective-permute-start | bytes 3145736 | tf_op jit(solution)/shard_map/ppermute | solution.py:422
  58.6 1.3 collective-permute-start.15
  59.9 1.6 %collective-permute-start.13 = (bf16[32,128,128]{2,1,0:T(8,128)(2,1)}, bf16[32,128,128]{2,1,0:T(8,128)(2,1)}, u32[]{:S(2)}, u32[]{:S(2)}) collective-permute-start(bf16[32,128,128]{2,1,0:T(8,128)(2,1)} %tie.14.refs_2_), channel_id=1, source_target_pairs={{0,2},{1,5},{2,0},{3,7},{4,6},{5,1},{6,4},{7,3},{8,10},{9,13},{10,... | collective-permute-start | bytes 3145736 | tf_op jit(solution)/shard_map/ppermute | solution.py:364
  61.5 9.0 %product.6.refs_1_.refs_3_ = f32[512,2048]{1,0:T(8,128)} custom-call(s32[17,64]{1,0:T(8,128)} %pad_add_fusion.refs_1_.numbers, bf16[4,3,256,256]{3,2,1,0:T(8,128)(2,1)} %get-tuple-element.17.refs_1_.mine, bf16[4,3,256,256]{3,2,1,0:T(8,128)(2,1)} %collective-permute-done.5.theirs.refs_1_, bf16[32,128,128]{2,1,0:T(8,128)(2,1)} %get-tuple-element.19.refs_0_, ...), custom_call_target="tpu_custom_call" | custom-call | tf_op jit(solution)/shard_map/product/pallas_call | solution.py:188
  70.6 1.0 collective-permute-done.11.refs_0_
  71.6 0.5 collective-permute-start.18
  72.1 12.2 %collective-permute-done.15.refs_6_.refs_0_ = bf16[32,128,128]{2,1,0:T(8,128)(2,1)} collective-permute-done((bf16[32,128,128]{2,1,0:T(8,128)(2,1)}, bf16[32,128,128]{2,1,0:T(8,128)(2,1)}, u32[]{:S(2)}, u32[]{:S(2)}) %collective-permute-start.15) | collective-permute-done | bytes 1048608 | tf_op jit(solution)/shard_map/ppermute | solution.py:422
  84.3 2.9 %choose.1.refs_0_ = bf16[32,128,128]{2,1,0:T(8,128)(2,1)} custom-call(s32[48]{0:T(128)} %copy-done, bf16[32,128,128]{2,1,0:T(8,128)(2,1)} %tie.18.refs_6_.a_ref, bf16[32,128,128]{2,1,0:T(8,128)(2,1)} %tie.19.b_ref), custom_call_target="tpu_custom_call" | custom-call | tf_op jit(solution)/shard_map/choose/pallas_call | solution.py:242
  87.2 0.6 collective-permute-start.20
  87.8 0.4 collective-permute-start.17
  88.2 7.3 %product.7 = (bf16[256,16384]{1,0:T(8,128)(2,1)}, bf16[256,2048]{1,0:T(8,128)(2,1)}) custom-call(s32[17,64]{1,0:T(8,128)} %pad_add_fusion.refs_1_.numbers, bf16[4,3,256,256]{3,2,1,0:T(8,128)(2,1)} %get-tuple-element.17.refs_1_.mine, bf16[4,3,256,256]{3,2,1,0:T(8,128)(2,1)} %collective-permute-done.5.theirs.refs_1_, bf16[32,128,128]{2,1,0:T(8,128)(2,1)} %choose.1.refs_0_, ...), custom_call_target="tpu_custom_call" | custom-call | tf_op jit(solution)/shard_map/product/pallas_call | solution.py:188
  95.6 1.7 %collective-permute-start.23 = (bf16[256,2048]{1,0:T(8,128)(2,1)}, bf16[256,2048]{1,0:T(8,128)(2,1)}, u32[]{:S(2)}, u32[]{:S(2)}) collective-permute-start(bf16[256,2048]{1,0:T(8,128)(2,1)} %get-tuple-element.21.refs_1_), channel_id=1, source_target_pairs={{0,4},{1,3},{2,6},{3,1},{4,0},{5,7},{6,2},{7,5},{8,12},{9,11},{10,... | collective-permute-start | bytes 3145736 | tf_op jit(solution)/shard_map/ppermute | solution.py:364
  97.3 10.5 %product.8 = (bf16[256,16384]{1,0:T(8,128)(2,1)}, bf16[256,2048]{1,0:T(8,128)(2,1)}) custom-call(s32[17,64]{1,0:T(8,128)} %pad_add_fusion.refs_1_.numbers, bf16[4,3,256,256]{3,2,1,0:T(8,128)(2,1)} %get-tuple-element.17.refs_1_.mine, bf16[4,3,256,256]{3,2,1,0:T(8,128)(2,1)} %collective-permute-done.5.theirs.refs_1_, ...), custom_call_target="tpu_custom_call", output_to_operand_aliasing={{0}: (7, {})} | custom-call | tf_op jit(solution)/shard_map/product/pallas_call | solution.py:188
  107.9 1.6 %collective-permute-start.22 = (bf16[256,2048]{1,0:T(8,128)(2,1)}, bf16[256,2048]{1,0:T(8,128)(2,1)}, u32[]{:S(2)}, u32[]{:S(2)}) collective-permute-start(bf16[256,2048]{1,0:T(8,128)(2,1)} %get-tuple-element.23.refs_1_), channel_id=1, source_target_pairs={{0,2},{1,5},{2,0},{3,7},{4,6},{5,1},{6,4},{7,3},{8,10},{9,13},{10,... | collective-permute-start | bytes 3145736 | tf_op jit(solution)/shard_map/ppermute | solution.py:364
  109.4 10.5 %product.9 = (bf16[256,16384]{1,0:T(8,128)(2,1)}, bf16[256,2048]{1,0:T(8,128)(2,1)}) custom-call(s32[17,64]{1,0:T(8,128)} %pad_add_fusion.refs_1_.numbers, bf16[4,3,256,256]{3,2,1,0:T(8,128)(2,1)} %get-tuple-element.17.refs_1_.mine, bf16[4,3,256,256]{3,2,1,0:T(8,128)(2,1)} %collective-permute-done.5.theirs.refs_1_, ...), custom_call_target="tpu_custom_call", output_to_operand_aliasing={{0}: (7, {})} | custom-call | tf_op jit(solution)/shard_map/product/pallas_call | solution.py:188
  119.9 0.7 collective-permute-start.25
  120.7 2.7 %put.3.refs_2_.refs_0_ = bf16[256,16384]{1,0:T(8,128)(2,1)} custom-call(s32[48]{0:T(128)} %copy-done, bf16[256,2048]{1,0:T(8,128)(2,1)} %collective-permute-done.23.refs_0_, bf16[256,16384]{1,0:T(8,128)(2,1)} %get-tuple-element.25.refs_1_), custom_call_target="tpu_custom_call", output_to_operand_aliasing={{}: (2, {})} | custom-call | tf_op jit(solution)/shard_map/put/pallas_call | solution.py:277
  123.4 3.9 %collective-permute-done.22.refs_1_.refs_0_ = bf16[256,2048]{1,0:T(8,128)(2,1)} collective-permute-done((bf16[256,2048]{1,0:T(8,128)(2,1)}, bf16[256,2048]{1,0:T(8,128)(2,1)}, u32[]{:S(2)}, u32[]{:S(2)}) %collective-permute-start.22) | collective-permute-done | bytes 1048608 | tf_op jit(solution)/shard_map/ppermute | solution.py:364
  127.3 8.1 %product.10.refs_1_ = bf16[256,2048]{1,0:T(8,128)(2,1)} custom-call(s32[17,64]{1,0:T(8,128)} %pad_add_fusion.refs_1_.numbers, bf16[4,3,256,256]{3,2,1,0:T(8,128)(2,1)} %get-tuple-element.17.refs_1_.mine, bf16[4,3,256,256]{3,2,1,0:T(8,128)(2,1)} %collective-permute-done.5.theirs.refs_1_, bf16[32,128,128]{2,1,0:T(8,128)(2,1)} %collective-permute-done.10.refs_4_.refs_0_, ...), custom_call_target="tpu_custom_call" | custom-call | tf_op jit(solution)/shard_map/product/pallas_call | solution.py:188
  135.3 0.4 collective-permute-start.24
  135.8 8.0 %product.11.refs_2_ = bf16[256,16384]{1,0:T(8,128)(2,1)} custom-call(s32[17,64]{1,0:T(8,128)} %pad_add_fusion.refs_1_.numbers, bf16[4,3,256,256]{3,2,1,0:T(8,128)(2,1)} %get-tuple-element.17.refs_1_.mine, bf16[4,3,256,256]{3,2,1,0:T(8,128)(2,1)} %collective-permute-done.5.theirs.refs_1_, ...), custom_call_target="tpu_custom_call", output_to_operand_aliasing={{}: (7, {})} | custom-call | tf_op jit(solution)/shard_map/product/pallas_call | solution.py:188
  143.8 4.8 %put.4.refs_1_ = bf16[256,16384]{1,0:T(8,128)(2,1)} custom-call(s32[48]{0:T(128)} %copy-done, bf16[256,2048]{1,0:T(8,128)(2,1)} %collective-permute-done.22.refs_1_.refs_0_, bf16[256,2048]{1,0:T(8,128)(2,1)} %collective-permute-done.25.refs_1_, bf16[256,16384]{1,0:T(8,128)(2,1)} %product.11.refs_2_), custom_call_target="tpu_custom_call", output_to_operand_aliasing={{}: (3, {})} | custom-call | tf_op jit(solution)/shard_map/put/pallas_call | solution.py:277
  148.6 1.9 %collective-permute-done.24.refs_0_ = bf16[256,2048]{1,0:T(8,128)(2,1)} collective-permute-done((bf16[256,2048]{1,0:T(8,128)(2,1)}, bf16[256,2048]{1,0:T(8,128)(2,1)}, u32[]{:S(2)}, u32[]{:S(2)}) %collective-permute-start.24) | collective-permute-done | bytes 1048608 | tf_op jit(solution)/shard_map/ppermute | solution.py:364
  150.5 2.7 %put.5 = bf16[256,16384]{1,0:T(8,128)(2,1)} custom-call(s32[48]{0:T(128)} %copy-done, bf16[256,2048]{1,0:T(8,128)(2,1)} %collective-permute-done.24.refs_0_, bf16[256,16384]{1,0:T(8,128)(2,1)} %put.4.refs_1_), custom_call_target="tpu_custom_call", output_to_operand_aliasing={{}: (2, {})} | custom-call | tf_op jit(solution)/shard_map/put/pallas_call | solution.py:277
  (42 shorter events, 0.7 us)
Async XLA Ops:
  3.7 20.8 %collective-permute-start.3 = (bf16[1024,256]{1,0:T(8,128)(2,1)}, bf16[1024,256]{1,0:T(8,128)(2,1)}, u32[]{:S(2)}, u32[]{:S(2)}) collective-permute-start(bf16[1024,256]{1,0:T(8,128)(2,1)} %get-tuple-element.16.refs_0_), channel_id=1, source_target_pairs={{0,4},{1,3},{2,6},{3,1},{4,0},{5,7},{6,2},{7,5},{8,12},{9,11},{10,... | collective-permute-start | bytes 1572872 | tf_op jit(solution)/shard_map/ppermute | solution.py:364
  6.6 12.2 %collective-permute-start.2 = (bf16[1024,256]{1,0:T(8,128)(2,1)}, bf16[1024,256]{1,0:T(8,128)(2,1)}, u32[]{:S(2)}, u32[]{:S(2)}) collective-permute-start(bf16[1024,256]{1,0:T(8,128)(2,1)} %get-tuple-element.16.refs_0_), channel_id=1, source_target_pairs={{0,2},{1,5},{2,0},{3,7},{4,6},{5,1},{6,4},{7,3},{8,10},{9,13},{10,... | collective-permute-start | bytes 1572872 | tf_op jit(solution)/shard_map/ppermute | solution.py:364
  8.1 48.1 %collective-permute-start.8 = (bf16[32,128,128]{2,1,0:T(8,128)(2,1)}, bf16[32,128,128]{2,1,0:T(8,128)(2,1)}, u32[]{:S(2)}, u32[]{:S(2)}) collective-permute-start(bf16[32,128,128]{2,1,0:T(8,128)(2,1)} %get-tuple-element.19.refs_0_), channel_id=1, source_target_pairs={{0,16},{16,0},{8,24},{24,8},{1,17},{17,1},{9,25},{25,9},{2,18},{18... | collective-permute-start | bytes 3145736 | tf_op jit(solution)/shard_map/ppermute | solution.py:422
  10.7 45.7 %collective-permute-start.7 = (bf16[32,128,128]{2,1,0:T(8,128)(2,1)}, bf16[32,128,128]{2,1,0:T(8,128)(2,1)}, u32[]{:S(2)}, u32[]{:S(2)}) collective-permute-start(bf16[32,128,128]{2,1,0:T(8,128)(2,1)} %get-tuple-element.19.refs_0_), channel_id=1, source_target_pairs={{0,8},{8,0},{16,24},{24,16},{1,9},{9,1},{17,25},{25,17},{2,10},{10... | collective-permute-start | bytes 3145736 | tf_op jit(solution)/shard_map/ppermute | solution.py:422
  13.1 9.5 %collective-permute-start = (s32[4,64]{1,0:T(4,128)S(1)}, s32[4,64]{1,0:T(4,128)S(1)}, u32[]{:S(2)}, u32[]{:S(2)}) collective-permute-start(s32[4,64]{1,0:T(4,128)S(1)} %select_reduce_fusion), channel_id=1, source_target_pairs={{0,2},{1,5},{2,0},{3,7},{4,6},{5,1},{6,4},{7,3},{8,10},{9,13},{10,... | collective-permute-start | bytes 3080 | tf_op jit(solution)/shard_map/ppermute | solution.py:364
  18.8 9.5 %collective-permute-start.4 = (bf16[1024,256]{1,0:T(8,128)(2,1)}, bf16[1024,256]{1,0:T(8,128)(2,1)}, u32[]{:S(2)}, u32[]{:S(2)}) collective-permute-start(bf16[1024,256]{1,0:T(8,128)(2,1)} %collective-permute-done.2.refs_1_), channel_id=1, source_target_pairs={{0,4},{1,3},{2,6},{3,1},{4,0},{5,7},{6,2},{7,5},{8,12},{9,11},{10,... | collective-permute-start | bytes 1572872 | tf_op jit(solution)/shard_map/ppermute | solution.py:364
  22.6 5.8 %copy-start = (s32[48]{0:T(128)}, s32[48]{0:T(128)S(1)}, u32[]{:S(2)}) copy-start(s32[48]{0:T(128)S(1)} %dynamic-slice_bitcast_fusion.scalars) | copy-start | bytes 580
  22.6 1.2 collective-permute-start.1
  40.1 21.3 %collective-permute-start.5 = (bf16[4,3,256,256]{3,2,1,0:T(8,128)(2,1)}, bf16[4,3,256,256]{3,2,1,0:T(8,128)(2,1)}, u32[]{:S(2)}, u32[]{:S(2)}) collective-permute-start(bf16[4,3,256,256]{3,2,1,0:T(8,128)(2,1)} %get-tuple-element.18), channel_id=1, source_target_pairs={{0,1},{1,0},{2,3},{3,2},{4,5},{5,4},{6,7},{7,6},{8,9},{9,8},{10,11... | collective-permute-start | bytes 4718600 | tf_op jit(solution)/shard_map/ppermute | solution.py:364
  40.3 18.3 %collective-permute-start.9 = (bf16[32,128,128]{2,1,0:T(8,128)(2,1)}, bf16[32,128,128]{2,1,0:T(8,128)(2,1)}, u32[]{:S(2)}, u32[]{:S(2)}) collective-permute-start(bf16[32,128,128]{2,1,0:T(8,128)(2,1)} %get-tuple-element.19.refs_0_), channel_id=1, source_target_pairs={{0,1},{1,0},{2,3},{3,2},{4,5},{5,4},{6,7},{7,6},{8,9},{9,8},{10,11... | collective-permute-start | bytes 3145736 | tf_op jit(solution)/shard_map/ppermute | solution.py:364
  40.7 18.0 %collective-permute-start.6 = (bf16[32,128,128]{2,1,0:T(8,128)(2,1)}, bf16[32,128,128]{2,1,0:T(8,128)(2,1)}, u32[]{:S(2)}, u32[]{:S(2)}) collective-permute-start(bf16[32,128,128]{2,1,0:T(8,128)(2,1)} %get-tuple-element.19.refs_0_), channel_id=1, source_target_pairs={{0,2},{1,5},{2,0},{3,7},{4,6},{5,1},{6,4},{7,3},{8,10},{9,13},{10,... | collective-permute-start | bytes 3145736 | tf_op jit(solution)/shard_map/ppermute | solution.py:364
  56.5 15.1 %collective-permute-start.11 = (bf16[32,128,128]{2,1,0:T(8,128)(2,1)}, bf16[32,128,128]{2,1,0:T(8,128)(2,1)}, u32[]{:S(2)}, u32[]{:S(2)}) collective-permute-start(bf16[32,128,128]{2,1,0:T(8,128)(2,1)} %tie.13.refs_1_), channel_id=1, source_target_pairs={{0,2},{1,5},{2,0},{3,7},{4,6},{5,1},{6,4},{7,3},{8,10},{9,13},{10,... | collective-permute-start | bytes 3145736 | tf_op jit(solution)/shard_map/ppermute | solution.py:364
  57.0 14.6 %collective-permute-start.14 = (bf16[32,128,128]{2,1,0:T(8,128)(2,1)}, bf16[32,128,128]{2,1,0:T(8,128)(2,1)}, u32[]{:S(2)}, u32[]{:S(2)}) collective-permute-start(bf16[32,128,128]{2,1,0:T(8,128)(2,1)} %tie.17), channel_id=1, source_target_pairs={{8,16},{16,8},{9,17},{17,9},{10,18},{18,10},{11,19},{19,11},{12,20... | collective-permute-start | bytes 3145736 | tf_op jit(solution)/shard_map/ppermute | solution.py:422
  58.6 25.6 %collective-permute-start.15 = (bf16[32,128,128]{2,1,0:T(8,128)(2,1)}, bf16[32,128,128]{2,1,0:T(8,128)(2,1)}, u32[]{:S(2)}, u32[]{:S(2)}) collective-permute-start(bf16[32,128,128]{2,1,0:T(8,128)(2,1)} %tie.14.refs_2_), channel_id=1, source_target_pairs={{8,0},{16,24},{9,1},{17,25},{10,2},{18,26},{11,3},{19,27},{12,4},{... | collective-permute-start | bytes 3145736 | tf_op jit(solution)/shard_map/ppermute | solution.py:422
  59.9 24.4 %collective-permute-start.13 = (bf16[32,128,128]{2,1,0:T(8,128)(2,1)}, bf16[32,128,128]{2,1,0:T(8,128)(2,1)}, u32[]{:S(2)}, u32[]{:S(2)}) collective-permute-start(bf16[32,128,128]{2,1,0:T(8,128)(2,1)} %tie.14.refs_2_), channel_id=1, source_target_pairs={{0,2},{1,5},{2,0},{3,7},{4,6},{5,1},{6,4},{7,3},{8,10},{9,13},{10,... | collective-permute-start | bytes 3145736 | tf_op jit(solution)/shard_map/ppermute | solution.py:364
  70.5 13.8 %collective-permute-start.10 = (bf16[32,128,128]{2,1,0:T(8,128)(2,1)}, bf16[32,128,128]{2,1,0:T(8,128)(2,1)}, u32[]{:S(2)}, u32[]{:S(2)}) collective-permute-start(bf16[32,128,128]{2,1,0:T(8,128)(2,1)} %tie.15.refs_0_), channel_id=1, source_target_pairs={{0,1},{1,0},{2,3},{3,2},{4,5},{5,4},{6,7},{7,6},{8,9},{9,8},{10,11... | collective-permute-start | bytes 3145736 | tf_op jit(solution)/shard_map/ppermute | solution.py:364
  71.6 12.7 %collective-permute-start.12 = (bf16[32,128,128]{2,1,0:T(8,128)(2,1)}, bf16[32,128,128]{2,1,0:T(8,128)(2,1)}, u32[]{:S(2)}, u32[]{:S(2)}) collective-permute-start(bf16[32,128,128]{2,1,0:T(8,128)(2,1)} %tie.16.refs_1_), channel_id=1, source_target_pairs={{0,1},{1,0},{2,3},{3,2},{4,5},{5,4},{6,7},{7,6},{8,9},{9,8},{10,11... | collective-permute-start | bytes 3145736 | tf_op jit(solution)/shard_map/ppermute | solution.py:364
  71.6 25.7 %collective-permute-start.18 = (bf16[32,128,128]{2,1,0:T(8,128)(2,1)}, bf16[32,128,128]{2,1,0:T(8,128)(2,1)}, u32[]{:S(2)}, u32[]{:S(2)}) collective-permute-start(bf16[32,128,128]{2,1,0:T(8,128)(2,1)} %tie.13.refs_1_), channel_id=1, source_target_pairs={{0,1},{1,0},{2,3},{3,2},{4,5},{5,4},{6,7},{7,6},{8,9},{9,8},{10,11... | collective-permute-start | bytes 3145736 | tf_op jit(solution)/shard_map/ppermute | solution.py:364
  84.3 13.0 %collective-permute-start.19 = (bf16[32,128,128]{2,1,0:T(8,128)(2,1)}, bf16[32,128,128]{2,1,0:T(8,128)(2,1)}, u32[]{:S(2)}, u32[]{:S(2)}) collective-permute-start(bf16[32,128,128]{2,1,0:T(8,128)(2,1)} %tie.14.refs_2_), channel_id=1, source_target_pairs={{0,1},{1,0},{2,3},{3,2},{4,5},{5,4},{6,7},{7,6},{8,9},{9,8},{10,11... | collective-permute-start | bytes 3145736 | tf_op jit(solution)/shard_map/ppermute | solution.py:364
  87.2 10.0 %collective-permute-start.20 = (bf16[32,128,128]{2,1,0:T(8,128)(2,1)}, bf16[32,128,128]{2,1,0:T(8,128)(2,1)}, u32[]{:S(2)}, u32[]{:S(2)}) collective-permute-start(bf16[32,128,128]{2,1,0:T(8,128)(2,1)} %choose.1.refs_0_), channel_id=1, source_target_pairs={{0,1},{1,0},{2,3},{3,2},{4,5},{5,4},{6,7},{7,6},{8,9},{9,8},{10,11... | collective-permute-start | bytes 3145736 | tf_op jit(solution)/shard_map/ppermute | solution.py:364
  87.8 20.0 %collective-permute-start.17 = (bf16[32,128,128]{2,1,0:T(8,128)(2,1)}, bf16[32,128,128]{2,1,0:T(8,128)(2,1)}, u32[]{:S(2)}, u32[]{:S(2)}) collective-permute-start(bf16[32,128,128]{2,1,0:T(8,128)(2,1)} %choose.1.refs_0_), channel_id=1, source_target_pairs={{0,2},{1,5},{2,0},{3,7},{4,6},{5,1},{6,4},{7,3},{8,10},{9,13},{10,... | collective-permute-start | bytes 3145736 | tf_op jit(solution)/shard_map/ppermute | solution.py:364
  95.6 25.1 %collective-permute-start.23 = (bf16[256,2048]{1,0:T(8,128)(2,1)}, bf16[256,2048]{1,0:T(8,128)(2,1)}, u32[]{:S(2)}, u32[]{:S(2)}) collective-permute-start(bf16[256,2048]{1,0:T(8,128)(2,1)} %get-tuple-element.21.refs_1_), channel_id=1, source_target_pairs={{0,4},{1,3},{2,6},{3,1},{4,0},{5,7},{6,2},{7,5},{8,12},{9,11},{10,... | collective-permute-start | bytes 3145736 | tf_op jit(solution)/shard_map/ppermute | solution.py:364
  107.8 15.6 %collective-permute-start.21 = (bf16[32,128,128]{2,1,0:T(8,128)(2,1)}, bf16[32,128,128]{2,1,0:T(8,128)(2,1)}, u32[]{:S(2)}, u32[]{:S(2)}) collective-permute-start(bf16[32,128,128]{2,1,0:T(8,128)(2,1)} %tie.21.refs_3_), channel_id=1, source_target_pairs={{0,1},{1,0},{2,3},{3,2},{4,5},{5,4},{6,7},{7,6},{8,9},{9,8},{10,11... | collective-permute-start | bytes 3145736 | tf_op jit(solution)/shard_map/ppermute | solution.py:364
  107.9 19.4 %collective-permute-start.22 = (bf16[256,2048]{1,0:T(8,128)(2,1)}, bf16[256,2048]{1,0:T(8,128)(2,1)}, u32[]{:S(2)}, u32[]{:S(2)}) collective-permute-start(bf16[256,2048]{1,0:T(8,128)(2,1)} %get-tuple-element.23.refs_1_), channel_id=1, source_target_pairs={{0,2},{1,5},{2,0},{3,7},{4,6},{5,1},{6,4},{7,3},{8,10},{9,13},{10,... | collective-permute-start | bytes 3145736 | tf_op jit(solution)/shard_map/ppermute | solution.py:364
  109.4 17.8 %collective-permute-start.16 = (bf16[32,128,128]{2,1,0:T(8,128)(2,1)}, bf16[32,128,128]{2,1,0:T(8,128)(2,1)}, u32[]{:S(2)}, u32[]{:S(2)}) collective-permute-start(bf16[32,128,128]{2,1,0:T(8,128)(2,1)} %tie.20.refs_2_), channel_id=1, source_target_pairs={{0,1},{1,0},{2,3},{3,2},{4,5},{5,4},{6,7},{7,6},{8,9},{9,8},{10,11... | collective-permute-start | bytes 3145736 | tf_op jit(solution)/shard_map/ppermute | solution.py:364
  119.9 23.9 %collective-permute-start.25 = (bf16[256,2048]{1,0:T(8,128)(2,1)}, bf16[256,2048]{1,0:T(8,128)(2,1)}, u32[]{:S(2)}, u32[]{:S(2)}) collective-permute-start(bf16[256,2048]{1,0:T(8,128)(2,1)} %get-tuple-element.26), channel_id=1, source_target_pairs={{0,4},{1,3},{2,6},{3,1},{4,0},{5,7},{6,2},{7,5},{8,12},{9,11},{10,... | collective-permute-start | bytes 3145736 | tf_op jit(solution)/shard_map/ppermute | solution.py:364
  135.3 15.2 %collective-permute-start.24 = (bf16[256,2048]{1,0:T(8,128)(2,1)}, bf16[256,2048]{1,0:T(8,128)(2,1)}, u32[]{:S(2)}, u32[]{:S(2)}) collective-permute-start(bf16[256,2048]{1,0:T(8,128)(2,1)} %product.10.refs_1_), channel_id=1, source_target_pairs={{0,2},{1,5},{2,0},{3,7},{4,6},{5,1},{6,4},{7,3},{8,10},{9,13},{10,... | collective-permute-start | bytes 3145736 | tf_op jit(solution)/shard_map/ppermute | solution.py:364

commit v12 on v11

--- a/solution.py
+++ b/solution.py
@@ -159,7 +159,7 @@
     capacity, part = mine.shape[2:]
     slot_count, m = len(slots), len(picks) * capacity
     depth = 2 * part
-    width = min(MM_COLS, int_cols)
+    width = min(2 * MM_COLS, int_cols)
     steps = int_cols // width
     hbm = pl.BlockSpec(memory_space=pltpu.HBM)
     operands = [numbers, mine, theirs, *slots]

time: 155 us -> 154 us (level)
  Pallas kernels: 82 us -> 80.3 us
    pallas_call x6, Pallas kernels: 53.4 us -> 51.7 us  [product(): pl.pallas_call(functools.partial(product_body, at, acc is not None, whole...]
  transfers between devices with their start and end apart: 26 -> 26, of which waited for: 9 -> 10; matrix products, arithmetic and copies ran while one was open for 5% -> 5% of each run, Pallas kernels for 49% -> 48%
where the time goes in v12:
time: 154 us; the launch traced here: 153 us
  Pallas kernels  80.3 us (52%)
  waiting for transfers between devices  40 us (26%)
  starting transfers between devices  25.2 us (16%)
  other arithmetic  6.56 us (4%)
    pallas_call x6, Pallas kernels, product(): pl.pallas_call(functools.partial(product_body, at, acc is not None, whole...  51.7 us
    ppermute x4, waiting for transfers between devices, line_phase(): lax.ppermute(own if source < 0 else moved[source], 'row', pairs)  26.3 us
    ppermute x22, starting transfers between devices, permute(): lax.ppermute(value, 'col', [(col_index(*at), col_index(*moved_to(*at))) f...  18.1 us
    ppermute x22, waiting for transfers between devices, permute(): lax.ppermute(value, 'col', [(col_index(*at), col_index(*moved_to(*at))) f...  13.8 us
    pallas_call x1, Pallas kernels, pick_rows(): pl.pallas_call(functools.partial(pick_body, first, count, capacity), out_...  11.8 us
    pallas_call x3, Pallas kernels, put(): pl.pallas_call(put_body, out_shape=jax.ShapeDtypeStruct(whole.shape, whol...  10.2 us
    ppermute x4, starting transfers between devices, line_phase(): lax.ppermute(own if source < 0 else moved[source], 'row', pairs)  7.1 us
    pallas_call x1, Pallas kernels, pack(): pl.pallas_call(pack_body, out_shape=[jax.ShapeDtypeStruct((count, TILE, T...  3.67 us
  transfers between devices with their start and end apart: 26, of which 10 were waited for; matrix products, arithmetic and copies ran while one was open for 5% of the time, Pallas kernels for 48%

profile of v12, /device:TPU:0, one launch (start us, length us, event | category | flops | bytes accessed | tf_op | source)
XLA Modules:
  0.0 153.1 jit_solution(3415908626463187088)
XLA Ops:
  0.0 3.7 %pack_tiles.1 = (bf16[32,128,128]{2,1,0:T(8,128)(2,1)}, bf16[32,128,128]{2,1,0:T(8,128)(2,1)}, bf16[1024,256]{1,0:T(8,128)(2,1)}) custom-call(s32[1]{0:T(128)} %bitcast.6.row, s32[4,32]{1,0:T(4,128)} %bitcast.31, s32[2,8]{1,0:T(2,128)} %bitcast.33, bf16[512,2048]{1,0:T(8,128)(2,1)} %src_ref.1, bf16[1024,256]{1,0:T(8,128)(2,1)} %amp_ref.1), custom_call_target="tpu_custom_call" | custom-call | tf_op jit(solution)/shard_map/pack_tiles/pallas_call | solution.py:39
  3.7 3.0 %collective-permute-start.3 = (bf16[1024,256]{1,0:T(8,128)(2,1)}, bf16[1024,256]{1,0:T(8,128)(2,1)}, u32[]{:S(2)}, u32[]{:S(2)}) collective-permute-start(bf16[1024,256]{1,0:T(8,128)(2,1)} %get-tuple-element.16.refs_0_), channel_id=1, source_target_pairs={{0,4},{1,3},{2,6},{3,1},{4,0},{5,7},{6,2},{7,5},{8,12},{9,11},{10,... | collective-permute-start | bytes 1572872 | tf_op jit(solution)/shard_map/ppermute | solution.py:364
  6.6 1.5 collective-permute-start.2
  8.1 2.6 %collective-permute-start.8 = (bf16[32,128,128]{2,1,0:T(8,128)(2,1)}, bf16[32,128,128]{2,1,0:T(8,128)(2,1)}, u32[]{:S(2)}, u32[]{:S(2)}) collective-permute-start(bf16[32,128,128]{2,1,0:T(8,128)(2,1)} %get-tuple-element.19.refs_0_), channel_id=1, source_target_pairs={{0,16},{16,0},{8,24},{24,8},{1,17},{17,1},{9,25},{25,9},{2,18},{18... | collective-permute-start | bytes 3145736 | tf_op jit(solution)/shard_map/ppermute | solution.py:422
  10.7 1.6 %collective-permute-start.7 = (bf16[32,128,128]{2,1,0:T(8,128)(2,1)}, bf16[32,128,128]{2,1,0:T(8,128)(2,1)}, u32[]{:S(2)}, u32[]{:S(2)}) collective-permute-start(bf16[32,128,128]{2,1,0:T(8,128)(2,1)} %get-tuple-element.19.refs_0_), channel_id=1, source_target_pairs={{0,8},{8,0},{16,24},{24,16},{1,9},{9,1},{17,25},{25,17},{2,10},{10... | collective-permute-start | bytes 3145736 | tf_op jit(solution)/shard_map/ppermute | solution.py:422
  12.3 0.8 select_reduce_fusion
  13.1 0.6 collective-permute-start
  13.7 0.7 fusion.3
  14.4 2.3 %reduce-window.6 = s32[8,8,128]{2,1,0:T(8,128)S(1)} reduce-window(s32[8,8,128]{2,1,0:T(8,128)S(1)} %fusion.3, s32[]{:T(128)} %constant.20.clone.1), window={size=1x1x128 pad=0_0x0_0x127_0}, to_apply=%region_1.2 | reduce-window | flops 1040384 | bytes 65540 | tf_op jit(solution)/shard_map/reduce-window
  16.6 0.3 slice_reduce_fusion
  17.1 0.7 fusion.2
  17.9 1.0 collective-permute-done.2.refs_1_
  18.8 1.8 %collective-permute-start.4 = (bf16[1024,256]{1,0:T(8,128)(2,1)}, bf16[1024,256]{1,0:T(8,128)(2,1)}, u32[]{:S(2)}, u32[]{:S(2)}) collective-permute-start(bf16[1024,256]{1,0:T(8,128)(2,1)} %collective-permute-done.2.refs_1_), channel_id=1, source_target_pairs={{0,4},{1,3},{2,6},{3,1},{4,0},{5,7},{6,2},{7,5},{8,12},{9,11},{10,... | collective-permute-start | bytes 1572872 | tf_op jit(solution)/shard_map/ppermute | solution.py:364
  20.6 1.3 multiply_add_fusion.refs_0_
  21.9 0.7 dynamic-slice_bitcast_fusion.scalars
  22.7 1.1 collective-permute-done.1
  23.8 0.6 pad_add_fusion.refs_1_.numbers
  24.4 3.9 %collective-permute-done.4.refs_3_ = bf16[1024,256]{1,0:T(8,128)(2,1)} collective-permute-done((bf16[1024,256]{1,0:T(8,128)(2,1)}, bf16[1024,256]{1,0:T(8,128)(2,1)}, u32[]{:S(2)}, u32[]{:S(2)}) %collective-permute-start.4) | collective-permute-done | bytes 524320 | tf_op jit(solution)/shard_map/ppermute | solution.py:364
  28.3 11.8 %pick_rows.1 = (bf16[4,3,256,256]{3,2,1,0:T(8,128)(2,1)}, bf16[4,3,256,256]{3,2,1,0:T(8,128)(2,1)}) custom-call(s32[48]{0:T(128)} %copy-done, s32[1,1024]{1,0:T(1,128)} %bitcast.28, bf16[1024,256]{1,0:T(8,128)(2,1)} %get-tuple-element.16.refs_0_, bf16[1024,256]{1,0:T(8,128)(2,1)} %collective-permute-done.2.refs_1_, ...), custom_call_target="tpu_custom_call" | custom-call | tf_op jit(solution)/shard_map/pick_rows/pallas_call | solution.py:78
  40.3 0.4 collective-permute-start.9
  40.7 1.7 %collective-permute-start.6 = (bf16[32,128,128]{2,1,0:T(8,128)(2,1)}, bf16[32,128,128]{2,1,0:T(8,128)(2,1)}, u32[]{:S(2)}, u32[]{:S(2)}) collective-permute-start(bf16[32,128,128]{2,1,0:T(8,128)(2,1)} %get-tuple-element.19.refs_0_), channel_id=1, source_target_pairs={{0,2},{1,5},{2,0},{3,7},{4,6},{5,1},{6,4},{7,3},{8,10},{9,13},{10,... | collective-permute-start | bytes 3145736 | tf_op jit(solution)/shard_map/ppermute | solution.py:364
  42.4 13.9 %collective-permute-done.8.refs_2_.refs_0_.refs_1_ = bf16[32,128,128]{2,1,0:T(8,128)(2,1)} collective-permute-done((bf16[32,128,128]{2,1,0:T(8,128)(2,1)}, bf16[32,128,128]{2,1,0:T(8,128)(2,1)}, u32[]{:S(2)}, u32[]{:S(2)}) %collective-permute-start.8) | collective-permute-done | bytes 1048608 | tf_op jit(solution)/shard_map/ppermute | solution.py:422
  56.5 0.5 collective-permute-start.11
  57.0 1.6 %collective-permute-start.14 = (bf16[32,128,128]{2,1,0:T(8,128)(2,1)}, bf16[32,128,128]{2,1,0:T(8,128)(2,1)}, u32[]{:S(2)}, u32[]{:S(2)}) collective-permute-start(bf16[32,128,128]{2,1,0:T(8,128)(2,1)} %tie.17), channel_id=1, source_target_pairs={{8,16},{16,8},{9,17},{17,9},{10,18},{18,10},{11,19},{19,11},{12,20... | collective-permute-start | bytes 3145736 | tf_op jit(solution)/shard_map/ppermute | solution.py:422
  58.6 1.3 collective-permute-start.15
  59.9 1.6 %collective-permute-start.13 = (bf16[32,128,128]{2,1,0:T(8,128)(2,1)}, bf16[32,128,128]{2,1,0:T(8,128)(2,1)}, u32[]{:S(2)}, u32[]{:S(2)}) collective-permute-start(bf16[32,128,128]{2,1,0:T(8,128)(2,1)} %tie.14.refs_2_), channel_id=1, source_target_pairs={{0,2},{1,5},{2,0},{3,7},{4,6},{5,1},{6,4},{7,3},{8,10},{9,13},{10,... | collective-permute-start | bytes 3145736 | tf_op jit(solution)/shard_map/ppermute | solution.py:364
  61.5 9.1 %product.6.refs_1_.refs_3_ = f32[512,2048]{1,0:T(8,128)} custom-call(s32[17,64]{1,0:T(8,128)} %pad_add_fusion.refs_1_.numbers, bf16[4,3,256,256]{3,2,1,0:T(8,128)(2,1)} %get-tuple-element.17.refs_1_.mine, bf16[4,3,256,256]{3,2,1,0:T(8,128)(2,1)} %collective-permute-done.5.theirs.refs_1_, bf16[32,128,128]{2,1,0:T(8,128)(2,1)} %get-tuple-element.19.refs_0_, ...), custom_call_target="tpu_custom_call" | custom-call | tf_op jit(solution)/shard_map/product/pallas_call | solution.py:188
  70.7 0.8 collective-permute-done.11.refs_0_
  71.6 0.5 collective-permute-start.18
  72.1 12.2 %collective-permute-done.15.refs_6_.refs_0_ = bf16[32,128,128]{2,1,0:T(8,128)(2,1)} collective-permute-done((bf16[32,128,128]{2,1,0:T(8,128)(2,1)}, bf16[32,128,128]{2,1,0:T(8,128)(2,1)}, u32[]{:S(2)}, u32[]{:S(2)}) %collective-permute-start.15) | collective-permute-done | bytes 1048608 | tf_op jit(solution)/shard_map/ppermute | solution.py:422
  84.3 2.9 %choose.1.refs_0_ = bf16[32,128,128]{2,1,0:T(8,128)(2,1)} custom-call(s32[48]{0:T(128)} %copy-done, bf16[32,128,128]{2,1,0:T(8,128)(2,1)} %tie.18.refs_6_.a_ref, bf16[32,128,128]{2,1,0:T(8,128)(2,1)} %tie.19.b_ref), custom_call_target="tpu_custom_call" | custom-call | tf_op jit(solution)/shard_map/choose/pallas_call | solution.py:242
  87.2 0.6 collective-permute-start.20
  87.8 0.4 collective-permute-start.17
  88.2 6.6 %product.7 = (bf16[256,16384]{1,0:T(8,128)(2,1)}, bf16[256,2048]{1,0:T(8,128)(2,1)}) custom-call(s32[17,64]{1,0:T(8,128)} %pad_add_fusion.refs_1_.numbers, bf16[4,3,256,256]{3,2,1,0:T(8,128)(2,1)} %get-tuple-element.17.refs_1_.mine, bf16[4,3,256,256]{3,2,1,0:T(8,128)(2,1)} %collective-permute-done.5.theirs.refs_1_, bf16[32,128,128]{2,1,0:T(8,128)(2,1)} %choose.1.refs_0_, ...), custom_call_target="tpu_custom_call" | custom-call | tf_op jit(solution)/shard_map/product/pallas_call | solution.py:188
  94.8 1.7 %collective-permute-start.23 = (bf16[256,2048]{1,0:T(8,128)(2,1)}, bf16[256,2048]{1,0:T(8,128)(2,1)}, u32[]{:S(2)}, u32[]{:S(2)}) collective-permute-start(bf16[256,2048]{1,0:T(8,128)(2,1)} %get-tuple-element.21.refs_1_), channel_id=1, source_target_pairs={{0,4},{1,3},{2,6},{3,1},{4,0},{5,7},{6,2},{7,5},{8,12},{9,11},{10,... | collective-permute-start | bytes 3145736 | tf_op jit(solution)/shard_map/ppermute | solution.py:364
  96.5 10.3 %product.8 = (bf16[256,16384]{1,0:T(8,128)(2,1)}, bf16[256,2048]{1,0:T(8,128)(2,1)}) custom-call(s32[17,64]{1,0:T(8,128)} %pad_add_fusion.refs_1_.numbers, bf16[4,3,256,256]{3,2,1,0:T(8,128)(2,1)} %get-tuple-element.17.refs_1_.mine, bf16[4,3,256,256]{3,2,1,0:T(8,128)(2,1)} %collective-permute-done.5.theirs.refs_1_, ...), custom_call_target="tpu_custom_call", output_to_operand_aliasing={{0}: (7, {})} | custom-call | tf_op jit(solution)/shard_map/product/pallas_call | solution.py:188
  107.0 1.4 collective-permute-start.22
  108.5 1.3 collective-permute-start.16
  109.8 10.3 %product.9 = (bf16[256,16384]{1,0:T(8,128)(2,1)}, bf16[256,2048]{1,0:T(8,128)(2,1)}) custom-call(s32[17,64]{1,0:T(8,128)} %pad_add_fusion.refs_1_.numbers, bf16[4,3,256,256]{3,2,1,0:T(8,128)(2,1)} %get-tuple-element.17.refs_1_.mine, bf16[4,3,256,256]{3,2,1,0:T(8,128)(2,1)} %collective-permute-done.5.theirs.refs_1_, ...), custom_call_target="tpu_custom_call", output_to_operand_aliasing={{0}: (7, {})} | custom-call | tf_op jit(solution)/shard_map/product/pallas_call | solution.py:188
  120.1 0.5 collective-permute-start.25
  120.6 2.7 %put.3.refs_2_.refs_0_ = bf16[256,16384]{1,0:T(8,128)(2,1)} custom-call(s32[48]{0:T(128)} %copy-done, bf16[256,2048]{1,0:T(8,128)(2,1)} %collective-permute-done.23.refs_0_, bf16[256,16384]{1,0:T(8,128)(2,1)} %get-tuple-element.25.refs_1_), custom_call_target="tpu_custom_call", output_to_operand_aliasing={{}: (2, {})} | custom-call | tf_op jit(solution)/shard_map/put/pallas_call | solution.py:277
  123.3 4.2 %collective-permute-done.22.refs_1_.refs_0_ = bf16[256,2048]{1,0:T(8,128)(2,1)} collective-permute-done((bf16[256,2048]{1,0:T(8,128)(2,1)}, bf16[256,2048]{1,0:T(8,128)(2,1)}, u32[]{:S(2)}, u32[]{:S(2)}) %collective-permute-start.22) | collective-permute-done | bytes 1048608 | tf_op jit(solution)/shard_map/ppermute | solution.py:364
  127.6 7.7 %product.10.refs_1_ = bf16[256,2048]{1,0:T(8,128)(2,1)} custom-call(s32[17,64]{1,0:T(8,128)} %pad_add_fusion.refs_1_.numbers, bf16[4,3,256,256]{3,2,1,0:T(8,128)(2,1)} %get-tuple-element.17.refs_1_.mine, bf16[4,3,256,256]{3,2,1,0:T(8,128)(2,1)} %collective-permute-done.5.theirs.refs_1_, bf16[32,128,128]{2,1,0:T(8,128)(2,1)} %collective-permute-done.10.refs_4_.refs_0_, ...), custom_call_target="tpu_custom_call" | custom-call | tf_op jit(solution)/shard_map/product/pallas_call | solution.py:188
  135.2 0.3 collective-permute-start.24
  135.6 7.7 %product.11.refs_2_ = bf16[256,16384]{1,0:T(8,128)(2,1)} custom-call(s32[17,64]{1,0:T(8,128)} %pad_add_fusion.refs_1_.numbers, bf16[4,3,256,256]{3,2,1,0:T(8,128)(2,1)} %get-tuple-element.17.refs_1_.mine, bf16[4,3,256,256]{3,2,1,0:T(8,128)(2,1)} %collective-permute-done.5.theirs.refs_1_, ...), custom_call_target="tpu_custom_call", output_to_operand_aliasing={{}: (7, {})} | custom-call | tf_op jit(solution)/shard_map/product/pallas_call | solution.py:188
  143.3 4.8 %put.4.refs_1_ = bf16[256,16384]{1,0:T(8,128)(2,1)} custom-call(s32[48]{0:T(128)} %copy-done, bf16[256,2048]{1,0:T(8,128)(2,1)} %collective-permute-done.22.refs_1_.refs_0_, bf16[256,2048]{1,0:T(8,128)(2,1)} %collective-permute-done.25.refs_1_, bf16[256,16384]{1,0:T(8,128)(2,1)} %product.11.refs_2_), custom_call_target="tpu_custom_call", output_to_operand_aliasing={{}: (3, {})} | custom-call | tf_op jit(solution)/shard_map/put/pallas_call | solution.py:277
  148.0 2.4 %collective-permute-done.24.refs_0_ = bf16[256,2048]{1,0:T(8,128)(2,1)} collective-permute-done((bf16[256,2048]{1,0:T(8,128)(2,1)}, bf16[256,2048]{1,0:T(8,128)(2,1)}, u32[]{:S(2)}, u32[]{:S(2)}) %collective-permute-start.24) | collective-permute-done | bytes 1048608 | tf_op jit(solution)/shard_map/ppermute | solution.py:364
  150.4 2.7 %put.5 = bf16[256,16384]{1,0:T(8,128)(2,1)} custom-call(s32[48]{0:T(128)} %copy-done, bf16[256,2048]{1,0:T(8,128)(2,1)} %collective-permute-done.24.refs_0_, bf16[256,16384]{1,0:T(8,128)(2,1)} %put.4.refs_1_), custom_call_target="tpu_custom_call", output_to_operand_aliasing={{}: (2, {})} | custom-call | tf_op jit(solution)/shard_map/put/pallas_call | solution.py:277
  (42 shorter events, 1.0 us)
Async XLA Ops:
  3.7 20.8 %collective-permute-start.3 = (bf16[1024,256]{1,0:T(8,128)(2,1)}, bf16[1024,256]{1,0:T(8,128)(2,1)}, u32[]{:S(2)}, u32[]{:S(2)}) collective-permute-start(bf16[1024,256]{1,0:T(8,128)(2,1)} %get-tuple-element.16.refs_0_), channel_id=1, source_target_pairs={{0,4},{1,3},{2,6},{3,1},{4,0},{5,7},{6,2},{7,5},{8,12},{9,11},{10,... | collective-permute-start | bytes 1572872 | tf_op jit(solution)/shard_map/ppermute | solution.py:364
  6.6 12.2 %collective-permute-start.2 = (bf16[1024,256]{1,0:T(8,128)(2,1)}, bf16[1024,256]{1,0:T(8,128)(2,1)}, u32[]{:S(2)}, u32[]{:S(2)}) collective-permute-start(bf16[1024,256]{1,0:T(8,128)(2,1)} %get-tuple-element.16.refs_0_), channel_id=1, source_target_pairs={{0,2},{1,5},{2,0},{3,7},{4,6},{5,1},{6,4},{7,3},{8,10},{9,13},{10,... | collective-permute-start | bytes 1572872 | tf_op jit(solution)/shard_map/ppermute | solution.py:364
  8.1 48.1 %collective-permute-start.8 = (bf16[32,128,128]{2,1,0:T(8,128)(2,1)}, bf16[32,128,128]{2,1,0:T(8,128)(2,1)}, u32[]{:S(2)}, u32[]{:S(2)}) collective-permute-start(bf16[32,128,128]{2,1,0:T(8,128)(2,1)} %get-tuple-element.19.refs_0_), channel_id=1, source_target_pairs={{0,16},{16,0},{8,24},{24,8},{1,17},{17,1},{9,25},{25,9},{2,18},{18... | collective-permute-start | bytes 3145736 | tf_op jit(solution)/shard_map/ppermute | solution.py:422
  10.7 45.7 %collective-permute-start.7 = (bf16[32,128,128]{2,1,0:T(8,128)(2,1)}, bf16[32,128,128]{2,1,0:T(8,128)(2,1)}, u32[]{:S(2)}, u32[]{:S(2)}) collective-permute-start(bf16[32,128,128]{2,1,0:T(8,128)(2,1)} %get-tuple-element.19.refs_0_), channel_id=1, source_target_pairs={{0,8},{8,0},{16,24},{24,16},{1,9},{9,1},{17,25},{25,17},{2,10},{10... | collective-permute-start | bytes 3145736 | tf_op jit(solution)/shard_map/ppermute | solution.py:422
  13.1 9.5 %collective-permute-start = (s32[4,64]{1,0:T(4,128)S(1)}, s32[4,64]{1,0:T(4,128)S(1)}, u32[]{:S(2)}, u32[]{:S(2)}) collective-permute-start(s32[4,64]{1,0:T(4,128)S(1)} %select_reduce_fusion), channel_id=1, source_target_pairs={{0,2},{1,5},{2,0},{3,7},{4,6},{5,1},{6,4},{7,3},{8,10},{9,13},{10,... | collective-permute-start | bytes 3080 | tf_op jit(solution)/shard_map/ppermute | solution.py:364
  18.8 9.5 %collective-permute-start.4 = (bf16[1024,256]{1,0:T(8,128)(2,1)}, bf16[1024,256]{1,0:T(8,128)(2,1)}, u32[]{:S(2)}, u32[]{:S(2)}) collective-permute-start(bf16[1024,256]{1,0:T(8,128)(2,1)} %collective-permute-done.2.refs_1_), channel_id=1, source_target_pairs={{0,4},{1,3},{2,6},{3,1},{4,0},{5,7},{6,2},{7,5},{8,12},{9,11},{10,... | collective-permute-start | bytes 1572872 | tf_op jit(solution)/shard_map/ppermute | solution.py:364
  22.6 5.8 %copy-start = (s32[48]{0:T(128)}, s32[48]{0:T(128)S(1)}, u32[]{:S(2)}) copy-start(s32[48]{0:T(128)S(1)} %dynamic-slice_bitcast_fusion.scalars) | copy-start | bytes 580
  22.6 1.2 collective-permute-start.1
  40.1 21.3 %collective-permute-start.5 = (bf16[4,3,256,256]{3,2,1,0:T(8,128)(2,1)}, bf16[4,3,256,256]{3,2,1,0:T(8,128)(2,1)}, u32[]{:S(2)}, u32[]{:S(2)}) collective-permute-start(bf16[4,3,256,256]{3,2,1,0:T(8,128)(2,1)} %get-tuple-element.18), channel_id=1, source_target_pairs={{0,1},{1,0},{2,3},{3,2},{4,5},{5,4},{6,7},{7,6},{8,9},{9,8},{10,11... | collective-permute-start | bytes 4718600 | tf_op jit(solution)/shard_map/ppermute | solution.py:364
  40.3 18.3 %collective-permute-start.9 = (bf16[32,128,128]{2,1,0:T(8,128)(2,1)}, bf16[32,128,128]{2,1,0:T(8,128)(2,1)}, u32[]{:S(2)}, u32[]{:S(2)}) collective-permute-start(bf16[32,128,128]{2,1,0:T(8,128)(2,1)} %get-tuple-element.19.refs_0_), channel_id=1, source_target_pairs={{0,1},{1,0},{2,3},{3,2},{4,5},{5,4},{6,7},{7,6},{8,9},{9,8},{10,11... | collective-permute-start | bytes 3145736 | tf_op jit(solution)/shard_map/ppermute | solution.py:364
  40.7 18.0 %collective-permute-start.6 = (bf16[32,128,128]{2,1,0:T(8,128)(2,1)}, bf16[32,128,128]{2,1,0:T(8,128)(2,1)}, u32[]{:S(2)}, u32[]{:S(2)}) collective-permute-start(bf16[32,128,128]{2,1,0:T(8,128)(2,1)} %get-tuple-element.19.refs_0_), channel_id=1, source_target_pairs={{0,2},{1,5},{2,0},{3,7},{4,6},{5,1},{6,4},{7,3},{8,10},{9,13},{10,... | collective-permute-start | bytes 3145736 | tf_op jit(solution)/shard_map/ppermute | solution.py:364
  56.5 15.1 %collective-permute-start.11 = (bf16[32,128,128]{2,1,0:T(8,128)(2,1)}, bf16[32,128,128]{2,1,0:T(8,128)(2,1)}, u32[]{:S(2)}, u32[]{:S(2)}) collective-permute-start(bf16[32,128,128]{2,1,0:T(8,128)(2,1)} %tie.13.refs_1_), channel_id=1, source_target_pairs={{0,2},{1,5},{2,0},{3,7},{4,6},{5,1},{6,4},{7,3},{8,10},{9,13},{10,... | collective-permute-start | bytes 3145736 | tf_op jit(solution)/shard_map/ppermute | solution.py:364
  57.0 14.6 %collective-permute-start.14 = (bf16[32,128,128]{2,1,0:T(8,128)(2,1)}, bf16[32,128,128]{2,1,0:T(8,128)(2,1)}, u32[]{:S(2)}, u32[]{:S(2)}) collective-permute-start(bf16[32,128,128]{2,1,0:T(8,128)(2,1)} %tie.17), channel_id=1, source_target_pairs={{8,16},{16,8},{9,17},{17,9},{10,18},{18,10},{11,19},{19,11},{12,20... | collective-permute-start | bytes 3145736 | tf_op jit(solution)/shard_map/ppermute | solution.py:422
  58.6 25.6 %collective-permute-start.15 = (bf16[32,128,128]{2,1,0:T(8,128)(2,1)}, bf16[32,128,128]{2,1,0:T(8,128)(2,1)}, u32[]{:S(2)}, u32[]{:S(2)}) collective-permute-start(bf16[32,128,128]{2,1,0:T(8,128)(2,1)} %tie.14.refs_2_), channel_id=1, source_target_pairs={{8,0},{16,24},{9,1},{17,25},{10,2},{18,26},{11,3},{19,27},{12,4},{... | collective-permute-start | bytes 3145736 | tf_op jit(solution)/shard_map/ppermute | solution.py:422
  59.9 24.4 %collective-permute-start.13 = (bf16[32,128,128]{2,1,0:T(8,128)(2,1)}, bf16[32,128,128]{2,1,0:T(8,128)(2,1)}, u32[]{:S(2)}, u32[]{:S(2)}) collective-permute-start(bf16[32,128,128]{2,1,0:T(8,128)(2,1)} %tie.14.refs_2_), channel_id=1, source_target_pairs={{0,2},{1,5},{2,0},{3,7},{4,6},{5,1},{6,4},{7,3},{8,10},{9,13},{10,... | collective-permute-start | bytes 3145736 | tf_op jit(solution)/shard_map/ppermute | solution.py:364
  70.6 13.7 %collective-permute-start.10 = (bf16[32,128,128]{2,1,0:T(8,128)(2,1)}, bf16[32,128,128]{2,1,0:T(8,128)(2,1)}, u32[]{:S(2)}, u32[]{:S(2)}) collective-permute-start(bf16[32,128,128]{2,1,0:T(8,128)(2,1)} %tie.15.refs_0_), channel_id=1, source_target_pairs={{0,1},{1,0},{2,3},{3,2},{4,5},{5,4},{6,7},{7,6},{8,9},{9,8},{10,11... | collective-permute-start | bytes 3145736 | tf_op jit(solution)/shard_map/ppermute | solution.py:364
  71.6 12.7 %collective-permute-start.12 = (bf16[32,128,128]{2,1,0:T(8,128)(2,1)}, bf16[32,128,128]{2,1,0:T(8,128)(2,1)}, u32[]{:S(2)}, u32[]{:S(2)}) collective-permute-start(bf16[32,128,128]{2,1,0:T(8,128)(2,1)} %tie.16.refs_1_), channel_id=1, source_target_pairs={{0,1},{1,0},{2,3},{3,2},{4,5},{5,4},{6,7},{7,6},{8,9},{9,8},{10,11... | collective-permute-start | bytes 3145736 | tf_op jit(solution)/shard_map/ppermute | solution.py:364
  71.6 24.9 %collective-permute-start.18 = (bf16[32,128,128]{2,1,0:T(8,128)(2,1)}, bf16[32,128,128]{2,1,0:T(8,128)(2,1)}, u32[]{:S(2)}, u32[]{:S(2)}) collective-permute-start(bf16[32,128,128]{2,1,0:T(8,128)(2,1)} %tie.13.refs_1_), channel_id=1, source_target_pairs={{0,1},{1,0},{2,3},{3,2},{4,5},{5,4},{6,7},{7,6},{8,9},{9,8},{10,11... | collective-permute-start | bytes 3145736 | tf_op jit(solution)/shard_map/ppermute | solution.py:364
  84.3 12.2 %collective-permute-start.19 = (bf16[32,128,128]{2,1,0:T(8,128)(2,1)}, bf16[32,128,128]{2,1,0:T(8,128)(2,1)}, u32[]{:S(2)}, u32[]{:S(2)}) collective-permute-start(bf16[32,128,128]{2,1,0:T(8,128)(2,1)} %tie.14.refs_2_), channel_id=1, source_target_pairs={{0,1},{1,0},{2,3},{3,2},{4,5},{5,4},{6,7},{7,6},{8,9},{9,8},{10,11... | collective-permute-start | bytes 3145736 | tf_op jit(solution)/shard_map/ppermute | solution.py:364
  87.2 9.3 %collective-permute-start.20 = (bf16[32,128,128]{2,1,0:T(8,128)(2,1)}, bf16[32,128,128]{2,1,0:T(8,128)(2,1)}, u32[]{:S(2)}, u32[]{:S(2)}) collective-permute-start(bf16[32,128,128]{2,1,0:T(8,128)(2,1)} %choose.1.refs_0_), channel_id=1, source_target_pairs={{0,1},{1,0},{2,3},{3,2},{4,5},{5,4},{6,7},{7,6},{8,9},{9,8},{10,11... | collective-permute-start | bytes 3145736 | tf_op jit(solution)/shard_map/ppermute | solution.py:364
  87.8 19.3 %collective-permute-start.17 = (bf16[32,128,128]{2,1,0:T(8,128)(2,1)}, bf16[32,128,128]{2,1,0:T(8,128)(2,1)}, u32[]{:S(2)}, u32[]{:S(2)}) collective-permute-start(bf16[32,128,128]{2,1,0:T(8,128)(2,1)} %choose.1.refs_0_), channel_id=1, source_target_pairs={{0,2},{1,5},{2,0},{3,7},{4,6},{5,1},{6,4},{7,3},{8,10},{9,13},{10,... | collective-permute-start | bytes 3145736 | tf_op jit(solution)/shard_map/ppermute | solution.py:364
  94.8 25.8 %collective-permute-start.23 = (bf16[256,2048]{1,0:T(8,128)(2,1)}, bf16[256,2048]{1,0:T(8,128)(2,1)}, u32[]{:S(2)}, u32[]{:S(2)}) collective-permute-start(bf16[256,2048]{1,0:T(8,128)(2,1)} %get-tuple-element.21.refs_1_), channel_id=1, source_target_pairs={{0,4},{1,3},{2,6},{3,1},{4,0},{5,7},{6,2},{7,5},{8,12},{9,11},{10,... | collective-permute-start | bytes 3145736 | tf_op jit(solution)/shard_map/ppermute | solution.py:364
  107.0 16.3 %collective-permute-start.21 = (bf16[32,128,128]{2,1,0:T(8,128)(2,1)}, bf16[32,128,128]{2,1,0:T(8,128)(2,1)}, u32[]{:S(2)}, u32[]{:S(2)}) collective-permute-start(bf16[32,128,128]{2,1,0:T(8,128)(2,1)} %tie.21.refs_3_), channel_id=1, source_target_pairs={{0,1},{1,0},{2,3},{3,2},{4,5},{5,4},{6,7},{7,6},{8,9},{9,8},{10,11... | collective-permute-start | bytes 3145736 | tf_op jit(solution)/shard_map/ppermute | solution.py:364
  107.0 20.5 %collective-permute-start.22 = (bf16[256,2048]{1,0:T(8,128)(2,1)}, bf16[256,2048]{1,0:T(8,128)(2,1)}, u32[]{:S(2)}, u32[]{:S(2)}) collective-permute-start(bf16[256,2048]{1,0:T(8,128)(2,1)} %get-tuple-element.23.refs_1_), channel_id=1, source_target_pairs={{0,2},{1,5},{2,0},{3,7},{4,6},{5,1},{6,4},{7,3},{8,10},{9,13},{10,... | collective-permute-start | bytes 3145736 | tf_op jit(solution)/shard_map/ppermute | solution.py:364
  108.5 19.1 %collective-permute-start.16 = (bf16[32,128,128]{2,1,0:T(8,128)(2,1)}, bf16[32,128,128]{2,1,0:T(8,128)(2,1)}, u32[]{:S(2)}, u32[]{:S(2)}) collective-permute-start(bf16[32,128,128]{2,1,0:T(8,128)(2,1)} %tie.20.refs_2_), channel_id=1, source_target_pairs={{0,1},{1,0},{2,3},{3,2},{4,5},{5,4},{6,7},{7,6},{8,9},{9,8},{10,11... | collective-permute-start | bytes 3145736 | tf_op jit(solution)/shard_map/ppermute | solution.py:364
  120.1 23.1 %collective-permute-start.25 = (bf16[256,2048]{1,0:T(8,128)(2,1)}, bf16[256,2048]{1,0:T(8,128)(2,1)}, u32[]{:S(2)}, u32[]{:S(2)}) collective-permute-start(bf16[256,2048]{1,0:T(8,128)(2,1)} %get-tuple-element.26), channel_id=1, source_target_pairs={{0,4},{1,3},{2,6},{3,1},{4,0},{5,7},{6,2},{7,5},{8,12},{9,11},{10,... | collective-permute-start | bytes 3145736 | tf_op jit(solution)/shard_map/ppermute | solution.py:364
  135.2 15.2 %collective-permute-start.24 = (bf16[256,2048]{1,0:T(8,128)(2,1)}, bf16[256,2048]{1,0:T(8,128)(2,1)}, u32[]{:S(2)}, u32[]{:S(2)}) collective-permute-start(bf16[256,2048]{1,0:T(8,128)(2,1)} %product.10.refs_1_), channel_id=1, source_target_pairs={{0,2},{1,5},{2,0},{3,7},{4,6},{5,1},{6,4},{7,3},{8,10},{9,13},{10,... | collective-permute-start | bytes 3145736 | tf_op jit(solution)/shard_map/ppermute | solution.py:364

commit v13 on v12

--- a/solution.py
+++ b/solution.py
@@ -262,7 +262,7 @@
 
 def put(pieces, whole, scalars, places):
     m, n = pieces[0].shape
-    width = min(2 * MM_COLS, n)
+    width = min(MM_COLS, n)
     steps = n // width
 
     def piece_at(p):

time: 154 us -> 156 us (1.013)
  Pallas kernels: 80.3 us -> 84.4 us
  waiting for transfers between devices: 40 us -> 37 us
    pallas_call x3, Pallas kernels: 10.2 us -> 14.6 us  [put(): pl.pallas_call(put_body, out_shape=jax.ShapeDtypeStruct(whole.shape, whol...]
    ppermute x22, waiting for transfers between devices: 13.8 us -> 10.7 us  [permute(): lax.ppermute(value, 'col', [(col_index(*at), col_index(*moved_to(*at))) f...]
  transfers between devices with their start and end apart: 26 -> 26, of which waited for: 10 -> 10; matrix products, arithmetic and copies ran while one was open for 5% -> 5% of each run, Pallas kernels for 48% -> 50%
where the time goes in v13:
time: 156 us; the launch traced here: 154 us
  Pallas kernels  84.4 us (54%)
  waiting for transfers between devices  37 us (24%)
  starting transfers between devices  25.3 us (16%)
  other arithmetic  6.56 us (4%)
    pallas_call x6, Pallas kernels, product(): pl.pallas_call(functools.partial(product_body, at, acc is not None, whole...  51.5 us
    ppermute x4, waiting for transfers between devices, line_phase(): lax.ppermute(own if source < 0 else moved[source], 'row', pairs)  26.3 us
    ppermute x22, starting transfers between devices, permute(): lax.ppermute(value, 'col', [(col_index(*at), col_index(*moved_to(*at))) f...  18.1 us
    pallas_call x3, Pallas kernels, put(): pl.pallas_call(put_body, out_shape=jax.ShapeDtypeStruct(whole.shape, whol...  14.6 us
    pallas_call x1, Pallas kernels, pick_rows(): pl.pallas_call(functools.partial(pick_body, first, count, capacity), out_...  11.8 us
    ppermute x22, waiting for transfers between devices, permute(): lax.ppermute(value, 'col', [(col_index(*at), col_index(*moved_to(*at))) f...  10.7 us
    ppermute x4, starting transfers between devices, line_phase(): lax.ppermute(own if source < 0 else moved[source], 'row', pairs)  7.28 us
    pallas_call x1, Pallas kernels, pack(): pl.pallas_call(pack_body, out_shape=[jax.ShapeDtypeStruct((count, TILE, T...  3.67 us
  transfers between devices with their start and end apart: 26, of which 10 were waited for; matrix products, arithmetic and copies ran while one was open for 5% of the time, Pallas kernels for 50%

profile of v13, /device:TPU:0, one launch (start us, length us, event | category | flops | bytes accessed | tf_op | source)
XLA Modules:
  0.0 154.5 jit_solution(4807508609223562462)
XLA Ops:
  0.0 3.7 %pack_tiles.1 = (bf16[32,128,128]{2,1,0:T(8,128)(2,1)}, bf16[32,128,128]{2,1,0:T(8,128)(2,1)}, bf16[1024,256]{1,0:T(8,128)(2,1)}) custom-call(s32[1]{0:T(128)} %bitcast.6.row, s32[4,32]{1,0:T(4,128)} %bitcast.31, s32[2,8]{1,0:T(2,128)} %bitcast.33, bf16[512,2048]{1,0:T(8,128)(2,1)} %src_ref.1, bf16[1024,256]{1,0:T(8,128)(2,1)} %amp_ref.1), custom_call_target="tpu_custom_call" | custom-call | tf_op jit(solution)/shard_map/pack_tiles/pallas_call | solution.py:39
  3.7 3.0 %collective-permute-start.3 = (bf16[1024,256]{1,0:T(8,128)(2,1)}, bf16[1024,256]{1,0:T(8,128)(2,1)}, u32[]{:S(2)}, u32[]{:S(2)}) collective-permute-start(bf16[1024,256]{1,0:T(8,128)(2,1)} %get-tuple-element.16.refs_0_), channel_id=1, source_target_pairs={{0,4},{1,3},{2,6},{3,1},{4,0},{5,7},{6,2},{7,5},{8,12},{9,11},{10,... | collective-permute-start | bytes 1572872 | tf_op jit(solution)/shard_map/ppermute | solution.py:364
  6.6 1.5 collective-permute-start.2
  8.1 2.6 %collective-permute-start.8 = (bf16[32,128,128]{2,1,0:T(8,128)(2,1)}, bf16[32,128,128]{2,1,0:T(8,128)(2,1)}, u32[]{:S(2)}, u32[]{:S(2)}) collective-permute-start(bf16[32,128,128]{2,1,0:T(8,128)(2,1)} %get-tuple-element.19.refs_0_), channel_id=1, source_target_pairs={{0,16},{16,0},{8,24},{24,8},{1,17},{17,1},{9,25},{25,9},{2,18},{18... | collective-permute-start | bytes 3145736 | tf_op jit(solution)/shard_map/ppermute | solution.py:422
  10.7 1.6 %collective-permute-start.7 = (bf16[32,128,128]{2,1,0:T(8,128)(2,1)}, bf16[32,128,128]{2,1,0:T(8,128)(2,1)}, u32[]{:S(2)}, u32[]{:S(2)}) collective-permute-start(bf16[32,128,128]{2,1,0:T(8,128)(2,1)} %get-tuple-element.19.refs_0_), channel_id=1, source_target_pairs={{0,8},{8,0},{16,24},{24,16},{1,9},{9,1},{17,25},{25,17},{2,10},{10... | collective-permute-start | bytes 3145736 | tf_op jit(solution)/shard_map/ppermute | solution.py:422
  12.3 0.8 select_reduce_fusion
  13.1 0.6 collective-permute-start
  13.7 0.7 fusion.3
  14.4 2.3 %reduce-window.6 = s32[8,8,128]{2,1,0:T(8,128)S(1)} reduce-window(s32[8,8,128]{2,1,0:T(8,128)S(1)} %fusion.3, s32[]{:T(128)} %constant.20.clone.1), window={size=1x1x128 pad=0_0x0_0x127_0}, to_apply=%region_1.2 | reduce-window | flops 1040384 | bytes 65540 | tf_op jit(solution)/shard_map/reduce-window
  16.6 0.3 slice_reduce_fusion
  17.1 0.7 fusion.2
  17.9 1.0 collective-permute-done.2.refs_1_
  18.8 1.8 %collective-permute-start.4 = (bf16[1024,256]{1,0:T(8,128)(2,1)}, bf16[1024,256]{1,0:T(8,128)(2,1)}, u32[]{:S(2)}, u32[]{:S(2)}) collective-permute-start(bf16[1024,256]{1,0:T(8,128)(2,1)} %collective-permute-done.2.refs_1_), channel_id=1, source_target_pairs={{0,4},{1,3},{2,6},{3,1},{4,0},{5,7},{6,2},{7,5},{8,12},{9,11},{10,... | collective-permute-start | bytes 1572872 | tf_op jit(solution)/shard_map/ppermute | solution.py:364
  20.6 1.3 multiply_add_fusion.refs_0_
  21.9 0.7 dynamic-slice_bitcast_fusion.scalars
  22.7 1.1 collective-permute-done.1
  23.8 0.6 pad_add_fusion.refs_1_.numbers
  24.4 3.9 %collective-permute-done.4.refs_3_ = bf16[1024,256]{1,0:T(8,128)(2,1)} collective-permute-done((bf16[1024,256]{1,0:T(8,128)(2,1)}, bf16[1024,256]{1,0:T(8,128)(2,1)}, u32[]{:S(2)}, u32[]{:S(2)}) %collective-permute-start.4) | collective-permute-done | bytes 524320 | tf_op jit(solution)/shard_map/ppermute | solution.py:364
  28.3 11.8 %pick_rows.1 = (bf16[4,3,256,256]{3,2,1,0:T(8,128)(2,1)}, bf16[4,3,256,256]{3,2,1,0:T(8,128)(2,1)}) custom-call(s32[48]{0:T(128)} %copy-done, s32[1,1024]{1,0:T(1,128)} %bitcast.28, bf16[1024,256]{1,0:T(8,128)(2,1)} %get-tuple-element.16.refs_0_, bf16[1024,256]{1,0:T(8,128)(2,1)} %collective-permute-done.2.refs_1_, ...), custom_call_target="tpu_custom_call" | custom-call | tf_op jit(solution)/shard_map/pick_rows/pallas_call | solution.py:78
  40.3 0.4 collective-permute-start.9
  40.7 1.7 %collective-permute-start.6 = (bf16[32,128,128]{2,1,0:T(8,128)(2,1)}, bf16[32,128,128]{2,1,0:T(8,128)(2,1)}, u32[]{:S(2)}, u32[]{:S(2)}) collective-permute-start(bf16[32,128,128]{2,1,0:T(8,128)(2,1)} %get-tuple-element.19.refs_0_), channel_id=1, source_target_pairs={{0,2},{1,5},{2,0},{3,7},{4,6},{5,1},{6,4},{7,3},{8,10},{9,13},{10,... | collective-permute-start | bytes 3145736 | tf_op jit(solution)/shard_map/ppermute | solution.py:364
  42.4 13.9 %collective-permute-done.8.refs_2_.refs_0_.refs_1_ = bf16[32,128,128]{2,1,0:T(8,128)(2,1)} collective-permute-done((bf16[32,128,128]{2,1,0:T(8,128)(2,1)}, bf16[32,128,128]{2,1,0:T(8,128)(2,1)}, u32[]{:S(2)}, u32[]{:S(2)}) %collective-permute-start.8) | collective-permute-done | bytes 1048608 | tf_op jit(solution)/shard_map/ppermute | solution.py:422
  56.5 0.5 collective-permute-start.11
  57.0 1.6 %collective-permute-start.14 = (bf16[32,128,128]{2,1,0:T(8,128)(2,1)}, bf16[32,128,128]{2,1,0:T(8,128)(2,1)}, u32[]{:S(2)}, u32[]{:S(2)}) collective-permute-start(bf16[32,128,128]{2,1,0:T(8,128)(2,1)} %tie.17), channel_id=1, source_target_pairs={{8,16},{16,8},{9,17},{17,9},{10,18},{18,10},{11,19},{19,11},{12,20... | collective-permute-start | bytes 3145736 | tf_op jit(solution)/shard_map/ppermute | solution.py:422
  58.6 1.5 collective-permute-start.15
  60.1 1.6 %collective-permute-start.13 = (bf16[32,128,128]{2,1,0:T(8,128)(2,1)}, bf16[32,128,128]{2,1,0:T(8,128)(2,1)}, u32[]{:S(2)}, u32[]{:S(2)}) collective-permute-start(bf16[32,128,128]{2,1,0:T(8,128)(2,1)} %tie.14.refs_2_), channel_id=1, source_target_pairs={{0,2},{1,5},{2,0},{3,7},{4,6},{5,1},{6,4},{7,3},{8,10},{9,13},{10,... | collective-permute-start | bytes 3145736 | tf_op jit(solution)/shard_map/ppermute | solution.py:364
  61.7 8.9 %product.6.refs_1_.refs_3_ = f32[512,2048]{1,0:T(8,128)} custom-call(s32[17,64]{1,0:T(8,128)} %pad_add_fusion.refs_1_.numbers, bf16[4,3,256,256]{3,2,1,0:T(8,128)(2,1)} %get-tuple-element.17.refs_1_.mine, bf16[4,3,256,256]{3,2,1,0:T(8,128)(2,1)} %collective-permute-done.5.theirs.refs_1_, bf16[32,128,128]{2,1,0:T(8,128)(2,1)} %get-tuple-element.19.refs_0_, ...), custom_call_target="tpu_custom_call" | custom-call | tf_op jit(solution)/shard_map/product/pallas_call | solution.py:188
  70.7 0.8 collective-permute-done.11.refs_0_
  71.6 0.5 collective-permute-start.18
  72.1 12.2 %collective-permute-done.15.refs_6_.refs_0_ = bf16[32,128,128]{2,1,0:T(8,128)(2,1)} collective-permute-done((bf16[32,128,128]{2,1,0:T(8,128)(2,1)}, bf16[32,128,128]{2,1,0:T(8,128)(2,1)}, u32[]{:S(2)}, u32[]{:S(2)}) %collective-permute-start.15) | collective-permute-done | bytes 1048608 | tf_op jit(solution)/shard_map/ppermute | solution.py:422
  84.3 2.9 %choose.1.refs_0_ = bf16[32,128,128]{2,1,0:T(8,128)(2,1)} custom-call(s32[48]{0:T(128)} %copy-done, bf16[32,128,128]{2,1,0:T(8,128)(2,1)} %tie.18.refs_6_.a_ref, bf16[32,128,128]{2,1,0:T(8,128)(2,1)} %tie.19.b_ref), custom_call_target="tpu_custom_call" | custom-call | tf_op jit(solution)/shard_map/choose/pallas_call | solution.py:242
  87.2 0.6 collective-permute-start.20
  87.8 0.4 collective-permute-start.17
  88.2 6.6 %product.7 = (bf16[256,16384]{1,0:T(8,128)(2,1)}, bf16[256,2048]{1,0:T(8,128)(2,1)}) custom-call(s32[17,64]{1,0:T(8,128)} %pad_add_fusion.refs_1_.numbers, bf16[4,3,256,256]{3,2,1,0:T(8,128)(2,1)} %get-tuple-element.17.refs_1_.mine, bf16[4,3,256,256]{3,2,1,0:T(8,128)(2,1)} %collective-permute-done.5.theirs.refs_1_, bf16[32,128,128]{2,1,0:T(8,128)(2,1)} %choose.1.refs_0_, ...), custom_call_target="tpu_custom_call" | custom-call | tf_op jit(solution)/shard_map/product/pallas_call | solution.py:188
  94.8 1.7 %collective-permute-start.23 = (bf16[256,2048]{1,0:T(8,128)(2,1)}, bf16[256,2048]{1,0:T(8,128)(2,1)}, u32[]{:S(2)}, u32[]{:S(2)}) collective-permute-start(bf16[256,2048]{1,0:T(8,128)(2,1)} %get-tuple-element.21.refs_1_), channel_id=1, source_target_pairs={{0,4},{1,3},{2,6},{3,1},{4,0},{5,7},{6,2},{7,5},{8,12},{9,11},{10,... | collective-permute-start | bytes 3145736 | tf_op jit(solution)/shard_map/ppermute | solution.py:364
  96.5 10.3 %product.8 = (bf16[256,16384]{1,0:T(8,128)(2,1)}, bf16[256,2048]{1,0:T(8,128)(2,1)}) custom-call(s32[17,64]{1,0:T(8,128)} %pad_add_fusion.refs_1_.numbers, bf16[4,3,256,256]{3,2,1,0:T(8,128)(2,1)} %get-tuple-element.17.refs_1_.mine, bf16[4,3,256,256]{3,2,1,0:T(8,128)(2,1)} %collective-permute-done.5.theirs.refs_1_, ...), custom_call_target="tpu_custom_call", output_to_operand_aliasing={{0}: (7, {})} | custom-call | tf_op jit(solution)/shard_map/product/pallas_call | solution.py:188
  107.0 1.4 collective-permute-start.22
  108.5 1.3 collective-permute-start.16
  109.8 10.3 %product.9 = (bf16[256,16384]{1,0:T(8,128)(2,1)}, bf16[256,2048]{1,0:T(8,128)(2,1)}) custom-call(s32[17,64]{1,0:T(8,128)} %pad_add_fusion.refs_1_.numbers, bf16[4,3,256,256]{3,2,1,0:T(8,128)(2,1)} %get-tuple-element.17.refs_1_.mine, bf16[4,3,256,256]{3,2,1,0:T(8,128)(2,1)} %collective-permute-done.5.theirs.refs_1_, ...), custom_call_target="tpu_custom_call", output_to_operand_aliasing={{0}: (7, {})} | custom-call | tf_op jit(solution)/shard_map/product/pallas_call | solution.py:188
  120.1 0.5 collective-permute-start.25
  120.6 4.0 %put.3.refs_2_.refs_0_ = bf16[256,16384]{1,0:T(8,128)(2,1)} custom-call(s32[48]{0:T(128)} %copy-done, bf16[256,2048]{1,0:T(8,128)(2,1)} %collective-permute-done.23.refs_0_, bf16[256,16384]{1,0:T(8,128)(2,1)} %get-tuple-element.25.refs_1_), custom_call_target="tpu_custom_call", output_to_operand_aliasing={{}: (2, {})} | custom-call | tf_op jit(solution)/shard_map/put/pallas_call | solution.py:277
  124.6 2.9 %collective-permute-done.22.refs_1_.refs_0_ = bf16[256,2048]{1,0:T(8,128)(2,1)} collective-permute-done((bf16[256,2048]{1,0:T(8,128)(2,1)}, bf16[256,2048]{1,0:T(8,128)(2,1)}, u32[]{:S(2)}, u32[]{:S(2)}) %collective-permute-start.22) | collective-permute-done | bytes 1048608 | tf_op jit(solution)/shard_map/ppermute | solution.py:364
  127.6 7.7 %product.10.refs_1_ = bf16[256,2048]{1,0:T(8,128)(2,1)} custom-call(s32[17,64]{1,0:T(8,128)} %pad_add_fusion.refs_1_.numbers, bf16[4,3,256,256]{3,2,1,0:T(8,128)(2,1)} %get-tuple-element.17.refs_1_.mine, bf16[4,3,256,256]{3,2,1,0:T(8,128)(2,1)} %collective-permute-done.5.theirs.refs_1_, bf16[32,128,128]{2,1,0:T(8,128)(2,1)} %collective-permute-done.10.refs_4_.refs_0_, ...), custom_call_target="tpu_custom_call" | custom-call | tf_op jit(solution)/shard_map/product/pallas_call | solution.py:188
  135.2 0.3 collective-permute-start.24
  135.6 7.7 %product.11.refs_2_ = bf16[256,16384]{1,0:T(8,128)(2,1)} custom-call(s32[17,64]{1,0:T(8,128)} %pad_add_fusion.refs_1_.numbers, bf16[4,3,256,256]{3,2,1,0:T(8,128)(2,1)} %get-tuple-element.17.refs_1_.mine, bf16[4,3,256,256]{3,2,1,0:T(8,128)(2,1)} %collective-permute-done.5.theirs.refs_1_, ...), custom_call_target="tpu_custom_call", output_to_operand_aliasing={{}: (7, {})} | custom-call | tf_op jit(solution)/shard_map/product/pallas_call | solution.py:188
  143.3 6.5 %put.4.refs_1_ = bf16[256,16384]{1,0:T(8,128)(2,1)} custom-call(s32[48]{0:T(128)} %copy-done, bf16[256,2048]{1,0:T(8,128)(2,1)} %collective-permute-done.22.refs_1_.refs_0_, bf16[256,2048]{1,0:T(8,128)(2,1)} %collective-permute-done.25.refs_1_, bf16[256,16384]{1,0:T(8,128)(2,1)} %product.11.refs_2_), custom_call_target="tpu_custom_call", output_to_operand_aliasing={{}: (3, {})} | custom-call | tf_op jit(solution)/shard_map/put/pallas_call | solution.py:277
  149.8 0.7 collective-permute-done.24.refs_0_
  150.4 4.0 %put.5 = bf16[256,16384]{1,0:T(8,128)(2,1)} custom-call(s32[48]{0:T(128)} %copy-done, bf16[256,2048]{1,0:T(8,128)(2,1)} %collective-permute-done.24.refs_0_, bf16[256,16384]{1,0:T(8,128)(2,1)} %put.4.refs_1_), custom_call_target="tpu_custom_call", output_to_operand_aliasing={{}: (2, {})} | custom-call | tf_op jit(solution)/shard_map/put/pallas_call | solution.py:277
  (42 shorter events, 1.0 us)
Async XLA Ops:
  3.7 20.8 %collective-permute-start.3 = (bf16[1024,256]{1,0:T(8,128)(2,1)}, bf16[1024,256]{1,0:T(8,128)(2,1)}, u32[]{:S(2)}, u32[]{:S(2)}) collective-permute-start(bf16[1024,256]{1,0:T(8,128)(2,1)} %get-tuple-element.16.refs_0_), channel_id=1, source_target_pairs={{0,4},{1,3},{2,6},{3,1},{4,0},{5,7},{6,2},{7,5},{8,12},{9,11},{10,... | collective-permute-start | bytes 1572872 | tf_op jit(solution)/shard_map/ppermute | solution.py:364
  6.6 12.2 %collective-permute-start.2 = (bf16[1024,256]{1,0:T(8,128)(2,1)}, bf16[1024,256]{1,0:T(8,128)(2,1)}, u32[]{:S(2)}, u32[]{:S(2)}) collective-permute-start(bf16[1024,256]{1,0:T(8,128)(2,1)} %get-tuple-element.16.refs_0_), channel_id=1, source_target_pairs={{0,2},{1,5},{2,0},{3,7},{4,6},{5,1},{6,4},{7,3},{8,10},{9,13},{10,... | collective-permute-start | bytes 1572872 | tf_op jit(solution)/shard_map/ppermute | solution.py:364
  8.1 48.1 %collective-permute-start.8 = (bf16[32,128,128]{2,1,0:T(8,128)(2,1)}, bf16[32,128,128]{2,1,0:T(8,128)(2,1)}, u32[]{:S(2)}, u32[]{:S(2)}) collective-permute-start(bf16[32,128,128]{2,1,0:T(8,128)(2,1)} %get-tuple-element.19.refs_0_), channel_id=1, source_target_pairs={{0,16},{16,0},{8,24},{24,8},{1,17},{17,1},{9,25},{25,9},{2,18},{18... | collective-permute-start | bytes 3145736 | tf_op jit(solution)/shard_map/ppermute | solution.py:422
  10.7 45.7 %collective-permute-start.7 = (bf16[32,128,128]{2,1,0:T(8,128)(2,1)}, bf16[32,128,128]{2,1,0:T(8,128)(2,1)}, u32[]{:S(2)}, u32[]{:S(2)}) collective-permute-start(bf16[32,128,128]{2,1,0:T(8,128)(2,1)} %get-tuple-element.19.refs_0_), channel_id=1, source_target_pairs={{0,8},{8,0},{16,24},{24,16},{1,9},{9,1},{17,25},{25,17},{2,10},{10... | collective-permute-start | bytes 3145736 | tf_op jit(solution)/shard_map/ppermute | solution.py:422
  13.1 9.5 %collective-permute-start = (s32[4,64]{1,0:T(4,128)S(1)}, s32[4,64]{1,0:T(4,128)S(1)}, u32[]{:S(2)}, u32[]{:S(2)}) collective-permute-start(s32[4,64]{1,0:T(4,128)S(1)} %select_reduce_fusion), channel_id=1, source_target_pairs={{0,2},{1,5},{2,0},{3,7},{4,6},{5,1},{6,4},{7,3},{8,10},{9,13},{10,... | collective-permute-start | bytes 3080 | tf_op jit(solution)/shard_map/ppermute | solution.py:364
  18.8 9.5 %collective-permute-start.4 = (bf16[1024,256]{1,0:T(8,128)(2,1)}, bf16[1024,256]{1,0:T(8,128)(2,1)}, u32[]{:S(2)}, u32[]{:S(2)}) collective-permute-start(bf16[1024,256]{1,0:T(8,128)(2,1)} %collective-permute-done.2.refs_1_), channel_id=1, source_target_pairs={{0,4},{1,3},{2,6},{3,1},{4,0},{5,7},{6,2},{7,5},{8,12},{9,11},{10,... | collective-permute-start | bytes 1572872 | tf_op jit(solution)/shard_map/ppermute | solution.py:364
  22.6 5.8 %copy-start = (s32[48]{0:T(128)}, s32[48]{0:T(128)S(1)}, u32[]{:S(2)}) copy-start(s32[48]{0:T(128)S(1)} %dynamic-slice_bitcast_fusion.scalars) | copy-start | bytes 580
  22.6 1.2 collective-permute-start.1
  40.1 21.5 %collective-permute-start.5 = (bf16[4,3,256,256]{3,2,1,0:T(8,128)(2,1)}, bf16[4,3,256,256]{3,2,1,0:T(8,128)(2,1)}, u32[]{:S(2)}, u32[]{:S(2)}) collective-permute-start(bf16[4,3,256,256]{3,2,1,0:T(8,128)(2,1)} %get-tuple-element.18), channel_id=1, source_target_pairs={{0,1},{1,0},{2,3},{3,2},{4,5},{5,4},{6,7},{7,6},{8,9},{9,8},{10,11... | collective-permute-start | bytes 4718600 | tf_op jit(solution)/shard_map/ppermute | solution.py:364
  40.3 18.3 %collective-permute-start.9 = (bf16[32,128,128]{2,1,0:T(8,128)(2,1)}, bf16[32,128,128]{2,1,0:T(8,128)(2,1)}, u32[]{:S(2)}, u32[]{:S(2)}) collective-permute-start(bf16[32,128,128]{2,1,0:T(8,128)(2,1)} %get-tuple-element.19.refs_0_), channel_id=1, source_target_pairs={{0,1},{1,0},{2,3},{3,2},{4,5},{5,4},{6,7},{7,6},{8,9},{9,8},{10,11... | collective-permute-start | bytes 3145736 | tf_op jit(solution)/shard_map/ppermute | solution.py:364
  40.7 18.0 %collective-permute-start.6 = (bf16[32,128,128]{2,1,0:T(8,128)(2,1)}, bf16[32,128,128]{2,1,0:T(8,128)(2,1)}, u32[]{:S(2)}, u32[]{:S(2)}) collective-permute-start(bf16[32,128,128]{2,1,0:T(8,128)(2,1)} %get-tuple-element.19.refs_0_), channel_id=1, source_target_pairs={{0,2},{1,5},{2,0},{3,7},{4,6},{5,1},{6,4},{7,3},{8,10},{9,13},{10,... | collective-permute-start | bytes 3145736 | tf_op jit(solution)/shard_map/ppermute | solution.py:364
  56.5 15.1 %collective-permute-start.11 = (bf16[32,128,128]{2,1,0:T(8,128)(2,1)}, bf16[32,128,128]{2,1,0:T(8,128)(2,1)}, u32[]{:S(2)}, u32[]{:S(2)}) collective-permute-start(bf16[32,128,128]{2,1,0:T(8,128)(2,1)} %tie.13.refs_1_), channel_id=1, source_target_pairs={{0,2},{1,5},{2,0},{3,7},{4,6},{5,1},{6,4},{7,3},{8,10},{9,13},{10,... | collective-permute-start | bytes 3145736 | tf_op jit(solution)/shard_map/ppermute | solution.py:364
  57.0 14.6 %collective-permute-start.14 = (bf16[32,128,128]{2,1,0:T(8,128)(2,1)}, bf16[32,128,128]{2,1,0:T(8,128)(2,1)}, u32[]{:S(2)}, u32[]{:S(2)}) collective-permute-start(bf16[32,128,128]{2,1,0:T(8,128)(2,1)} %tie.17), channel_id=1, source_target_pairs={{8,16},{16,8},{9,17},{17,9},{10,18},{18,10},{11,19},{19,11},{12,20... | collective-permute-start | bytes 3145736 | tf_op jit(solution)/shard_map/ppermute | solution.py:422
  58.6 25.6 %collective-permute-start.15 = (bf16[32,128,128]{2,1,0:T(8,128)(2,1)}, bf16[32,128,128]{2,1,0:T(8,128)(2,1)}, u32[]{:S(2)}, u32[]{:S(2)}) collective-permute-start(bf16[32,128,128]{2,1,0:T(8,128)(2,1)} %tie.14.refs_2_), channel_id=1, source_target_pairs={{8,0},{16,24},{9,1},{17,25},{10,2},{18,26},{11,3},{19,27},{12,4},{... | collective-permute-start | bytes 3145736 | tf_op jit(solution)/shard_map/ppermute | solution.py:422
  60.1 24.2 %collective-permute-start.13 = (bf16[32,128,128]{2,1,0:T(8,128)(2,1)}, bf16[32,128,128]{2,1,0:T(8,128)(2,1)}, u32[]{:S(2)}, u32[]{:S(2)}) collective-permute-start(bf16[32,128,128]{2,1,0:T(8,128)(2,1)} %tie.14.refs_2_), channel_id=1, source_target_pairs={{0,2},{1,5},{2,0},{3,7},{4,6},{5,1},{6,4},{7,3},{8,10},{9,13},{10,... | collective-permute-start | bytes 3145736 | tf_op jit(solution)/shard_map/ppermute | solution.py:364
  70.6 13.7 %collective-permute-start.10 = (bf16[32,128,128]{2,1,0:T(8,128)(2,1)}, bf16[32,128,128]{2,1,0:T(8,128)(2,1)}, u32[]{:S(2)}, u32[]{:S(2)}) collective-permute-start(bf16[32,128,128]{2,1,0:T(8,128)(2,1)} %tie.15.refs_0_), channel_id=1, source_target_pairs={{0,1},{1,0},{2,3},{3,2},{4,5},{5,4},{6,7},{7,6},{8,9},{9,8},{10,11... | collective-permute-start | bytes 3145736 | tf_op jit(solution)/shard_map/ppermute | solution.py:364
  71.6 12.7 %collective-permute-start.12 = (bf16[32,128,128]{2,1,0:T(8,128)(2,1)}, bf16[32,128,128]{2,1,0:T(8,128)(2,1)}, u32[]{:S(2)}, u32[]{:S(2)}) collective-permute-start(bf16[32,128,128]{2,1,0:T(8,128)(2,1)} %tie.16.refs_1_), channel_id=1, source_target_pairs={{0,1},{1,0},{2,3},{3,2},{4,5},{5,4},{6,7},{7,6},{8,9},{9,8},{10,11... | collective-permute-start | bytes 3145736 | tf_op jit(solution)/shard_map/ppermute | solution.py:364
  71.6 24.9 %collective-permute-start.18 = (bf16[32,128,128]{2,1,0:T(8,128)(2,1)}, bf16[32,128,128]{2,1,0:T(8,128)(2,1)}, u32[]{:S(2)}, u32[]{:S(2)}) collective-permute-start(bf16[32,128,128]{2,1,0:T(8,128)(2,1)} %tie.13.refs_1_), channel_id=1, source_target_pairs={{0,1},{1,0},{2,3},{3,2},{4,5},{5,4},{6,7},{7,6},{8,9},{9,8},{10,11... | collective-permute-start | bytes 3145736 | tf_op jit(solution)/shard_map/ppermute | solution.py:364
  84.3 12.2 %collective-permute-start.19 = (bf16[32,128,128]{2,1,0:T(8,128)(2,1)}, bf16[32,128,128]{2,1,0:T(8,128)(2,1)}, u32[]{:S(2)}, u32[]{:S(2)}) collective-permute-start(bf16[32,128,128]{2,1,0:T(8,128)(2,1)} %tie.14.refs_2_), channel_id=1, source_target_pairs={{0,1},{1,0},{2,3},{3,2},{4,5},{5,4},{6,7},{7,6},{8,9},{9,8},{10,11... | collective-permute-start | bytes 3145736 | tf_op jit(solution)/shard_map/ppermute | solution.py:364
  87.2 9.3 %collective-permute-start.20 = (bf16[32,128,128]{2,1,0:T(8,128)(2,1)}, bf16[32,128,128]{2,1,0:T(8,128)(2,1)}, u32[]{:S(2)}, u32[]{:S(2)}) collective-permute-start(bf16[32,128,128]{2,1,0:T(8,128)(2,1)} %choose.1.refs_0_), channel_id=1, source_target_pairs={{0,1},{1,0},{2,3},{3,2},{4,5},{5,4},{6,7},{7,6},{8,9},{9,8},{10,11... | collective-permute-start | bytes 3145736 | tf_op jit(solution)/shard_map/ppermute | solution.py:364
  87.8 19.3 %collective-permute-start.17 = (bf16[32,128,128]{2,1,0:T(8,128)(2,1)}, bf16[32,128,128]{2,1,0:T(8,128)(2,1)}, u32[]{:S(2)}, u32[]{:S(2)}) collective-permute-start(bf16[32,128,128]{2,1,0:T(8,128)(2,1)} %choose.1.refs_0_), channel_id=1, source_target_pairs={{0,2},{1,5},{2,0},{3,7},{4,6},{5,1},{6,4},{7,3},{8,10},{9,13},{10,... | collective-permute-start | bytes 3145736 | tf_op jit(solution)/shard_map/ppermute | solution.py:364
  94.8 25.8 %collective-permute-start.23 = (bf16[256,2048]{1,0:T(8,128)(2,1)}, bf16[256,2048]{1,0:T(8,128)(2,1)}, u32[]{:S(2)}, u32[]{:S(2)}) collective-permute-start(bf16[256,2048]{1,0:T(8,128)(2,1)} %get-tuple-element.21.refs_1_), channel_id=1, source_target_pairs={{0,4},{1,3},{2,6},{3,1},{4,0},{5,7},{6,2},{7,5},{8,12},{9,11},{10,... | collective-permute-start | bytes 3145736 | tf_op jit(solution)/shard_map/ppermute | solution.py:364
  107.0 17.6 %collective-permute-start.21 = (bf16[32,128,128]{2,1,0:T(8,128)(2,1)}, bf16[32,128,128]{2,1,0:T(8,128)(2,1)}, u32[]{:S(2)}, u32[]{:S(2)}) collective-permute-start(bf16[32,128,128]{2,1,0:T(8,128)(2,1)} %tie.21.refs_3_), channel_id=1, source_target_pairs={{0,1},{1,0},{2,3},{3,2},{4,5},{5,4},{6,7},{7,6},{8,9},{9,8},{10,11... | collective-permute-start | bytes 3145736 | tf_op jit(solution)/shard_map/ppermute | solution.py:364
  107.0 20.5 %collective-permute-start.22 = (bf16[256,2048]{1,0:T(8,128)(2,1)}, bf16[256,2048]{1,0:T(8,128)(2,1)}, u32[]{:S(2)}, u32[]{:S(2)}) collective-permute-start(bf16[256,2048]{1,0:T(8,128)(2,1)} %get-tuple-element.23.refs_1_), channel_id=1, source_target_pairs={{0,2},{1,5},{2,0},{3,7},{4,6},{5,1},{6,4},{7,3},{8,10},{9,13},{10,... | collective-permute-start | bytes 3145736 | tf_op jit(solution)/shard_map/ppermute | solution.py:364
  108.5 19.1 %collective-permute-start.16 = (bf16[32,128,128]{2,1,0:T(8,128)(2,1)}, bf16[32,128,128]{2,1,0:T(8,128)(2,1)}, u32[]{:S(2)}, u32[]{:S(2)}) collective-permute-start(bf16[32,128,128]{2,1,0:T(8,128)(2,1)} %tie.20.refs_2_), channel_id=1, source_target_pairs={{0,1},{1,0},{2,3},{3,2},{4,5},{5,4},{6,7},{7,6},{8,9},{9,8},{10,11... | collective-permute-start | bytes 3145736 | tf_op jit(solution)/shard_map/ppermute | solution.py:364
  120.1 23.1 %collective-permute-start.25 = (bf16[256,2048]{1,0:T(8,128)(2,1)}, bf16[256,2048]{1,0:T(8,128)(2,1)}, u32[]{:S(2)}, u32[]{:S(2)}) collective-permute-start(bf16[256,2048]{1,0:T(8,128)(2,1)} %get-tuple-element.26), channel_id=1, source_target_pairs={{0,4},{1,3},{2,6},{3,1},{4,0},{5,7},{6,2},{7,5},{8,12},{9,11},{10,... | collective-permute-start | bytes 3145736 | tf_op jit(solution)/shard_map/ppermute | solution.py:364
  135.2 15.2 %collective-permute-start.24 = (bf16[256,2048]{1,0:T(8,128)(2,1)}, bf16[256,2048]{1,0:T(8,128)(2,1)}, u32[]{:S(2)}, u32[]{:S(2)}) collective-permute-start(bf16[256,2048]{1,0:T(8,128)(2,1)} %product.10.refs_1_), channel_id=1, source_target_pairs={{0,2},{1,5},{2,0},{3,7},{4,6},{5,1},{6,4},{7,3},{8,10},{9,13},{10,... | collective-permute-start | bytes 3145736 | tf_op jit(solution)/shard_map/ppermute | solution.py:364
